TPU v7x, 128 devices: a whole 4x4x4 slice. The times are simulated.
128 devices in a mesh: dp: 8 (over y, x_lo), tensor: 8 (over z, core), pipe: 2 (over x_hi).
Axes of the slice: x: 4 (x_hi: 2, x_lo: 2; x = x_hi * 2 + x_lo), y: 4, z: 4, core: 2. Of those that a mesh axis runs over, the one named last changes fastest.
Arguments:
- attention_out: bfloat16 [2, 1024, 16384], P('pipe', 'dp', 'tensor'), may hold values from -6 to 6
- signs: int32 [2, 16384], P('pipe', 'tensor'), may hold values from -1 to 1, as said below
- out_weight: bfloat16 [2, 16384, 16384], P('pipe', 'tensor', 'dp'), may hold values from -0.046875 to 0.046875
- residual_in: bfloat16 [1024, 16384], P('tensor', 'dp'), may hold values from -6 to 6
Outputs:
- residual_out: bfloat16 [2, 1024, 16384], P('pipe', 'tensor', 'dp')
Inputs may be any that keep to these rules, and one draw needn't show every extreme that they name: `signs`: each entry is 1 or -1.
All inputs are finite; a program needn't handle non-finite values.
Results may differ from a plain program's by a relative error of at most 0.018.
Values may be sent and summed in bfloat16 or wider, within the bound.
No kernel may reach another device: no remote copies, remote signals or barrier semaphores. Data moves between devices by JAX's collectives and lax.ppermute only.
A program may use at most 192 MiB of HBM per device.

v0:
```python
import math

import jax
import jax.numpy as jnp
from jax import lax
from jax.sharding import PartitionSpec as P


def from_behind(value, axis, steps):
    count = lax.axis_size(axis)
    first, last = (max(0, -steps), min(count, count - steps))
    return lax.ppermute(value, axis, [(source, source + steps) for source in range(first, last)])


def hadamard_table(length, dtype):
    indices = jnp.arange(length, dtype=jnp.int32)
    common = indices[:, None] & indices[None, :]
    parity = jnp.zeros((length, length), jnp.int32)
    for bit_number in range(max(length.bit_length() - 1, 0)):
        parity = parity ^ common >> bit_number & 1
    return (1 - 2 * parity).astype(dtype)


def rotate(flipped, length):
    inner_size = min(length, 128)
    outer_size = length // inner_size
    blocks = flipped.reshape(flipped.shape[:-1] + (outer_size, inner_size))
    blocks = jnp.einsum(
        "rab,bc->rac",
        blocks,
        hadamard_table(inner_size, jnp.bfloat16),
        preferred_element_type=jnp.float32,
    )
    blocks = jnp.einsum(
        "rab,ac->rcb",
        blocks,
        hadamard_table(outer_size, jnp.float32),
        precision=lax.Precision.HIGHEST,
    )
    return blocks.reshape(flipped.shape)


def on_device(attention_out, signs, out_weight, residual_in):
    flipped = attention_out[0] * signs[0].astype(jnp.bfloat16)[None, :]
    local_width = flipped.shape[1]
    tensor_count = lax.axis_size("tensor")
    norm_factor = jnp.float32(1.0 / math.sqrt(local_width * tensor_count))
    full_rows = lax.all_to_all(flipped, "tensor", split_axis=0, concat_axis=1, tiled=True)
    turned = (rotate(full_rows, local_width * tensor_count) * norm_factor).astype(jnp.bfloat16)
    rotated = lax.all_to_all(turned, "tensor", split_axis=1, concat_axis=0, tiled=True)
    weight = out_weight[0]
    partial_value = jnp.dot(
        rotated,
        lax.all_gather(weight, "dp", axis=1, tiled=True),
        preferred_element_type=jnp.float32,
    ).astype(jnp.bfloat16)
    partial_terms = lax.all_to_all(partial_value, "dp", split_axis=1, concat_axis=0, tiled=True)
    summed = lax.psum_scatter(
        partial_terms.astype(jnp.float32).astype(jnp.bfloat16),
        "tensor",
        scatter_dimension=0,
        tiled=True,
    ).astype(jnp.float32)
    is_first = lax.axis_index("pipe") == 0
    leading = (residual_in.astype(jnp.float32) + summed).astype(jnp.bfloat16)
    passed = from_behind(leading, "pipe", 1)
    downstream = (passed.astype(jnp.float32) + summed).astype(jnp.bfloat16)
    return jnp.where(is_first, leading, downstream)[None]


def solution(mesh):
    in_specs = (
        P("pipe", "dp", "tensor"),
        P("pipe", "tensor"),
        P("pipe", "tensor", "dp"),
        P("tensor", "dp"),
    )
    out_specs = P("pipe", "tensor", "dp")
    return jax.shard_map(
        on_device, mesh=mesh, in_specs=in_specs, out_specs=out_specs, check_vma=False
    )
```

profile of v0, /device:TPU:4, one launch (start us, length us, event | category | flops | bytes accessed | tf_op | source)
XLA Modules:
  0.0 1425.5 jit_solution(7028962890193229490)
XLA Ops:
  6.5 0.0 copy-start.2
  6.5 0.0 copy-start.1
  6.5 0.0 all-gather.3.cloned.1.call-start
  6.5 0.7 all-gather.3.cloned.1.call-update
  7.3 0.0 reduce-scatter.2.cloned.1.call-start
  7.3 0.0 copy-done.2
  7.4 0.2 copy-done.1
  7.6 15.5 %all_to_all.48 = bf16[8,16,2048]{2,1,0:T(8,128)(2,1)S(1)} all-to-all(bf16[8,16,2048]{2,1,0:T(8,128)(2,1)S(1)} %broadcast_multiply_fusion), channel_id=1, replica_groups=mesh['dp'=8,'tensor'=8,'pipe'=2] {'tensor'}, dimensions={0} | all-to-all | bytes 1048576 | tf_op jit(solution)/shard_map/all_to_all | solution.py:48
  23.1 0.3 copy.9
  23.4 0.2 reshape.24
  23.7 0.3 fusion.13
  24.0 1.1 fusion.6
  25.1 0.2 convert_element_type.46
  25.3 0.3 copy.11
  25.6 12.8 all_to_all.49
  38.4 1242.0 %all-gather.3.cloned.1.call-done = bf16[1,2048,16384]{2,1,0:T(8,128)(2,1)} async-done(((bf16[1,2048,2048]{2,1,0:T(8,128)(2,1)}), bf16[1,2048,16384]{2,1,0:T(8,128)(2,1)}) %all-gather.3.cloned.1.call-update) | async-done | bytes 67108880 | tf_op jit(solution)/shard_map/all_gather | solution.py:54
  1280.5 25.3 %fusion.2 = bf16[128,16384]{1,0:T(8,128)(2,1)} fusion(bf16[128,2048]{1,0:T(8,128)(2,1)S(1)} %bitcast.33, bf16[1,2048,16384]{2,1,0:T(8,128)(2,1)} %all-gather.3.cloned.1.call-done), kind=kOutput, calls=%fused_computation.2 | convolution fusion | flops 8592031744 | bytes 71827456 | tf_op jit(solution)/shard_map/dot_general | solution.py:52
  1305.7 2.5 copy.17
  1308.2 0.0 copy-start
  1308.3 55.3 %all_to_all.50 = bf16[128,8,2048]{2,0,1:T(8,128)(2,1)} all-to-all(bf16[128,8,2048]{2,0,1:T(8,128)(2,1)S(1)} %bitcast.32), channel_id=1, replica_groups=mesh['dp'=8,'tensor'=8,'pipe'=2] {'dp'}, dimensions={1} | all-to-all | bytes 8388608 | tf_op jit(solution)/shard_map/all_to_all | solution.py:57
  1363.6 0.0 reduce-scatter.2.cloned.1.call-update
  1363.6 37.8 %reduce-scatter.2.cloned.1.call-done = bf16[128,2048]{1,0:T(8,128)(2,1)} async-done(((bf16[1024,2048]{1,0:T(8,128)(2,1)}), bf16[128,2048]{1,0:T(8,128)(2,1)}) %reduce-scatter.2.cloned.1.call-update) | async-done | bytes 524304 | tf_op jit(solution)/shard_map/reduce_scatter | solution.py:58
  1401.4 0.0 copy-done
  1401.4 1.2 fusion.7
  1402.6 1.3 collective-permute-start
  1403.9 12.7 collective-permute-done
  1416.6 2.1 fusion.10
  (2 shorter events, 0.1 us)
Async XLA Ops:
  6.5 0.8 copy-start.2
  6.5 1.1 copy-start.1
  6.5 1273.9 %all-gather.3.cloned.1.call-start = ((), (), s32[]{:S(2)}) async-start(), calls=%async_computation.5 | async-start | bytes 75497472 | tf_op jit(solution)/shard_map/all_gather | solution.py:54
  7.3 1394.1 %reduce-scatter.2.cloned.1.call-start = ((), (), s32[]{:S(2)}) async-start(), calls=%async_computation.4 | async-start | bytes 4718592 | tf_op jit(solution)/shard_map/reduce_scatter | solution.py:58
  1308.2 93.1 %copy-start = (bf16[128,2048]{1,0:T(8,128)(2,1)S(1)}, bf16[128,2048]{1,0:T(8,128)(2,1)}, u32[]{:S(2)}) copy-start(bf16[128,2048]{1,0:T(8,128)(2,1)} %param.7) | copy-start | bytes 1572868
  1402.6 14.0 collective-permute-start
Sparse Core Ops, SparseCore 0:
  9.0 1271.4 all-gather.2
  1363.7 37.6 reduce-scatter.1
where the time goes:
time: 1430 us
  waiting for transfers between devices  1290 us (90%)
  blocking collectives  83.6 us (6%)
  matrix products  26.7 us (2%)
    all_gather x1, waiting for transfers between devices, on_device(): lax.all_gather(weight, 'dp', axis=1, tiled=True)  1240 us
    all_to_all x1, blocking collectives, on_device(): lax.all_to_all(partial_value, 'dp', split_axis=1, concat_axis=0, tiled=True)  55.3 us
    reduce_scatter x1, waiting for transfers between devices, on_device(): lax.psum_scatter(partial_terms.astype(jnp.float32).astype(jnp.bfloat16),...  37.8 us
  transfers between devices with their start and end apart: 3, of which 3 were waited for; matrix products, arithmetic and copies ran while one was open for 0% of the time, Pallas kernels for 0%

commit v1 on v0

v1 whole, which is shorter than its diff:
```python
import math

import jax
import jax.numpy as jnp
import numpy as np
from jax import lax
from jax.experimental import pallas as pl
from jax.experimental.pallas import tpu as pltpu
from jax.sharding import PartitionSpec as P

CHUNKS = 2
LANES = 128


def hadamard(length):
    table = np.array([[1]], np.int32)
    while table.shape[0] < length:
        table = np.block([[table, table], [table, -table]])
    return table


def move(value, axis, target):
    return lax.ppermute(value, axis, [(i, target(i)) for i in range(lax.axis_size(axis))])


def ring(steps, flip=0):
    return lambda i: (i // 2 + steps) % 4 * 2 + (i % 2 ^ flip)


def rotate_kernel(scale, x_ref, s_ref, h_ref, o_ref):
    rows, width = o_ref.shape
    pieces = width // LANES
    signs = s_ref[...].astype(jnp.float32)
    for r in range(0, rows, 32):
        part = []
        for a in range(pieces):
            cols = slice(a * LANES, (a + 1) * LANES)
            x = (x_ref[r : r + 32, cols].astype(jnp.float32) * signs[:, cols]).astype(jnp.bfloat16)
            part.append(jnp.dot(x, h_ref[...], preferred_element_type=jnp.float32))
        step = 1
        while step < pieces:
            nxt = list(part)
            for a in range(pieces):
                if not a & step:
                    nxt[a] = part[a] + part[a | step]
                    nxt[a | step] = part[a] - part[a | step]
            part = nxt
            step *= 2
        for a in range(pieces):
            o_ref[r : r + 32, a * LANES : (a + 1) * LANES] = (part[a] * scale).astype(jnp.bfloat16)


def rotate_local(x, signs, scale):
    return pl.pallas_call(
        lambda *refs: rotate_kernel(scale, *refs),
        out_shape=jax.ShapeDtypeStruct(x.shape, jnp.bfloat16),
        compiler_params=pltpu.CompilerParams(vmem_limit_bytes=16 << 20),
        cost_estimate=pl.CostEstimate(flops=2 * x.size * LANES, bytes_accessed=4 * x.size, transcendentals=0),
        name="rotate_local",
    )(x, signs.reshape(1, -1), jnp.asarray(hadamard(LANES), jnp.bfloat16))


def project_kernel(slot_ref, *refs):
    blocks, (w_ref, keep_ref, send_ref, lhs) = refs[:8], refs[8:]
    rows = blocks[0].shape[0]

    @pl.when(pl.program_id(0) == 0)
    def _():
        for i, ref in enumerate(blocks):
            start = pl.multiple_of(slot_ref[i] * rows, rows)
            lhs[pl.ds(start, rows), :] = ref[...]

    out = jnp.dot(lhs[...], w_ref[...], preferred_element_type=jnp.float32).astype(jnp.bfloat16)
    keep_ref[...] = out[: 4 * rows]
    send_ref[...] = out[4 * rows :]


def project(slots, blocks, weight, tile=512):
    rows, depth = blocks[0].shape
    width = weight.shape[1]
    half = jax.ShapeDtypeStruct((4 * rows, width), jnp.bfloat16)
    whole = pl.BlockSpec((rows, depth), lambda n, s: (0, 0))
    out = pl.BlockSpec((4 * rows, tile), lambda n, s: (0, n))
    return pl.pallas_call(
        project_kernel,
        out_shape=(half, half),
        grid_spec=pltpu.PrefetchScalarGridSpec(
            num_scalar_prefetch=1,
            grid=(width // tile,),
            in_specs=[whole] * 8 + [pl.BlockSpec((depth, tile), lambda n, s: (0, n))],
            out_specs=(out, out),
            scratch_shapes=[pltpu.VMEM((8 * rows, depth), jnp.bfloat16)],
        ),
        compiler_params=pltpu.CompilerParams(vmem_limit_bytes=32 << 20),
        cost_estimate=pl.CostEstimate(
            flops=2 * 8 * rows * depth * width, bytes_accessed=2 * (depth * width + 16 * rows * depth), transcendentals=0
        ),
        name="project",
    )(slots, *blocks, weight)


def f32(value):
    return value.astype(jnp.float32)


def after(value, earlier):
    return lax.optimization_barrier((value, earlier))[0]


def on_device(attention_out, signs, out_weight, residual_in):
    d, t = lax.axis_index("dp"), lax.axis_index("tensor")
    y, x, z, c = d // 2, d % 2, t // 2, t % 2
    first = lax.axis_index("pipe") == 0
    width = attention_out.shape[2]
    scale = 1.0 / math.sqrt(width * lax.axis_size("tensor"))
    weight = out_weight[0]

    local = rotate_local(attention_out[0], signs[0], scale)
    other = move(local, "tensor", lambda i: i ^ 1)
    paired = (f32(other) + (1 - 2 * c).astype(jnp.float32) * f32(local)).astype(jnp.bfloat16)

    def sign(k):
        u = z & ((z + k) % 4)
        return (1 - 2 * ((u ^ (u >> 1)) & 1)).astype(jnp.float32)

    rows = attention_out.shape[1] // CHUNKS
    slots = []
    for dy, dx in ORDER:
        by, bx = (y + dy) % 4, x ^ dx
        slots.append(((bx ^ c) * 4 + (by - z) % 4).astype(jnp.int32))
    slots = jnp.stack(slots)

    result = []
    for chunk in range(CHUNKS):
        at = slice(chunk * rows, (chunk + 1) * rows)
        mine = paired[at]
        terms = [mine] + [move(mine, "tensor", ring(-k)) for k in (1, 3, 2)]
        if chunk:
            terms = after(terms, own)
        total = f32(terms[0]) * sign(0)
        for k, term in zip((1, 3, 2), terms[1:]):
            total = total + f32(term) * sign(k)
        own = total.astype(jnp.bfloat16)

        got = {(0, 0): own}
        got[0, 1] = move(own, "dp", ring(0, 1))
        for dy in (1, 3, 2):
            got[dy, 0] = move(own, "dp", ring(-dy))
        for dy in (1, 3):
            got[dy, 1] = move(got[0, 1], "dp", ring(-dy))
        got[2, 1] = move(got[2, 0], "dp", ring(0, 1))

        keep, send = project(slots, [got[o] for o in ORDER], weight)
        came = move(send, "tensor", lambda i: i ^ 1)
        if chunk:
            keep, came = after((keep, came), leading)

        def part(k):
            return f32(keep[k * rows : (k + 1) * rows]) + f32(came[k * rows : (k + 1) * rows])

        summed = part(0)
        for k in (1, 3, 2):
            summed = summed + f32(move(part(k).astype(jnp.bfloat16), "tensor", ring(k)))
        leading = (f32(residual_in[at]) + summed).astype(jnp.bfloat16)
        passed = lax.ppermute(leading, "pipe", [(0, 1)])
        downstream = (f32(passed) + summed).astype(jnp.bfloat16)
        result.append(jnp.where(first, leading, downstream))
    return jnp.concatenate(result, axis=0)[None]


ORDER = [(0, 0), (0, 1), (1, 0), (3, 0), (2, 0), (1, 1), (3, 1), (2, 1)]


def solution(mesh):
    in_specs = (
        P("pipe", "dp", "tensor"),
        P("pipe", "tensor"),
        P("pipe", "tensor", "dp"),
        P("tensor", "dp"),
    )
    out_specs = P("pipe", "tensor", "dp")
    return jax.shard_map(
        on_device, mesh=mesh, in_specs=in_specs, out_specs=out_specs, check_vma=False
    )
```

time: 1430 us -> 140 us (0.10)
  waiting for transfers between devices: 1290 us -> 69.4 us
  blocking collectives: 83.6 us -> 0 us
  starting transfers between devices: 1.33 us -> 39.7 us
  matrix products: 26.7 us -> 0 us
    all_gather x1 -> x0, waiting for transfers between devices: 1240 us -> none  [on_device(): lax.all_gather(weight, 'dp', axis=1, tiled=True)]
    all_to_all x3 -> x0, blocking collectives: 83.6 us -> none  [the longest x1 55.3 us: on_device(): lax.all_to_all(partial_value, 'dp', split_axis=1, concat_axis=0, tiled=True)]
    ppermute x1 -> x31, waiting for transfers between devices: 12.7 us -> 69.4 us  [the longest x29 61.6 us: move(): lax.ppermute(value, axis, [(i, target(i)) for i in range(lax.axis_size(ax...]
    ppermute x1 -> x31, starting transfers between devices: 1.29 us -> 39.7 us  [the longest x29 37.1 us: move(): lax.ppermute(value, axis, [(i, target(i)) for i in range(lax.axis_size(ax...]
    reduce_scatter x1 -> x0, waiting for transfers between devices: 37.8 us -> none  [on_device(): lax.psum_scatter(partial_terms.astype(jnp.float32).astype(jnp.bfloat16),...]
    dot_general x3 -> x0, matrix products: 26.7 us -> none  [the longest x1 25.3 us: on_device(): jnp.dot(rotated, lax.all_gather(weight, 'dp', axis=1, tiled=True), prefer...]
  transfers between devices with their start and end apart: 3 -> 31, of which waited for: 3 -> 22; matrix products, arithmetic and copies ran while one was open for 0% -> 4% of each run, Pallas kernels for 0% -> 5%
where the time goes in v1:
time: 140 us; the launch traced here: 139 us
  waiting for transfers between devices  69.4 us (50%)
  starting transfers between devices  39.7 us (28%)
  Pallas kernels  13.7 us (10%)
  other arithmetic  8.93 us (6%)
  local copies, waits for them, and re-layouts  7.01 us (5%)
    ppermute x29, waiting for transfers between devices, move(): lax.ppermute(value, axis, [(i, target(i)) for i in range(lax.axis_size(ax...  61.6 us
    ppermute x29, starting transfers between devices, move(): lax.ppermute(value, axis, [(i, target(i)) for i in range(lax.axis_size(ax...  37.1 us
    pallas_call x2, Pallas kernels, project(): pl.pallas_call(project_kernel, out_shape=(half, half), grid_spec=pltpu.Pr...  13 us
    ppermute x2, waiting for transfers between devices, on_device(): passed = lax.ppermute(leading, 'pipe', [(0, 1)])  7.8 us
    unnamed x18, local copies, waits for them, and re-layouts  6.88 us
  transfers between devices with their start and end apart: 31, of which 22 were waited for; matrix products, arithmetic and copies ran while one was open for 4% of the time, Pallas kernels for 5%

profile of v1, /device:TPU:4, one launch (start us, length us, event | category | flops | bytes accessed | tf_op | source)
XLA Modules:
  0.0 138.9 jit_solution(6676882682173857046)
XLA Ops:
  0.0 1.0 copy-done
  1.0 0.8 copy-done.1
  1.8 0.7 copy-done.2
  2.5 0.7 rotate_local.1
  3.3 1.9 %collective-permute-done = bf16[128,2048]{1,0:T(8,128)(2,1)S(1)} collective-permute-done((bf16[128,2048]{1,0:T(8,128)(2,1)S(1)}, bf16[128,2048]{1,0:T(8,128)(2,1)S(1)}, u32[]{:S(2)}, u32[]{:S(2)}) %collective-permute-start) | collective-permute-done | bytes 524320 | tf_op jit(solution)/shard_map/ppermute | solution.py:23
  5.2 0.2 add_convert_fusion
  5.4 4.1 %collective-permute-start.1 = (bf16[64,2048]{1,0:T(8,128)(2,1)S(1)}, bf16[64,2048]{1,0:T(8,128)(2,1)S(1)}, u32[]{:S(2)}, u32[]{:S(2)}) collective-permute-start(bf16[64,2048]{1,0:T(8,128)(2,1)S(1)} %get-tuple-element.31), channel_id=1, source_target_pairs={{0,12},{2,14},{4,0},{6,2},{8,4},{10,6},{12,8},{14,10},{1,13},{3,15... | collective-permute-start | bytes 786440 | tf_op jit(solution)/shard_map/ppermute | solution.py:23
  9.5 1.9 %collective-permute-start.3 = (bf16[64,2048]{1,0:T(8,128)(2,1)S(1)}, bf16[64,2048]{1,0:T(8,128)(2,1)S(1)}, u32[]{:S(2)}, u32[]{:S(2)}) collective-permute-start(bf16[64,2048]{1,0:T(8,128)(2,1)S(1)} %get-tuple-element.31), channel_id=1, source_target_pairs={{0,8},{2,10},{4,12},{6,14},{8,0},{10,2},{12,4},{14,6},{1,9},{3,11}... | collective-permute-start | bytes 786440 | tf_op jit(solution)/shard_map/ppermute | solution.py:23
  11.4 1.4 collective-permute-start.16
  12.8 0.9 collective-permute-start.17
  13.6 8.2 %collective-permute-done.1 = bf16[64,2048]{1,0:T(8,128)(2,1)S(1)} collective-permute-done((bf16[64,2048]{1,0:T(8,128)(2,1)S(1)}, bf16[64,2048]{1,0:T(8,128)(2,1)S(1)}, u32[]{:S(2)}, u32[]{:S(2)}) %collective-permute-start.1) | collective-permute-done | bytes 262176 | tf_op jit(solution)/shard_map/ppermute | solution.py:23
  21.8 3.7 %collective-permute-done.2 = bf16[64,2048]{1,0:T(8,128)(2,1)S(1)} collective-permute-done((bf16[64,2048]{1,0:T(8,128)(2,1)S(1)}, bf16[64,2048]{1,0:T(8,128)(2,1)S(1)}, u32[]{:S(2)}, u32[]{:S(2)}) %collective-permute-start.2) | collective-permute-done | bytes 262176 | tf_op jit(solution)/shard_map/ppermute | solution.py:23
  25.5 0.2 add_convert_fusion.12.refs_0_
  25.8 3.3 %collective-permute-start.7 = (bf16[64,2048]{1,0:T(8,128)(2,1)S(1)}, bf16[64,2048]{1,0:T(8,128)(2,1)S(1)}, u32[]{:S(2)}, u32[]{:S(2)}) collective-permute-start(bf16[64,2048]{1,0:T(8,128)(2,1)S(1)} %add_convert_fusion.12.refs_0_), channel_id=1, source_target_pairs={{0,64},{16,80},{32,96},{48,112},{64,0},{80,16},{96,32},{112,48},{1... | collective-permute-start | bytes 786440 | tf_op jit(solution)/shard_map/ppermute | solution.py:23
  29.0 1.2 collective-permute-start.4
  30.2 0.3 collective-permute-start.18
  30.5 1.1 collective-permute-start.5
  31.6 2.9 %collective-permute-start.6 = (bf16[64,2048]{1,0:T(8,128)(2,1)S(1)}, bf16[64,2048]{1,0:T(8,128)(2,1)S(1)}, u32[]{:S(2)}, u32[]{:S(2)}) collective-permute-start(bf16[64,2048]{1,0:T(8,128)(2,1)S(1)} %add_convert_fusion.12.refs_0_), channel_id=1, source_target_pairs={{0,32},{16,48},{32,64},{48,80},{64,96},{80,112},{96,0},{112,16},{1... | collective-permute-start | bytes 786440 | tf_op jit(solution)/shard_map/ppermute | solution.py:23
  34.5 0.5 collective-permute-done.7.refs_4_
  35.1 1.2 collective-permute-start.10
  36.3 1.6 %collective-permute-done.4.refs_1_ = bf16[64,2048]{1,0:T(8,128)(2,1)S(1)} collective-permute-done((bf16[64,2048]{1,0:T(8,128)(2,1)S(1)}, bf16[64,2048]{1,0:T(8,128)(2,1)S(1)}, u32[]{:S(2)}, u32[]{:S(2)}) %collective-permute-start.4) | collective-permute-done | bytes 262176 | tf_op jit(solution)/shard_map/ppermute | solution.py:23
  37.9 2.1 %collective-permute-start.8 = (bf16[64,2048]{1,0:T(8,128)(2,1)S(1)}, bf16[64,2048]{1,0:T(8,128)(2,1)S(1)}, u32[]{:S(2)}, u32[]{:S(2)}) collective-permute-start(bf16[64,2048]{1,0:T(8,128)(2,1)S(1)} %collective-permute-done.4.refs_1_), channel_id=1, source_target_pairs={{0,96},{16,112},{32,0},{48,16},{64,32},{80,48},{96,64},{112,80},{1... | collective-permute-start | bytes 786440 | tf_op jit(solution)/shard_map/ppermute | solution.py:23
  40.0 0.2 collective-permute-start.9
  40.3 1.5 %collective-permute-done.5.refs_2_ = bf16[64,2048]{1,0:T(8,128)(2,1)S(1)} collective-permute-done((bf16[64,2048]{1,0:T(8,128)(2,1)S(1)}, bf16[64,2048]{1,0:T(8,128)(2,1)S(1)}, u32[]{:S(2)}, u32[]{:S(2)}) %collective-permute-start.5) | collective-permute-done | bytes 262176 | tf_op jit(solution)/shard_map/ppermute | solution.py:23
  41.8 1.5 %collective-permute-done.6.refs_3_ = bf16[64,2048]{1,0:T(8,128)(2,1)S(1)} collective-permute-done((bf16[64,2048]{1,0:T(8,128)(2,1)S(1)}, bf16[64,2048]{1,0:T(8,128)(2,1)S(1)}, u32[]{:S(2)}, u32[]{:S(2)}) %collective-permute-start.6) | collective-permute-done | bytes 262176 | tf_op jit(solution)/shard_map/ppermute | solution.py:23
  43.3 1.6 %collective-permute-done.8.refs_5_ = bf16[64,2048]{1,0:T(8,128)(2,1)S(1)} collective-permute-done((bf16[64,2048]{1,0:T(8,128)(2,1)S(1)}, bf16[64,2048]{1,0:T(8,128)(2,1)S(1)}, u32[]{:S(2)}, u32[]{:S(2)}) %collective-permute-start.8) | collective-permute-done | bytes 262176 | tf_op jit(solution)/shard_map/ppermute | solution.py:23
  44.8 2.7 %collective-permute-done.9.refs_6_ = bf16[64,2048]{1,0:T(8,128)(2,1)S(1)} collective-permute-done((bf16[64,2048]{1,0:T(8,128)(2,1)S(1)}, bf16[64,2048]{1,0:T(8,128)(2,1)S(1)}, u32[]{:S(2)}, u32[]{:S(2)}) %collective-permute-start.9) | collective-permute-done | bytes 262176 | tf_op jit(solution)/shard_map/ppermute | solution.py:23
  47.6 3.4 %copy-done.3 = bf16[1,2048,2048]{2,1,0:T(8,128)(2,1)S(1)} copy-done((bf16[1,2048,2048]{2,1,0:T(8,128)(2,1)S(1)}, bf16[1,2048,2048]{2,1,0:T(8,128)(2,1)}, u32[]{:S(2)}) %copy-start.3) | copy-done | bytes 8388632
  50.9 6.5 %project.2 = (bf16[256,2048]{1,0:T(8,128)(2,1)S(1)}, bf16[256,2048]{1,0:T(8,128)(2,1)S(1)}) custom-call(s32[8]{0:T(128)S(1)} %stack.35.slot_ref, bf16[64,2048]{1,0:T(8,128)(2,1)S(1)} %add_convert_fusion.12.refs_0_, bf16[64,2048]{1,0:T(8,128)(2,1)S(1)} %collective-permute-done.4.refs_1_, bf16[64,2048]{1,0:T(8,128)(2,1)S(1)} %collective-permute-done.5.refs_2_, ...), custom_call_target="tpu_custom_call" | custom-call | flops 4294967296 | bytes 12582912 | tf_op jit(solution)/shard_map/project/pallas_call | solution.py:84
  57.5 1.3 add_convert_fusion.6.refs_0_
  58.9 1.3 collective-permute-start.19
  60.1 2.1 %collective-permute-start.22 = (bf16[64,2048]{1,0:T(8,128)(2,1)S(1)}, bf16[64,2048]{1,0:T(8,128)(2,1)S(1)}, u32[]{:S(2)}, u32[]{:S(2)}) collective-permute-start(bf16[64,2048]{1,0:T(8,128)(2,1)S(1)} %add_convert_fusion.6.refs_0_), channel_id=1, source_target_pairs={{0,64},{16,80},{32,96},{48,112},{64,0},{80,16},{96,32},{112,48},{1... | collective-permute-start | bytes 786440 | tf_op jit(solution)/shard_map/ppermute | solution.py:23
  62.4 1.9 %collective-permute-start.21 = (bf16[64,2048]{1,0:T(8,128)(2,1)S(1)}, bf16[64,2048]{1,0:T(8,128)(2,1)S(1)}, u32[]{:S(2)}, u32[]{:S(2)}) collective-permute-start(bf16[64,2048]{1,0:T(8,128)(2,1)S(1)} %add_convert_fusion.6.refs_0_), channel_id=1, source_target_pairs={{0,32},{16,48},{32,64},{48,80},{64,96},{80,112},{96,0},{112,16},{1... | collective-permute-start | bytes 786440 | tf_op jit(solution)/shard_map/ppermute | solution.py:23
  64.2 3.4 %collective-permute-done.19.refs_1_ = bf16[64,2048]{1,0:T(8,128)(2,1)S(1)} collective-permute-done((bf16[64,2048]{1,0:T(8,128)(2,1)S(1)}, bf16[64,2048]{1,0:T(8,128)(2,1)S(1)}, u32[]{:S(2)}, u32[]{:S(2)}) %collective-permute-start.19) | collective-permute-done | bytes 262176 | tf_op jit(solution)/shard_map/ppermute | solution.py:23
  67.6 1.2 collective-permute-start.23
  68.9 1.9 %collective-permute-done.22.refs_4_ = bf16[64,2048]{1,0:T(8,128)(2,1)S(1)} collective-permute-done((bf16[64,2048]{1,0:T(8,128)(2,1)S(1)}, bf16[64,2048]{1,0:T(8,128)(2,1)S(1)}, u32[]{:S(2)}, u32[]{:S(2)}) %collective-permute-start.22) | collective-permute-done | bytes 262176 | tf_op jit(solution)/shard_map/ppermute | solution.py:23
  70.8 4.2 %collective-permute-done.20.refs_2_ = bf16[64,2048]{1,0:T(8,128)(2,1)S(1)} collective-permute-done((bf16[64,2048]{1,0:T(8,128)(2,1)S(1)}, bf16[64,2048]{1,0:T(8,128)(2,1)S(1)}, u32[]{:S(2)}, u32[]{:S(2)}) %collective-permute-start.20) | collective-permute-done | bytes 262176 | tf_op jit(solution)/shard_map/ppermute | solution.py:23
  75.0 0.8 collective-permute-start.25
  75.8 4.1 %collective-permute-done.23.refs_5_ = bf16[64,2048]{1,0:T(8,128)(2,1)S(1)} collective-permute-done((bf16[64,2048]{1,0:T(8,128)(2,1)S(1)}, bf16[64,2048]{1,0:T(8,128)(2,1)S(1)}, u32[]{:S(2)}, u32[]{:S(2)}) %collective-permute-start.23) | collective-permute-done | bytes 262176 | tf_op jit(solution)/shard_map/ppermute | solution.py:23
  79.9 1.4 collective-permute-done.24.refs_6_
  81.3 0.6 collective-permute-done.25.refs_7_
  81.9 6.5 %project.3 = (bf16[256,2048]{1,0:T(8,128)(2,1)S(1)}, bf16[256,2048]{1,0:T(8,128)(2,1)S(1)}) custom-call(s32[8]{0:T(128)S(1)} %stack.35.slot_ref, bf16[64,2048]{1,0:T(8,128)(2,1)S(1)} %add_convert_fusion.6.refs_0_, bf16[64,2048]{1,0:T(8,128)(2,1)S(1)} %collective-permute-done.19.refs_1_, bf16[64,2048]{1,0:T(8,128)(2,1)S(1)} %collective-permute-done.20.refs_2_, ...), custom_call_target="tpu_custom_call" | custom-call | flops 4294967296 | bytes 12582912 | tf_op jit(solution)/shard_map/project/pallas_call | solution.py:84
  88.5 0.3 add_convert_fusion.11
  88.8 4.1 %collective-permute-start.13 = (bf16[64,2048]{1,0:T(8,128)(2,1)S(1)}, bf16[64,2048]{1,0:T(8,128)(2,1)S(1)}, u32[]{:S(2)}, u32[]{:S(2)}) collective-permute-start(bf16[64,2048]{1,0:T(8,128)(2,1)S(1)} %get-tuple-element.30), channel_id=1, source_target_pairs={{0,12},{2,14},{4,0},{6,2},{8,4},{10,6},{12,8},{14,10},{1,13},{3,15... | collective-permute-start | bytes 786440 | tf_op jit(solution)/shard_map/ppermute | solution.py:23
  93.0 1.2 collective-permute-start.14
  94.2 5.5 %collective-permute-done.12 = bf16[64,2048]{1,0:T(8,128)(2,1)S(1)} collective-permute-done((bf16[64,2048]{1,0:T(8,128)(2,1)S(1)}, bf16[64,2048]{1,0:T(8,128)(2,1)S(1)}, u32[]{:S(2)}, u32[]{:S(2)}) %collective-permute-start.12) | collective-permute-done | bytes 262176 | tf_op jit(solution)/shard_map/ppermute | solution.py:23
  99.7 5.1 %collective-permute-done.13 = bf16[64,2048]{1,0:T(8,128)(2,1)S(1)} collective-permute-done((bf16[64,2048]{1,0:T(8,128)(2,1)S(1)}, bf16[64,2048]{1,0:T(8,128)(2,1)S(1)}, u32[]{:S(2)}, u32[]{:S(2)}) %collective-permute-start.13) | collective-permute-done | bytes 262176 | tf_op jit(solution)/shard_map/ppermute | solution.py:23
  104.8 1.7 %collective-permute-done.14 = bf16[64,2048]{1,0:T(8,128)(2,1)S(1)} collective-permute-done((bf16[64,2048]{1,0:T(8,128)(2,1)S(1)}, bf16[64,2048]{1,0:T(8,128)(2,1)S(1)}, u32[]{:S(2)}, u32[]{:S(2)}) %collective-permute-start.14) | collective-permute-done | bytes 262176 | tf_op jit(solution)/shard_map/ppermute | solution.py:23
  106.5 0.9 add_convert_fusion.8
  107.4 1.0 copy-done.5
  108.4 1.0 add_convert_fusion.5
  109.4 1.1 collective-permute-start.27
  110.5 2.1 %collective-permute-start.28 = (bf16[64,2048]{1,0:T(8,128)(2,1)}, bf16[64,2048]{1,0:T(8,128)(2,1)}, u32[]{:S(2)}, u32[]{:S(2)}) collective-permute-start(bf16[64,2048]{1,0:T(8,128)(2,1)} %get-tuple-element.27), channel_id=1, source_target_pairs={{0,12},{2,14},{4,0},{6,2},{8,4},{10,6},{12,8},{14,10},{1,13},{3,15... | collective-permute-start | bytes 786440 | tf_op jit(solution)/shard_map/ppermute | solution.py:23
  112.6 0.3 collective-permute-start.29
  112.9 1.3 collective-permute-start.15
  114.2 5.6 %collective-permute-done.27 = bf16[64,2048]{1,0:T(8,128)(2,1)} collective-permute-done((bf16[64,2048]{1,0:T(8,128)(2,1)}, bf16[64,2048]{1,0:T(8,128)(2,1)}, u32[]{:S(2)}, u32[]{:S(2)}) %collective-permute-start.27) | collective-permute-done | bytes 262176 | tf_op jit(solution)/shard_map/ppermute | solution.py:23
  119.8 3.9 %collective-permute-done.28 = bf16[64,2048]{1,0:T(8,128)(2,1)} collective-permute-done((bf16[64,2048]{1,0:T(8,128)(2,1)}, bf16[64,2048]{1,0:T(8,128)(2,1)}, u32[]{:S(2)}, u32[]{:S(2)}) %collective-permute-start.28) | collective-permute-done | bytes 262176 | tf_op jit(solution)/shard_map/ppermute | solution.py:23
  123.7 1.0 collective-permute-done.29
  124.7 1.5 %add_convert_fusion.2 = bf16[64,2048]{1,0:T(8,128)(2,1)S(1)} fusion(bf16[128,2048]{1,0:T(8,128)(2,1)} %param.8, bf16[64,2048]{1,0:T(8,128)(2,1)} %collective-permute-done.29, bf16[64,2048]{1,0:T(8,128)(2,1)} %collective-permute-done.28, bf16[64,2048]{1,0:T(8,128)(2,1)} %collective-permute-done.27, bf16[256,2048]{1,0:T(8,128)(2,1)} %copy-done.5, ...), kind=kLoop, calls=%fused_computation.3 | loop fusion | flops 1572864 | bytes 1835008 | tf_op jit(solution)/shard_map/convert_element_type | solution.py:164
  126.2 1.3 collective-permute-start.30
  127.5 1.3 fusion
  128.8 7.8 %collective-permute-done.30 = bf16[64,2048]{1,0:T(8,128)(2,1)S(1)} collective-permute-done((bf16[64,2048]{1,0:T(8,128)(2,1)S(1)}, bf16[64,2048]{1,0:T(8,128)(2,1)S(1)}, u32[]{:S(2)}, u32[]{:S(2)}) %collective-permute-start.30) | collective-permute-done | bytes 262176 | tf_op jit(solution)/shard_map/ppermute | solution.py:165
  136.6 1.5 %fusion.1 = bf16[64,2048]{1,0:T(8,128)(2,1)S(1)} fusion(bf16[64,2048]{1,0:T(8,128)(2,1)S(1)} %add_convert_fusion.2, bf16[64,2048]{1,0:T(8,128)(2,1)S(1)} %collective-permute-done.30, pred[]{:T(512)S(6)} %eq.30, bf16[64,2048]{1,0:T(8,128)(2,1)} %collective-permute-done.29, bf16[64,2048]{1,0:T(8,128)(2,1)} %collective-permute-done.28, ...), kind=kLoop, calls=%fused_computation.17 | loop fusion | flops 1703936 | bytes 2097153 | tf_op jit(solution)/shard_map/jit(_where)/select_n | solution.py:167
  138.1 0.8 maximum_bitcast_fusion
  (31 shorter events, 0.7 us)
Async XLA Ops:
  0.0 1.0 copy-start
  1.0 0.8 copy-start.1
  1.8 0.7 copy-start.2
  3.2 2.0 %collective-permute-start = (bf16[128,2048]{1,0:T(8,128)(2,1)S(1)}, bf16[128,2048]{1,0:T(8,128)(2,1)S(1)}, u32[]{:S(2)}, u32[]{:S(2)}) collective-permute-start(bf16[128,2048]{1,0:T(8,128)(2,1)S(1)} %rotate_local.1), channel_id=1, source_target_pairs={{0,2},{2,0},{4,6},{6,4},{8,10},{10,8},{12,14},{14,12},{1,3},{3,1},... | collective-permute-start | bytes 1572872 | tf_op jit(solution)/shard_map/ppermute | solution.py:23
  5.4 16.4 %collective-permute-start.1 = (bf16[64,2048]{1,0:T(8,128)(2,1)S(1)}, bf16[64,2048]{1,0:T(8,128)(2,1)S(1)}, u32[]{:S(2)}, u32[]{:S(2)}) collective-permute-start(bf16[64,2048]{1,0:T(8,128)(2,1)S(1)} %get-tuple-element.31), channel_id=1, source_target_pairs={{0,12},{2,14},{4,0},{6,2},{8,4},{10,6},{12,8},{14,10},{1,13},{3,15... | collective-permute-start | bytes 786440 | tf_op jit(solution)/shard_map/ppermute | solution.py:23
  9.5 16.0 %collective-permute-start.2 = (bf16[64,2048]{1,0:T(8,128)(2,1)S(1)}, bf16[64,2048]{1,0:T(8,128)(2,1)S(1)}, u32[]{:S(2)}, u32[]{:S(2)}) collective-permute-start(bf16[64,2048]{1,0:T(8,128)(2,1)S(1)} %get-tuple-element.31), channel_id=1, source_target_pairs={{0,4},{2,6},{4,8},{6,10},{8,12},{10,14},{12,0},{14,2},{1,5},{3,7},... | collective-permute-start | bytes 786440 | tf_op jit(solution)/shard_map/ppermute | solution.py:23
  9.5 16.0 %collective-permute-start.3 = (bf16[64,2048]{1,0:T(8,128)(2,1)S(1)}, bf16[64,2048]{1,0:T(8,128)(2,1)S(1)}, u32[]{:S(2)}, u32[]{:S(2)}) collective-permute-start(bf16[64,2048]{1,0:T(8,128)(2,1)S(1)} %get-tuple-element.31), channel_id=1, source_target_pairs={{0,8},{2,10},{4,12},{6,14},{8,0},{10,2},{12,4},{14,6},{1,9},{3,11}... | collective-permute-start | bytes 786440 | tf_op jit(solution)/shard_map/ppermute | solution.py:23
  11.4 19.1 %collective-permute-start.16 = (bf16[64,2048]{1,0:T(8,128)(2,1)S(1)}, bf16[64,2048]{1,0:T(8,128)(2,1)}, u32[]{:S(2)}, u32[]{:S(2)}) collective-permute-start(bf16[64,2048]{1,0:T(8,128)(2,1)S(1)} %get-tuple-element.17), channel_id=1, source_target_pairs={{0,12},{2,14},{4,0},{6,2},{8,4},{10,6},{12,8},{14,10},{1,13},{3,15... | collective-permute-start | bytes 786440 | tf_op jit(solution)/shard_map/ppermute | solution.py:23
  12.8 18.8 %collective-permute-start.17 = (bf16[64,2048]{1,0:T(8,128)(2,1)S(1)}, bf16[64,2048]{1,0:T(8,128)(2,1)}, u32[]{:S(2)}, u32[]{:S(2)}) collective-permute-start(bf16[64,2048]{1,0:T(8,128)(2,1)S(1)} %get-tuple-element.17), channel_id=1, source_target_pairs={{0,4},{2,6},{4,8},{6,10},{8,12},{10,14},{12,0},{14,2},{1,5},{3,7},... | collective-permute-start | bytes 786440 | tf_op jit(solution)/shard_map/ppermute | solution.py:23
  25.8 9.3 %collective-permute-start.7 = (bf16[64,2048]{1,0:T(8,128)(2,1)S(1)}, bf16[64,2048]{1,0:T(8,128)(2,1)S(1)}, u32[]{:S(2)}, u32[]{:S(2)}) collective-permute-start(bf16[64,2048]{1,0:T(8,128)(2,1)S(1)} %add_convert_fusion.12.refs_0_), channel_id=1, source_target_pairs={{0,64},{16,80},{32,96},{48,112},{64,0},{80,16},{96,32},{112,48},{1... | collective-permute-start | bytes 786440 | tf_op jit(solution)/shard_map/ppermute | solution.py:23
  29.0 8.8 %collective-permute-start.4 = (bf16[64,2048]{1,0:T(8,128)(2,1)S(1)}, bf16[64,2048]{1,0:T(8,128)(2,1)S(1)}, u32[]{:S(2)}, u32[]{:S(2)}) collective-permute-start(bf16[64,2048]{1,0:T(8,128)(2,1)S(1)} %add_convert_fusion.12.refs_0_), channel_id=1, source_target_pairs={{0,16},{16,0},{32,48},{48,32},{64,80},{80,64},{96,112},{112,96},{1... | collective-permute-start | bytes 786440 | tf_op jit(solution)/shard_map/ppermute | solution.py:23
  30.2 9.7 %collective-permute-start.18 = (bf16[64,2048]{1,0:T(8,128)(2,1)S(1)}, bf16[64,2048]{1,0:T(8,128)(2,1)}, u32[]{:S(2)}, u32[]{:S(2)}) collective-permute-start(bf16[64,2048]{1,0:T(8,128)(2,1)S(1)} %get-tuple-element.17), channel_id=1, source_target_pairs={{0,8},{2,10},{4,12},{6,14},{8,0},{10,2},{12,4},{14,6},{1,9},{3,11}... | collective-permute-start | bytes 786440 | tf_op jit(solution)/shard_map/ppermute | solution.py:23
  30.5 11.2 %collective-permute-start.5 = (bf16[64,2048]{1,0:T(8,128)(2,1)S(1)}, bf16[64,2048]{1,0:T(8,128)(2,1)S(1)}, u32[]{:S(2)}, u32[]{:S(2)}) collective-permute-start(bf16[64,2048]{1,0:T(8,128)(2,1)S(1)} %add_convert_fusion.12.refs_0_), channel_id=1, source_target_pairs={{0,96},{16,112},{32,0},{48,16},{64,32},{80,48},{96,64},{112,80},{1... | collective-permute-start | bytes 786440 | tf_op jit(solution)/shard_map/ppermute | solution.py:23
  31.6 11.7 %collective-permute-start.6 = (bf16[64,2048]{1,0:T(8,128)(2,1)S(1)}, bf16[64,2048]{1,0:T(8,128)(2,1)S(1)}, u32[]{:S(2)}, u32[]{:S(2)}) collective-permute-start(bf16[64,2048]{1,0:T(8,128)(2,1)S(1)} %add_convert_fusion.12.refs_0_), channel_id=1, source_target_pairs={{0,32},{16,48},{32,64},{48,80},{64,96},{80,112},{96,0},{112,16},{1... | collective-permute-start | bytes 786440 | tf_op jit(solution)/shard_map/ppermute | solution.py:23
  35.1 8.2 %collective-permute-start.10 = (bf16[64,2048]{1,0:T(8,128)(2,1)S(1)}, bf16[64,2048]{1,0:T(8,128)(2,1)S(1)}, u32[]{:S(2)}, u32[]{:S(2)}) collective-permute-start(bf16[64,2048]{1,0:T(8,128)(2,1)S(1)} %collective-permute-done.7.refs_4_), channel_id=1, source_target_pairs={{0,16},{16,0},{32,48},{48,32},{64,80},{80,64},{96,112},{112,96},{1... | collective-permute-start | bytes 786440 | tf_op jit(solution)/shard_map/ppermute | solution.py:23
  37.9 7.0 %collective-permute-start.8 = (bf16[64,2048]{1,0:T(8,128)(2,1)S(1)}, bf16[64,2048]{1,0:T(8,128)(2,1)S(1)}, u32[]{:S(2)}, u32[]{:S(2)}) collective-permute-start(bf16[64,2048]{1,0:T(8,128)(2,1)S(1)} %collective-permute-done.4.refs_1_), channel_id=1, source_target_pairs={{0,96},{16,112},{32,0},{48,16},{64,32},{80,48},{96,64},{112,80},{1... | collective-permute-start | bytes 786440 | tf_op jit(solution)/shard_map/ppermute | solution.py:23
  40.0 7.6 %collective-permute-start.9 = (bf16[64,2048]{1,0:T(8,128)(2,1)S(1)}, bf16[64,2048]{1,0:T(8,128)(2,1)S(1)}, u32[]{:S(2)}, u32[]{:S(2)}) collective-permute-start(bf16[64,2048]{1,0:T(8,128)(2,1)S(1)} %collective-permute-done.4.refs_1_), channel_id=1, source_target_pairs={{0,32},{16,48},{32,64},{48,80},{64,96},{80,112},{96,0},{112,16},{1... | collective-permute-start | bytes 786440 | tf_op jit(solution)/shard_map/ppermute | solution.py:23
  47.6 3.4 %copy-start.3 = (bf16[1,2048,2048]{2,1,0:T(8,128)(2,1)S(1)}, bf16[1,2048,2048]{2,1,0:T(8,128)(2,1)}, u32[]{:S(2)}) copy-start(bf16[1,2048,2048]{2,1,0:T(8,128)(2,1)} %param.7) | copy-start | bytes 25165828
  50.9 31.0 %copy-start.4 = (bf16[1,2048,2048]{2,1,0:T(8,128)(2,1)S(1)}, bf16[1,2048,2048]{2,1,0:T(8,128)(2,1)}, u32[]{:S(2)}) copy-start(bf16[1,2048,2048]{2,1,0:T(8,128)(2,1)} %param.7) | copy-start | bytes 25165828
  57.4 31.0 %collective-permute-start.11 = (bf16[256,2048]{1,0:T(8,128)(2,1)S(1)}, bf16[256,2048]{1,0:T(8,128)(2,1)S(1)}, u32[]{:S(2)}, u32[]{:S(2)}) collective-permute-start(bf16[256,2048]{1,0:T(8,128)(2,1)S(1)} %get-tuple-element.16), channel_id=1, source_target_pairs={{0,2},{2,0},{4,6},{6,4},{8,10},{10,8},{12,14},{14,12},{1,3},{3,1},... | collective-permute-start | bytes 3145736 | tf_op jit(solution)/shard_map/ppermute | solution.py:23
  58.9 47.6 %copy-start.8 = (bf16[128,2048]{1,0:T(8,128)(2,1)S(1)}, bf16[128,2048]{1,0:T(8,128)(2,1)}, u32[]{:S(2)}) copy-start(bf16[128,2048]{1,0:T(8,128)(2,1)} %param.8) | copy-start | bytes 1572868
  58.9 8.8 %collective-permute-start.19 = (bf16[64,2048]{1,0:T(8,128)(2,1)S(1)}, bf16[64,2048]{1,0:T(8,128)(2,1)S(1)}, u32[]{:S(2)}, u32[]{:S(2)}) collective-permute-start(bf16[64,2048]{1,0:T(8,128)(2,1)S(1)} %add_convert_fusion.6.refs_0_), channel_id=1, source_target_pairs={{0,16},{16,0},{32,48},{48,32},{64,80},{80,64},{96,112},{112,96},{1... | collective-permute-start | bytes 786440 | tf_op jit(solution)/shard_map/ppermute | solution.py:23
  60.1 10.7 %collective-permute-start.22 = (bf16[64,2048]{1,0:T(8,128)(2,1)S(1)}, bf16[64,2048]{1,0:T(8,128)(2,1)S(1)}, u32[]{:S(2)}, u32[]{:S(2)}) collective-permute-start(bf16[64,2048]{1,0:T(8,128)(2,1)S(1)} %add_convert_fusion.6.refs_0_), channel_id=1, source_target_pairs={{0,64},{16,80},{32,96},{48,112},{64,0},{80,16},{96,32},{112,48},{1... | collective-permute-start | bytes 786440 | tf_op jit(solution)/shard_map/ppermute | solution.py:23
  62.2 12.8 %collective-permute-start.20 = (bf16[64,2048]{1,0:T(8,128)(2,1)S(1)}, bf16[64,2048]{1,0:T(8,128)(2,1)S(1)}, u32[]{:S(2)}, u32[]{:S(2)}) collective-permute-start(bf16[64,2048]{1,0:T(8,128)(2,1)S(1)} %add_convert_fusion.6.refs_0_), channel_id=1, source_target_pairs={{0,96},{16,112},{32,0},{48,16},{64,32},{80,48},{96,64},{112,80},{1... | collective-permute-start | bytes 786440 | tf_op jit(solution)/shard_map/ppermute | solution.py:23
  62.4 13.5 %collective-permute-start.21 = (bf16[64,2048]{1,0:T(8,128)(2,1)S(1)}, bf16[64,2048]{1,0:T(8,128)(2,1)S(1)}, u32[]{:S(2)}, u32[]{:S(2)}) collective-permute-start(bf16[64,2048]{1,0:T(8,128)(2,1)S(1)} %add_convert_fusion.6.refs_0_), channel_id=1, source_target_pairs={{0,32},{16,48},{32,64},{48,80},{64,96},{80,112},{96,0},{112,16},{1... | collective-permute-start | bytes 786440 | tf_op jit(solution)/shard_map/ppermute | solution.py:23
  67.6 12.3 %collective-permute-start.23 = (bf16[64,2048]{1,0:T(8,128)(2,1)S(1)}, bf16[64,2048]{1,0:T(8,128)(2,1)S(1)}, u32[]{:S(2)}, u32[]{:S(2)}) collective-permute-start(bf16[64,2048]{1,0:T(8,128)(2,1)S(1)} %collective-permute-done.19.refs_1_), channel_id=1, source_target_pairs={{0,96},{16,112},{32,0},{48,16},{64,32},{80,48},{96,64},{112,80},{1... | collective-permute-start | bytes 786440 | tf_op jit(solution)/shard_map/ppermute | solution.py:23
  70.8 10.5 %collective-permute-start.24 = (bf16[64,2048]{1,0:T(8,128)(2,1)S(1)}, bf16[64,2048]{1,0:T(8,128)(2,1)S(1)}, u32[]{:S(2)}, u32[]{:S(2)}) collective-permute-start(bf16[64,2048]{1,0:T(8,128)(2,1)S(1)} %collective-permute-done.19.refs_1_), channel_id=1, source_target_pairs={{0,32},{16,48},{32,64},{48,80},{64,96},{80,112},{96,0},{112,16},{1... | collective-permute-start | bytes 786440 | tf_op jit(solution)/shard_map/ppermute | solution.py:23
  75.0 6.9 %collective-permute-start.25 = (bf16[64,2048]{1,0:T(8,128)(2,1)S(1)}, bf16[64,2048]{1,0:T(8,128)(2,1)S(1)}, u32[]{:S(2)}, u32[]{:S(2)}) collective-permute-start(bf16[64,2048]{1,0:T(8,128)(2,1)S(1)} %collective-permute-done.22.refs_4_), channel_id=1, source_target_pairs={{0,16},{16,0},{32,48},{48,32},{64,80},{80,64},{96,112},{112,96},{1... | collective-permute-start | bytes 786440 | tf_op jit(solution)/shard_map/ppermute | solution.py:23
  88.4 19.0 %collective-permute-start.26 = (bf16[256,2048]{1,0:T(8,128)(2,1)S(1)}, bf16[256,2048]{1,0:T(8,128)(2,1)S(1)}, u32[]{:S(2)}, u32[]{:S(2)}) collective-permute-start(bf16[256,2048]{1,0:T(8,128)(2,1)S(1)} %get-tuple-element.22), channel_id=1, source_target_pairs={{0,2},{2,0},{4,6},{6,4},{8,10},{10,8},{12,14},{14,12},{1,3},{3,1},... | collective-permute-start | bytes 3145736 | tf_op jit(solution)/shard_map/ppermute | solution.py:23
  88.8 10.9 %collective-permute-start.12 = (bf16[64,2048]{1,0:T(8,128)(2,1)S(1)}, bf16[64,2048]{1,0:T(8,128)(2,1)S(1)}, u32[]{:S(2)}, u32[]{:S(2)}) collective-permute-start(bf16[64,2048]{1,0:T(8,128)(2,1)S(1)} %get-tuple-element.28), channel_id=1, source_target_pairs={{0,4},{2,6},{4,8},{6,10},{8,12},{10,14},{12,0},{14,2},{1,5},{3,7},... | collective-permute-start | bytes 786440 | tf_op jit(solution)/shard_map/ppermute | solution.py:23
  88.8 16.0 %collective-permute-start.13 = (bf16[64,2048]{1,0:T(8,128)(2,1)S(1)}, bf16[64,2048]{1,0:T(8,128)(2,1)S(1)}, u32[]{:S(2)}, u32[]{:S(2)}) collective-permute-start(bf16[64,2048]{1,0:T(8,128)(2,1)S(1)} %get-tuple-element.30), channel_id=1, source_target_pairs={{0,12},{2,14},{4,0},{6,2},{8,4},{10,6},{12,8},{14,10},{1,13},{3,15... | collective-permute-start | bytes 786440 | tf_op jit(solution)/shard_map/ppermute | solution.py:23
  93.0 13.5 %collective-permute-start.14 = (bf16[64,2048]{1,0:T(8,128)(2,1)S(1)}, bf16[64,2048]{1,0:T(8,128)(2,1)S(1)}, u32[]{:S(2)}, u32[]{:S(2)}) collective-permute-start(bf16[64,2048]{1,0:T(8,128)(2,1)S(1)} %get-tuple-element.29), channel_id=1, source_target_pairs={{0,8},{2,10},{4,12},{6,14},{8,0},{10,2},{12,4},{14,6},{1,9},{3,11}... | collective-permute-start | bytes 786440 | tf_op jit(solution)/shard_map/ppermute | solution.py:23
  104.8 4.6 %copy-start.6 = (bf16[64,2048]{1,0:T(8,128)(2,1)}, bf16[64,2048]{1,0:T(8,128)(2,1)S(1)}, u32[]{:S(2)}) copy-start(bf16[64,2048]{1,0:T(8,128)(2,1)S(1)} %collective-permute-done.13) | copy-start | bytes 786436
  106.5 2.9 %copy-start.7 = (bf16[64,2048]{1,0:T(8,128)(2,1)}, bf16[64,2048]{1,0:T(8,128)(2,1)S(1)}, u32[]{:S(2)}) copy-start(bf16[64,2048]{1,0:T(8,128)(2,1)S(1)} %collective-permute-done.14) | copy-start | bytes 786436
  107.4 1.0 copy-start.5
  109.4 10.5 %collective-permute-start.27 = (bf16[64,2048]{1,0:T(8,128)(2,1)}, bf16[64,2048]{1,0:T(8,128)(2,1)}, u32[]{:S(2)}, u32[]{:S(2)}) collective-permute-start(bf16[64,2048]{1,0:T(8,128)(2,1)} %get-tuple-element.25), channel_id=1, source_target_pairs={{0,4},{2,6},{4,8},{6,10},{8,12},{10,14},{12,0},{14,2},{1,5},{3,7},... | collective-permute-start | bytes 786440 | tf_op jit(solution)/shard_map/ppermute | solution.py:23
  110.5 13.2 %collective-permute-start.28 = (bf16[64,2048]{1,0:T(8,128)(2,1)}, bf16[64,2048]{1,0:T(8,128)(2,1)}, u32[]{:S(2)}, u32[]{:S(2)}) collective-permute-start(bf16[64,2048]{1,0:T(8,128)(2,1)} %get-tuple-element.27), channel_id=1, source_target_pairs={{0,12},{2,14},{4,0},{6,2},{8,4},{10,6},{12,8},{14,10},{1,13},{3,15... | collective-permute-start | bytes 786440 | tf_op jit(solution)/shard_map/ppermute | solution.py:23
  112.6 12.1 %collective-permute-start.29 = (bf16[64,2048]{1,0:T(8,128)(2,1)}, bf16[64,2048]{1,0:T(8,128)(2,1)}, u32[]{:S(2)}, u32[]{:S(2)}) collective-permute-start(bf16[64,2048]{1,0:T(8,128)(2,1)} %get-tuple-element.26), channel_id=1, source_target_pairs={{0,8},{2,10},{4,12},{6,14},{8,0},{10,2},{12,4},{14,6},{1,9},{3,11}... | collective-permute-start | bytes 786440 | tf_op jit(solution)/shard_map/ppermute | solution.py:23
  112.9 14.6 %collective-permute-start.15 = (bf16[64,2048]{1,0:T(8,128)(2,1)}, bf16[64,2048]{1,0:T(8,128)(2,1)S(1)}, u32[]{:S(2)}, u32[]{:S(2)}) collective-permute-start(bf16[64,2048]{1,0:T(8,128)(2,1)} %add_convert_fusion.8), channel_id=1, source_target_pairs={{0,1},{2,3},{4,5},{6,7},{8,9},{10,11},{12,13},{14,15},{16,17},{18,... | collective-permute-start | bytes 786440 | tf_op jit(solution)/shard_map/ppermute | solution.py:165
  126.2 10.4 %collective-permute-start.30 = (bf16[64,2048]{1,0:T(8,128)(2,1)S(1)}, bf16[64,2048]{1,0:T(8,128)(2,1)S(1)}, u32[]{:S(2)}, u32[]{:S(2)}) collective-permute-start(bf16[64,2048]{1,0:T(8,128)(2,1)S(1)} %add_convert_fusion.2), channel_id=1, source_target_pairs={{0,1},{2,3},{4,5},{6,7},{8,9},{10,11},{12,13},{14,15},{16,17},{18,... | collective-permute-start | bytes 786440 | tf_op jit(solution)/shard_map/ppermute | solution.py:165

commit v2 on v0

v2 whole, which is shorter than its diff:
```python
import math

import jax
import jax.numpy as jnp
from jax import lax
from jax.experimental import pallas as pl
from jax.experimental.pallas import tpu as pltpu
from jax.sharding import PartitionSpec as P

LANES = 128
BF16 = jnp.bfloat16
TILES = 4


def f32(value):
    return value.astype(jnp.float32)


def place():
    d, t = lax.axis_index("dp"), lax.axis_index("tensor")
    return d >> 1, d & 1, t >> 1, t & 1


def shape(rows, columns, kind=BF16):
    return jax.ShapeDtypeStruct((rows, columns), kind)


VMEM = pl.BlockSpec(memory_space=pltpu.VMEM)
HBM = pl.BlockSpec(memory_space=pltpu.HBM)
ANY = pl.BlockSpec(memory_space=pl.ANY)


def call(name, kernel, operands, out_shape, behind=(), specs=None, scratch=(), flops=0, limit=16, weigh=1):
    specs = specs or [VMEM] * len(operands)
    count = len(operands)
    outs = out_shape if isinstance(out_shape, tuple) else (out_shape,)
    size = sum(2 * math.prod(o.shape) for o in tuple(operands) + outs)
    return pl.pallas_call(
        lambda *refs: kernel(*refs[:count], *refs[count + len(behind) :]),
        out_shape=out_shape,
        in_specs=list(specs) + [ANY] * len(behind),
        out_specs=jax.tree.map(lambda _: VMEM, out_shape),
        scratch_shapes=list(scratch),
        compiler_params=pltpu.CompilerParams(vmem_limit_bytes=limit << 20),
        cost_estimate=pl.CostEstimate(flops=flops, bytes_accessed=size * weigh, transcendentals=0),
        name=name,
    )(*operands, *behind)


def rotate_kernel(scale, x_ref, s_ref, o_ref):
    rows, width = o_ref.shape
    pieces = width // LANES
    signs = f32(s_ref[...])
    i = lax.broadcasted_iota(jnp.int32, (LANES, LANES), 0) & lax.broadcasted_iota(jnp.int32, (LANES, LANES), 1)
    for bits in (4, 2, 1):
        i = i ^ (i >> bits)
    table = f32(1 - 2 * (i & 1)).astype(BF16)
    for r in range(0, rows, 32):
        part = []
        for a in range(pieces):
            cols = slice(a * LANES, (a + 1) * LANES)
            x = (f32(x_ref[0, r : r + 32, cols]) * signs[:, cols]).astype(BF16)
            part.append(jnp.dot(x, table, preferred_element_type=jnp.float32))
        step = 1
        while step < pieces:
            nxt = list(part)
            for a in range(pieces):
                if not a & step:
                    nxt[a] = part[a] + part[a | step]
                    nxt[a | step] = part[a] - part[a | step]
            part = nxt
            step *= 2
        for a in range(pieces):
            o_ref[r : r + 32, a * LANES : (a + 1) * LANES] = (part[a] * scale).astype(BF16)


def pair_kernel(at, mine_ref, other_ref, out_ref):
    sign = f32(1 - 2 * place()[3])
    out_ref[...] = (f32(other_ref[at]) + sign * f32(mine_ref[at])).astype(BF16)


def mix_kernel(*refs):
    z = place()[2]
    total = 0
    for k, ref in enumerate(refs[:4]):
        u = z & ((z + k) & 3)
        total = total + f32(1 - 2 * ((u ^ (u >> 1)) & 1)) * f32(ref[...])
    refs[4][...] = total.astype(BF16)


def load_kernel(w_ref, out_ref, sem):
    copy = pltpu.make_async_copy(w_ref.at[0], out_ref, sem)
    copy.start()
    copy.wait()


def products(blocks, w_ref, lhs, store):
    width = w_ref.shape[1] // TILES
    y, _, z, _ = place()
    rows = blocks[0].shape[0]
    for dy, ref in enumerate(blocks):
        lhs[pl.ds(pl.multiple_of(((y + dy - z) & 3) * rows, rows), rows), :] = ref[...]
    for n in range(TILES):
        cols = slice(n * width, (n + 1) * width)
        out = jnp.dot(lhs[...], w_ref[:, cols], preferred_element_type=jnp.float32)
        store(cols, out.astype(BF16))


def column_kernel(*refs):
    blocks, (w_ref, out_ref, lhs) = refs[:4], refs[4:]

    def store(cols, out):
        out_ref[:, cols] = out

    products(blocks, w_ref, lhs, store)


def mate_kernel(*refs):
    blocks, (w_ref, column_ref, keep_ref, send_ref, lhs) = refs[:4], refs[4:]
    _, x, _, c = place()

    def store(cols, out):
        @pl.when(x == c)
        def _():
            keep_ref[:, cols] = column_ref[:, cols]
            send_ref[:, cols] = out

        @pl.when(x != c)
        def _():
            keep_ref[:, cols] = out
            send_ref[:, cols] = column_ref[:, cols]

    products(blocks, w_ref, lhs, store)


def project(blocks, weight, column=None, behind=()):
    rows, depth = blocks[0].shape
    width = weight.shape[1]
    half = shape(4 * rows, width)
    return call(
        "project_column" if column is None else "project_mate",
        column_kernel if column is None else mate_kernel,
        (*blocks, weight) + (() if column is None else (column,)),
        half if column is None else (half, half),
        behind,
        scratch=[pltpu.VMEM((4 * rows, depth), BF16)],
        flops=2 * 4 * rows * depth * width,
        limit=24,
    )


def halves_kernel(keep_ref, came_ref, *out_refs):
    rows = out_refs[0].shape[0]
    for k, ref in enumerate(out_refs, 1):
        at = slice(k * rows, (k + 1) * rows)
        ref[...] = (f32(keep_ref[at]) + f32(came_ref[at])).astype(BF16)


def finish_kernel(at, keep_ref, came_ref, a_ref, b_ref, c_ref, residual_ref, leading_ref, summed_ref):
    rows = leading_ref.shape[0]
    total = f32(keep_ref[:rows]) + f32(came_ref[:rows]) + f32(a_ref[...]) + f32(b_ref[...]) + f32(c_ref[...])
    summed_ref[...] = total
    leading_ref[...] = (f32(residual_ref[at]) + total).astype(BF16)


def end_kernel(*refs):
    out_ref = refs[-1]
    first = lax.axis_index("pipe") == 0
    at = 0
    for leading_ref, summed_ref, passed_ref in zip(refs[0:-1:3], refs[1:-1:3], refs[2:-1:3]):
        rows = leading_ref.shape[0]
        later = (f32(passed_ref[...]) + summed_ref[...]).astype(BF16)
        out_ref[0, at : at + rows, :] = jnp.where(first, leading_ref[...], later)
        at += rows


def on_device(attention_out, signs, out_weight, residual_in):
    tokens, width = attention_out.shape[1:]
    columns = out_weight.shape[2]
    scale = 1.0 / math.sqrt(width * lax.axis_size("tensor"))
    rows = tokens // 2
    cut = [slice(0, rows), slice(rows, tokens)]

    def move(value, axis, target):
        return lax.ppermute(value, axis, [(i, target(i)) for i in range(lax.axis_size(axis))])

    def ring(steps, flip=0):
        return lambda i: (i // 2 + steps) % 4 * 2 + (i % 2 ^ flip)

    def swap(value):
        return move(value, "tensor", lambda i: i ^ 1)

    def pipe(value):
        return lax.ppermute(value, "pipe", [(0, 1)])

    def pair(chunk, mine, other, behind=()):
        return call(
            "hadamard_core", lambda *refs: pair_kernel(cut[chunk], *refs), (mine, other), shape(rows, width), behind
        )

    def spread_z(mine):
        return [mine] + [move(mine, "tensor", ring(-k)) for k in (1, 2, 3)]

    def mix(terms, behind=()):
        return call("hadamard_z", mix_kernel, terms, shape(rows, width), behind)

    def spread_column(own):
        mate = move(own, "dp", ring(0, 1))
        return [own] + [move(own, "dp", ring(-dy)) for dy in (1, 2, 3)], mate

    def spread_mate(column, mate):
        return [mate, move(mate, "dp", ring(-1)), move(column[2], "dp", ring(0, 1)), move(mate, "dp", ring(-3))]

    def halves(keep, came, behind=()):
        return call("core_sum", halves_kernel, (keep, came), (shape(rows, columns),) * 3, behind)

    def gather_z(parts):
        return [move(part, "tensor", ring(k)) for k, part in enumerate(parts, 1)]

    def finish(chunk, keep, came, arrived, behind=()):
        return call(
            "residual",
            lambda *refs: finish_kernel(cut[chunk], *refs),
            (keep, came, *arrived, residual_in),
            (shape(rows, columns), shape(rows, columns, jnp.float32)),
            behind,
            weigh=20,
        )

    local = call(
        "rotate_local",
        lambda *refs: rotate_kernel(scale, *refs),
        (attention_out, signs),
        shape(tokens, width),
        flops=2 * tokens * width * LANES,
    )
    other = swap(local)
    terms0 = spread_z(pair(0, local, other))
    terms1 = spread_z(pair(1, local, other, [terms0[1]]))
    weight = call(
        "load_weight",
        load_kernel,
        (out_weight,),
        shape(*out_weight.shape[1:]),
        [terms0[0]],
        specs=[HBM],
        scratch=[pltpu.SemaphoreType.DMA],
        limit=48,
    )
    own0 = mix(terms0, [weight])
    own1 = mix(terms1, [own0])
    column0, mate0 = spread_column(own0)
    column1, mate1 = spread_column(own1)
    mates0 = spread_mate(column0, mate0)
    products0 = project(column0, weight, None, [own1])
    keep0, send0 = project(mates0, weight, products0, [*column1[1:], mate1])
    came0 = swap(send0)
    mates1 = spread_mate(column1, mate1)
    products1 = project(column1, weight, None, [send0])
    parts0 = halves(keep0, came0, [products1])
    arrived0 = gather_z(parts0)
    keep1, send1 = project(mates1, weight, products1, [parts0[0]])
    came1 = swap(send1)
    leading0, summed0 = finish(0, keep0, came0, arrived0, [send1])
    passed0 = pipe(leading0)
    parts1 = halves(keep1, came1, [leading0])
    arrived1 = gather_z(parts1)
    leading1, summed1 = finish(1, keep1, came1, arrived1)
    passed1 = pipe(leading1)
    return call(
        "end",
        end_kernel,
        (leading0, summed0, passed0, leading1, summed1, passed1),
        jax.ShapeDtypeStruct((1, tokens, columns), BF16),
    )


def solution(mesh):
    in_specs = (
        P("pipe", "dp", "tensor"),
        P("pipe", "tensor"),
        P("pipe", "tensor", "dp"),
        P("tensor", "dp"),
    )
    out_specs = P("pipe", "tensor", "dp")
    return jax.shard_map(
        on_device, mesh=mesh, in_specs=in_specs, out_specs=out_specs, check_vma=False
    )
```

time: 1430 us -> 131 us (0.09)
  waiting for transfers between devices: 1290 us -> 66 us
  blocking collectives: 83.6 us -> 0 us
  starting transfers between devices: 1.33 us -> 38.9 us
  matrix products: 26.7 us -> 0 us
  Pallas kernels: 0 us -> 20.5 us
    all_gather x1 -> x0, waiting for transfers between devices: 1240 us -> none  [on_device(): lax.all_gather(weight, 'dp', axis=1, tiled=True)]
    all_to_all x3 -> x0, blocking collectives: 83.6 us -> none  [the longest x1 55.3 us: on_device(): lax.all_to_all(partial_value, 'dp', split_axis=1, concat_axis=0, tiled=True)]
    ppermute x1 -> x31, waiting for transfers between devices: 12.7 us -> 66 us  [the longest x29 56.8 us: move(): lax.ppermute(value, axis, [(i, target(i)) for i in range(lax.axis_size(ax...]
    reduce_scatter x1 -> x0, waiting for transfers between devices: 37.8 us -> none  [on_device(): lax.psum_scatter(partial_terms.astype(jnp.float32).astype(jnp.bfloat16),...]
    ppermute x1 -> x31, starting transfers between devices: 1.29 us -> 38.9 us  [the longest x29 36.3 us: move(): lax.ppermute(value, axis, [(i, target(i)) for i in range(lax.axis_size(ax...]
    dot_general x3 -> x0, matrix products: 26.7 us -> none  [the longest x1 25.3 us: on_device(): jnp.dot(rotated, lax.all_gather(weight, 'dp', axis=1, tiled=True), prefer...]
    pallas_call x0 -> x15, Pallas kernels: none -> 20.5 us  [call(): pl.pallas_call(lambda *refs: kernel(*refs[:count], *refs[count + len(behi...]
  transfers between devices with their start and end apart: 3 -> 31, of which waited for: 3 -> 19; matrix products, arithmetic and copies ran while one was open for 0% -> 0% of each run, Pallas kernels for 0% -> 10%
where the time goes in v2:
time: 131 us
  waiting for transfers between devices  66 us (50%)
  starting transfers between devices  38.9 us (30%)
  Pallas kernels  20.5 us (16%)
  local copies, waits for them, and re-layouts  5.12 us (4%)
    ppermute x29, waiting for transfers between devices, move(): lax.ppermute(value, axis, [(i, target(i)) for i in range(lax.axis_size(ax...  56.8 us
    ppermute x29, starting transfers between devices, move(): lax.ppermute(value, axis, [(i, target(i)) for i in range(lax.axis_size(ax...  36.3 us
    pallas_call x15, Pallas kernels, call(): pl.pallas_call(lambda *refs: kernel(*refs[:count], *refs[count + len(behi...  20.5 us
    ppermute x2, waiting for transfers between devices, pipe(): return lax.ppermute(value, 'pipe', [(0, 1)])  9.19 us
    unnamed x10, local copies, waits for them, and re-layouts  5.12 us
  transfers between devices with their start and end apart: 31, of which 19 were waited for; matrix products, arithmetic and copies ran while one was open for 0% of the time, Pallas kernels for 10%

profile of v2, /device:TPU:4, one launch (start us, length us, event | category | flops | bytes accessed | tf_op | source)
XLA Modules:
  0.0 130.7 jit_solution(13682723458595008073)
XLA Ops:
  0.0 1.0 copy-done.3
  1.0 0.7 copy-done.4
  1.7 0.7 rotate_local.1.refs_0_
  2.5 0.1 collective-permute-start
  2.6 1.9 %collective-permute-done.refs_1_ = bf16[128,2048]{1,0:T(8,128)(2,1)S(1)} collective-permute-done((bf16[128,2048]{1,0:T(8,128)(2,1)S(1)}, bf16[128,2048]{1,0:T(8,128)(2,1)S(1)}, u32[]{:S(2)}, u32[]{:S(2)}) %collective-permute-start) | collective-permute-done | bytes 524320 | tf_op jit(solution)/shard_map/ppermute | solution.py:185
  4.5 0.1 hadamard_core.2.refs_1_.refs_0_
  4.6 4.1 %collective-permute-start.1 = (bf16[64,2048]{1,0:T(8,128)(2,1)S(1)}, bf16[64,2048]{1,0:T(8,128)(2,1)S(1)}, u32[]{:S(2)}, u32[]{:S(2)}) collective-permute-start(bf16[64,2048]{1,0:T(8,128)(2,1)S(1)} %hadamard_core.2.refs_1_.refs_0_), channel_id=1, source_target_pairs={{0,12},{2,14},{4,0},{6,2},{8,4},{10,6},{12,8},{14,10},{1,13},{3,15... | collective-permute-start | bytes 786440 | tf_op jit(solution)/shard_map/ppermute | solution.py:185
  8.7 1.9 %collective-permute-start.2 = (bf16[64,2048]{1,0:T(8,128)(2,1)S(1)}, bf16[64,2048]{1,0:T(8,128)(2,1)S(1)}, u32[]{:S(2)}, u32[]{:S(2)}) collective-permute-start(bf16[64,2048]{1,0:T(8,128)(2,1)S(1)} %hadamard_core.2.refs_1_.refs_0_), channel_id=1, source_target_pairs={{0,8},{2,10},{4,12},{6,14},{8,0},{10,2},{12,4},{14,6},{1,9},{3,11}... | collective-permute-start | bytes 786440 | tf_op jit(solution)/shard_map/ppermute | solution.py:185
  10.5 9.6 %collective-permute-done.1.refs_1_.refs_2_ = bf16[64,2048]{1,0:T(8,128)(2,1)S(1)} collective-permute-done((bf16[64,2048]{1,0:T(8,128)(2,1)S(1)}, bf16[64,2048]{1,0:T(8,128)(2,1)S(1)}, u32[]{:S(2)}, u32[]{:S(2)}) %collective-permute-start.1) | collective-permute-done | bytes 262176 | tf_op jit(solution)/shard_map/ppermute | solution.py:185
  20.1 0.1 hadamard_core.3.refs_0_
  20.2 0.1 collective-permute-start.13
  20.3 6.7 %load_weight.1.refs_4_ = bf16[2048,2048]{1,0:T(8,128)(2,1)} custom-call(bf16[1,2048,2048]{2,1,0:T(8,128)(2,1)} %refs_0_.3, bf16[64,2048]{1,0:T(8,128)(2,1)S(1)} %hadamard_core.2.refs_1_.refs_0_), custom_call_target="tpu_custom_call" | custom-call | bytes 16777216 | tf_op jit(solution)/shard_map/load_weight/pallas_call | solution.py:38
  27.0 5.2 %collective-permute-start.12 = (bf16[64,2048]{1,0:T(8,128)(2,1)S(1)}, bf16[64,2048]{1,0:T(8,128)(2,1)S(1)}, u32[]{:S(2)}, u32[]{:S(2)}) collective-permute-start(bf16[64,2048]{1,0:T(8,128)(2,1)S(1)} %hadamard_core.3.refs_0_), channel_id=1, source_target_pairs={{0,8},{2,10},{4,12},{6,14},{8,0},{10,2},{12,4},{14,6},{1,9},{3,11}... | collective-permute-start | bytes 786440 | tf_op jit(solution)/shard_map/ppermute | solution.py:185
  32.3 3.4 %copy-done = bf16[2048,2048]{1,0:T(8,128)(2,1)S(1)} copy-done((bf16[2048,2048]{1,0:T(8,128)(2,1)S(1)}, bf16[2048,2048]{1,0:T(8,128)(2,1)}, u32[]{:S(2)}) %copy-start) | copy-done | bytes 8388632
  35.6 0.2 hadamard_z.2.refs_4_.refs_0_
  35.8 1.6 %collective-permute-start.10 = (bf16[64,2048]{1,0:T(8,128)(2,1)S(1)}, bf16[64,2048]{1,0:T(8,128)(2,1)S(1)}, u32[]{:S(2)}, u32[]{:S(2)}) collective-permute-start(bf16[64,2048]{1,0:T(8,128)(2,1)S(1)} %hadamard_z.2.refs_4_.refs_0_), channel_id=1, source_target_pairs={{0,32},{16,48},{32,64},{48,80},{64,96},{80,112},{96,0},{112,16},{1... | collective-permute-start | bytes 786440 | tf_op jit(solution)/shard_map/ppermute | solution.py:185
  37.5 1.7 %collective-permute-start.9 = (bf16[64,2048]{1,0:T(8,128)(2,1)S(1)}, bf16[64,2048]{1,0:T(8,128)(2,1)S(1)}, u32[]{:S(2)}, u32[]{:S(2)}) collective-permute-start(bf16[64,2048]{1,0:T(8,128)(2,1)S(1)} %hadamard_z.2.refs_4_.refs_0_), channel_id=1, source_target_pairs={{0,96},{16,112},{32,0},{48,16},{64,32},{80,48},{96,64},{112,80},{1... | collective-permute-start | bytes 786440 | tf_op jit(solution)/shard_map/ppermute | solution.py:185
  39.1 2.0 %collective-permute-start.6 = (bf16[64,2048]{1,0:T(8,128)(2,1)S(1)}, bf16[64,2048]{1,0:T(8,128)(2,1)S(1)}, u32[]{:S(2)}, u32[]{:S(2)}) collective-permute-start(bf16[64,2048]{1,0:T(8,128)(2,1)S(1)} %hadamard_z.2.refs_4_.refs_0_), channel_id=1, source_target_pairs={{0,64},{16,80},{32,96},{48,112},{64,0},{80,16},{96,32},{112,48},{1... | collective-permute-start | bytes 786440 | tf_op jit(solution)/shard_map/ppermute | solution.py:185
  41.1 1.2 collective-permute-start.4
  42.3 0.5 collective-permute-done.11.refs_1_
  42.8 0.2 hadamard_z.3.refs_5_.refs_0_
  43.0 1.3 collective-permute-start.17
  44.3 1.0 collective-permute-done.10.refs_3_
  45.2 1.5 %collective-permute-start.16 = (bf16[64,2048]{1,0:T(8,128)(2,1)S(1)}, bf16[64,2048]{1,0:T(8,128)(2,1)S(1)}, u32[]{:S(2)}, u32[]{:S(2)}) collective-permute-start(bf16[64,2048]{1,0:T(8,128)(2,1)S(1)} %hadamard_z.3.refs_5_.refs_0_), channel_id=1, source_target_pairs={{0,32},{16,48},{32,64},{48,80},{64,96},{80,112},{96,0},{112,16},{1... | collective-permute-start | bytes 786440 | tf_op jit(solution)/shard_map/ppermute | solution.py:185
  46.7 5.2 %collective-permute-done.9.refs_1_ = bf16[64,2048]{1,0:T(8,128)(2,1)S(1)} collective-permute-done((bf16[64,2048]{1,0:T(8,128)(2,1)S(1)}, bf16[64,2048]{1,0:T(8,128)(2,1)S(1)}, u32[]{:S(2)}, u32[]{:S(2)}) %collective-permute-start.9) | collective-permute-done | bytes 262176 | tf_op jit(solution)/shard_map/ppermute | solution.py:185
  51.9 1.3 %collective-permute-done.6.refs_2_ = bf16[64,2048]{1,0:T(8,128)(2,1)S(1)} collective-permute-done((bf16[64,2048]{1,0:T(8,128)(2,1)S(1)}, bf16[64,2048]{1,0:T(8,128)(2,1)S(1)}, u32[]{:S(2)}, u32[]{:S(2)}) %collective-permute-start.6) | collective-permute-done | bytes 262176 | tf_op jit(solution)/shard_map/ppermute | solution.py:185
  53.3 2.5 %collective-permute-start.14 = (bf16[64,2048]{1,0:T(8,128)(2,1)S(1)}, bf16[64,2048]{1,0:T(8,128)(2,1)S(1)}, u32[]{:S(2)}, u32[]{:S(2)}) collective-permute-start(bf16[64,2048]{1,0:T(8,128)(2,1)S(1)} %hadamard_z.3.refs_5_.refs_0_), channel_id=1, source_target_pairs={{0,96},{16,112},{32,0},{48,16},{64,32},{80,48},{96,64},{112,80},{1... | collective-permute-start | bytes 786440 | tf_op jit(solution)/shard_map/ppermute | solution.py:185
  55.8 1.2 collective-permute-start.7
  57.0 0.9 collective-permute-start.8
  57.9 3.4 %collective-permute-done.16.refs_8_.refs_3_ = bf16[64,2048]{1,0:T(8,128)(2,1)S(1)} collective-permute-done((bf16[64,2048]{1,0:T(8,128)(2,1)S(1)}, bf16[64,2048]{1,0:T(8,128)(2,1)S(1)}, u32[]{:S(2)}, u32[]{:S(2)}) %collective-permute-start.16) | collective-permute-done | bytes 262176 | tf_op jit(solution)/shard_map/ppermute | solution.py:185
  61.3 2.4 %project_column.2.refs_5_ = bf16[256,2048]{1,0:T(8,128)(2,1)S(1)} custom-call(bf16[64,2048]{1,0:T(8,128)(2,1)S(1)} %hadamard_z.2.refs_4_.refs_0_, bf16[64,2048]{1,0:T(8,128)(2,1)S(1)} %collective-permute-done.9.refs_1_, bf16[64,2048]{1,0:T(8,128)(2,1)S(1)} %collective-permute-done.6.refs_2_, bf16[64,2048]{1,0:T(8,128)(2,1)S(1)} %collective-permute-done.10.refs_3_, ...), custom_call_target="tpu_custom_call" | custom-call | flops 2147483648 | bytes 10485760 | tf_op jit(solution)/shard_map/project_column/pallas_call | solution.py:38
  63.7 0.8 collective-permute-done.15.refs_7_.refs_2_
  64.5 2.0 %collective-permute-done.14.refs_6_.refs_1_ = bf16[64,2048]{1,0:T(8,128)(2,1)S(1)} collective-permute-done((bf16[64,2048]{1,0:T(8,128)(2,1)S(1)}, bf16[64,2048]{1,0:T(8,128)(2,1)S(1)}, u32[]{:S(2)}, u32[]{:S(2)}) %collective-permute-start.14) | collective-permute-done | bytes 262176 | tf_op jit(solution)/shard_map/ppermute | solution.py:185
  66.6 0.8 collective-permute-done.8.refs_3_
  67.4 2.0 %collective-permute-done.5.refs_1_ = bf16[64,2048]{1,0:T(8,128)(2,1)S(1)} collective-permute-done((bf16[64,2048]{1,0:T(8,128)(2,1)S(1)}, bf16[64,2048]{1,0:T(8,128)(2,1)S(1)}, u32[]{:S(2)}, u32[]{:S(2)}) %collective-permute-start.5) | collective-permute-done | bytes 262176 | tf_op jit(solution)/shard_map/ppermute | solution.py:185
  69.4 3.1 %project_mate.2 = (bf16[256,2048]{1,0:T(8,128)(2,1)S(1)}, bf16[256,2048]{1,0:T(8,128)(2,1)S(1)}) custom-call(bf16[64,2048]{1,0:T(8,128)(2,1)S(1)} %collective-permute-done.4.refs_0_, bf16[64,2048]{1,0:T(8,128)(2,1)S(1)} %collective-permute-done.5.refs_1_, bf16[64,2048]{1,0:T(8,128)(2,1)S(1)} %collective-permute-done.7.refs_2_, ...), custom_call_target="tpu_custom_call" | custom-call | flops 2147483648 | bytes 12582912 | tf_op jit(solution)/shard_map/project_mate/pallas_call | solution.py:38
  72.5 0.1 collective-permute-start.18
  72.6 0.1 collective-permute-start.24
  72.6 3.2 %collective-permute-start.22 = (bf16[64,2048]{1,0:T(8,128)(2,1)S(1)}, bf16[64,2048]{1,0:T(8,128)(2,1)S(1)}, u32[]{:S(2)}, u32[]{:S(2)}) collective-permute-start(bf16[64,2048]{1,0:T(8,128)(2,1)S(1)} %collective-permute-done.17.refs_9_.refs_0_), channel_id=1, source_target_pairs={{0,96},{16,112},{32,0},{48,16},{64,32},{80,48},{96,64},{112,80},{1... | collective-permute-start | bytes 786440 | tf_op jit(solution)/shard_map/ppermute | solution.py:185
  75.9 0.7 collective-permute-start.23
  76.6 2.4 %project_column.3.refs_2_.refs_5_ = bf16[256,2048]{1,0:T(8,128)(2,1)S(1)} custom-call(bf16[64,2048]{1,0:T(8,128)(2,1)S(1)} %hadamard_z.3.refs_5_.refs_0_, bf16[64,2048]{1,0:T(8,128)(2,1)S(1)} %collective-permute-done.14.refs_6_.refs_1_, bf16[64,2048]{1,0:T(8,128)(2,1)S(1)} %collective-permute-done.15.refs_7_.refs_2_, ...), custom_call_target="tpu_custom_call" | custom-call | flops 2147483648 | bytes 10485760 | tf_op jit(solution)/shard_map/project_column/pallas_call | solution.py:38
  78.9 0.0 copy-start.2
  78.9 0.2 core_sum.2
  79.1 3.4 %collective-permute-done.24.refs_3_ = bf16[64,2048]{1,0:T(8,128)(2,1)S(1)} collective-permute-done((bf16[64,2048]{1,0:T(8,128)(2,1)S(1)}, bf16[64,2048]{1,0:T(8,128)(2,1)S(1)}, u32[]{:S(2)}, u32[]{:S(2)}) %collective-permute-start.24) | collective-permute-done | bytes 262176 | tf_op jit(solution)/shard_map/ppermute | solution.py:185
  82.5 1.5 %collective-permute-done.23.refs_2_ = bf16[64,2048]{1,0:T(8,128)(2,1)S(1)} collective-permute-done((bf16[64,2048]{1,0:T(8,128)(2,1)S(1)}, bf16[64,2048]{1,0:T(8,128)(2,1)S(1)}, u32[]{:S(2)}, u32[]{:S(2)}) %collective-permute-start.23) | collective-permute-done | bytes 262176 | tf_op jit(solution)/shard_map/ppermute | solution.py:185
  84.0 3.0 %project_mate.3 = (bf16[256,2048]{1,0:T(8,128)(2,1)S(1)}, bf16[256,2048]{1,0:T(8,128)(2,1)S(1)}) custom-call(bf16[64,2048]{1,0:T(8,128)(2,1)S(1)} %collective-permute-done.17.refs_9_.refs_0_, bf16[64,2048]{1,0:T(8,128)(2,1)S(1)} %collective-permute-done.22.refs_1_, bf16[64,2048]{1,0:T(8,128)(2,1)S(1)} %collective-permute-done.23.refs_2_, ...), custom_call_target="tpu_custom_call" | custom-call | flops 2147483648 | bytes 12582912 | tf_op jit(solution)/shard_map/project_mate/pallas_call | solution.py:38
  87.0 0.1 collective-permute-start.26
  87.1 0.6 collective-permute-start.20
  87.7 2.5 %collective-permute-start.21 = (bf16[64,2048]{1,0:T(8,128)(2,1)S(1)}, bf16[64,2048]{1,0:T(8,128)(2,1)S(1)}, u32[]{:S(2)}, u32[]{:S(2)}) collective-permute-start(bf16[64,2048]{1,0:T(8,128)(2,1)S(1)} %get-tuple-element.23), channel_id=1, source_target_pairs={{0,12},{2,14},{4,0},{6,2},{8,4},{10,6},{12,8},{14,10},{1,13},{3,15... | collective-permute-start | bytes 786440 | tf_op jit(solution)/shard_map/ppermute | solution.py:185
  90.3 7.6 %collective-permute-done.20.refs_3_ = bf16[64,2048]{1,0:T(8,128)(2,1)S(1)} collective-permute-done((bf16[64,2048]{1,0:T(8,128)(2,1)S(1)}, bf16[64,2048]{1,0:T(8,128)(2,1)S(1)}, u32[]{:S(2)}, u32[]{:S(2)}) %collective-permute-start.20) | collective-permute-done | bytes 262176 | tf_op jit(solution)/shard_map/ppermute | solution.py:185
  97.9 2.3 %collective-permute-done.21.refs_4_ = bf16[64,2048]{1,0:T(8,128)(2,1)S(1)} collective-permute-done((bf16[64,2048]{1,0:T(8,128)(2,1)S(1)}, bf16[64,2048]{1,0:T(8,128)(2,1)S(1)}, u32[]{:S(2)}, u32[]{:S(2)}) %collective-permute-start.21) | collective-permute-done | bytes 262176 | tf_op jit(solution)/shard_map/ppermute | solution.py:185
  100.1 2.8 %collective-permute-done.19.refs_2_ = bf16[64,2048]{1,0:T(8,128)(2,1)S(1)} collective-permute-done((bf16[64,2048]{1,0:T(8,128)(2,1)S(1)}, bf16[64,2048]{1,0:T(8,128)(2,1)S(1)}, u32[]{:S(2)}, u32[]{:S(2)}) %collective-permute-start.19) | collective-permute-done | bytes 262176 | tf_op jit(solution)/shard_map/ppermute | solution.py:185
  103.0 0.2 residual.2
  103.2 0.2 core_sum.3
  103.4 0.1 collective-permute-start.27
  103.4 2.1 %collective-permute-start.28 = (bf16[64,2048]{1,0:T(8,128)(2,1)S(1)}, bf16[64,2048]{1,0:T(8,128)(2,1)S(1)}, u32[]{:S(2)}, u32[]{:S(2)}) collective-permute-start(bf16[64,2048]{1,0:T(8,128)(2,1)S(1)} %get-tuple-element.29), channel_id=1, source_target_pairs={{0,8},{2,10},{4,12},{6,14},{8,0},{10,2},{12,4},{14,6},{1,9},{3,11}... | collective-permute-start | bytes 786440 | tf_op jit(solution)/shard_map/ppermute | solution.py:185
  105.5 1.6 %collective-permute-start.29 = (bf16[64,2048]{1,0:T(8,128)(2,1)S(1)}, bf16[64,2048]{1,0:T(8,128)(2,1)S(1)}, u32[]{:S(2)}, u32[]{:S(2)}) collective-permute-start(bf16[64,2048]{1,0:T(8,128)(2,1)S(1)} %get-tuple-element.30), channel_id=1, source_target_pairs={{0,12},{2,14},{4,0},{6,2},{8,4},{10,6},{12,8},{14,10},{1,13},{3,15... | collective-permute-start | bytes 786440 | tf_op jit(solution)/shard_map/ppermute | solution.py:185
  107.1 1.3 collective-permute-start.25
  108.4 10.1 %collective-permute-done.27.refs_2_ = bf16[64,2048]{1,0:T(8,128)(2,1)S(1)} collective-permute-done((bf16[64,2048]{1,0:T(8,128)(2,1)S(1)}, bf16[64,2048]{1,0:T(8,128)(2,1)S(1)}, u32[]{:S(2)}, u32[]{:S(2)}) %collective-permute-start.27) | collective-permute-done | bytes 262176 | tf_op jit(solution)/shard_map/ppermute | solution.py:185
  118.5 0.6 collective-permute-done.29.refs_4_
  119.1 0.2 residual.3
  119.3 1.3 collective-permute-start.30
  120.6 9.2 %collective-permute-done.30.refs_5_ = bf16[64,2048]{1,0:T(8,128)(2,1)S(1)} collective-permute-done((bf16[64,2048]{1,0:T(8,128)(2,1)S(1)}, bf16[64,2048]{1,0:T(8,128)(2,1)S(1)}, u32[]{:S(2)}, u32[]{:S(2)}) %collective-permute-start.30) | collective-permute-done | bytes 262176 | tf_op jit(solution)/shard_map/ppermute | solution.py:194
  129.8 0.9 end.1
  (23 shorter events, 0.1 us)
Async XLA Ops:
  0.0 1.0 copy-start.3
  1.0 0.7 copy-start.4
  2.5 2.0 %collective-permute-start = (bf16[128,2048]{1,0:T(8,128)(2,1)S(1)}, bf16[128,2048]{1,0:T(8,128)(2,1)S(1)}, u32[]{:S(2)}, u32[]{:S(2)}) collective-permute-start(bf16[128,2048]{1,0:T(8,128)(2,1)S(1)} %rotate_local.1.refs_0_), channel_id=1, source_target_pairs={{0,2},{2,0},{4,6},{6,4},{8,10},{10,8},{12,14},{14,12},{1,3},{3,1},... | collective-permute-start | bytes 1572872 | tf_op jit(solution)/shard_map/ppermute | solution.py:185
  4.6 15.6 %collective-permute-start.1 = (bf16[64,2048]{1,0:T(8,128)(2,1)S(1)}, bf16[64,2048]{1,0:T(8,128)(2,1)S(1)}, u32[]{:S(2)}, u32[]{:S(2)}) collective-permute-start(bf16[64,2048]{1,0:T(8,128)(2,1)S(1)} %hadamard_core.2.refs_1_.refs_0_), channel_id=1, source_target_pairs={{0,12},{2,14},{4,0},{6,2},{8,4},{10,6},{12,8},{14,10},{1,13},{3,15... | collective-permute-start | bytes 786440 | tf_op jit(solution)/shard_map/ppermute | solution.py:185
  8.7 23.6 %collective-permute-start.3 = (bf16[64,2048]{1,0:T(8,128)(2,1)S(1)}, bf16[64,2048]{1,0:T(8,128)(2,1)S(1)}, u32[]{:S(2)}, u32[]{:S(2)}) collective-permute-start(bf16[64,2048]{1,0:T(8,128)(2,1)S(1)} %hadamard_core.2.refs_1_.refs_0_), channel_id=1, source_target_pairs={{0,4},{2,6},{4,8},{6,10},{8,12},{10,14},{12,0},{14,2},{1,5},{3,7},... | collective-permute-start | bytes 786440 | tf_op jit(solution)/shard_map/ppermute | solution.py:185
  8.7 23.6 %collective-permute-start.2 = (bf16[64,2048]{1,0:T(8,128)(2,1)S(1)}, bf16[64,2048]{1,0:T(8,128)(2,1)S(1)}, u32[]{:S(2)}, u32[]{:S(2)}) collective-permute-start(bf16[64,2048]{1,0:T(8,128)(2,1)S(1)} %hadamard_core.2.refs_1_.refs_0_), channel_id=1, source_target_pairs={{0,8},{2,10},{4,12},{6,14},{8,0},{10,2},{12,4},{14,6},{1,9},{3,11}... | collective-permute-start | bytes 786440 | tf_op jit(solution)/shard_map/ppermute | solution.py:185
  20.2 18.9 %collective-permute-start.13 = (bf16[64,2048]{1,0:T(8,128)(2,1)S(1)}, bf16[64,2048]{1,0:T(8,128)(2,1)S(1)}, u32[]{:S(2)}, u32[]{:S(2)}) collective-permute-start(bf16[64,2048]{1,0:T(8,128)(2,1)S(1)} %hadamard_core.3.refs_0_), channel_id=1, source_target_pairs={{0,4},{2,6},{4,8},{6,10},{8,12},{10,14},{12,0},{14,2},{1,5},{3,7},... | collective-permute-start | bytes 786440 | tf_op jit(solution)/shard_map/ppermute | solution.py:185
  27.0 14.1 %collective-permute-start.12 = (bf16[64,2048]{1,0:T(8,128)(2,1)S(1)}, bf16[64,2048]{1,0:T(8,128)(2,1)S(1)}, u32[]{:S(2)}, u32[]{:S(2)}) collective-permute-start(bf16[64,2048]{1,0:T(8,128)(2,1)S(1)} %hadamard_core.3.refs_0_), channel_id=1, source_target_pairs={{0,8},{2,10},{4,12},{6,14},{8,0},{10,2},{12,4},{14,6},{1,9},{3,11}... | collective-permute-start | bytes 786440 | tf_op jit(solution)/shard_map/ppermute | solution.py:185
  32.2 10.6 %collective-permute-start.11 = (bf16[64,2048]{1,0:T(8,128)(2,1)S(1)}, bf16[64,2048]{1,0:T(8,128)(2,1)S(1)}, u32[]{:S(2)}, u32[]{:S(2)}) collective-permute-start(bf16[64,2048]{1,0:T(8,128)(2,1)S(1)} %hadamard_core.3.refs_0_), channel_id=1, source_target_pairs={{0,12},{2,14},{4,0},{6,2},{8,4},{10,6},{12,8},{14,10},{1,13},{3,15... | collective-permute-start | bytes 786440 | tf_op jit(solution)/shard_map/ppermute | solution.py:185
  32.2 3.4 %copy-start = (bf16[2048,2048]{1,0:T(8,128)(2,1)S(1)}, bf16[2048,2048]{1,0:T(8,128)(2,1)}, u32[]{:S(2)}) copy-start(bf16[2048,2048]{1,0:T(8,128)(2,1)} %load_weight.1.refs_4_) | copy-start | bytes 25165828
  35.6 25.7 %copy-start.1 = (bf16[2048,2048]{1,0:T(8,128)(2,1)S(1)}, bf16[2048,2048]{1,0:T(8,128)(2,1)}, u32[]{:S(2)}) copy-start(bf16[2048,2048]{1,0:T(8,128)(2,1)} %load_weight.1.refs_4_) | copy-start | bytes 25165828
  35.8 9.4 %collective-permute-start.10 = (bf16[64,2048]{1,0:T(8,128)(2,1)S(1)}, bf16[64,2048]{1,0:T(8,128)(2,1)S(1)}, u32[]{:S(2)}, u32[]{:S(2)}) collective-permute-start(bf16[64,2048]{1,0:T(8,128)(2,1)S(1)} %hadamard_z.2.refs_4_.refs_0_), channel_id=1, source_target_pairs={{0,32},{16,48},{32,64},{48,80},{64,96},{80,112},{96,0},{112,16},{1... | collective-permute-start | bytes 786440 | tf_op jit(solution)/shard_map/ppermute | solution.py:185
  37.5 14.5 %collective-permute-start.9 = (bf16[64,2048]{1,0:T(8,128)(2,1)S(1)}, bf16[64,2048]{1,0:T(8,128)(2,1)S(1)}, u32[]{:S(2)}, u32[]{:S(2)}) collective-permute-start(bf16[64,2048]{1,0:T(8,128)(2,1)S(1)} %hadamard_z.2.refs_4_.refs_0_), channel_id=1, source_target_pairs={{0,96},{16,112},{32,0},{48,16},{64,32},{80,48},{96,64},{112,80},{1... | collective-permute-start | bytes 786440 | tf_op jit(solution)/shard_map/ppermute | solution.py:185
  39.1 14.1 %collective-permute-start.6 = (bf16[64,2048]{1,0:T(8,128)(2,1)S(1)}, bf16[64,2048]{1,0:T(8,128)(2,1)S(1)}, u32[]{:S(2)}, u32[]{:S(2)}) collective-permute-start(bf16[64,2048]{1,0:T(8,128)(2,1)S(1)} %hadamard_z.2.refs_4_.refs_0_), channel_id=1, source_target_pairs={{0,64},{16,80},{32,96},{48,112},{64,0},{80,16},{96,32},{112,48},{1... | collective-permute-start | bytes 786440 | tf_op jit(solution)/shard_map/ppermute | solution.py:185
  41.1 14.6 %collective-permute-start.4 = (bf16[64,2048]{1,0:T(8,128)(2,1)S(1)}, bf16[64,2048]{1,0:T(8,128)(2,1)S(1)}, u32[]{:S(2)}, u32[]{:S(2)}) collective-permute-start(bf16[64,2048]{1,0:T(8,128)(2,1)S(1)} %hadamard_z.2.refs_4_.refs_0_), channel_id=1, source_target_pairs={{0,16},{16,0},{32,48},{48,32},{64,80},{80,64},{96,112},{112,96},{1... | collective-permute-start | bytes 786440 | tf_op jit(solution)/shard_map/ppermute | solution.py:185
  43.0 14.0 %collective-permute-start.17 = (bf16[64,2048]{1,0:T(8,128)(2,1)S(1)}, bf16[64,2048]{1,0:T(8,128)(2,1)S(1)}, u32[]{:S(2)}, u32[]{:S(2)}) collective-permute-start(bf16[64,2048]{1,0:T(8,128)(2,1)S(1)} %hadamard_z.3.refs_5_.refs_0_), channel_id=1, source_target_pairs={{0,16},{16,0},{32,48},{48,32},{64,80},{80,64},{96,112},{112,96},{1... | collective-permute-start | bytes 786440 | tf_op jit(solution)/shard_map/ppermute | solution.py:185
  45.2 16.1 %collective-permute-start.16 = (bf16[64,2048]{1,0:T(8,128)(2,1)S(1)}, bf16[64,2048]{1,0:T(8,128)(2,1)S(1)}, u32[]{:S(2)}, u32[]{:S(2)}) collective-permute-start(bf16[64,2048]{1,0:T(8,128)(2,1)S(1)} %hadamard_z.3.refs_5_.refs_0_), channel_id=1, source_target_pairs={{0,32},{16,48},{32,64},{48,80},{64,96},{80,112},{96,0},{112,16},{1... | collective-permute-start | bytes 786440 | tf_op jit(solution)/shard_map/ppermute | solution.py:185
  51.9 12.6 %collective-permute-start.15 = (bf16[64,2048]{1,0:T(8,128)(2,1)S(1)}, bf16[64,2048]{1,0:T(8,128)(2,1)S(1)}, u32[]{:S(2)}, u32[]{:S(2)}) collective-permute-start(bf16[64,2048]{1,0:T(8,128)(2,1)S(1)} %hadamard_z.3.refs_5_.refs_0_), channel_id=1, source_target_pairs={{0,64},{16,80},{32,96},{48,112},{64,0},{80,16},{96,32},{112,48},{1... | collective-permute-start | bytes 786440 | tf_op jit(solution)/shard_map/ppermute | solution.py:185
  53.3 13.3 %collective-permute-start.14 = (bf16[64,2048]{1,0:T(8,128)(2,1)S(1)}, bf16[64,2048]{1,0:T(8,128)(2,1)S(1)}, u32[]{:S(2)}, u32[]{:S(2)}) collective-permute-start(bf16[64,2048]{1,0:T(8,128)(2,1)S(1)} %hadamard_z.3.refs_5_.refs_0_), channel_id=1, source_target_pairs={{0,96},{16,112},{32,0},{48,16},{64,32},{80,48},{96,64},{112,80},{1... | collective-permute-start | bytes 786440 | tf_op jit(solution)/shard_map/ppermute | solution.py:185
  55.8 10.8 %collective-permute-start.7 = (bf16[64,2048]{1,0:T(8,128)(2,1)S(1)}, bf16[64,2048]{1,0:T(8,128)(2,1)S(1)}, u32[]{:S(2)}, u32[]{:S(2)}) collective-permute-start(bf16[64,2048]{1,0:T(8,128)(2,1)S(1)} %collective-permute-done.6.refs_2_), channel_id=1, source_target_pairs={{0,16},{16,0},{32,48},{48,32},{64,80},{80,64},{96,112},{112,96},{1... | collective-permute-start | bytes 786440 | tf_op jit(solution)/shard_map/ppermute | solution.py:185
  57.0 10.4 %collective-permute-start.8 = (bf16[64,2048]{1,0:T(8,128)(2,1)S(1)}, bf16[64,2048]{1,0:T(8,128)(2,1)S(1)}, u32[]{:S(2)}, u32[]{:S(2)}) collective-permute-start(bf16[64,2048]{1,0:T(8,128)(2,1)S(1)} %collective-permute-done.4.refs_0_), channel_id=1, source_target_pairs={{0,32},{16,48},{32,64},{48,80},{64,96},{80,112},{96,0},{112,16},{1... | collective-permute-start | bytes 786440 | tf_op jit(solution)/shard_map/ppermute | solution.py:185
  61.3 8.1 %collective-permute-start.5 = (bf16[64,2048]{1,0:T(8,128)(2,1)S(1)}, bf16[64,2048]{1,0:T(8,128)(2,1)S(1)}, u32[]{:S(2)}, u32[]{:S(2)}) collective-permute-start(bf16[64,2048]{1,0:T(8,128)(2,1)S(1)} %collective-permute-done.4.refs_0_), channel_id=1, source_target_pairs={{0,96},{16,112},{32,0},{48,16},{64,32},{80,48},{96,64},{112,80},{1... | collective-permute-start | bytes 786440 | tf_op jit(solution)/shard_map/ppermute | solution.py:185
  72.5 6.5 %collective-permute-start.18 = (bf16[256,2048]{1,0:T(8,128)(2,1)S(1)}, bf16[256,2048]{1,0:T(8,128)(2,1)S(1)}, u32[]{:S(2)}, u32[]{:S(2)}) collective-permute-start(bf16[256,2048]{1,0:T(8,128)(2,1)S(1)} %get-tuple-element.20.refs_5_), channel_id=1, source_target_pairs={{0,2},{2,0},{4,6},{6,4},{8,10},{10,8},{12,14},{14,12},{1,3},{3,1},... | collective-permute-start | bytes 3145736 | tf_op jit(solution)/shard_map/ppermute | solution.py:185
  72.6 9.9 %collective-permute-start.24 = (bf16[64,2048]{1,0:T(8,128)(2,1)S(1)}, bf16[64,2048]{1,0:T(8,128)(2,1)S(1)}, u32[]{:S(2)}, u32[]{:S(2)}) collective-permute-start(bf16[64,2048]{1,0:T(8,128)(2,1)S(1)} %collective-permute-done.17.refs_9_.refs_0_), channel_id=1, source_target_pairs={{0,32},{16,48},{32,64},{48,80},{64,96},{80,112},{96,0},{112,16},{1... | collective-permute-start | bytes 786440 | tf_op jit(solution)/shard_map/ppermute | solution.py:185
  72.6 9.9 %collective-permute-start.22 = (bf16[64,2048]{1,0:T(8,128)(2,1)S(1)}, bf16[64,2048]{1,0:T(8,128)(2,1)S(1)}, u32[]{:S(2)}, u32[]{:S(2)}) collective-permute-start(bf16[64,2048]{1,0:T(8,128)(2,1)S(1)} %collective-permute-done.17.refs_9_.refs_0_), channel_id=1, source_target_pairs={{0,96},{16,112},{32,0},{48,16},{64,32},{80,48},{96,64},{112,80},{1... | collective-permute-start | bytes 786440 | tf_op jit(solution)/shard_map/ppermute | solution.py:185
  75.9 8.1 %collective-permute-start.23 = (bf16[64,2048]{1,0:T(8,128)(2,1)S(1)}, bf16[64,2048]{1,0:T(8,128)(2,1)S(1)}, u32[]{:S(2)}, u32[]{:S(2)}) collective-permute-start(bf16[64,2048]{1,0:T(8,128)(2,1)S(1)} %collective-permute-done.15.refs_7_.refs_2_), channel_id=1, source_target_pairs={{0,16},{16,0},{32,48},{48,32},{64,80},{80,64},{96,112},{112,96},{1... | collective-permute-start | bytes 786440 | tf_op jit(solution)/shard_map/ppermute | solution.py:185
  78.9 24.0 %copy-start.2 = (bf16[128,2048]{1,0:T(8,128)(2,1)S(1)}, bf16[128,2048]{1,0:T(8,128)(2,1)}, u32[]{:S(2)}) copy-start(bf16[128,2048]{1,0:T(8,128)(2,1)} %refs_5_.3) | copy-start | bytes 1572868
  87.0 16.1 %collective-permute-start.26 = (bf16[256,2048]{1,0:T(8,128)(2,1)S(1)}, bf16[256,2048]{1,0:T(8,128)(2,1)S(1)}, u32[]{:S(2)}, u32[]{:S(2)}) collective-permute-start(bf16[256,2048]{1,0:T(8,128)(2,1)S(1)} %get-tuple-element.24.refs_6_), channel_id=1, source_target_pairs={{0,2},{2,0},{4,6},{6,4},{8,10},{10,8},{12,14},{14,12},{1,3},{3,1},... | collective-permute-start | bytes 3145736 | tf_op jit(solution)/shard_map/ppermute | solution.py:185
  87.1 10.7 %collective-permute-start.20 = (bf16[64,2048]{1,0:T(8,128)(2,1)S(1)}, bf16[64,2048]{1,0:T(8,128)(2,1)S(1)}, u32[]{:S(2)}, u32[]{:S(2)}) collective-permute-start(bf16[64,2048]{1,0:T(8,128)(2,1)S(1)} %get-tuple-element.22), channel_id=1, source_target_pairs={{0,8},{2,10},{4,12},{6,14},{8,0},{10,2},{12,4},{14,6},{1,9},{3,11}... | collective-permute-start | bytes 786440 | tf_op jit(solution)/shard_map/ppermute | solution.py:185
  87.7 12.4 %collective-permute-start.21 = (bf16[64,2048]{1,0:T(8,128)(2,1)S(1)}, bf16[64,2048]{1,0:T(8,128)(2,1)S(1)}, u32[]{:S(2)}, u32[]{:S(2)}) collective-permute-start(bf16[64,2048]{1,0:T(8,128)(2,1)S(1)} %get-tuple-element.23), channel_id=1, source_target_pairs={{0,12},{2,14},{4,0},{6,2},{8,4},{10,6},{12,8},{14,10},{1,13},{3,15... | collective-permute-start | bytes 786440 | tf_op jit(solution)/shard_map/ppermute | solution.py:185
  90.3 12.7 %collective-permute-start.19 = (bf16[64,2048]{1,0:T(8,128)(2,1)S(1)}, bf16[64,2048]{1,0:T(8,128)(2,1)S(1)}, u32[]{:S(2)}, u32[]{:S(2)}) collective-permute-start(bf16[64,2048]{1,0:T(8,128)(2,1)S(1)} %get-tuple-element.21.refs_6_), channel_id=1, source_target_pairs={{0,4},{2,6},{4,8},{6,10},{8,12},{10,14},{12,0},{14,2},{1,5},{3,7},... | collective-permute-start | bytes 786440 | tf_op jit(solution)/shard_map/ppermute | solution.py:185
  103.4 15.1 %collective-permute-start.27 = (bf16[64,2048]{1,0:T(8,128)(2,1)S(1)}, bf16[64,2048]{1,0:T(8,128)(2,1)S(1)}, u32[]{:S(2)}, u32[]{:S(2)}) collective-permute-start(bf16[64,2048]{1,0:T(8,128)(2,1)S(1)} %get-tuple-element.28), channel_id=1, source_target_pairs={{0,4},{2,6},{4,8},{6,10},{8,12},{10,14},{12,0},{14,2},{1,5},{3,7},... | collective-permute-start | bytes 786440 | tf_op jit(solution)/shard_map/ppermute | solution.py:185
  103.4 15.0 %collective-permute-start.28 = (bf16[64,2048]{1,0:T(8,128)(2,1)S(1)}, bf16[64,2048]{1,0:T(8,128)(2,1)S(1)}, u32[]{:S(2)}, u32[]{:S(2)}) collective-permute-start(bf16[64,2048]{1,0:T(8,128)(2,1)S(1)} %get-tuple-element.29), channel_id=1, source_target_pairs={{0,8},{2,10},{4,12},{6,14},{8,0},{10,2},{12,4},{14,6},{1,9},{3,11}... | collective-permute-start | bytes 786440 | tf_op jit(solution)/shard_map/ppermute | solution.py:185
  105.5 13.6 %collective-permute-start.29 = (bf16[64,2048]{1,0:T(8,128)(2,1)S(1)}, bf16[64,2048]{1,0:T(8,128)(2,1)S(1)}, u32[]{:S(2)}, u32[]{:S(2)}) collective-permute-start(bf16[64,2048]{1,0:T(8,128)(2,1)S(1)} %get-tuple-element.30), channel_id=1, source_target_pairs={{0,12},{2,14},{4,0},{6,2},{8,4},{10,6},{12,8},{14,10},{1,13},{3,15... | collective-permute-start | bytes 786440 | tf_op jit(solution)/shard_map/ppermute | solution.py:185
  107.1 13.5 %collective-permute-start.25 = (bf16[64,2048]{1,0:T(8,128)(2,1)S(1)}, bf16[64,2048]{1,0:T(8,128)(2,1)S(1)}, u32[]{:S(2)}, u32[]{:S(2)}) collective-permute-start(bf16[64,2048]{1,0:T(8,128)(2,1)S(1)} %get-tuple-element.25.refs_2_.refs_0_), channel_id=1, source_target_pairs={{0,1},{2,3},{4,5},{6,7},{8,9},{10,11},{12,13},{14,15},{16,17},{18,... | collective-permute-start | bytes 786440 | tf_op jit(solution)/shard_map/ppermute | solution.py:194
  119.3 10.5 %collective-permute-start.30 = (bf16[64,2048]{1,0:T(8,128)(2,1)S(1)}, bf16[64,2048]{1,0:T(8,128)(2,1)S(1)}, u32[]{:S(2)}, u32[]{:S(2)}) collective-permute-start(bf16[64,2048]{1,0:T(8,128)(2,1)S(1)} %get-tuple-element.31.refs_3_), channel_id=1, source_target_pairs={{0,1},{2,3},{4,5},{6,7},{8,9},{10,11},{12,13},{14,15},{16,17},{18,... | collective-permute-start | bytes 786440 | tf_op jit(solution)/shard_map/ppermute | solution.py:194

commit v3 on v2

--- a/solution.py
+++ b/solution.py
@@ -42,7 +42,7 @@
         out_specs=jax.tree.map(lambda _: VMEM, out_shape),
         scratch_shapes=list(scratch),
         compiler_params=pltpu.CompilerParams(vmem_limit_bytes=limit << 20),
-        cost_estimate=pl.CostEstimate(flops=flops, bytes_accessed=size * weigh, transcendentals=0),
+        cost_estimate=pl.CostEstimate(flops=flops * weigh, bytes_accessed=size * weigh, transcendentals=0),
         name=name,
     )(*operands, *behind)
 
@@ -88,21 +88,19 @@
     refs[4][...] = total.astype(BF16)
 
 
-def load_kernel(w_ref, out_ref, sem):
-    copy = pltpu.make_async_copy(w_ref.at[0], out_ref, sem)
-    copy.start()
-    copy.wait()
+def touch_kernel(w_ref, out_ref):
+    out_ref[...] = jnp.zeros_like(out_ref)
 
 
 def products(blocks, w_ref, lhs, store):
-    width = w_ref.shape[1] // TILES
+    width = w_ref.shape[2] // TILES
     y, _, z, _ = place()
     rows = blocks[0].shape[0]
     for dy, ref in enumerate(blocks):
         lhs[pl.ds(pl.multiple_of(((y + dy - z) & 3) * rows, rows), rows), :] = ref[...]
     for n in range(TILES):
         cols = slice(n * width, (n + 1) * width)
-        out = jnp.dot(lhs[...], w_ref[:, cols], preferred_element_type=jnp.float32)
+        out = jnp.dot(lhs[...], w_ref[0, :, cols], preferred_element_type=jnp.float32)
         store(cols, out.astype(BF16))
 
 
@@ -135,7 +133,7 @@
 
 def project(blocks, weight, column=None, behind=()):
     rows, depth = blocks[0].shape
-    width = weight.shape[1]
+    width = weight.shape[2]
     half = shape(4 * rows, width)
     return call(
         "project_column" if column is None else "project_mate",
@@ -145,6 +143,7 @@
         behind,
         scratch=[pltpu.VMEM((4 * rows, depth), BF16)],
         flops=2 * 4 * rows * depth * width,
+        weigh=5,
         limit=24,
     )
 
@@ -202,7 +201,7 @@
         return [mine] + [move(mine, "tensor", ring(-k)) for k in (1, 2, 3)]
 
     def mix(terms, behind=()):
-        return call("hadamard_z", mix_kernel, terms, shape(rows, width), behind)
+        return call("hadamard_z", mix_kernel, terms, shape(rows, width), behind, weigh=20)
 
     def spread_column(own):
         mate = move(own, "dp", ring(0, 1))
@@ -236,30 +235,21 @@
     )
     other = swap(local)
     terms0 = spread_z(pair(0, local, other))
-    terms1 = spread_z(pair(1, local, other, [terms0[1]]))
-    weight = call(
-        "load_weight",
-        load_kernel,
-        (out_weight,),
-        shape(*out_weight.shape[1:]),
-        [terms0[0]],
-        specs=[HBM],
-        scratch=[pltpu.SemaphoreType.DMA],
-        limit=48,
-    )
-    own0 = mix(terms0, [weight])
-    own1 = mix(terms1, [own0])
+    ready = call("weight", touch_kernel, (out_weight,), shape(8, LANES), [terms0[0]], weigh=9)
+    terms1 = spread_z(pair(1, local, other, [terms0[1], ready]))
+    own0 = mix(terms0, [terms1[0]])
     column0, mate0 = spread_column(own0)
+    own1 = mix(terms1, [mate0, column0[2]])
+    mates0 = spread_mate(column0, mate0)
     column1, mate1 = spread_column(own1)
-    mates0 = spread_mate(column0, mate0)
-    products0 = project(column0, weight, None, [own1])
-    keep0, send0 = project(mates0, weight, products0, [*column1[1:], mate1])
+    products0 = project(column0, out_weight, None, [own1])
+    keep0, send0 = project(mates0, out_weight, products0)
     came0 = swap(send0)
     mates1 = spread_mate(column1, mate1)
-    products1 = project(column1, weight, None, [send0])
+    products1 = project(column1, out_weight, None, [send0])
     parts0 = halves(keep0, came0, [products1])
     arrived0 = gather_z(parts0)
-    keep1, send1 = project(mates1, weight, products1, [parts0[0]])
+    keep1, send1 = project(mates1, out_weight, products1, [parts0[0]])
     came1 = swap(send1)
     leading0, summed0 = finish(0, keep0, came0, arrived0, [send1])
     passed0 = pipe(leading0)

time: 131 us -> 121 us (0.924)
  Pallas kernels: 20.5 us -> 13.8 us
  waiting for transfers between devices: 66 us -> 63.5 us
    pallas_call x15, Pallas kernels: 20.5 us -> 13.8 us  [call(): pl.pallas_call(lambda *refs: kernel(*refs[:count], *refs[count + len(behi...]
    ppermute x29, waiting for transfers between devices: 56.8 us -> 54.3 us  [move(): lax.ppermute(value, axis, [(i, target(i)) for i in range(lax.axis_size(ax...]
  transfers between devices with their start and end apart: 31 -> 31, of which waited for: 19 -> 17; matrix products, arithmetic and copies ran while one was open for 0% -> 0% of each run, Pallas kernels for 10% -> 7%
where the time goes in v3:
time: 121 us
  waiting for transfers between devices  63.5 us (52%)
  starting transfers between devices  38.1 us (31%)
  Pallas kernels  13.8 us (11%)
  local copies, waits for them, and re-layouts  5.13 us (4%)
    ppermute x29, waiting for transfers between devices, move(): lax.ppermute(value, axis, [(i, target(i)) for i in range(lax.axis_size(ax...  54.3 us
    ppermute x29, starting transfers between devices, move(): lax.ppermute(value, axis, [(i, target(i)) for i in range(lax.axis_size(ax...  35.6 us
    pallas_call x15, Pallas kernels, call(): pl.pallas_call(lambda *refs: kernel(*refs[:count], *refs[count + len(behi...  13.8 us
    ppermute x2, waiting for transfers between devices, pipe(): return lax.ppermute(value, 'pipe', [(0, 1)])  9.26 us
    unnamed x10, local copies, waits for them, and re-layouts  5.13 us
    ppermute x2, starting transfers between devices, pipe(): return lax.ppermute(value, 'pipe', [(0, 1)])  2.57 us
  transfers between devices with their start and end apart: 31, of which 17 were waited for; matrix products, arithmetic and copies ran while one was open for 0% of the time, Pallas kernels for 7%

profile of v3, /device:TPU:4, one launch (start us, length us, event | category | flops | bytes accessed | tf_op | source)
XLA Modules:
  0.0 120.7 jit_solution(8480874245813678026)
XLA Ops:
  0.0 1.0 copy-done.3
  1.0 0.7 copy-done.4
  1.7 0.7 rotate_local.1.refs_0_
  2.5 0.1 collective-permute-start
  2.6 1.9 %collective-permute-done.refs_1_ = bf16[128,2048]{1,0:T(8,128)(2,1)S(1)} collective-permute-done((bf16[128,2048]{1,0:T(8,128)(2,1)S(1)}, bf16[128,2048]{1,0:T(8,128)(2,1)S(1)}, u32[]{:S(2)}, u32[]{:S(2)}) %collective-permute-start) | collective-permute-done | bytes 524320 | tf_op jit(solution)/shard_map/ppermute | solution.py:184
  4.5 0.1 hadamard_core.2.refs_1_.refs_0_
  4.6 4.1 %collective-permute-start.1 = (bf16[64,2048]{1,0:T(8,128)(2,1)S(1)}, bf16[64,2048]{1,0:T(8,128)(2,1)S(1)}, u32[]{:S(2)}, u32[]{:S(2)}) collective-permute-start(bf16[64,2048]{1,0:T(8,128)(2,1)S(1)} %hadamard_core.2.refs_1_.refs_0_), channel_id=1, source_target_pairs={{0,12},{2,14},{4,0},{6,2},{8,4},{10,6},{12,8},{14,10},{1,13},{3,15... | collective-permute-start | bytes 786440 | tf_op jit(solution)/shard_map/ppermute | solution.py:184
  8.7 0.0 collective-permute-start.3
  8.7 1.9 %collective-permute-start.2 = (bf16[64,2048]{1,0:T(8,128)(2,1)S(1)}, bf16[64,2048]{1,0:T(8,128)(2,1)S(1)}, u32[]{:S(2)}, u32[]{:S(2)}) collective-permute-start(bf16[64,2048]{1,0:T(8,128)(2,1)S(1)} %hadamard_core.2.refs_1_.refs_0_), channel_id=1, source_target_pairs={{0,8},{2,10},{4,12},{6,14},{8,0},{10,2},{12,4},{14,6},{1,9},{3,11}... | collective-permute-start | bytes 786440 | tf_op jit(solution)/shard_map/ppermute | solution.py:184
  10.5 3.4 %copy-done = bf16[1,2048,2048]{2,1,0:T(8,128)(2,1)S(1)} copy-done((bf16[1,2048,2048]{2,1,0:T(8,128)(2,1)S(1)}, bf16[1,2048,2048]{2,1,0:T(8,128)(2,1)}, u32[]{:S(2)}) %copy-start) | copy-done | bytes 8388632
  13.9 6.2 %collective-permute-done.1.refs_2_.refs_1_ = bf16[64,2048]{1,0:T(8,128)(2,1)S(1)} collective-permute-done((bf16[64,2048]{1,0:T(8,128)(2,1)S(1)}, bf16[64,2048]{1,0:T(8,128)(2,1)S(1)}, u32[]{:S(2)}, u32[]{:S(2)}) %collective-permute-start.1) | collective-permute-done | bytes 262176 | tf_op jit(solution)/shard_map/ppermute | solution.py:184
  20.1 0.1 hadamard_core.3.refs_4_.refs_0_
  20.2 3.3 %collective-permute-done.3.refs_3_ = bf16[64,2048]{1,0:T(8,128)(2,1)S(1)} collective-permute-done((bf16[64,2048]{1,0:T(8,128)(2,1)S(1)}, bf16[64,2048]{1,0:T(8,128)(2,1)S(1)}, u32[]{:S(2)}, u32[]{:S(2)}) %collective-permute-start.3) | collective-permute-done | bytes 262176 | tf_op jit(solution)/shard_map/ppermute | solution.py:184
  23.6 0.0 collective-permute-done.2.refs_2_
  23.6 0.2 hadamard_z.2.refs_0_
  23.8 3.3 %collective-permute-start.6 = (bf16[64,2048]{1,0:T(8,128)(2,1)S(1)}, bf16[64,2048]{1,0:T(8,128)(2,1)S(1)}, u32[]{:S(2)}, u32[]{:S(2)}) collective-permute-start(bf16[64,2048]{1,0:T(8,128)(2,1)S(1)} %hadamard_z.2.refs_0_), channel_id=1, source_target_pairs={{0,64},{16,80},{32,96},{48,112},{64,0},{80,16},{96,32},{112,48},{1... | collective-permute-start | bytes 786440 | tf_op jit(solution)/shard_map/ppermute | solution.py:184
  27.0 1.2 collective-permute-start.4
  28.2 0.0 collective-permute-start.13
  28.2 1.9 %collective-permute-start.12 = (bf16[64,2048]{1,0:T(8,128)(2,1)S(1)}, bf16[64,2048]{1,0:T(8,128)(2,1)S(1)}, u32[]{:S(2)}, u32[]{:S(2)}) collective-permute-start(bf16[64,2048]{1,0:T(8,128)(2,1)S(1)} %hadamard_core.3.refs_4_.refs_0_), channel_id=1, source_target_pairs={{0,8},{2,10},{4,12},{6,14},{8,0},{10,2},{12,4},{14,6},{1,9},{3,11}... | collective-permute-start | bytes 786440 | tf_op jit(solution)/shard_map/ppermute | solution.py:184
  30.1 1.4 %collective-permute-start.11 = (bf16[64,2048]{1,0:T(8,128)(2,1)S(1)}, bf16[64,2048]{1,0:T(8,128)(2,1)S(1)}, u32[]{:S(2)}, u32[]{:S(2)}) collective-permute-start(bf16[64,2048]{1,0:T(8,128)(2,1)S(1)} %hadamard_core.3.refs_4_.refs_0_), channel_id=1, source_target_pairs={{0,12},{2,14},{4,0},{6,2},{8,4},{10,6},{12,8},{14,10},{1,13},{3,15... | collective-permute-start | bytes 786440 | tf_op jit(solution)/shard_map/ppermute | solution.py:184
  31.5 1.1 collective-permute-done.6.refs_5_.refs_2_
  32.6 1.6 %collective-permute-start.10 = (bf16[64,2048]{1,0:T(8,128)(2,1)S(1)}, bf16[64,2048]{1,0:T(8,128)(2,1)S(1)}, u32[]{:S(2)}, u32[]{:S(2)}) collective-permute-start(bf16[64,2048]{1,0:T(8,128)(2,1)S(1)} %hadamard_z.2.refs_0_), channel_id=1, source_target_pairs={{0,32},{16,48},{32,64},{48,80},{64,96},{80,112},{96,0},{112,16},{1... | collective-permute-start | bytes 786440 | tf_op jit(solution)/shard_map/ppermute | solution.py:184
  34.1 1.7 %collective-permute-start.9 = (bf16[64,2048]{1,0:T(8,128)(2,1)S(1)}, bf16[64,2048]{1,0:T(8,128)(2,1)S(1)}, u32[]{:S(2)}, u32[]{:S(2)}) collective-permute-start(bf16[64,2048]{1,0:T(8,128)(2,1)S(1)} %hadamard_z.2.refs_0_), channel_id=1, source_target_pairs={{0,96},{16,112},{32,0},{48,16},{64,32},{80,48},{96,64},{112,80},{1... | collective-permute-start | bytes 786440 | tf_op jit(solution)/shard_map/ppermute | solution.py:184
  35.8 5.9 %collective-permute-done.13.refs_3_ = bf16[64,2048]{1,0:T(8,128)(2,1)S(1)} collective-permute-done((bf16[64,2048]{1,0:T(8,128)(2,1)S(1)}, bf16[64,2048]{1,0:T(8,128)(2,1)S(1)}, u32[]{:S(2)}, u32[]{:S(2)}) %collective-permute-start.13) | collective-permute-done | bytes 262176 | tf_op jit(solution)/shard_map/ppermute | solution.py:184
  41.7 0.6 collective-permute-done.11.refs_1_
  42.3 0.2 hadamard_z.3.refs_5_.refs_0_
  42.5 0.9 collective-permute-start.21
  43.5 0.7 collective-permute-start.17
  44.1 1.2 collective-permute-start.7
  45.3 0.0 collective-permute-start.8
  45.3 3.2 %collective-permute-start.5 = (bf16[64,2048]{1,0:T(8,128)(2,1)S(1)}, bf16[64,2048]{1,0:T(8,128)(2,1)S(1)}, u32[]{:S(2)}, u32[]{:S(2)}) collective-permute-start(bf16[64,2048]{1,0:T(8,128)(2,1)S(1)} %collective-permute-done.4.refs_4_.refs_0_), channel_id=1, source_target_pairs={{0,96},{16,112},{32,0},{48,16},{64,32},{80,48},{96,64},{112,80},{1... | collective-permute-start | bytes 786440 | tf_op jit(solution)/shard_map/ppermute | solution.py:184
  48.6 2.4 %project_column.2.refs_5_ = bf16[256,2048]{1,0:T(8,128)(2,1)S(1)} custom-call(bf16[64,2048]{1,0:T(8,128)(2,1)S(1)} %hadamard_z.2.refs_0_, bf16[64,2048]{1,0:T(8,128)(2,1)S(1)} %collective-permute-done.9.refs_1_, bf16[64,2048]{1,0:T(8,128)(2,1)S(1)} %collective-permute-done.6.refs_5_.refs_2_, bf16[64,2048]{1,0:T(8,128)(2,1)S(1)} %collective-permute-done.10.refs_3_, ...), custom_call_target="tpu_custom_call" | custom-call | flops 10737418240 | bytes 52428800 | tf_op jit(solution)/shard_map/project_column/pallas_call | solution.py:38
  50.9 3.8 %collective-permute-done.7.refs_2_ = bf16[64,2048]{1,0:T(8,128)(2,1)S(1)} collective-permute-done((bf16[64,2048]{1,0:T(8,128)(2,1)S(1)}, bf16[64,2048]{1,0:T(8,128)(2,1)S(1)}, u32[]{:S(2)}, u32[]{:S(2)}) %collective-permute-start.7) | collective-permute-done | bytes 262176 | tf_op jit(solution)/shard_map/ppermute | solution.py:184
  54.8 0.4 collective-permute-start.16
  55.2 4.2 %collective-permute-done.8.refs_3_ = bf16[64,2048]{1,0:T(8,128)(2,1)S(1)} collective-permute-done((bf16[64,2048]{1,0:T(8,128)(2,1)S(1)}, bf16[64,2048]{1,0:T(8,128)(2,1)S(1)}, u32[]{:S(2)}, u32[]{:S(2)}) %collective-permute-start.8) | collective-permute-done | bytes 262176 | tf_op jit(solution)/shard_map/ppermute | solution.py:184
  59.4 3.0 %project_mate.2 = (bf16[256,2048]{1,0:T(8,128)(2,1)S(1)}, bf16[256,2048]{1,0:T(8,128)(2,1)S(1)}) custom-call(bf16[64,2048]{1,0:T(8,128)(2,1)S(1)} %collective-permute-done.4.refs_4_.refs_0_, bf16[64,2048]{1,0:T(8,128)(2,1)S(1)} %collective-permute-done.5.refs_1_, bf16[64,2048]{1,0:T(8,128)(2,1)S(1)} %collective-permute-done.7.refs_2_, ...), custom_call_target="tpu_custom_call" | custom-call | flops 10737418240 | bytes 62914560 | tf_op jit(solution)/shard_map/project_mate/pallas_call | solution.py:38
  62.4 0.1 collective-permute-start.14
  62.5 2.1 %collective-permute-start.24 = (bf16[64,2048]{1,0:T(8,128)(2,1)S(1)}, bf16[64,2048]{1,0:T(8,128)(2,1)S(1)}, u32[]{:S(2)}, u32[]{:S(2)}) collective-permute-start(bf16[64,2048]{1,0:T(8,128)(2,1)S(1)} %collective-permute-done.21.refs_0_), channel_id=1, source_target_pairs={{0,32},{16,48},{32,64},{48,80},{64,96},{80,112},{96,0},{112,16},{1... | collective-permute-start | bytes 786440 | tf_op jit(solution)/shard_map/ppermute | solution.py:184
  64.6 1.2 %collective-permute-start.22 = (bf16[64,2048]{1,0:T(8,128)(2,1)S(1)}, bf16[64,2048]{1,0:T(8,128)(2,1)S(1)}, u32[]{:S(2)}, u32[]{:S(2)}) collective-permute-start(bf16[64,2048]{1,0:T(8,128)(2,1)S(1)} %collective-permute-done.21.refs_0_), channel_id=1, source_target_pairs={{0,96},{16,112},{32,0},{48,16},{64,32},{80,48},{96,64},{112,80},{1... | collective-permute-start | bytes 786440 | tf_op jit(solution)/shard_map/ppermute | solution.py:184
  65.8 1.2 collective-permute-start.23
  67.0 2.4 %project_column.3.refs_2_.refs_5_ = bf16[256,2048]{1,0:T(8,128)(2,1)S(1)} custom-call(bf16[64,2048]{1,0:T(8,128)(2,1)S(1)} %hadamard_z.3.refs_5_.refs_0_, bf16[64,2048]{1,0:T(8,128)(2,1)S(1)} %collective-permute-done.15.refs_1_, bf16[64,2048]{1,0:T(8,128)(2,1)S(1)} %collective-permute-done.16.refs_2_, bf16[64,2048]{1,0:T(8,128)(2,1)S(1)} %collective-permute-done.17.refs_3_, ...), custom_call_target="tpu_custom_call" | custom-call | flops 10737418240 | bytes 52428800 | tf_op jit(solution)/shard_map/project_column/pallas_call | solution.py:38
  69.4 0.2 core_sum.2
  69.6 2.8 %collective-permute-done.24.refs_3_ = bf16[64,2048]{1,0:T(8,128)(2,1)S(1)} collective-permute-done((bf16[64,2048]{1,0:T(8,128)(2,1)S(1)}, bf16[64,2048]{1,0:T(8,128)(2,1)S(1)}, u32[]{:S(2)}, u32[]{:S(2)}) %collective-permute-start.24) | collective-permute-done | bytes 262176 | tf_op jit(solution)/shard_map/ppermute | solution.py:184
  72.4 0.5 collective-permute-done.22.refs_1_
  73.0 0.9 collective-permute-done.23.refs_2_
  73.9 3.0 %project_mate.3 = (bf16[256,2048]{1,0:T(8,128)(2,1)S(1)}, bf16[256,2048]{1,0:T(8,128)(2,1)S(1)}) custom-call(bf16[64,2048]{1,0:T(8,128)(2,1)S(1)} %collective-permute-done.21.refs_0_, bf16[64,2048]{1,0:T(8,128)(2,1)S(1)} %collective-permute-done.22.refs_1_, bf16[64,2048]{1,0:T(8,128)(2,1)S(1)} %collective-permute-done.23.refs_2_, ...), custom_call_target="tpu_custom_call" | custom-call | flops 10737418240 | bytes 62914560 | tf_op jit(solution)/shard_map/project_mate/pallas_call | solution.py:38
  77.0 0.1 collective-permute-start.26
  77.1 0.9 collective-permute-start.19
  77.9 2.0 %collective-permute-start.20 = (bf16[64,2048]{1,0:T(8,128)(2,1)S(1)}, bf16[64,2048]{1,0:T(8,128)(2,1)S(1)}, u32[]{:S(2)}, u32[]{:S(2)}) collective-permute-start(bf16[64,2048]{1,0:T(8,128)(2,1)S(1)} %get-tuple-element.23), channel_id=1, source_target_pairs={{0,12},{2,14},{4,0},{6,2},{8,4},{10,6},{12,8},{14,10},{1,13},{3,15... | collective-permute-start | bytes 786440 | tf_op jit(solution)/shard_map/ppermute | solution.py:184
  79.9 0.8 collective-permute-start.18
  80.7 7.1 %collective-permute-done.19.refs_3_ = bf16[64,2048]{1,0:T(8,128)(2,1)S(1)} collective-permute-done((bf16[64,2048]{1,0:T(8,128)(2,1)S(1)}, bf16[64,2048]{1,0:T(8,128)(2,1)S(1)}, u32[]{:S(2)}, u32[]{:S(2)}) %collective-permute-start.19) | collective-permute-done | bytes 262176 | tf_op jit(solution)/shard_map/ppermute | solution.py:184
  87.8 5.2 %collective-permute-done.20.refs_4_ = bf16[64,2048]{1,0:T(8,128)(2,1)S(1)} collective-permute-done((bf16[64,2048]{1,0:T(8,128)(2,1)S(1)}, bf16[64,2048]{1,0:T(8,128)(2,1)S(1)}, u32[]{:S(2)}, u32[]{:S(2)}) %collective-permute-start.20) | collective-permute-done | bytes 262176 | tf_op jit(solution)/shard_map/ppermute | solution.py:184
  93.0 0.2 residual.2
  93.2 0.2 core_sum.3
  93.4 0.3 collective-permute-start.27
  93.7 3.6 %collective-permute-start.28 = (bf16[64,2048]{1,0:T(8,128)(2,1)S(1)}, bf16[64,2048]{1,0:T(8,128)(2,1)S(1)}, u32[]{:S(2)}, u32[]{:S(2)}) collective-permute-start(bf16[64,2048]{1,0:T(8,128)(2,1)S(1)} %get-tuple-element.29), channel_id=1, source_target_pairs={{0,8},{2,10},{4,12},{6,14},{8,0},{10,2},{12,4},{14,6},{1,9},{3,11}... | collective-permute-start | bytes 786440 | tf_op jit(solution)/shard_map/ppermute | solution.py:184
  97.2 1.3 %collective-permute-start.25 = (bf16[64,2048]{1,0:T(8,128)(2,1)S(1)}, bf16[64,2048]{1,0:T(8,128)(2,1)S(1)}, u32[]{:S(2)}, u32[]{:S(2)}) collective-permute-start(bf16[64,2048]{1,0:T(8,128)(2,1)S(1)} %get-tuple-element.25.refs_2_.refs_0_), channel_id=1, source_target_pairs={{0,1},{2,3},{4,5},{6,7},{8,9},{10,11},{12,13},{14,15},{16,17},{18,... | collective-permute-start | bytes 786440 | tf_op jit(solution)/shard_map/ppermute | solution.py:193
  98.5 5.2 %collective-permute-done.27.refs_2_ = bf16[64,2048]{1,0:T(8,128)(2,1)S(1)} collective-permute-done((bf16[64,2048]{1,0:T(8,128)(2,1)S(1)}, bf16[64,2048]{1,0:T(8,128)(2,1)S(1)}, u32[]{:S(2)}, u32[]{:S(2)}) %collective-permute-start.27) | collective-permute-done | bytes 262176 | tf_op jit(solution)/shard_map/ppermute | solution.py:184
  103.7 5.1 %collective-permute-done.28.refs_3_ = bf16[64,2048]{1,0:T(8,128)(2,1)S(1)} collective-permute-done((bf16[64,2048]{1,0:T(8,128)(2,1)S(1)}, bf16[64,2048]{1,0:T(8,128)(2,1)S(1)}, u32[]{:S(2)}, u32[]{:S(2)}) %collective-permute-start.28) | collective-permute-done | bytes 262176 | tf_op jit(solution)/shard_map/ppermute | solution.py:184
  108.8 0.3 collective-permute-done.29.refs_4_
  109.1 0.2 residual.3
  109.3 1.3 %collective-permute-start.30 = (bf16[64,2048]{1,0:T(8,128)(2,1)S(1)}, bf16[64,2048]{1,0:T(8,128)(2,1)S(1)}, u32[]{:S(2)}, u32[]{:S(2)}) collective-permute-start(bf16[64,2048]{1,0:T(8,128)(2,1)S(1)} %get-tuple-element.31.refs_3_), channel_id=1, source_target_pairs={{0,1},{2,3},{4,5},{6,7},{8,9},{10,11},{12,13},{14,15},{16,17},{18,... | collective-permute-start | bytes 786440 | tf_op jit(solution)/shard_map/ppermute | solution.py:193
  110.6 9.3 %collective-permute-done.30.refs_5_ = bf16[64,2048]{1,0:T(8,128)(2,1)S(1)} collective-permute-done((bf16[64,2048]{1,0:T(8,128)(2,1)S(1)}, bf16[64,2048]{1,0:T(8,128)(2,1)S(1)}, u32[]{:S(2)}, u32[]{:S(2)}) %collective-permute-start.30) | collective-permute-done | bytes 262176 | tf_op jit(solution)/shard_map/ppermute | solution.py:193
  119.8 0.9 end.1
  (23 shorter events, 0.1 us)
Async XLA Ops:
  0.0 1.0 copy-start.3
  1.0 0.7 copy-start.4
  2.5 2.0 %collective-permute-start = (bf16[128,2048]{1,0:T(8,128)(2,1)S(1)}, bf16[128,2048]{1,0:T(8,128)(2,1)S(1)}, u32[]{:S(2)}, u32[]{:S(2)}) collective-permute-start(bf16[128,2048]{1,0:T(8,128)(2,1)S(1)} %rotate_local.1.refs_0_), channel_id=1, source_target_pairs={{0,2},{2,0},{4,6},{6,4},{8,10},{10,8},{12,14},{14,12},{1,3},{3,1},... | collective-permute-start | bytes 1572872 | tf_op jit(solution)/shard_map/ppermute | solution.py:184
  4.6 15.6 %collective-permute-start.1 = (bf16[64,2048]{1,0:T(8,128)(2,1)S(1)}, bf16[64,2048]{1,0:T(8,128)(2,1)S(1)}, u32[]{:S(2)}, u32[]{:S(2)}) collective-permute-start(bf16[64,2048]{1,0:T(8,128)(2,1)S(1)} %hadamard_core.2.refs_1_.refs_0_), channel_id=1, source_target_pairs={{0,12},{2,14},{4,0},{6,2},{8,4},{10,6},{12,8},{14,10},{1,13},{3,15... | collective-permute-start | bytes 786440 | tf_op jit(solution)/shard_map/ppermute | solution.py:184
  8.7 14.9 %collective-permute-start.3 = (bf16[64,2048]{1,0:T(8,128)(2,1)S(1)}, bf16[64,2048]{1,0:T(8,128)(2,1)S(1)}, u32[]{:S(2)}, u32[]{:S(2)}) collective-permute-start(bf16[64,2048]{1,0:T(8,128)(2,1)S(1)} %hadamard_core.2.refs_1_.refs_0_), channel_id=1, source_target_pairs={{0,4},{2,6},{4,8},{6,10},{8,12},{10,14},{12,0},{14,2},{1,5},{3,7},... | collective-permute-start | bytes 786440 | tf_op jit(solution)/shard_map/ppermute | solution.py:184
  8.7 14.9 %collective-permute-start.2 = (bf16[64,2048]{1,0:T(8,128)(2,1)S(1)}, bf16[64,2048]{1,0:T(8,128)(2,1)S(1)}, u32[]{:S(2)}, u32[]{:S(2)}) collective-permute-start(bf16[64,2048]{1,0:T(8,128)(2,1)S(1)} %hadamard_core.2.refs_1_.refs_0_), channel_id=1, source_target_pairs={{0,8},{2,10},{4,12},{6,14},{8,0},{10,2},{12,4},{14,6},{1,9},{3,11}... | collective-permute-start | bytes 786440 | tf_op jit(solution)/shard_map/ppermute | solution.py:184
  10.5 3.4 %copy-start = (bf16[1,2048,2048]{2,1,0:T(8,128)(2,1)S(1)}, bf16[1,2048,2048]{2,1,0:T(8,128)(2,1)}, u32[]{:S(2)}) copy-start(bf16[1,2048,2048]{2,1,0:T(8,128)(2,1)} %refs_4_.7) | copy-start | bytes 25165828
  13.9 34.7 %copy-start.1 = (bf16[1,2048,2048]{2,1,0:T(8,128)(2,1)S(1)}, bf16[1,2048,2048]{2,1,0:T(8,128)(2,1)}, u32[]{:S(2)}) copy-start(bf16[1,2048,2048]{2,1,0:T(8,128)(2,1)} %refs_4_.7) | copy-start | bytes 25165828
  23.8 8.8 %collective-permute-start.6 = (bf16[64,2048]{1,0:T(8,128)(2,1)S(1)}, bf16[64,2048]{1,0:T(8,128)(2,1)S(1)}, u32[]{:S(2)}, u32[]{:S(2)}) collective-permute-start(bf16[64,2048]{1,0:T(8,128)(2,1)S(1)} %hadamard_z.2.refs_0_), channel_id=1, source_target_pairs={{0,64},{16,80},{32,96},{48,112},{64,0},{80,16},{96,32},{112,48},{1... | collective-permute-start | bytes 786440 | tf_op jit(solution)/shard_map/ppermute | solution.py:184
  27.0 7.1 %collective-permute-start.4 = (bf16[64,2048]{1,0:T(8,128)(2,1)S(1)}, bf16[64,2048]{1,0:T(8,128)(2,1)S(1)}, u32[]{:S(2)}, u32[]{:S(2)}) collective-permute-start(bf16[64,2048]{1,0:T(8,128)(2,1)S(1)} %hadamard_z.2.refs_0_), channel_id=1, source_target_pairs={{0,16},{16,0},{32,48},{48,32},{64,80},{80,64},{96,112},{112,96},{1... | collective-permute-start | bytes 786440 | tf_op jit(solution)/shard_map/ppermute | solution.py:184
  28.2 13.5 %collective-permute-start.13 = (bf16[64,2048]{1,0:T(8,128)(2,1)S(1)}, bf16[64,2048]{1,0:T(8,128)(2,1)S(1)}, u32[]{:S(2)}, u32[]{:S(2)}) collective-permute-start(bf16[64,2048]{1,0:T(8,128)(2,1)S(1)} %hadamard_core.3.refs_4_.refs_0_), channel_id=1, source_target_pairs={{0,4},{2,6},{4,8},{6,10},{8,12},{10,14},{12,0},{14,2},{1,5},{3,7},... | collective-permute-start | bytes 786440 | tf_op jit(solution)/shard_map/ppermute | solution.py:184
  28.2 13.5 %collective-permute-start.12 = (bf16[64,2048]{1,0:T(8,128)(2,1)S(1)}, bf16[64,2048]{1,0:T(8,128)(2,1)S(1)}, u32[]{:S(2)}, u32[]{:S(2)}) collective-permute-start(bf16[64,2048]{1,0:T(8,128)(2,1)S(1)} %hadamard_core.3.refs_4_.refs_0_), channel_id=1, source_target_pairs={{0,8},{2,10},{4,12},{6,14},{8,0},{10,2},{12,4},{14,6},{1,9},{3,11}... | collective-permute-start | bytes 786440 | tf_op jit(solution)/shard_map/ppermute | solution.py:184
  30.1 12.2 %collective-permute-start.11 = (bf16[64,2048]{1,0:T(8,128)(2,1)S(1)}, bf16[64,2048]{1,0:T(8,128)(2,1)S(1)}, u32[]{:S(2)}, u32[]{:S(2)}) collective-permute-start(bf16[64,2048]{1,0:T(8,128)(2,1)S(1)} %hadamard_core.3.refs_4_.refs_0_), channel_id=1, source_target_pairs={{0,12},{2,14},{4,0},{6,2},{8,4},{10,6},{12,8},{14,10},{1,13},{3,15... | collective-permute-start | bytes 786440 | tf_op jit(solution)/shard_map/ppermute | solution.py:184
  32.6 12.8 %collective-permute-start.10 = (bf16[64,2048]{1,0:T(8,128)(2,1)S(1)}, bf16[64,2048]{1,0:T(8,128)(2,1)S(1)}, u32[]{:S(2)}, u32[]{:S(2)}) collective-permute-start(bf16[64,2048]{1,0:T(8,128)(2,1)S(1)} %hadamard_z.2.refs_0_), channel_id=1, source_target_pairs={{0,32},{16,48},{32,64},{48,80},{64,96},{80,112},{96,0},{112,16},{1... | collective-permute-start | bytes 786440 | tf_op jit(solution)/shard_map/ppermute | solution.py:184
  34.1 11.2 %collective-permute-start.9 = (bf16[64,2048]{1,0:T(8,128)(2,1)S(1)}, bf16[64,2048]{1,0:T(8,128)(2,1)S(1)}, u32[]{:S(2)}, u32[]{:S(2)}) collective-permute-start(bf16[64,2048]{1,0:T(8,128)(2,1)S(1)} %hadamard_z.2.refs_0_), channel_id=1, source_target_pairs={{0,96},{16,112},{32,0},{48,16},{64,32},{80,48},{96,64},{112,80},{1... | collective-permute-start | bytes 786440 | tf_op jit(solution)/shard_map/ppermute | solution.py:184
  42.5 20.0 %collective-permute-start.21 = (bf16[64,2048]{1,0:T(8,128)(2,1)S(1)}, bf16[64,2048]{1,0:T(8,128)(2,1)S(1)}, u32[]{:S(2)}, u32[]{:S(2)}) collective-permute-start(bf16[64,2048]{1,0:T(8,128)(2,1)S(1)} %hadamard_z.3.refs_5_.refs_0_), channel_id=1, source_target_pairs={{0,16},{16,0},{32,48},{48,32},{64,80},{80,64},{96,112},{112,96},{1... | collective-permute-start | bytes 786440 | tf_op jit(solution)/shard_map/ppermute | solution.py:184
  43.5 21.2 %collective-permute-start.17 = (bf16[64,2048]{1,0:T(8,128)(2,1)S(1)}, bf16[64,2048]{1,0:T(8,128)(2,1)S(1)}, u32[]{:S(2)}, u32[]{:S(2)}) collective-permute-start(bf16[64,2048]{1,0:T(8,128)(2,1)S(1)} %hadamard_z.3.refs_5_.refs_0_), channel_id=1, source_target_pairs={{0,32},{16,48},{32,64},{48,80},{64,96},{80,112},{96,0},{112,16},{1... | collective-permute-start | bytes 786440 | tf_op jit(solution)/shard_map/ppermute | solution.py:184
  44.1 10.6 %collective-permute-start.7 = (bf16[64,2048]{1,0:T(8,128)(2,1)S(1)}, bf16[64,2048]{1,0:T(8,128)(2,1)S(1)}, u32[]{:S(2)}, u32[]{:S(2)}) collective-permute-start(bf16[64,2048]{1,0:T(8,128)(2,1)S(1)} %collective-permute-done.6.refs_5_.refs_2_), channel_id=1, source_target_pairs={{0,16},{16,0},{32,48},{48,32},{64,80},{80,64},{96,112},{112,96},{1... | collective-permute-start | bytes 786440 | tf_op jit(solution)/shard_map/ppermute | solution.py:184
  45.3 14.0 %collective-permute-start.8 = (bf16[64,2048]{1,0:T(8,128)(2,1)S(1)}, bf16[64,2048]{1,0:T(8,128)(2,1)S(1)}, u32[]{:S(2)}, u32[]{:S(2)}) collective-permute-start(bf16[64,2048]{1,0:T(8,128)(2,1)S(1)} %collective-permute-done.4.refs_4_.refs_0_), channel_id=1, source_target_pairs={{0,32},{16,48},{32,64},{48,80},{64,96},{80,112},{96,0},{112,16},{1... | collective-permute-start | bytes 786440 | tf_op jit(solution)/shard_map/ppermute | solution.py:184
  45.3 14.0 %collective-permute-start.5 = (bf16[64,2048]{1,0:T(8,128)(2,1)S(1)}, bf16[64,2048]{1,0:T(8,128)(2,1)S(1)}, u32[]{:S(2)}, u32[]{:S(2)}) collective-permute-start(bf16[64,2048]{1,0:T(8,128)(2,1)S(1)} %collective-permute-done.4.refs_4_.refs_0_), channel_id=1, source_target_pairs={{0,96},{16,112},{32,0},{48,16},{64,32},{80,48},{96,64},{112,80},{1... | collective-permute-start | bytes 786440 | tf_op jit(solution)/shard_map/ppermute | solution.py:184
  54.8 11.0 %collective-permute-start.16 = (bf16[64,2048]{1,0:T(8,128)(2,1)S(1)}, bf16[64,2048]{1,0:T(8,128)(2,1)S(1)}, u32[]{:S(2)}, u32[]{:S(2)}) collective-permute-start(bf16[64,2048]{1,0:T(8,128)(2,1)S(1)} %hadamard_z.3.refs_5_.refs_0_), channel_id=1, source_target_pairs={{0,64},{16,80},{32,96},{48,112},{64,0},{80,16},{96,32},{112,48},{1... | collective-permute-start | bytes 786440 | tf_op jit(solution)/shard_map/ppermute | solution.py:184
  59.3 7.7 %collective-permute-start.15 = (bf16[64,2048]{1,0:T(8,128)(2,1)S(1)}, bf16[64,2048]{1,0:T(8,128)(2,1)S(1)}, u32[]{:S(2)}, u32[]{:S(2)}) collective-permute-start(bf16[64,2048]{1,0:T(8,128)(2,1)S(1)} %hadamard_z.3.refs_5_.refs_0_), channel_id=1, source_target_pairs={{0,96},{16,112},{32,0},{48,16},{64,32},{80,48},{96,64},{112,80},{1... | collective-permute-start | bytes 786440 | tf_op jit(solution)/shard_map/ppermute | solution.py:184
  62.4 7.0 %collective-permute-start.14 = (bf16[256,2048]{1,0:T(8,128)(2,1)S(1)}, bf16[256,2048]{1,0:T(8,128)(2,1)S(1)}, u32[]{:S(2)}, u32[]{:S(2)}) collective-permute-start(bf16[256,2048]{1,0:T(8,128)(2,1)S(1)} %get-tuple-element.20.refs_5_), channel_id=1, source_target_pairs={{0,2},{2,0},{4,6},{6,4},{8,10},{10,8},{12,14},{14,12},{1,3},{3,1},... | collective-permute-start | bytes 3145736 | tf_op jit(solution)/shard_map/ppermute | solution.py:184
  62.5 9.9 %collective-permute-start.24 = (bf16[64,2048]{1,0:T(8,128)(2,1)S(1)}, bf16[64,2048]{1,0:T(8,128)(2,1)S(1)}, u32[]{:S(2)}, u32[]{:S(2)}) collective-permute-start(bf16[64,2048]{1,0:T(8,128)(2,1)S(1)} %collective-permute-done.21.refs_0_), channel_id=1, source_target_pairs={{0,32},{16,48},{32,64},{48,80},{64,96},{80,112},{96,0},{112,16},{1... | collective-permute-start | bytes 786440 | tf_op jit(solution)/shard_map/ppermute | solution.py:184
  64.6 8.4 %collective-permute-start.22 = (bf16[64,2048]{1,0:T(8,128)(2,1)S(1)}, bf16[64,2048]{1,0:T(8,128)(2,1)S(1)}, u32[]{:S(2)}, u32[]{:S(2)}) collective-permute-start(bf16[64,2048]{1,0:T(8,128)(2,1)S(1)} %collective-permute-done.21.refs_0_), channel_id=1, source_target_pairs={{0,96},{16,112},{32,0},{48,16},{64,32},{80,48},{96,64},{112,80},{1... | collective-permute-start | bytes 786440 | tf_op jit(solution)/shard_map/ppermute | solution.py:184
  65.8 8.1 %collective-permute-start.23 = (bf16[64,2048]{1,0:T(8,128)(2,1)S(1)}, bf16[64,2048]{1,0:T(8,128)(2,1)S(1)}, u32[]{:S(2)}, u32[]{:S(2)}) collective-permute-start(bf16[64,2048]{1,0:T(8,128)(2,1)S(1)} %collective-permute-done.16.refs_2_), channel_id=1, source_target_pairs={{0,16},{16,0},{32,48},{48,32},{64,80},{80,64},{96,112},{112,96},{1... | collective-permute-start | bytes 786440 | tf_op jit(solution)/shard_map/ppermute | solution.py:184
  73.9 19.1 %copy-start.2 = (bf16[128,2048]{1,0:T(8,128)(2,1)S(1)}, bf16[128,2048]{1,0:T(8,128)(2,1)}, u32[]{:S(2)}) copy-start(bf16[128,2048]{1,0:T(8,128)(2,1)} %refs_5_.3) | copy-start | bytes 1572868
  77.0 16.2 %collective-permute-start.26 = (bf16[256,2048]{1,0:T(8,128)(2,1)S(1)}, bf16[256,2048]{1,0:T(8,128)(2,1)S(1)}, u32[]{:S(2)}, u32[]{:S(2)}) collective-permute-start(bf16[256,2048]{1,0:T(8,128)(2,1)S(1)} %get-tuple-element.24.refs_6_), channel_id=1, source_target_pairs={{0,2},{2,0},{4,6},{6,4},{8,10},{10,8},{12,14},{14,12},{1,3},{3,1},... | collective-permute-start | bytes 3145736 | tf_op jit(solution)/shard_map/ppermute | solution.py:184
  77.1 10.7 %collective-permute-start.19 = (bf16[64,2048]{1,0:T(8,128)(2,1)S(1)}, bf16[64,2048]{1,0:T(8,128)(2,1)S(1)}, u32[]{:S(2)}, u32[]{:S(2)}) collective-permute-start(bf16[64,2048]{1,0:T(8,128)(2,1)S(1)} %get-tuple-element.22), channel_id=1, source_target_pairs={{0,8},{2,10},{4,12},{6,14},{8,0},{10,2},{12,4},{14,6},{1,9},{3,11}... | collective-permute-start | bytes 786440 | tf_op jit(solution)/shard_map/ppermute | solution.py:184
  77.9 15.0 %collective-permute-start.20 = (bf16[64,2048]{1,0:T(8,128)(2,1)S(1)}, bf16[64,2048]{1,0:T(8,128)(2,1)S(1)}, u32[]{:S(2)}, u32[]{:S(2)}) collective-permute-start(bf16[64,2048]{1,0:T(8,128)(2,1)S(1)} %get-tuple-element.23), channel_id=1, source_target_pairs={{0,12},{2,14},{4,0},{6,2},{8,4},{10,6},{12,8},{14,10},{1,13},{3,15... | collective-permute-start | bytes 786440 | tf_op jit(solution)/shard_map/ppermute | solution.py:184
  79.9 13.1 %collective-permute-start.18 = (bf16[64,2048]{1,0:T(8,128)(2,1)S(1)}, bf16[64,2048]{1,0:T(8,128)(2,1)S(1)}, u32[]{:S(2)}, u32[]{:S(2)}) collective-permute-start(bf16[64,2048]{1,0:T(8,128)(2,1)S(1)} %get-tuple-element.21.refs_6_), channel_id=1, source_target_pairs={{0,4},{2,6},{4,8},{6,10},{8,12},{10,14},{12,0},{14,2},{1,5},{3,7},... | collective-permute-start | bytes 786440 | tf_op jit(solution)/shard_map/ppermute | solution.py:184
  93.4 10.3 %collective-permute-start.27 = (bf16[64,2048]{1,0:T(8,128)(2,1)S(1)}, bf16[64,2048]{1,0:T(8,128)(2,1)S(1)}, u32[]{:S(2)}, u32[]{:S(2)}) collective-permute-start(bf16[64,2048]{1,0:T(8,128)(2,1)S(1)} %get-tuple-element.28), channel_id=1, source_target_pairs={{0,4},{2,6},{4,8},{6,10},{8,12},{10,14},{12,0},{14,2},{1,5},{3,7},... | collective-permute-start | bytes 786440 | tf_op jit(solution)/shard_map/ppermute | solution.py:184
  93.7 15.1 %collective-permute-start.28 = (bf16[64,2048]{1,0:T(8,128)(2,1)S(1)}, bf16[64,2048]{1,0:T(8,128)(2,1)S(1)}, u32[]{:S(2)}, u32[]{:S(2)}) collective-permute-start(bf16[64,2048]{1,0:T(8,128)(2,1)S(1)} %get-tuple-element.29), channel_id=1, source_target_pairs={{0,8},{2,10},{4,12},{6,14},{8,0},{10,2},{12,4},{14,6},{1,9},{3,11}... | collective-permute-start | bytes 786440 | tf_op jit(solution)/shard_map/ppermute | solution.py:184
  97.2 11.8 %collective-permute-start.29 = (bf16[64,2048]{1,0:T(8,128)(2,1)S(1)}, bf16[64,2048]{1,0:T(8,128)(2,1)S(1)}, u32[]{:S(2)}, u32[]{:S(2)}) collective-permute-start(bf16[64,2048]{1,0:T(8,128)(2,1)S(1)} %get-tuple-element.30), channel_id=1, source_target_pairs={{0,12},{2,14},{4,0},{6,2},{8,4},{10,6},{12,8},{14,10},{1,13},{3,15... | collective-permute-start | bytes 786440 | tf_op jit(solution)/shard_map/ppermute | solution.py:184
  97.2 13.3 %collective-permute-start.25 = (bf16[64,2048]{1,0:T(8,128)(2,1)S(1)}, bf16[64,2048]{1,0:T(8,128)(2,1)S(1)}, u32[]{:S(2)}, u32[]{:S(2)}) collective-permute-start(bf16[64,2048]{1,0:T(8,128)(2,1)S(1)} %get-tuple-element.25.refs_2_.refs_0_), channel_id=1, source_target_pairs={{0,1},{2,3},{4,5},{6,7},{8,9},{10,11},{12,13},{14,15},{16,17},{18,... | collective-permute-start | bytes 786440 | tf_op jit(solution)/shard_map/ppermute | solution.py:193
  109.3 10.6 %collective-permute-start.30 = (bf16[64,2048]{1,0:T(8,128)(2,1)S(1)}, bf16[64,2048]{1,0:T(8,128)(2,1)S(1)}, u32[]{:S(2)}, u32[]{:S(2)}) collective-permute-start(bf16[64,2048]{1,0:T(8,128)(2,1)S(1)} %get-tuple-element.31.refs_3_), channel_id=1, source_target_pairs={{0,1},{2,3},{4,5},{6,7},{8,9},{10,11},{12,13},{14,15},{16,17},{18,... | collective-permute-start | bytes 786440 | tf_op jit(solution)/shard_map/ppermute | solution.py:193

commit v4 on v3

--- a/solution.py
+++ b/solution.py
@@ -79,13 +79,17 @@
     out_ref[...] = (f32(other_ref[at]) + sign * f32(mine_ref[at])).astype(BF16)
 
 
-def mix_kernel(*refs):
+def mix_kernel(mine_ref, next_ref, last_ref, low_ref, high_ref, out_ref):
     z = place()[2]
-    total = 0
-    for k, ref in enumerate(refs[:4]):
+    half = low_ref.shape[0]
+
+    def sign(k):
         u = z & ((z + k) & 3)
-        total = total + f32(1 - 2 * ((u ^ (u >> 1)) & 1)) * f32(ref[...])
-    refs[4][...] = total.astype(BF16)
+        return f32(1 - 2 * ((u ^ (u >> 1)) & 1))
+
+    for at, far_ref in ((slice(0, half), low_ref), (slice(half, 2 * half), high_ref)):
+        total = sign(0) * f32(mine_ref[at]) + sign(1) * f32(next_ref[at]) + sign(3) * f32(last_ref[at])
+        out_ref[at] = (total + sign(2) * f32(far_ref[...])).astype(BF16)
 
 
 def touch_kernel(w_ref, out_ref):
@@ -148,16 +152,28 @@
     )
 
 
-def halves_kernel(keep_ref, came_ref, *out_refs):
-    rows = out_refs[0].shape[0]
-    for k, ref in enumerate(out_refs, 1):
-        at = slice(k * rows, (k + 1) * rows)
-        ref[...] = (f32(keep_ref[at]) + f32(came_ref[at])).astype(BF16)
-
-
-def finish_kernel(at, keep_ref, came_ref, a_ref, b_ref, c_ref, residual_ref, leading_ref, summed_ref):
-    rows = leading_ref.shape[0]
-    total = f32(keep_ref[:rows]) + f32(came_ref[:rows]) + f32(a_ref[...]) + f32(b_ref[...]) + f32(c_ref[...])
+def core_sum(keep_ref, came_ref, k, low=0, high=None):
+    rows = keep_ref.shape[0] // 4
+    at = slice(k * rows + low, k * rows + (high or rows))
+    return f32(keep_ref[at]) + f32(came_ref[at])
+
+
+def far_kernel(keep_ref, came_ref, low_ref, high_ref):
+    half = low_ref.shape[0]
+    low_ref[...] = core_sum(keep_ref, came_ref, 2, 0, half).astype(BF16)
+    high_ref[...] = core_sum(keep_ref, came_ref, 2, half).astype(BF16)
+
+
+def near_kernel(keep_ref, came_ref, low_ref, high_ref, next_ref, last_ref):
+    half = low_ref.shape[0]
+    next_ref[:half] = (core_sum(keep_ref, came_ref, 1, 0, half) + f32(low_ref[...])).astype(BF16)
+    next_ref[half:] = core_sum(keep_ref, came_ref, 1, half).astype(BF16)
+    last_ref[:half] = core_sum(keep_ref, came_ref, 3, 0, half).astype(BF16)
+    last_ref[half:] = (core_sum(keep_ref, came_ref, 3, half) + f32(high_ref[...])).astype(BF16)
+
+
+def finish_kernel(at, keep_ref, came_ref, a_ref, b_ref, residual_ref, leading_ref, summed_ref):
+    total = core_sum(keep_ref, came_ref, 0) + f32(a_ref[...]) + f32(b_ref[...])
     summed_ref[...] = total
     leading_ref[...] = (f32(residual_ref[at]) + total).astype(BF16)
 
@@ -197,8 +213,19 @@
             "hadamard_core", lambda *refs: pair_kernel(cut[chunk], *refs), (mine, other), shape(rows, width), behind
         )
 
-    def spread_z(mine):
-        return [mine] + [move(mine, "tensor", ring(-k)) for k in (1, 2, 3)]
+    half = rows // 2
+
+    def up(value):
+        return move(value, "tensor", ring(1))
+
+    def down(value):
+        return move(value, "tensor", ring(-1))
+
+    def near_z(mine):
+        return [mine, down(mine), up(mine)]
+
+    def far_z(terms):
+        return terms + [up(terms[2][:half]), down(terms[1][half:])]
 
     def mix(terms, behind=()):
         return call("hadamard_z", mix_kernel, terms, shape(rows, width), behind, weigh=20)
@@ -210,11 +237,15 @@
     def spread_mate(column, mate):
         return [mate, move(mate, "dp", ring(-1)), move(column[2], "dp", ring(0, 1)), move(mate, "dp", ring(-3))]
 
-    def halves(keep, came, behind=()):
-        return call("core_sum", halves_kernel, (keep, came), (shape(rows, columns),) * 3, behind)
-
-    def gather_z(parts):
-        return [move(part, "tensor", ring(k)) for k, part in enumerate(parts, 1)]
+    def far_sum(keep, came, behind=()):
+        low, high = call("far_sum", far_kernel, (keep, came), (shape(half, columns),) * 2, behind)
+        return up(low), down(high)
+
+    def near_sum(keep, came, far, behind=()):
+        return call("near_sum", near_kernel, (keep, came, *far), (shape(rows, columns),) * 2, behind)
+
+    def last_sum(near):
+        return up(near[0]), down(near[1])
 
     def finish(chunk, keep, came, arrived, behind=()):
         return call(
@@ -234,28 +265,28 @@
         flops=2 * tokens * width * LANES,
     )
     other = swap(local)
-    terms0 = spread_z(pair(0, local, other))
+    terms0 = near_z(pair(0, local, other))
     ready = call("weight", touch_kernel, (out_weight,), shape(8, LANES), [terms0[0]], weigh=9)
-    terms1 = spread_z(pair(1, local, other, [terms0[1], ready]))
-    own0 = mix(terms0, [terms1[0]])
+    terms1 = near_z(pair(1, local, other, [terms0[1], ready]))
+    own0 = mix(far_z(terms0), [terms1[0]])
     column0, mate0 = spread_column(own0)
-    own1 = mix(terms1, [mate0, column0[2]])
     mates0 = spread_mate(column0, mate0)
+    own1 = mix(far_z(terms1), [mates0[1], mates0[3]])
     column1, mate1 = spread_column(own1)
     products0 = project(column0, out_weight, None, [own1])
-    keep0, send0 = project(mates0, out_weight, products0)
+    keep0, send0 = project(mates0, out_weight, products0, [mate1, column1[1], column1[3]])
     came0 = swap(send0)
     mates1 = spread_mate(column1, mate1)
-    products1 = project(column1, out_weight, None, [send0])
-    parts0 = halves(keep0, came0, [products1])
-    arrived0 = gather_z(parts0)
-    keep1, send1 = project(mates1, out_weight, products1, [parts0[0]])
+    far0 = far_sum(keep0, came0)
+    products1 = project(column1, out_weight, None, [far0[0]])
+    near0 = near_sum(keep0, came0, far0)
+    keep1, send1 = project(mates1, out_weight, products1, [near0[0]])
     came1 = swap(send1)
-    leading0, summed0 = finish(0, keep0, came0, arrived0, [send1])
+    far1 = far_sum(keep1, came1)
+    leading0, summed0 = finish(0, keep0, came0, last_sum(near0), [far1[0]])
     passed0 = pipe(leading0)
-    parts1 = halves(keep1, came1, [leading0])
-    arrived1 = gather_z(parts1)
-    leading1, summed1 = finish(1, keep1, came1, arrived1)
+    near1 = near_sum(keep1, came1, far1)
+    leading1, summed1 = finish(1, keep1, came1, last_sum(near1), [leading0])
     passed1 = pipe(leading1)
     return call(
         "end",

time: 121 us -> 114 us (0.942)
  waiting for transfers between devices: 63.5 us -> 46.7 us
  starting transfers between devices: 38.1 us -> 48.1 us
    ppermute x29 -> x33, waiting for transfers between devices: 54.3 us -> 36.9 us  [move(): lax.ppermute(value, axis, [(i, target(i)) for i in range(lax.axis_size(ax...]
    ppermute x29 -> x33, starting transfers between devices: 35.6 us -> 45.5 us  [move(): lax.ppermute(value, axis, [(i, target(i)) for i in range(lax.axis_size(ax...]
    pallas_call x15 -> x17, Pallas kernels: 13.8 us -> 13.8 us  [call(): pl.pallas_call(lambda *refs: kernel(*refs[:count], *refs[count + len(behi...]
  transfers between devices with their start and end apart: 31 -> 35, of which waited for: 17 -> 18; matrix products, arithmetic and copies ran while one was open for 0% -> 0% of each run, Pallas kernels for 7% -> 5%
where the time goes in v4:
time: 114 us
  starting transfers between devices  48.1 us (42%)
  waiting for transfers between devices  46.7 us (41%)
  Pallas kernels  13.8 us (12%)
  local copies, waits for them, and re-layouts  5.16 us (5%)
    ppermute x33, starting transfers between devices, move(): lax.ppermute(value, axis, [(i, target(i)) for i in range(lax.axis_size(ax...  45.5 us
    ppermute x33, waiting for transfers between devices, move(): lax.ppermute(value, axis, [(i, target(i)) for i in range(lax.axis_size(ax...  36.9 us
    pallas_call x17, Pallas kernels, call(): pl.pallas_call(lambda *refs: kernel(*refs[:count], *refs[count + len(behi...  13.8 us
    ppermute x2, waiting for transfers between devices, pipe(): return lax.ppermute(value, 'pipe', [(0, 1)])  9.79 us
    unnamed x10, local copies, waits for them, and re-layouts  5.13 us
    ppermute x2, starting transfers between devices, pipe(): return lax.ppermute(value, 'pipe', [(0, 1)])  2.58 us
  transfers between devices with their start and end apart: 35, of which 18 were waited for; matrix products, arithmetic and copies ran while one was open for 0% of the time, Pallas kernels for 5%

profile of v4, /device:TPU:4, one launch (start us, length us, event | category | flops | bytes accessed | tf_op | source)
XLA Modules:
  0.0 114.0 jit_solution(4575638881626084132)
XLA Ops:
  0.0 1.0 copy-done.3
  1.0 0.7 copy-done.4
  1.7 0.7 rotate_local.1.refs_0_
  2.5 0.1 collective-permute-start
  2.6 1.9 %collective-permute-done.refs_1_ = bf16[128,2048]{1,0:T(8,128)(2,1)S(1)} collective-permute-done((bf16[128,2048]{1,0:T(8,128)(2,1)S(1)}, bf16[128,2048]{1,0:T(8,128)(2,1)S(1)}, u32[]{:S(2)}, u32[]{:S(2)}) %collective-permute-start) | collective-permute-done | bytes 524320 | tf_op jit(solution)/shard_map/ppermute | solution.py:200
  4.5 0.1 hadamard_core.2.refs_1_.refs_0_
  4.6 2.0 %collective-permute-start.2 = (bf16[64,2048]{1,0:T(8,128)(2,1)S(1)}, bf16[64,2048]{1,0:T(8,128)(2,1)S(1)}, u32[]{:S(2)}, u32[]{:S(2)}) collective-permute-start(bf16[64,2048]{1,0:T(8,128)(2,1)S(1)} %hadamard_core.2.refs_1_.refs_0_), channel_id=1, source_target_pairs={{0,4},{2,6},{4,8},{6,10},{8,12},{10,14},{12,0},{14,2},{1,5},{3,7},... | collective-permute-start | bytes 786440 | tf_op jit(solution)/shard_map/ppermute | solution.py:200
  6.5 2.2 %collective-permute-start.1 = (bf16[64,2048]{1,0:T(8,128)(2,1)S(1)}, bf16[64,2048]{1,0:T(8,128)(2,1)S(1)}, u32[]{:S(2)}, u32[]{:S(2)}) collective-permute-start(bf16[64,2048]{1,0:T(8,128)(2,1)S(1)} %hadamard_core.2.refs_1_.refs_0_), channel_id=1, source_target_pairs={{0,12},{2,14},{4,0},{6,2},{8,4},{10,6},{12,8},{14,10},{1,13},{3,15... | collective-permute-start | bytes 786440 | tf_op jit(solution)/shard_map/ppermute | solution.py:200
  8.7 6.5 %collective-permute-done.2.refs_2_ = bf16[64,2048]{1,0:T(8,128)(2,1)S(1)} collective-permute-done((bf16[64,2048]{1,0:T(8,128)(2,1)S(1)}, bf16[64,2048]{1,0:T(8,128)(2,1)S(1)}, u32[]{:S(2)}, u32[]{:S(2)}) %collective-permute-start.2) | collective-permute-done | bytes 262176 | tf_op jit(solution)/shard_map/ppermute | solution.py:200
  15.3 0.1 collective-permute-start.3
  15.4 3.3 %collective-permute-start.4 = (bf16[32,2048]{1,0:T(8,128)(2,1)S(1)}, bf16[32,2048]{1,0:T(8,128)(2,1)S(1)}, u32[]{:S(2)}, u32[]{:S(2)}) collective-permute-start(bf16[32,2048]{1,0:T(8,128)(2,1)S(1)} %slice.17), channel_id=1, source_target_pairs={{0,12},{2,14},{4,0},{6,2},{8,4},{10,6},{12,8},{14,10},{1,13},{3,15... | collective-permute-start | bytes 393224 | tf_op jit(solution)/shard_map/ppermute | solution.py:200
  18.7 3.4 %copy-done = bf16[1,2048,2048]{2,1,0:T(8,128)(2,1)S(1)} copy-done((bf16[1,2048,2048]{2,1,0:T(8,128)(2,1)S(1)}, bf16[1,2048,2048]{2,1,0:T(8,128)(2,1)}, u32[]{:S(2)}) %copy-start) | copy-done | bytes 8388632
  22.1 0.1 hadamard_core.3.refs_5_.refs_0_
  22.3 0.2 hadamard_z.2.refs_0_
  22.5 1.3 %collective-permute-start.5 = (bf16[64,2048]{1,0:T(8,128)(2,1)S(1)}, bf16[64,2048]{1,0:T(8,128)(2,1)S(1)}, u32[]{:S(2)}, u32[]{:S(2)}) collective-permute-start(bf16[64,2048]{1,0:T(8,128)(2,1)S(1)} %hadamard_z.2.refs_0_), channel_id=1, source_target_pairs={{0,16},{16,0},{32,48},{48,32},{64,80},{80,64},{96,112},{112,96},{1... | collective-permute-start | bytes 786440 | tf_op jit(solution)/shard_map/ppermute | solution.py:200
  23.8 3.2 %collective-permute-start.12 = (bf16[64,2048]{1,0:T(8,128)(2,1)S(1)}, bf16[64,2048]{1,0:T(8,128)(2,1)S(1)}, u32[]{:S(2)}, u32[]{:S(2)}) collective-permute-start(bf16[64,2048]{1,0:T(8,128)(2,1)S(1)} %hadamard_core.3.refs_5_.refs_0_), channel_id=1, source_target_pairs={{0,12},{2,14},{4,0},{6,2},{8,4},{10,6},{12,8},{14,10},{1,13},{3,15... | collective-permute-start | bytes 786440 | tf_op jit(solution)/shard_map/ppermute | solution.py:200
  27.0 3.2 %collective-permute-start.7 = (bf16[64,2048]{1,0:T(8,128)(2,1)S(1)}, bf16[64,2048]{1,0:T(8,128)(2,1)S(1)}, u32[]{:S(2)}, u32[]{:S(2)}) collective-permute-start(bf16[64,2048]{1,0:T(8,128)(2,1)S(1)} %hadamard_z.2.refs_0_), channel_id=1, source_target_pairs={{0,64},{16,80},{32,96},{48,112},{64,0},{80,16},{96,32},{112,48},{1... | collective-permute-start | bytes 786440 | tf_op jit(solution)/shard_map/ppermute | solution.py:200
  30.2 0.6 collective-permute-done.13.refs_2_
  30.8 1.6 %collective-permute-start.9 = (bf16[64,2048]{1,0:T(8,128)(2,1)S(1)}, bf16[64,2048]{1,0:T(8,128)(2,1)S(1)}, u32[]{:S(2)}, u32[]{:S(2)}) collective-permute-start(bf16[64,2048]{1,0:T(8,128)(2,1)S(1)} %collective-permute-done.5.refs_0_), channel_id=1, source_target_pairs={{0,32},{16,48},{32,64},{48,80},{64,96},{80,112},{96,0},{112,16},{1... | collective-permute-start | bytes 786440 | tf_op jit(solution)/shard_map/ppermute | solution.py:200
  32.5 1.7 %collective-permute-start.6 = (bf16[64,2048]{1,0:T(8,128)(2,1)S(1)}, bf16[64,2048]{1,0:T(8,128)(2,1)S(1)}, u32[]{:S(2)}, u32[]{:S(2)}) collective-permute-start(bf16[64,2048]{1,0:T(8,128)(2,1)S(1)} %collective-permute-done.5.refs_0_), channel_id=1, source_target_pairs={{0,96},{16,112},{32,0},{48,16},{64,32},{80,48},{96,64},{112,80},{1... | collective-permute-start | bytes 786440 | tf_op jit(solution)/shard_map/ppermute | solution.py:200
  34.1 0.4 collective-permute-start.11
  34.5 2.4 %collective-permute-done.7.refs_2_ = bf16[64,2048]{1,0:T(8,128)(2,1)S(1)} collective-permute-done((bf16[64,2048]{1,0:T(8,128)(2,1)S(1)}, bf16[64,2048]{1,0:T(8,128)(2,1)S(1)}, u32[]{:S(2)}, u32[]{:S(2)}) %collective-permute-start.7) | collective-permute-done | bytes 262176 | tf_op jit(solution)/shard_map/ppermute | solution.py:200
  36.9 3.4 %collective-permute-start.10 = (bf16[64,2048]{1,0:T(8,128)(2,1)S(1)}, bf16[64,2048]{1,0:T(8,128)(2,1)S(1)}, u32[]{:S(2)}, u32[]{:S(2)}) collective-permute-start(bf16[64,2048]{1,0:T(8,128)(2,1)S(1)} %hadamard_z.2.refs_0_), channel_id=1, source_target_pairs={{0,96},{16,112},{32,0},{48,16},{64,32},{80,48},{96,64},{112,80},{1... | collective-permute-start | bytes 786440 | tf_op jit(solution)/shard_map/ppermute | solution.py:200
  40.3 0.3 collective-permute-start.15
  40.6 4.8 %collective-permute-done.15.refs_4_ = bf16[32,2048]{1,0:T(8,128)(2,1)S(1)} collective-permute-done((bf16[32,2048]{1,0:T(8,128)(2,1)S(1)}, bf16[32,2048]{1,0:T(8,128)(2,1)S(1)}, u32[]{:S(2)}, u32[]{:S(2)}) %collective-permute-start.15) | collective-permute-done | bytes 131104 | tf_op jit(solution)/shard_map/ppermute | solution.py:200
  45.4 0.4 collective-permute-start.8
  45.8 0.2 hadamard_z.3.refs_5_.refs_0_
  46.1 3.2 %collective-permute-start.17 = (bf16[64,2048]{1,0:T(8,128)(2,1)S(1)}, bf16[64,2048]{1,0:T(8,128)(2,1)S(1)}, u32[]{:S(2)}, u32[]{:S(2)}) collective-permute-start(bf16[64,2048]{1,0:T(8,128)(2,1)S(1)} %hadamard_z.3.refs_5_.refs_0_), channel_id=1, source_target_pairs={{0,96},{16,112},{32,0},{48,16},{64,32},{80,48},{96,64},{112,80},{1... | collective-permute-start | bytes 786440 | tf_op jit(solution)/shard_map/ppermute | solution.py:200
  49.3 1.6 %collective-permute-start.16 = (bf16[64,2048]{1,0:T(8,128)(2,1)S(1)}, bf16[64,2048]{1,0:T(8,128)(2,1)S(1)}, u32[]{:S(2)}, u32[]{:S(2)}) collective-permute-start(bf16[64,2048]{1,0:T(8,128)(2,1)S(1)} %hadamard_z.3.refs_5_.refs_0_), channel_id=1, source_target_pairs={{0,16},{16,0},{32,48},{48,32},{64,80},{80,64},{96,112},{112,96},{1... | collective-permute-start | bytes 786440 | tf_op jit(solution)/shard_map/ppermute | solution.py:200
  50.9 2.4 %project_column.2.refs_5_ = bf16[256,2048]{1,0:T(8,128)(2,1)S(1)} custom-call(bf16[64,2048]{1,0:T(8,128)(2,1)S(1)} %hadamard_z.2.refs_0_, bf16[64,2048]{1,0:T(8,128)(2,1)S(1)} %collective-permute-done.10.refs_1_, bf16[64,2048]{1,0:T(8,128)(2,1)S(1)} %collective-permute-done.7.refs_2_, bf16[64,2048]{1,0:T(8,128)(2,1)S(1)} %collective-permute-done.11.refs_3_, ...), custom_call_target="tpu_custom_call" | custom-call | flops 10737418240 | bytes 52428800 | tf_op jit(solution)/shard_map/project_column/pallas_call | solution.py:38
  53.3 0.3 collective-permute-done.8.refs_2_
  53.6 2.8 %collective-permute-done.16.refs_6_.refs_0_ = bf16[64,2048]{1,0:T(8,128)(2,1)S(1)} collective-permute-done((bf16[64,2048]{1,0:T(8,128)(2,1)S(1)}, bf16[64,2048]{1,0:T(8,128)(2,1)S(1)}, u32[]{:S(2)}, u32[]{:S(2)}) %collective-permute-start.16) | collective-permute-done | bytes 262176 | tf_op jit(solution)/shard_map/ppermute | solution.py:200
  56.4 3.0 %project_mate.2 = (bf16[256,2048]{1,0:T(8,128)(2,1)S(1)}, bf16[256,2048]{1,0:T(8,128)(2,1)S(1)}) custom-call(bf16[64,2048]{1,0:T(8,128)(2,1)S(1)} %collective-permute-done.5.refs_0_, bf16[64,2048]{1,0:T(8,128)(2,1)S(1)} %collective-permute-done.6.refs_5_.refs_1_, bf16[64,2048]{1,0:T(8,128)(2,1)S(1)} %collective-permute-done.8.refs_2_, ...), custom_call_target="tpu_custom_call" | custom-call | flops 10737418240 | bytes 62914560 | tf_op jit(solution)/shard_map/project_mate/pallas_call | solution.py:38
  59.5 0.3 collective-permute-start.19
  59.8 1.6 %collective-permute-start.25 = (bf16[64,2048]{1,0:T(8,128)(2,1)S(1)}, bf16[64,2048]{1,0:T(8,128)(2,1)S(1)}, u32[]{:S(2)}, u32[]{:S(2)}) collective-permute-start(bf16[64,2048]{1,0:T(8,128)(2,1)S(1)} %hadamard_z.3.refs_5_.refs_0_), channel_id=1, source_target_pairs={{0,64},{16,80},{32,96},{48,112},{64,0},{80,16},{96,32},{112,48},{1... | collective-permute-start | bytes 786440 | tf_op jit(solution)/shard_map/ppermute | solution.py:200
  61.4 1.0 collective-permute-done.19.refs_1_
  62.6 0.6 collective-permute-start.27
  63.2 2.7 %collective-permute-start.24 = (bf16[64,2048]{1,0:T(8,128)(2,1)S(1)}, bf16[64,2048]{1,0:T(8,128)(2,1)S(1)}, u32[]{:S(2)}, u32[]{:S(2)}) collective-permute-start(bf16[64,2048]{1,0:T(8,128)(2,1)S(1)} %collective-permute-done.16.refs_6_.refs_0_), channel_id=1, source_target_pairs={{0,96},{16,112},{32,0},{48,16},{64,32},{80,48},{96,64},{112,80},{1... | collective-permute-start | bytes 786440 | tf_op jit(solution)/shard_map/ppermute | solution.py:200
  65.9 4.6 %collective-permute-done.25.refs_2_ = bf16[64,2048]{1,0:T(8,128)(2,1)S(1)} collective-permute-done((bf16[64,2048]{1,0:T(8,128)(2,1)S(1)}, bf16[64,2048]{1,0:T(8,128)(2,1)S(1)}, u32[]{:S(2)}, u32[]{:S(2)}) %collective-permute-start.25) | collective-permute-done | bytes 262176 | tf_op jit(solution)/shard_map/ppermute | solution.py:200
  70.5 0.9 collective-permute-start.26
  71.4 1.4 %collective-permute-start.21 = (bf16[32,2048]{1,0:T(8,128)(2,1)S(1)}, bf16[32,2048]{1,0:T(8,128)(2,1)S(1)}, u32[]{:S(2)}, u32[]{:S(2)}) collective-permute-start(bf16[32,2048]{1,0:T(8,128)(2,1)S(1)} %get-tuple-element.24), channel_id=1, source_target_pairs={{0,12},{2,14},{4,0},{6,2},{8,4},{10,6},{12,8},{14,10},{1,13},{3,15... | collective-permute-start | bytes 393224 | tf_op jit(solution)/shard_map/ppermute | solution.py:200
  72.8 2.4 %project_column.3.refs_5_ = bf16[256,2048]{1,0:T(8,128)(2,1)S(1)} custom-call(bf16[64,2048]{1,0:T(8,128)(2,1)S(1)} %hadamard_z.3.refs_5_.refs_0_, bf16[64,2048]{1,0:T(8,128)(2,1)S(1)} %collective-permute-done.17.refs_7_.refs_1_, bf16[64,2048]{1,0:T(8,128)(2,1)S(1)} %collective-permute-done.25.refs_2_, ...), custom_call_target="tpu_custom_call" | custom-call | flops 10737418240 | bytes 52428800 | tf_op jit(solution)/shard_map/project_column/pallas_call | solution.py:38
  75.1 1.2 %collective-permute-done.21.refs_3_ = bf16[32,2048]{1,0:T(8,128)(2,1)S(1)} collective-permute-done((bf16[32,2048]{1,0:T(8,128)(2,1)S(1)}, bf16[32,2048]{1,0:T(8,128)(2,1)S(1)}, u32[]{:S(2)}, u32[]{:S(2)}) %collective-permute-start.21) | collective-permute-done | bytes 131104 | tf_op jit(solution)/shard_map/ppermute | solution.py:200
  76.3 0.2 near_sum.2
  76.5 1.4 %collective-permute-done.26.refs_2_ = bf16[64,2048]{1,0:T(8,128)(2,1)S(1)} collective-permute-done((bf16[64,2048]{1,0:T(8,128)(2,1)S(1)}, bf16[64,2048]{1,0:T(8,128)(2,1)S(1)}, u32[]{:S(2)}, u32[]{:S(2)}) %collective-permute-start.26) | collective-permute-done | bytes 262176 | tf_op jit(solution)/shard_map/ppermute | solution.py:200
  77.9 3.1 %project_mate.3 = (bf16[256,2048]{1,0:T(8,128)(2,1)S(1)}, bf16[256,2048]{1,0:T(8,128)(2,1)S(1)}) custom-call(bf16[64,2048]{1,0:T(8,128)(2,1)S(1)} %collective-permute-done.16.refs_6_.refs_0_, bf16[64,2048]{1,0:T(8,128)(2,1)S(1)} %collective-permute-done.24.refs_1_, bf16[64,2048]{1,0:T(8,128)(2,1)S(1)} %collective-permute-done.26.refs_2_, ...), custom_call_target="tpu_custom_call" | custom-call | flops 10737418240 | bytes 62914560 | tf_op jit(solution)/shard_map/project_mate/pallas_call | solution.py:38
  81.0 0.1 collective-permute-start.28
  81.1 2.6 %collective-permute-done.28.refs_1_ = bf16[256,2048]{1,0:T(8,128)(2,1)S(1)} collective-permute-done((bf16[256,2048]{1,0:T(8,128)(2,1)S(1)}, bf16[256,2048]{1,0:T(8,128)(2,1)S(1)}, u32[]{:S(2)}, u32[]{:S(2)}) %collective-permute-start.28) | collective-permute-done | bytes 1048608 | tf_op jit(solution)/shard_map/ppermute | solution.py:200
  83.8 3.2 %collective-permute-start.31 = (bf16[32,2048]{1,0:T(8,128)(2,1)S(1)}, bf16[32,2048]{1,0:T(8,128)(2,1)S(1)}, u32[]{:S(2)}, u32[]{:S(2)}) collective-permute-start(bf16[32,2048]{1,0:T(8,128)(2,1)S(1)} %get-tuple-element.32), channel_id=1, source_target_pairs={{0,12},{2,14},{4,0},{6,2},{8,4},{10,6},{12,8},{14,10},{1,13},{3,15... | collective-permute-start | bytes 393224 | tf_op jit(solution)/shard_map/ppermute | solution.py:200
  87.1 3.2 %collective-permute-start.23 = (bf16[64,2048]{1,0:T(8,128)(2,1)S(1)}, bf16[64,2048]{1,0:T(8,128)(2,1)S(1)}, u32[]{:S(2)}, u32[]{:S(2)}) collective-permute-start(bf16[64,2048]{1,0:T(8,128)(2,1)S(1)} %get-tuple-element.26), channel_id=1, source_target_pairs={{0,12},{2,14},{4,0},{6,2},{8,4},{10,6},{12,8},{14,10},{1,13},{3,15... | collective-permute-start | bytes 786440 | tf_op jit(solution)/shard_map/ppermute | solution.py:200
  90.3 0.3 collective-permute-done.29.refs_5_.refs_2_
  90.6 0.2 near_sum.3
  90.8 0.4 collective-permute-start.32
  91.2 2.9 %collective-permute-start.33 = (bf16[64,2048]{1,0:T(8,128)(2,1)S(1)}, bf16[64,2048]{1,0:T(8,128)(2,1)S(1)}, u32[]{:S(2)}, u32[]{:S(2)}) collective-permute-start(bf16[64,2048]{1,0:T(8,128)(2,1)S(1)} %get-tuple-element.34), channel_id=1, source_target_pairs={{0,12},{2,14},{4,0},{6,2},{8,4},{10,6},{12,8},{14,10},{1,13},{3,15... | collective-permute-start | bytes 786440 | tf_op jit(solution)/shard_map/ppermute | solution.py:200
  94.1 3.0 %collective-permute-done.23.refs_3_ = bf16[64,2048]{1,0:T(8,128)(2,1)S(1)} collective-permute-done((bf16[64,2048]{1,0:T(8,128)(2,1)S(1)}, bf16[64,2048]{1,0:T(8,128)(2,1)S(1)}, u32[]{:S(2)}, u32[]{:S(2)}) %collective-permute-start.23) | collective-permute-done | bytes 262176 | tf_op jit(solution)/shard_map/ppermute | solution.py:200
  97.1 0.4 collective-permute-done.22.refs_2_
  97.5 0.2 residual.2
  97.7 1.3 %collective-permute-start.30 = (bf16[64,2048]{1,0:T(8,128)(2,1)S(1)}, bf16[64,2048]{1,0:T(8,128)(2,1)S(1)}, u32[]{:S(2)}, u32[]{:S(2)}) collective-permute-start(bf16[64,2048]{1,0:T(8,128)(2,1)S(1)} %get-tuple-element.30.refs_5_.refs_0_), channel_id=1, source_target_pairs={{0,1},{2,3},{4,5},{6,7},{8,9},{10,11},{12,13},{14,15},{16,17},{18,... | collective-permute-start | bytes 786440 | tf_op jit(solution)/shard_map/ppermute | solution.py:209
  99.0 2.8 %collective-permute-done.32.refs_2_ = bf16[64,2048]{1,0:T(8,128)(2,1)S(1)} collective-permute-done((bf16[64,2048]{1,0:T(8,128)(2,1)S(1)}, bf16[64,2048]{1,0:T(8,128)(2,1)S(1)}, u32[]{:S(2)}, u32[]{:S(2)}) %collective-permute-start.32) | collective-permute-done | bytes 262176 | tf_op jit(solution)/shard_map/ppermute | solution.py:200
  101.8 0.2 residual.3
  102.0 1.3 %collective-permute-start.34 = (bf16[64,2048]{1,0:T(8,128)(2,1)S(1)}, bf16[64,2048]{1,0:T(8,128)(2,1)S(1)}, u32[]{:S(2)}, u32[]{:S(2)}) collective-permute-start(bf16[64,2048]{1,0:T(8,128)(2,1)S(1)} %get-tuple-element.35.refs_3_), channel_id=1, source_target_pairs={{0,1},{2,3},{4,5},{6,7},{8,9},{10,11},{12,13},{14,15},{16,17},{18,... | collective-permute-start | bytes 786440 | tf_op jit(solution)/shard_map/ppermute | solution.py:209
  103.3 4.8 %collective-permute-done.30.refs_2_ = bf16[64,2048]{1,0:T(8,128)(2,1)S(1)} collective-permute-done((bf16[64,2048]{1,0:T(8,128)(2,1)S(1)}, bf16[64,2048]{1,0:T(8,128)(2,1)S(1)}, u32[]{:S(2)}, u32[]{:S(2)}) %collective-permute-start.30) | collective-permute-done | bytes 262176 | tf_op jit(solution)/shard_map/ppermute | solution.py:209
  108.1 5.0 %collective-permute-done.34.refs_5_ = bf16[64,2048]{1,0:T(8,128)(2,1)S(1)} collective-permute-done((bf16[64,2048]{1,0:T(8,128)(2,1)S(1)}, bf16[64,2048]{1,0:T(8,128)(2,1)S(1)}, u32[]{:S(2)}, u32[]{:S(2)}) %collective-permute-start.34) | collective-permute-done | bytes 262176 | tf_op jit(solution)/shard_map/ppermute | solution.py:209
  113.1 0.9 end.1
  (37 shorter events, 0.6 us)
Async XLA Ops:
  0.0 1.0 copy-start.3
  1.0 0.7 copy-start.4
  2.5 2.0 %collective-permute-start = (bf16[128,2048]{1,0:T(8,128)(2,1)S(1)}, bf16[128,2048]{1,0:T(8,128)(2,1)S(1)}, u32[]{:S(2)}, u32[]{:S(2)}) collective-permute-start(bf16[128,2048]{1,0:T(8,128)(2,1)S(1)} %rotate_local.1.refs_0_), channel_id=1, source_target_pairs={{0,2},{2,0},{4,6},{6,4},{8,10},{10,8},{12,14},{14,12},{1,3},{3,1},... | collective-permute-start | bytes 1572872 | tf_op jit(solution)/shard_map/ppermute | solution.py:200
  4.6 10.7 %collective-permute-start.2 = (bf16[64,2048]{1,0:T(8,128)(2,1)S(1)}, bf16[64,2048]{1,0:T(8,128)(2,1)S(1)}, u32[]{:S(2)}, u32[]{:S(2)}) collective-permute-start(bf16[64,2048]{1,0:T(8,128)(2,1)S(1)} %hadamard_core.2.refs_1_.refs_0_), channel_id=1, source_target_pairs={{0,4},{2,6},{4,8},{6,10},{8,12},{10,14},{12,0},{14,2},{1,5},{3,7},... | collective-permute-start | bytes 786440 | tf_op jit(solution)/shard_map/ppermute | solution.py:200
  6.5 8.8 %collective-permute-start.1 = (bf16[64,2048]{1,0:T(8,128)(2,1)S(1)}, bf16[64,2048]{1,0:T(8,128)(2,1)S(1)}, u32[]{:S(2)}, u32[]{:S(2)}) collective-permute-start(bf16[64,2048]{1,0:T(8,128)(2,1)S(1)} %hadamard_core.2.refs_1_.refs_0_), channel_id=1, source_target_pairs={{0,12},{2,14},{4,0},{6,2},{8,4},{10,6},{12,8},{14,10},{1,13},{3,15... | collective-permute-start | bytes 786440 | tf_op jit(solution)/shard_map/ppermute | solution.py:200
  15.3 7.0 %collective-permute-start.3 = (bf16[32,2048]{1,0:T(8,128)(2,1)S(1)}, bf16[32,2048]{1,0:T(8,128)(2,1)S(1)}, u32[]{:S(2)}, u32[]{:S(2)}) collective-permute-start(bf16[32,2048]{1,0:T(8,128)(2,1)S(1)} %slice.16), channel_id=1, source_target_pairs={{0,4},{2,6},{4,8},{6,10},{8,12},{10,14},{12,0},{14,2},{1,5},{3,7},... | collective-permute-start | bytes 393224 | tf_op jit(solution)/shard_map/ppermute | solution.py:200
  15.4 6.9 %collective-permute-start.4 = (bf16[32,2048]{1,0:T(8,128)(2,1)S(1)}, bf16[32,2048]{1,0:T(8,128)(2,1)S(1)}, u32[]{:S(2)}, u32[]{:S(2)}) collective-permute-start(bf16[32,2048]{1,0:T(8,128)(2,1)S(1)} %slice.17), channel_id=1, source_target_pairs={{0,12},{2,14},{4,0},{6,2},{8,4},{10,6},{12,8},{14,10},{1,13},{3,15... | collective-permute-start | bytes 393224 | tf_op jit(solution)/shard_map/ppermute | solution.py:200
  18.7 3.4 %copy-start = (bf16[1,2048,2048]{2,1,0:T(8,128)(2,1)S(1)}, bf16[1,2048,2048]{2,1,0:T(8,128)(2,1)}, u32[]{:S(2)}) copy-start(bf16[1,2048,2048]{2,1,0:T(8,128)(2,1)} %refs_4_.9) | copy-start | bytes 25165828
  22.1 28.9 %copy-start.1 = (bf16[1,2048,2048]{2,1,0:T(8,128)(2,1)S(1)}, bf16[1,2048,2048]{2,1,0:T(8,128)(2,1)}, u32[]{:S(2)}) copy-start(bf16[1,2048,2048]{2,1,0:T(8,128)(2,1)} %refs_4_.9) | copy-start | bytes 25165828
  22.2 8.6 %collective-permute-start.13 = (bf16[64,2048]{1,0:T(8,128)(2,1)S(1)}, bf16[64,2048]{1,0:T(8,128)(2,1)S(1)}, u32[]{:S(2)}, u32[]{:S(2)}) collective-permute-start(bf16[64,2048]{1,0:T(8,128)(2,1)S(1)} %hadamard_core.3.refs_5_.refs_0_), channel_id=1, source_target_pairs={{0,4},{2,6},{4,8},{6,10},{8,12},{10,14},{12,0},{14,2},{1,5},{3,7},... | collective-permute-start | bytes 786440 | tf_op jit(solution)/shard_map/ppermute | solution.py:200
  22.5 8.3 %collective-permute-start.5 = (bf16[64,2048]{1,0:T(8,128)(2,1)S(1)}, bf16[64,2048]{1,0:T(8,128)(2,1)S(1)}, u32[]{:S(2)}, u32[]{:S(2)}) collective-permute-start(bf16[64,2048]{1,0:T(8,128)(2,1)S(1)} %hadamard_z.2.refs_0_), channel_id=1, source_target_pairs={{0,16},{16,0},{32,48},{48,32},{64,80},{80,64},{96,112},{112,96},{1... | collective-permute-start | bytes 786440 | tf_op jit(solution)/shard_map/ppermute | solution.py:200
  23.8 10.4 %collective-permute-start.12 = (bf16[64,2048]{1,0:T(8,128)(2,1)S(1)}, bf16[64,2048]{1,0:T(8,128)(2,1)S(1)}, u32[]{:S(2)}, u32[]{:S(2)}) collective-permute-start(bf16[64,2048]{1,0:T(8,128)(2,1)S(1)} %hadamard_core.3.refs_5_.refs_0_), channel_id=1, source_target_pairs={{0,12},{2,14},{4,0},{6,2},{8,4},{10,6},{12,8},{14,10},{1,13},{3,15... | collective-permute-start | bytes 786440 | tf_op jit(solution)/shard_map/ppermute | solution.py:200
  27.0 10.0 %collective-permute-start.7 = (bf16[64,2048]{1,0:T(8,128)(2,1)S(1)}, bf16[64,2048]{1,0:T(8,128)(2,1)S(1)}, u32[]{:S(2)}, u32[]{:S(2)}) collective-permute-start(bf16[64,2048]{1,0:T(8,128)(2,1)S(1)} %hadamard_z.2.refs_0_), channel_id=1, source_target_pairs={{0,64},{16,80},{32,96},{48,112},{64,0},{80,16},{96,32},{112,48},{1... | collective-permute-start | bytes 786440 | tf_op jit(solution)/shard_map/ppermute | solution.py:200
  30.7 9.6 %collective-permute-start.14 = (bf16[32,2048]{1,0:T(8,128)(2,1)S(1)}, bf16[32,2048]{1,0:T(8,128)(2,1)S(1)}, u32[]{:S(2)}, u32[]{:S(2)}) collective-permute-start(bf16[32,2048]{1,0:T(8,128)(2,1)S(1)} %slice.18), channel_id=1, source_target_pairs={{0,4},{2,6},{4,8},{6,10},{8,12},{10,14},{12,0},{14,2},{1,5},{3,7},... | collective-permute-start | bytes 393224 | tf_op jit(solution)/shard_map/ppermute | solution.py:200
  30.8 15.0 %collective-permute-start.9 = (bf16[64,2048]{1,0:T(8,128)(2,1)S(1)}, bf16[64,2048]{1,0:T(8,128)(2,1)S(1)}, u32[]{:S(2)}, u32[]{:S(2)}) collective-permute-start(bf16[64,2048]{1,0:T(8,128)(2,1)S(1)} %collective-permute-done.5.refs_0_), channel_id=1, source_target_pairs={{0,32},{16,48},{32,64},{48,80},{64,96},{80,112},{96,0},{112,16},{1... | collective-permute-start | bytes 786440 | tf_op jit(solution)/shard_map/ppermute | solution.py:200
  32.5 13.3 %collective-permute-start.6 = (bf16[64,2048]{1,0:T(8,128)(2,1)S(1)}, bf16[64,2048]{1,0:T(8,128)(2,1)S(1)}, u32[]{:S(2)}, u32[]{:S(2)}) collective-permute-start(bf16[64,2048]{1,0:T(8,128)(2,1)S(1)} %collective-permute-done.5.refs_0_), channel_id=1, source_target_pairs={{0,96},{16,112},{32,0},{48,16},{64,32},{80,48},{96,64},{112,80},{1... | collective-permute-start | bytes 786440 | tf_op jit(solution)/shard_map/ppermute | solution.py:200
  34.1 15.2 %collective-permute-start.11 = (bf16[64,2048]{1,0:T(8,128)(2,1)S(1)}, bf16[64,2048]{1,0:T(8,128)(2,1)S(1)}, u32[]{:S(2)}, u32[]{:S(2)}) collective-permute-start(bf16[64,2048]{1,0:T(8,128)(2,1)S(1)} %hadamard_z.2.refs_0_), channel_id=1, source_target_pairs={{0,32},{16,48},{32,64},{48,80},{64,96},{80,112},{96,0},{112,16},{1... | collective-permute-start | bytes 786440 | tf_op jit(solution)/shard_map/ppermute | solution.py:200
  36.9 14.0 %collective-permute-start.10 = (bf16[64,2048]{1,0:T(8,128)(2,1)S(1)}, bf16[64,2048]{1,0:T(8,128)(2,1)S(1)}, u32[]{:S(2)}, u32[]{:S(2)}) collective-permute-start(bf16[64,2048]{1,0:T(8,128)(2,1)S(1)} %hadamard_z.2.refs_0_), channel_id=1, source_target_pairs={{0,96},{16,112},{32,0},{48,16},{64,32},{80,48},{96,64},{112,80},{1... | collective-permute-start | bytes 786440 | tf_op jit(solution)/shard_map/ppermute | solution.py:200
  40.3 5.0 %collective-permute-start.15 = (bf16[32,2048]{1,0:T(8,128)(2,1)S(1)}, bf16[32,2048]{1,0:T(8,128)(2,1)S(1)}, u32[]{:S(2)}, u32[]{:S(2)}) collective-permute-start(bf16[32,2048]{1,0:T(8,128)(2,1)S(1)} %slice.19), channel_id=1, source_target_pairs={{0,12},{2,14},{4,0},{6,2},{8,4},{10,6},{12,8},{14,10},{1,13},{3,15... | collective-permute-start | bytes 393224 | tf_op jit(solution)/shard_map/ppermute | solution.py:200
  45.4 8.3 %collective-permute-start.8 = (bf16[64,2048]{1,0:T(8,128)(2,1)S(1)}, bf16[64,2048]{1,0:T(8,128)(2,1)S(1)}, u32[]{:S(2)}, u32[]{:S(2)}) collective-permute-start(bf16[64,2048]{1,0:T(8,128)(2,1)S(1)} %collective-permute-done.7.refs_2_), channel_id=1, source_target_pairs={{0,16},{16,0},{32,48},{48,32},{64,80},{80,64},{96,112},{112,96},{1... | collective-permute-start | bytes 786440 | tf_op jit(solution)/shard_map/ppermute | solution.py:200
  46.0 7.7 %collective-permute-start.18 = (bf16[64,2048]{1,0:T(8,128)(2,1)S(1)}, bf16[64,2048]{1,0:T(8,128)(2,1)S(1)}, u32[]{:S(2)}, u32[]{:S(2)}) collective-permute-start(bf16[64,2048]{1,0:T(8,128)(2,1)S(1)} %hadamard_z.3.refs_5_.refs_0_), channel_id=1, source_target_pairs={{0,32},{16,48},{32,64},{48,80},{64,96},{80,112},{96,0},{112,16},{1... | collective-permute-start | bytes 786440 | tf_op jit(solution)/shard_map/ppermute | solution.py:200
  46.1 7.6 %collective-permute-start.17 = (bf16[64,2048]{1,0:T(8,128)(2,1)S(1)}, bf16[64,2048]{1,0:T(8,128)(2,1)S(1)}, u32[]{:S(2)}, u32[]{:S(2)}) collective-permute-start(bf16[64,2048]{1,0:T(8,128)(2,1)S(1)} %hadamard_z.3.refs_5_.refs_0_), channel_id=1, source_target_pairs={{0,96},{16,112},{32,0},{48,16},{64,32},{80,48},{96,64},{112,80},{1... | collective-permute-start | bytes 786440 | tf_op jit(solution)/shard_map/ppermute | solution.py:200
  49.3 7.1 %collective-permute-start.16 = (bf16[64,2048]{1,0:T(8,128)(2,1)S(1)}, bf16[64,2048]{1,0:T(8,128)(2,1)S(1)}, u32[]{:S(2)}, u32[]{:S(2)}) collective-permute-start(bf16[64,2048]{1,0:T(8,128)(2,1)S(1)} %hadamard_z.3.refs_5_.refs_0_), channel_id=1, source_target_pairs={{0,16},{16,0},{32,48},{48,32},{64,80},{80,64},{96,112},{112,96},{1... | collective-permute-start | bytes 786440 | tf_op jit(solution)/shard_map/ppermute | solution.py:200
  59.5 2.9 %collective-permute-start.19 = (bf16[256,2048]{1,0:T(8,128)(2,1)S(1)}, bf16[256,2048]{1,0:T(8,128)(2,1)S(1)}, u32[]{:S(2)}, u32[]{:S(2)}) collective-permute-start(bf16[256,2048]{1,0:T(8,128)(2,1)S(1)} %get-tuple-element.22), channel_id=1, source_target_pairs={{0,2},{2,0},{4,6},{6,4},{8,10},{10,8},{12,14},{14,12},{1,3},{3,1},... | collective-permute-start | bytes 3145736 | tf_op jit(solution)/shard_map/ppermute | solution.py:200
  59.8 10.7 %collective-permute-start.25 = (bf16[64,2048]{1,0:T(8,128)(2,1)S(1)}, bf16[64,2048]{1,0:T(8,128)(2,1)S(1)}, u32[]{:S(2)}, u32[]{:S(2)}) collective-permute-start(bf16[64,2048]{1,0:T(8,128)(2,1)S(1)} %hadamard_z.3.refs_5_.refs_0_), channel_id=1, source_target_pairs={{0,64},{16,80},{32,96},{48,112},{64,0},{80,16},{96,32},{112,48},{1... | collective-permute-start | bytes 786440 | tf_op jit(solution)/shard_map/ppermute | solution.py:200
  62.5 10.3 %collective-permute-start.20 = (bf16[32,2048]{1,0:T(8,128)(2,1)S(1)}, bf16[32,2048]{1,0:T(8,128)(2,1)S(1)}, u32[]{:S(2)}, u32[]{:S(2)}) collective-permute-start(bf16[32,2048]{1,0:T(8,128)(2,1)S(1)} %get-tuple-element.23), channel_id=1, source_target_pairs={{0,4},{2,6},{4,8},{6,10},{8,12},{10,14},{12,0},{14,2},{1,5},{3,7},... | collective-permute-start | bytes 393224 | tf_op jit(solution)/shard_map/ppermute | solution.py:200
  62.6 15.3 %collective-permute-start.27 = (bf16[64,2048]{1,0:T(8,128)(2,1)S(1)}, bf16[64,2048]{1,0:T(8,128)(2,1)S(1)}, u32[]{:S(2)}, u32[]{:S(2)}) collective-permute-start(bf16[64,2048]{1,0:T(8,128)(2,1)S(1)} %collective-permute-done.16.refs_6_.refs_0_), channel_id=1, source_target_pairs={{0,32},{16,48},{32,64},{48,80},{64,96},{80,112},{96,0},{112,16},{1... | collective-permute-start | bytes 786440 | tf_op jit(solution)/shard_map/ppermute | solution.py:200
  63.2 14.7 %collective-permute-start.24 = (bf16[64,2048]{1,0:T(8,128)(2,1)S(1)}, bf16[64,2048]{1,0:T(8,128)(2,1)S(1)}, u32[]{:S(2)}, u32[]{:S(2)}) collective-permute-start(bf16[64,2048]{1,0:T(8,128)(2,1)S(1)} %collective-permute-done.16.refs_6_.refs_0_), channel_id=1, source_target_pairs={{0,96},{16,112},{32,0},{48,16},{64,32},{80,48},{96,64},{112,80},{1... | collective-permute-start | bytes 786440 | tf_op jit(solution)/shard_map/ppermute | solution.py:200
  70.5 7.4 %collective-permute-start.26 = (bf16[64,2048]{1,0:T(8,128)(2,1)S(1)}, bf16[64,2048]{1,0:T(8,128)(2,1)S(1)}, u32[]{:S(2)}, u32[]{:S(2)}) collective-permute-start(bf16[64,2048]{1,0:T(8,128)(2,1)S(1)} %collective-permute-done.25.refs_2_), channel_id=1, source_target_pairs={{0,16},{16,0},{32,48},{48,32},{64,80},{80,64},{96,112},{112,96},{1... | collective-permute-start | bytes 786440 | tf_op jit(solution)/shard_map/ppermute | solution.py:200
  71.4 5.0 %collective-permute-start.21 = (bf16[32,2048]{1,0:T(8,128)(2,1)S(1)}, bf16[32,2048]{1,0:T(8,128)(2,1)S(1)}, u32[]{:S(2)}, u32[]{:S(2)}) collective-permute-start(bf16[32,2048]{1,0:T(8,128)(2,1)S(1)} %get-tuple-element.24), channel_id=1, source_target_pairs={{0,12},{2,14},{4,0},{6,2},{8,4},{10,6},{12,8},{14,10},{1,13},{3,15... | collective-permute-start | bytes 393224 | tf_op jit(solution)/shard_map/ppermute | solution.py:200
  77.9 19.6 %copy-start.2 = (bf16[128,2048]{1,0:T(8,128)(2,1)S(1)}, bf16[128,2048]{1,0:T(8,128)(2,1)}, u32[]{:S(2)}) copy-start(bf16[128,2048]{1,0:T(8,128)(2,1)} %refs_4_.11) | copy-start | bytes 1572868
  81.0 2.7 %collective-permute-start.28 = (bf16[256,2048]{1,0:T(8,128)(2,1)S(1)}, bf16[256,2048]{1,0:T(8,128)(2,1)S(1)}, u32[]{:S(2)}, u32[]{:S(2)}) collective-permute-start(bf16[256,2048]{1,0:T(8,128)(2,1)S(1)} %get-tuple-element.28), channel_id=1, source_target_pairs={{0,2},{2,0},{4,6},{6,4},{8,10},{10,8},{12,14},{14,12},{1,3},{3,1},... | collective-permute-start | bytes 3145736 | tf_op jit(solution)/shard_map/ppermute | solution.py:200
  83.8 6.9 %collective-permute-start.29 = (bf16[32,2048]{1,0:T(8,128)(2,1)S(1)}, bf16[32,2048]{1,0:T(8,128)(2,1)S(1)}, u32[]{:S(2)}, u32[]{:S(2)}) collective-permute-start(bf16[32,2048]{1,0:T(8,128)(2,1)S(1)} %get-tuple-element.29), channel_id=1, source_target_pairs={{0,4},{2,6},{4,8},{6,10},{8,12},{10,14},{12,0},{14,2},{1,5},{3,7},... | collective-permute-start | bytes 393224 | tf_op jit(solution)/shard_map/ppermute | solution.py:200
  83.8 6.8 %collective-permute-start.31 = (bf16[32,2048]{1,0:T(8,128)(2,1)S(1)}, bf16[32,2048]{1,0:T(8,128)(2,1)S(1)}, u32[]{:S(2)}, u32[]{:S(2)}) collective-permute-start(bf16[32,2048]{1,0:T(8,128)(2,1)S(1)} %get-tuple-element.32), channel_id=1, source_target_pairs={{0,12},{2,14},{4,0},{6,2},{8,4},{10,6},{12,8},{14,10},{1,13},{3,15... | collective-permute-start | bytes 393224 | tf_op jit(solution)/shard_map/ppermute | solution.py:200
  87.1 10.4 %collective-permute-start.22 = (bf16[64,2048]{1,0:T(8,128)(2,1)S(1)}, bf16[64,2048]{1,0:T(8,128)(2,1)S(1)}, u32[]{:S(2)}, u32[]{:S(2)}) collective-permute-start(bf16[64,2048]{1,0:T(8,128)(2,1)S(1)} %get-tuple-element.25.refs_6_), channel_id=1, source_target_pairs={{0,4},{2,6},{4,8},{6,10},{8,12},{10,14},{12,0},{14,2},{1,5},{3,7},... | collective-permute-start | bytes 786440 | tf_op jit(solution)/shard_map/ppermute | solution.py:200
  87.1 10.0 %collective-permute-start.23 = (bf16[64,2048]{1,0:T(8,128)(2,1)S(1)}, bf16[64,2048]{1,0:T(8,128)(2,1)S(1)}, u32[]{:S(2)}, u32[]{:S(2)}) collective-permute-start(bf16[64,2048]{1,0:T(8,128)(2,1)S(1)} %get-tuple-element.26), channel_id=1, source_target_pairs={{0,12},{2,14},{4,0},{6,2},{8,4},{10,6},{12,8},{14,10},{1,13},{3,15... | collective-permute-start | bytes 786440 | tf_op jit(solution)/shard_map/ppermute | solution.py:200
  90.8 11.0 %collective-permute-start.32 = (bf16[64,2048]{1,0:T(8,128)(2,1)S(1)}, bf16[64,2048]{1,0:T(8,128)(2,1)S(1)}, u32[]{:S(2)}, u32[]{:S(2)}) collective-permute-start(bf16[64,2048]{1,0:T(8,128)(2,1)S(1)} %get-tuple-element.33), channel_id=1, source_target_pairs={{0,4},{2,6},{4,8},{6,10},{8,12},{10,14},{12,0},{14,2},{1,5},{3,7},... | collective-permute-start | bytes 786440 | tf_op jit(solution)/shard_map/ppermute | solution.py:200
  91.2 10.6 %collective-permute-start.33 = (bf16[64,2048]{1,0:T(8,128)(2,1)S(1)}, bf16[64,2048]{1,0:T(8,128)(2,1)S(1)}, u32[]{:S(2)}, u32[]{:S(2)}) collective-permute-start(bf16[64,2048]{1,0:T(8,128)(2,1)S(1)} %get-tuple-element.34), channel_id=1, source_target_pairs={{0,12},{2,14},{4,0},{6,2},{8,4},{10,6},{12,8},{14,10},{1,13},{3,15... | collective-permute-start | bytes 786440 | tf_op jit(solution)/shard_map/ppermute | solution.py:200
  97.7 10.4 %collective-permute-start.30 = (bf16[64,2048]{1,0:T(8,128)(2,1)S(1)}, bf16[64,2048]{1,0:T(8,128)(2,1)S(1)}, u32[]{:S(2)}, u32[]{:S(2)}) collective-permute-start(bf16[64,2048]{1,0:T(8,128)(2,1)S(1)} %get-tuple-element.30.refs_5_.refs_0_), channel_id=1, source_target_pairs={{0,1},{2,3},{4,5},{6,7},{8,9},{10,11},{12,13},{14,15},{16,17},{18,... | collective-permute-start | bytes 786440 | tf_op jit(solution)/shard_map/ppermute | solution.py:209
  102.0 11.1 %collective-permute-start.34 = (bf16[64,2048]{1,0:T(8,128)(2,1)S(1)}, bf16[64,2048]{1,0:T(8,128)(2,1)S(1)}, u32[]{:S(2)}, u32[]{:S(2)}) collective-permute-start(bf16[64,2048]{1,0:T(8,128)(2,1)S(1)} %get-tuple-element.35.refs_3_), channel_id=1, source_target_pairs={{0,1},{2,3},{4,5},{6,7},{8,9},{10,11},{12,13},{14,15},{16,17},{18,... | collective-permute-start | bytes 786440 | tf_op jit(solution)/shard_map/ppermute | solution.py:209

commit v5 on v4

--- a/solution.py
+++ b/solution.py
@@ -79,6 +79,12 @@
     out_ref[...] = (f32(other_ref[at]) + sign * f32(mine_ref[at])).astype(BF16)
 
 
+def cut_kernel(next_ref, last_ref, low_ref, high_ref):
+    half = low_ref.shape[0]
+    low_ref[...] = last_ref[:half]
+    high_ref[...] = next_ref[half:]
+
+
 def mix_kernel(mine_ref, next_ref, last_ref, low_ref, high_ref, out_ref):
     z = place()[2]
     half = low_ref.shape[0]
@@ -224,8 +230,9 @@
     def near_z(mine):
         return [mine, down(mine), up(mine)]
 
-    def far_z(terms):
-        return terms + [up(terms[2][:half]), down(terms[1][half:])]
+    def far_z(terms, behind=()):
+        low, high = call("cut", cut_kernel, terms[1:], (shape(half, width),) * 2, behind)
+        return terms + [up(low), down(high)]
 
     def mix(terms, behind=()):
         return call("hadamard_z", mix_kernel, terms, shape(rows, width), behind, weigh=20)
@@ -267,14 +274,15 @@
     other = swap(local)
     terms0 = near_z(pair(0, local, other))
     ready = call("weight", touch_kernel, (out_weight,), shape(8, LANES), [terms0[0]], weigh=9)
-    terms1 = near_z(pair(1, local, other, [terms0[1], ready]))
-    own0 = mix(far_z(terms0), [terms1[0]])
+    terms0 = far_z(terms0, [ready])
+    terms1 = near_z(pair(1, local, other, [terms0[1]]))
+    own0 = mix(terms0, [terms1[0]])
     column0, mate0 = spread_column(own0)
     mates0 = spread_mate(column0, mate0)
-    own1 = mix(far_z(terms1), [mates0[1], mates0[3]])
+    own1 = mix(far_z(terms1), mates0[1:])
     column1, mate1 = spread_column(own1)
     products0 = project(column0, out_weight, None, [own1])
-    keep0, send0 = project(mates0, out_weight, products0, [mate1, column1[1], column1[3]])
+    keep0, send0 = project(mates0, out_weight, products0, [mate1, *column1[1:]])
     came0 = swap(send0)
     mates1 = spread_mate(column1, mate1)
     far0 = far_sum(keep0, came0)

time: 114 us -> 114 us (level)
  waiting for transfers between devices: 46.7 us -> 41.4 us
  starting transfers between devices: 48.1 us -> 53.2 us
    ppermute x33, starting transfers between devices: 45.5 us -> 50.6 us  [move(): lax.ppermute(value, axis, [(i, target(i)) for i in range(lax.axis_size(ax...]
    ppermute x33, waiting for transfers between devices: 36.9 us -> 31.8 us  [move(): lax.ppermute(value, axis, [(i, target(i)) for i in range(lax.axis_size(ax...]
    pallas_call x17 -> x19, Pallas kernels: 13.8 us -> 14 us  [call(): pl.pallas_call(lambda *refs: kernel(*refs[:count], *refs[count + len(behi...]
  transfers between devices with their start and end apart: 35 -> 35, of which waited for: 18 -> 20; matrix products, arithmetic and copies ran while one was open for 0% -> 0% of each run, Pallas kernels for 5% -> 5%
where the time goes in v5:
time: 114 us
  starting transfers between devices  53.2 us (47%)
  waiting for transfers between devices  41.4 us (36%)
  Pallas kernels  14 us (12%)
  local copies, waits for them, and re-layouts  5.13 us (4%)
    ppermute x33, starting transfers between devices, move(): lax.ppermute(value, axis, [(i, target(i)) for i in range(lax.axis_size(ax...  50.6 us
    ppermute x33, waiting for transfers between devices, move(): lax.ppermute(value, axis, [(i, target(i)) for i in range(lax.axis_size(ax...  31.8 us
    pallas_call x19, Pallas kernels, call(): pl.pallas_call(lambda *refs: kernel(*refs[:count], *refs[count + len(behi...  14 us
    ppermute x2, waiting for transfers between devices, pipe(): return lax.ppermute(value, 'pipe', [(0, 1)])  9.6 us
    unnamed x10, local copies, waits for them, and re-layouts  5.13 us
    ppermute x2, starting transfers between devices, pipe(): return lax.ppermute(value, 'pipe', [(0, 1)])  2.58 us
  transfers between devices with their start and end apart: 35, of which 20 were waited for; matrix products, arithmetic and copies ran while one was open for 0% of the time, Pallas kernels for 5%

profile of v5, /device:TPU:4, one launch (start us, length us, event | category | flops | bytes accessed | tf_op | source)
XLA Modules:
  0.0 113.9 jit_solution(3644474282040540248)
XLA Ops:
  0.0 1.0 copy-done.3
  1.0 0.7 copy-done.4
  1.7 0.7 rotate_local.1.refs_0_
  2.6 1.9 %collective-permute-done.refs_1_ = bf16[128,2048]{1,0:T(8,128)(2,1)S(1)} collective-permute-done((bf16[128,2048]{1,0:T(8,128)(2,1)S(1)}, bf16[128,2048]{1,0:T(8,128)(2,1)S(1)}, u32[]{:S(2)}, u32[]{:S(2)}) %collective-permute-start) | collective-permute-done | bytes 524320 | tf_op jit(solution)/shard_map/ppermute | solution.py:206
  4.6 2.0 %collective-permute-start.2 = (bf16[64,2048]{1,0:T(8,128)(2,1)S(1)}, bf16[64,2048]{1,0:T(8,128)(2,1)S(1)}, u32[]{:S(2)}, u32[]{:S(2)}) collective-permute-start(bf16[64,2048]{1,0:T(8,128)(2,1)S(1)} %hadamard_core.2.refs_1_.refs_0_), channel_id=1, source_target_pairs={{0,4},{2,6},{4,8},{6,10},{8,12},{10,14},{12,0},{14,2},{1,5},{3,7},... | collective-permute-start | bytes 786440 | tf_op jit(solution)/shard_map/ppermute | solution.py:206
  6.5 2.2 %collective-permute-start.1 = (bf16[64,2048]{1,0:T(8,128)(2,1)S(1)}, bf16[64,2048]{1,0:T(8,128)(2,1)S(1)}, u32[]{:S(2)}, u32[]{:S(2)}) collective-permute-start(bf16[64,2048]{1,0:T(8,128)(2,1)S(1)} %hadamard_core.2.refs_1_.refs_0_), channel_id=1, source_target_pairs={{0,12},{2,14},{4,0},{6,2},{8,4},{10,6},{12,8},{14,10},{1,13},{3,15... | collective-permute-start | bytes 786440 | tf_op jit(solution)/shard_map/ppermute | solution.py:206
  8.7 3.4 %copy-done = bf16[1,2048,2048]{2,1,0:T(8,128)(2,1)S(1)} copy-done((bf16[1,2048,2048]{2,1,0:T(8,128)(2,1)S(1)}, bf16[1,2048,2048]{2,1,0:T(8,128)(2,1)}, u32[]{:S(2)}) %copy-start) | copy-done | bytes 8388632
  12.1 3.1 %collective-permute-done.2.refs_1_.refs_2_ = bf16[64,2048]{1,0:T(8,128)(2,1)S(1)} collective-permute-done((bf16[64,2048]{1,0:T(8,128)(2,1)S(1)}, bf16[64,2048]{1,0:T(8,128)(2,1)S(1)}, u32[]{:S(2)}, u32[]{:S(2)}) %collective-permute-start.2) | collective-permute-done | bytes 262176 | tf_op jit(solution)/shard_map/ppermute | solution.py:206
  15.3 1.3 %collective-permute-start.3 = (bf16[32,2048]{1,0:T(8,128)(2,1)S(1)}, bf16[32,2048]{1,0:T(8,128)(2,1)S(1)}, u32[]{:S(2)}, u32[]{:S(2)}) collective-permute-start(bf16[32,2048]{1,0:T(8,128)(2,1)S(1)} %get-tuple-element.25), channel_id=1, source_target_pairs={{0,4},{2,6},{4,8},{6,10},{8,12},{10,14},{12,0},{14,2},{1,5},{3,7},... | collective-permute-start | bytes 393224 | tf_op jit(solution)/shard_map/ppermute | solution.py:206
  16.6 2.0 %collective-permute-start.4 = (bf16[32,2048]{1,0:T(8,128)(2,1)S(1)}, bf16[32,2048]{1,0:T(8,128)(2,1)S(1)}, u32[]{:S(2)}, u32[]{:S(2)}) collective-permute-start(bf16[32,2048]{1,0:T(8,128)(2,1)S(1)} %get-tuple-element.26), channel_id=1, source_target_pairs={{0,12},{2,14},{4,0},{6,2},{8,4},{10,6},{12,8},{14,10},{1,13},{3,15... | collective-permute-start | bytes 393224 | tf_op jit(solution)/shard_map/ppermute | solution.py:206
  18.8 3.2 %collective-permute-start.12 = (bf16[64,2048]{1,0:T(8,128)(2,1)S(1)}, bf16[64,2048]{1,0:T(8,128)(2,1)S(1)}, u32[]{:S(2)}, u32[]{:S(2)}) collective-permute-start(bf16[64,2048]{1,0:T(8,128)(2,1)S(1)} %hadamard_core.3.refs_5_.refs_0_), channel_id=1, source_target_pairs={{0,12},{2,14},{4,0},{6,2},{8,4},{10,6},{12,8},{14,10},{1,13},{3,15... | collective-permute-start | bytes 786440 | tf_op jit(solution)/shard_map/ppermute | solution.py:206
  22.0 0.7 collective-permute-done.4.refs_4_
  22.7 0.2 hadamard_z.2.refs_0_
  22.9 3.3 %collective-permute-start.7 = (bf16[64,2048]{1,0:T(8,128)(2,1)S(1)}, bf16[64,2048]{1,0:T(8,128)(2,1)S(1)}, u32[]{:S(2)}, u32[]{:S(2)}) collective-permute-start(bf16[64,2048]{1,0:T(8,128)(2,1)S(1)} %hadamard_z.2.refs_0_), channel_id=1, source_target_pairs={{0,64},{16,80},{32,96},{48,112},{64,0},{80,16},{96,32},{112,48},{1... | collective-permute-start | bytes 786440 | tf_op jit(solution)/shard_map/ppermute | solution.py:206
  26.2 1.2 %collective-permute-start.5 = (bf16[64,2048]{1,0:T(8,128)(2,1)S(1)}, bf16[64,2048]{1,0:T(8,128)(2,1)S(1)}, u32[]{:S(2)}, u32[]{:S(2)}) collective-permute-start(bf16[64,2048]{1,0:T(8,128)(2,1)S(1)} %hadamard_z.2.refs_0_), channel_id=1, source_target_pairs={{0,16},{16,0},{32,48},{48,32},{64,80},{80,64},{96,112},{112,96},{1... | collective-permute-start | bytes 786440 | tf_op jit(solution)/shard_map/ppermute | solution.py:206
  27.4 1.9 %collective-permute-start.14 = (bf16[32,2048]{1,0:T(8,128)(2,1)S(1)}, bf16[32,2048]{1,0:T(8,128)(2,1)S(1)}, u32[]{:S(2)}, u32[]{:S(2)}) collective-permute-start(bf16[32,2048]{1,0:T(8,128)(2,1)S(1)} %get-tuple-element.27), channel_id=1, source_target_pairs={{0,4},{2,6},{4,8},{6,10},{8,12},{10,14},{12,0},{14,2},{1,5},{3,7},... | collective-permute-start | bytes 393224 | tf_op jit(solution)/shard_map/ppermute | solution.py:206
  29.3 1.4 %collective-permute-start.15 = (bf16[32,2048]{1,0:T(8,128)(2,1)S(1)}, bf16[32,2048]{1,0:T(8,128)(2,1)S(1)}, u32[]{:S(2)}, u32[]{:S(2)}) collective-permute-start(bf16[32,2048]{1,0:T(8,128)(2,1)S(1)} %get-tuple-element.28), channel_id=1, source_target_pairs={{0,12},{2,14},{4,0},{6,2},{8,4},{10,6},{12,8},{14,10},{1,13},{3,15... | collective-permute-start | bytes 393224 | tf_op jit(solution)/shard_map/ppermute | solution.py:206
  30.8 1.2 %collective-permute-start.8 = (bf16[64,2048]{1,0:T(8,128)(2,1)S(1)}, bf16[64,2048]{1,0:T(8,128)(2,1)S(1)}, u32[]{:S(2)}, u32[]{:S(2)}) collective-permute-start(bf16[64,2048]{1,0:T(8,128)(2,1)S(1)} %collective-permute-done.7.refs_2_), channel_id=1, source_target_pairs={{0,16},{16,0},{32,48},{48,32},{64,80},{80,64},{96,112},{112,96},{1... | collective-permute-start | bytes 786440 | tf_op jit(solution)/shard_map/ppermute | solution.py:206
  32.0 1.4 %collective-permute-done.5.refs_0_ = bf16[64,2048]{1,0:T(8,128)(2,1)S(1)} collective-permute-done((bf16[64,2048]{1,0:T(8,128)(2,1)S(1)}, bf16[64,2048]{1,0:T(8,128)(2,1)S(1)}, u32[]{:S(2)}, u32[]{:S(2)}) %collective-permute-start.5) | collective-permute-done | bytes 262176 | tf_op jit(solution)/shard_map/ppermute | solution.py:206
  33.4 0.2 collective-permute-start.9
  33.6 3.0 %collective-permute-start.6 = (bf16[64,2048]{1,0:T(8,128)(2,1)S(1)}, bf16[64,2048]{1,0:T(8,128)(2,1)S(1)}, u32[]{:S(2)}, u32[]{:S(2)}) collective-permute-start(bf16[64,2048]{1,0:T(8,128)(2,1)S(1)} %collective-permute-done.5.refs_0_), channel_id=1, source_target_pairs={{0,96},{16,112},{32,0},{48,16},{64,32},{80,48},{96,64},{112,80},{1... | collective-permute-start | bytes 786440 | tf_op jit(solution)/shard_map/ppermute | solution.py:206
  36.6 3.2 %collective-permute-start.10 = (bf16[64,2048]{1,0:T(8,128)(2,1)S(1)}, bf16[64,2048]{1,0:T(8,128)(2,1)S(1)}, u32[]{:S(2)}, u32[]{:S(2)}) collective-permute-start(bf16[64,2048]{1,0:T(8,128)(2,1)S(1)} %hadamard_z.2.refs_0_), channel_id=1, source_target_pairs={{0,96},{16,112},{32,0},{48,16},{64,32},{80,48},{96,64},{112,80},{1... | collective-permute-start | bytes 786440 | tf_op jit(solution)/shard_map/ppermute | solution.py:206
  39.9 3.6 %collective-permute-done.9.refs_7_.refs_3_ = bf16[64,2048]{1,0:T(8,128)(2,1)S(1)} collective-permute-done((bf16[64,2048]{1,0:T(8,128)(2,1)S(1)}, bf16[64,2048]{1,0:T(8,128)(2,1)S(1)}, u32[]{:S(2)}, u32[]{:S(2)}) %collective-permute-start.9) | collective-permute-done | bytes 262176 | tf_op jit(solution)/shard_map/ppermute | solution.py:206
  43.5 0.2 hadamard_z.3.refs_5_.refs_0_
  43.7 1.5 %collective-permute-start.19 = (bf16[64,2048]{1,0:T(8,128)(2,1)S(1)}, bf16[64,2048]{1,0:T(8,128)(2,1)S(1)}, u32[]{:S(2)}, u32[]{:S(2)}) collective-permute-start(bf16[64,2048]{1,0:T(8,128)(2,1)S(1)} %hadamard_z.3.refs_5_.refs_0_), channel_id=1, source_target_pairs={{0,32},{16,48},{32,64},{48,80},{64,96},{80,112},{96,0},{112,16},{1... | collective-permute-start | bytes 786440 | tf_op jit(solution)/shard_map/ppermute | solution.py:206
  45.2 2.7 %collective-permute-start.18 = (bf16[64,2048]{1,0:T(8,128)(2,1)S(1)}, bf16[64,2048]{1,0:T(8,128)(2,1)S(1)}, u32[]{:S(2)}, u32[]{:S(2)}) collective-permute-start(bf16[64,2048]{1,0:T(8,128)(2,1)S(1)} %hadamard_z.3.refs_5_.refs_0_), channel_id=1, source_target_pairs={{0,64},{16,80},{32,96},{48,112},{64,0},{80,16},{96,32},{112,48},{1... | collective-permute-start | bytes 786440 | tf_op jit(solution)/shard_map/ppermute | solution.py:206
  47.9 0.8 collective-permute-start.17
  48.7 0.8 collective-permute-start.16
  49.5 1.4 %collective-permute-done.10.refs_1_ = bf16[64,2048]{1,0:T(8,128)(2,1)S(1)} collective-permute-done((bf16[64,2048]{1,0:T(8,128)(2,1)S(1)}, bf16[64,2048]{1,0:T(8,128)(2,1)S(1)}, u32[]{:S(2)}, u32[]{:S(2)}) %collective-permute-start.10) | collective-permute-done | bytes 262176 | tf_op jit(solution)/shard_map/ppermute | solution.py:206
  50.9 2.4 %project_column.2.refs_5_ = bf16[256,2048]{1,0:T(8,128)(2,1)S(1)} custom-call(bf16[64,2048]{1,0:T(8,128)(2,1)S(1)} %hadamard_z.2.refs_0_, bf16[64,2048]{1,0:T(8,128)(2,1)S(1)} %collective-permute-done.10.refs_1_, bf16[64,2048]{1,0:T(8,128)(2,1)S(1)} %collective-permute-done.7.refs_2_, bf16[64,2048]{1,0:T(8,128)(2,1)S(1)} %collective-permute-done.11.refs_3_, ...), custom_call_target="tpu_custom_call" | custom-call | flops 10737418240 | bytes 52428800 | tf_op jit(solution)/shard_map/project_column/pallas_call | solution.py:38
  53.3 0.9 collective-permute-done.19.refs_9_.refs_3_
  54.2 3.2 %collective-permute-done.18.refs_8_.refs_2_ = bf16[64,2048]{1,0:T(8,128)(2,1)S(1)} collective-permute-done((bf16[64,2048]{1,0:T(8,128)(2,1)S(1)}, bf16[64,2048]{1,0:T(8,128)(2,1)S(1)}, u32[]{:S(2)}, u32[]{:S(2)}) %collective-permute-start.18) | collective-permute-done | bytes 262176 | tf_op jit(solution)/shard_map/ppermute | solution.py:206
  57.4 3.2 %project_mate.2 = (bf16[256,2048]{1,0:T(8,128)(2,1)S(1)}, bf16[256,2048]{1,0:T(8,128)(2,1)S(1)}) custom-call(bf16[64,2048]{1,0:T(8,128)(2,1)S(1)} %collective-permute-done.5.refs_0_, bf16[64,2048]{1,0:T(8,128)(2,1)S(1)} %collective-permute-done.6.refs_5_.refs_1_, bf16[64,2048]{1,0:T(8,128)(2,1)S(1)} %collective-permute-done.8.refs_6_.refs_2_, ...), custom_call_target="tpu_custom_call" | custom-call | flops 10737418240 | bytes 62914560 | tf_op jit(solution)/shard_map/project_mate/pallas_call | solution.py:38
  60.8 2.6 %collective-permute-done.20.refs_1_ = bf16[256,2048]{1,0:T(8,128)(2,1)S(1)} collective-permute-done((bf16[256,2048]{1,0:T(8,128)(2,1)S(1)}, bf16[256,2048]{1,0:T(8,128)(2,1)S(1)}, u32[]{:S(2)}, u32[]{:S(2)}) %collective-permute-start.20) | collective-permute-done | bytes 1048608 | tf_op jit(solution)/shard_map/ppermute | solution.py:206
  63.5 3.7 %collective-permute-start.21 = (bf16[32,2048]{1,0:T(8,128)(2,1)S(1)}, bf16[32,2048]{1,0:T(8,128)(2,1)S(1)}, u32[]{:S(2)}, u32[]{:S(2)}) collective-permute-start(bf16[32,2048]{1,0:T(8,128)(2,1)S(1)} %get-tuple-element.31), channel_id=1, source_target_pairs={{0,4},{2,6},{4,8},{6,10},{8,12},{10,14},{12,0},{14,2},{1,5},{3,7},... | collective-permute-start | bytes 393224 | tf_op jit(solution)/shard_map/ppermute | solution.py:206
  67.2 1.2 %collective-permute-start.26 = (bf16[64,2048]{1,0:T(8,128)(2,1)S(1)}, bf16[64,2048]{1,0:T(8,128)(2,1)S(1)}, u32[]{:S(2)}, u32[]{:S(2)}) collective-permute-start(bf16[64,2048]{1,0:T(8,128)(2,1)S(1)} %collective-permute-done.18.refs_8_.refs_2_), channel_id=1, source_target_pairs={{0,16},{16,0},{32,48},{48,32},{64,80},{80,64},{96,112},{112,96},{1... | collective-permute-start | bytes 786440 | tf_op jit(solution)/shard_map/ppermute | solution.py:206
  68.4 1.2 %collective-permute-start.27 = (bf16[64,2048]{1,0:T(8,128)(2,1)S(1)}, bf16[64,2048]{1,0:T(8,128)(2,1)S(1)}, u32[]{:S(2)}, u32[]{:S(2)}) collective-permute-start(bf16[64,2048]{1,0:T(8,128)(2,1)S(1)} %collective-permute-done.16.refs_6_.refs_0_), channel_id=1, source_target_pairs={{0,32},{16,48},{32,64},{48,80},{64,96},{80,112},{96,0},{112,16},{1... | collective-permute-start | bytes 786440 | tf_op jit(solution)/shard_map/ppermute | solution.py:206
  69.6 2.0 %collective-permute-start.25 = (bf16[64,2048]{1,0:T(8,128)(2,1)S(1)}, bf16[64,2048]{1,0:T(8,128)(2,1)S(1)}, u32[]{:S(2)}, u32[]{:S(2)}) collective-permute-start(bf16[64,2048]{1,0:T(8,128)(2,1)S(1)} %collective-permute-done.16.refs_6_.refs_0_), channel_id=1, source_target_pairs={{0,96},{16,112},{32,0},{48,16},{64,32},{80,48},{96,64},{112,80},{1... | collective-permute-start | bytes 786440 | tf_op jit(solution)/shard_map/ppermute | solution.py:206
  71.6 0.3 collective-permute-start.22
  72.0 2.4 %project_column.3.refs_5_ = bf16[256,2048]{1,0:T(8,128)(2,1)S(1)} custom-call(bf16[64,2048]{1,0:T(8,128)(2,1)S(1)} %hadamard_z.3.refs_5_.refs_0_, bf16[64,2048]{1,0:T(8,128)(2,1)S(1)} %collective-permute-done.17.refs_7_.refs_1_, bf16[64,2048]{1,0:T(8,128)(2,1)S(1)} %collective-permute-done.18.refs_8_.refs_2_, ...), custom_call_target="tpu_custom_call" | custom-call | flops 10737418240 | bytes 52428800 | tf_op jit(solution)/shard_map/project_column/pallas_call | solution.py:38
  74.3 2.3 %collective-permute-done.22.refs_3_ = bf16[32,2048]{1,0:T(8,128)(2,1)S(1)} collective-permute-done((bf16[32,2048]{1,0:T(8,128)(2,1)S(1)}, bf16[32,2048]{1,0:T(8,128)(2,1)S(1)}, u32[]{:S(2)}, u32[]{:S(2)}) %collective-permute-start.22) | collective-permute-done | bytes 131104 | tf_op jit(solution)/shard_map/ppermute | solution.py:206
  76.7 0.2 near_sum.2
  76.8 0.5 collective-permute-done.27.refs_3_
  77.4 3.1 %project_mate.3 = (bf16[256,2048]{1,0:T(8,128)(2,1)S(1)}, bf16[256,2048]{1,0:T(8,128)(2,1)S(1)}) custom-call(bf16[64,2048]{1,0:T(8,128)(2,1)S(1)} %collective-permute-done.16.refs_6_.refs_0_, bf16[64,2048]{1,0:T(8,128)(2,1)S(1)} %collective-permute-done.25.refs_1_, bf16[64,2048]{1,0:T(8,128)(2,1)S(1)} %collective-permute-done.26.refs_2_, ...), custom_call_target="tpu_custom_call" | custom-call | flops 10737418240 | bytes 62914560 | tf_op jit(solution)/shard_map/project_mate/pallas_call | solution.py:38
  80.5 2.6 %collective-permute-done.28.refs_1_ = bf16[256,2048]{1,0:T(8,128)(2,1)S(1)} collective-permute-done((bf16[256,2048]{1,0:T(8,128)(2,1)S(1)}, bf16[256,2048]{1,0:T(8,128)(2,1)S(1)}, u32[]{:S(2)}, u32[]{:S(2)}) %collective-permute-start.28) | collective-permute-done | bytes 1048608 | tf_op jit(solution)/shard_map/ppermute | solution.py:206
  83.3 2.2 %collective-permute-start.29 = (bf16[32,2048]{1,0:T(8,128)(2,1)S(1)}, bf16[32,2048]{1,0:T(8,128)(2,1)S(1)}, u32[]{:S(2)}, u32[]{:S(2)}) collective-permute-start(bf16[32,2048]{1,0:T(8,128)(2,1)S(1)} %get-tuple-element.37), channel_id=1, source_target_pairs={{0,4},{2,6},{4,8},{6,10},{8,12},{10,14},{12,0},{14,2},{1,5},{3,7},... | collective-permute-start | bytes 393224 | tf_op jit(solution)/shard_map/ppermute | solution.py:206
  85.4 1.1 collective-permute-start.31
  86.6 0.9 collective-permute-start.23
  87.5 2.3 %collective-permute-start.24 = (bf16[64,2048]{1,0:T(8,128)(2,1)S(1)}, bf16[64,2048]{1,0:T(8,128)(2,1)S(1)}, u32[]{:S(2)}, u32[]{:S(2)}) collective-permute-start(bf16[64,2048]{1,0:T(8,128)(2,1)S(1)} %get-tuple-element.34), channel_id=1, source_target_pairs={{0,12},{2,14},{4,0},{6,2},{8,4},{10,6},{12,8},{14,10},{1,13},{3,15... | collective-permute-start | bytes 786440 | tf_op jit(solution)/shard_map/ppermute | solution.py:206
  89.8 0.3 collective-permute-done.29.refs_5_.refs_2_
  90.1 1.7 %collective-permute-done.31.refs_3_ = bf16[32,2048]{1,0:T(8,128)(2,1)S(1)} collective-permute-done((bf16[32,2048]{1,0:T(8,128)(2,1)S(1)}, bf16[32,2048]{1,0:T(8,128)(2,1)S(1)}, u32[]{:S(2)}, u32[]{:S(2)}) %collective-permute-start.31) | collective-permute-done | bytes 131104 | tf_op jit(solution)/shard_map/ppermute | solution.py:206
  91.8 0.2 near_sum.3
  92.0 0.4 collective-permute-start.32
  92.4 2.9 %collective-permute-start.33 = (bf16[64,2048]{1,0:T(8,128)(2,1)S(1)}, bf16[64,2048]{1,0:T(8,128)(2,1)S(1)}, u32[]{:S(2)}, u32[]{:S(2)}) collective-permute-start(bf16[64,2048]{1,0:T(8,128)(2,1)S(1)} %get-tuple-element.42), channel_id=1, source_target_pairs={{0,12},{2,14},{4,0},{6,2},{8,4},{10,6},{12,8},{14,10},{1,13},{3,15... | collective-permute-start | bytes 786440 | tf_op jit(solution)/shard_map/ppermute | solution.py:206
  95.3 2.2 %collective-permute-done.24.refs_3_ = bf16[64,2048]{1,0:T(8,128)(2,1)S(1)} collective-permute-done((bf16[64,2048]{1,0:T(8,128)(2,1)S(1)}, bf16[64,2048]{1,0:T(8,128)(2,1)S(1)}, u32[]{:S(2)}, u32[]{:S(2)}) %collective-permute-start.24) | collective-permute-done | bytes 262176 | tf_op jit(solution)/shard_map/ppermute | solution.py:206
  97.4 0.2 residual.2
  97.6 1.3 %collective-permute-start.30 = (bf16[64,2048]{1,0:T(8,128)(2,1)S(1)}, bf16[64,2048]{1,0:T(8,128)(2,1)S(1)}, u32[]{:S(2)}, u32[]{:S(2)}) collective-permute-start(bf16[64,2048]{1,0:T(8,128)(2,1)S(1)} %get-tuple-element.38.refs_5_.refs_0_), channel_id=1, source_target_pairs={{0,1},{2,3},{4,5},{6,7},{8,9},{10,11},{12,13},{14,15},{16,17},{18,... | collective-permute-start | bytes 786440 | tf_op jit(solution)/shard_map/ppermute | solution.py:215
  98.9 2.4 %collective-permute-done.32.refs_2_ = bf16[64,2048]{1,0:T(8,128)(2,1)S(1)} collective-permute-done((bf16[64,2048]{1,0:T(8,128)(2,1)S(1)}, bf16[64,2048]{1,0:T(8,128)(2,1)S(1)}, u32[]{:S(2)}, u32[]{:S(2)}) %collective-permute-start.32) | collective-permute-done | bytes 262176 | tf_op jit(solution)/shard_map/ppermute | solution.py:206
  101.3 0.6 collective-permute-done.33.refs_3_
  101.9 0.2 residual.3
  102.1 1.3 %collective-permute-start.34 = (bf16[64,2048]{1,0:T(8,128)(2,1)S(1)}, bf16[64,2048]{1,0:T(8,128)(2,1)S(1)}, u32[]{:S(2)}, u32[]{:S(2)}) collective-permute-start(bf16[64,2048]{1,0:T(8,128)(2,1)S(1)} %get-tuple-element.43.refs_3_), channel_id=1, source_target_pairs={{0,1},{2,3},{4,5},{6,7},{8,9},{10,11},{12,13},{14,15},{16,17},{18,... | collective-permute-start | bytes 786440 | tf_op jit(solution)/shard_map/ppermute | solution.py:215
  103.4 4.2 %collective-permute-done.30.refs_2_ = bf16[64,2048]{1,0:T(8,128)(2,1)S(1)} collective-permute-done((bf16[64,2048]{1,0:T(8,128)(2,1)S(1)}, bf16[64,2048]{1,0:T(8,128)(2,1)S(1)}, u32[]{:S(2)}, u32[]{:S(2)}) %collective-permute-start.30) | collective-permute-done | bytes 262176 | tf_op jit(solution)/shard_map/ppermute | solution.py:215
  107.6 5.4 %collective-permute-done.34.refs_5_ = bf16[64,2048]{1,0:T(8,128)(2,1)S(1)} collective-permute-done((bf16[64,2048]{1,0:T(8,128)(2,1)S(1)}, bf16[64,2048]{1,0:T(8,128)(2,1)S(1)}, u32[]{:S(2)}, u32[]{:S(2)}) %collective-permute-start.34) | collective-permute-done | bytes 262176 | tf_op jit(solution)/shard_map/ppermute | solution.py:215
  113.0 0.9 end.1
  (35 shorter events, 0.9 us)
Async XLA Ops:
  0.0 1.0 copy-start.3
  1.0 0.7 copy-start.4
  2.5 2.0 %collective-permute-start = (bf16[128,2048]{1,0:T(8,128)(2,1)S(1)}, bf16[128,2048]{1,0:T(8,128)(2,1)S(1)}, u32[]{:S(2)}, u32[]{:S(2)}) collective-permute-start(bf16[128,2048]{1,0:T(8,128)(2,1)S(1)} %rotate_local.1.refs_0_), channel_id=1, source_target_pairs={{0,2},{2,0},{4,6},{6,4},{8,10},{10,8},{12,14},{14,12},{1,3},{3,1},... | collective-permute-start | bytes 1572872 | tf_op jit(solution)/shard_map/ppermute | solution.py:206
  4.6 10.7 %collective-permute-start.2 = (bf16[64,2048]{1,0:T(8,128)(2,1)S(1)}, bf16[64,2048]{1,0:T(8,128)(2,1)S(1)}, u32[]{:S(2)}, u32[]{:S(2)}) collective-permute-start(bf16[64,2048]{1,0:T(8,128)(2,1)S(1)} %hadamard_core.2.refs_1_.refs_0_), channel_id=1, source_target_pairs={{0,4},{2,6},{4,8},{6,10},{8,12},{10,14},{12,0},{14,2},{1,5},{3,7},... | collective-permute-start | bytes 786440 | tf_op jit(solution)/shard_map/ppermute | solution.py:206
  6.5 8.7 %collective-permute-start.1 = (bf16[64,2048]{1,0:T(8,128)(2,1)S(1)}, bf16[64,2048]{1,0:T(8,128)(2,1)S(1)}, u32[]{:S(2)}, u32[]{:S(2)}) collective-permute-start(bf16[64,2048]{1,0:T(8,128)(2,1)S(1)} %hadamard_core.2.refs_1_.refs_0_), channel_id=1, source_target_pairs={{0,12},{2,14},{4,0},{6,2},{8,4},{10,6},{12,8},{14,10},{1,13},{3,15... | collective-permute-start | bytes 786440 | tf_op jit(solution)/shard_map/ppermute | solution.py:206
  8.7 3.4 %copy-start = (bf16[1,2048,2048]{2,1,0:T(8,128)(2,1)S(1)}, bf16[1,2048,2048]{2,1,0:T(8,128)(2,1)}, u32[]{:S(2)}) copy-start(bf16[1,2048,2048]{2,1,0:T(8,128)(2,1)} %refs_4_.9) | copy-start | bytes 25165828
  12.1 38.8 %copy-start.1 = (bf16[1,2048,2048]{2,1,0:T(8,128)(2,1)S(1)}, bf16[1,2048,2048]{2,1,0:T(8,128)(2,1)}, u32[]{:S(2)}) copy-start(bf16[1,2048,2048]{2,1,0:T(8,128)(2,1)} %refs_4_.9) | copy-start | bytes 25165828
  15.3 6.7 %collective-permute-start.3 = (bf16[32,2048]{1,0:T(8,128)(2,1)S(1)}, bf16[32,2048]{1,0:T(8,128)(2,1)S(1)}, u32[]{:S(2)}, u32[]{:S(2)}) collective-permute-start(bf16[32,2048]{1,0:T(8,128)(2,1)S(1)} %get-tuple-element.25), channel_id=1, source_target_pairs={{0,4},{2,6},{4,8},{6,10},{8,12},{10,14},{12,0},{14,2},{1,5},{3,7},... | collective-permute-start | bytes 393224 | tf_op jit(solution)/shard_map/ppermute | solution.py:206
  16.6 6.0 %collective-permute-start.4 = (bf16[32,2048]{1,0:T(8,128)(2,1)S(1)}, bf16[32,2048]{1,0:T(8,128)(2,1)S(1)}, u32[]{:S(2)}, u32[]{:S(2)}) collective-permute-start(bf16[32,2048]{1,0:T(8,128)(2,1)S(1)} %get-tuple-element.26), channel_id=1, source_target_pairs={{0,12},{2,14},{4,0},{6,2},{8,4},{10,6},{12,8},{14,10},{1,13},{3,15... | collective-permute-start | bytes 393224 | tf_op jit(solution)/shard_map/ppermute | solution.py:206
  18.7 8.7 %collective-permute-start.13 = (bf16[64,2048]{1,0:T(8,128)(2,1)S(1)}, bf16[64,2048]{1,0:T(8,128)(2,1)S(1)}, u32[]{:S(2)}, u32[]{:S(2)}) collective-permute-start(bf16[64,2048]{1,0:T(8,128)(2,1)S(1)} %hadamard_core.3.refs_5_.refs_0_), channel_id=1, source_target_pairs={{0,4},{2,6},{4,8},{6,10},{8,12},{10,14},{12,0},{14,2},{1,5},{3,7},... | collective-permute-start | bytes 786440 | tf_op jit(solution)/shard_map/ppermute | solution.py:206
  18.8 8.6 %collective-permute-start.12 = (bf16[64,2048]{1,0:T(8,128)(2,1)S(1)}, bf16[64,2048]{1,0:T(8,128)(2,1)S(1)}, u32[]{:S(2)}, u32[]{:S(2)}) collective-permute-start(bf16[64,2048]{1,0:T(8,128)(2,1)S(1)} %hadamard_core.3.refs_5_.refs_0_), channel_id=1, source_target_pairs={{0,12},{2,14},{4,0},{6,2},{8,4},{10,6},{12,8},{14,10},{1,13},{3,15... | collective-permute-start | bytes 786440 | tf_op jit(solution)/shard_map/ppermute | solution.py:206
  22.9 8.0 %collective-permute-start.7 = (bf16[64,2048]{1,0:T(8,128)(2,1)S(1)}, bf16[64,2048]{1,0:T(8,128)(2,1)S(1)}, u32[]{:S(2)}, u32[]{:S(2)}) collective-permute-start(bf16[64,2048]{1,0:T(8,128)(2,1)S(1)} %hadamard_z.2.refs_0_), channel_id=1, source_target_pairs={{0,64},{16,80},{32,96},{48,112},{64,0},{80,16},{96,32},{112,48},{1... | collective-permute-start | bytes 786440 | tf_op jit(solution)/shard_map/ppermute | solution.py:206
  26.2 7.2 %collective-permute-start.5 = (bf16[64,2048]{1,0:T(8,128)(2,1)S(1)}, bf16[64,2048]{1,0:T(8,128)(2,1)S(1)}, u32[]{:S(2)}, u32[]{:S(2)}) collective-permute-start(bf16[64,2048]{1,0:T(8,128)(2,1)S(1)} %hadamard_z.2.refs_0_), channel_id=1, source_target_pairs={{0,16},{16,0},{32,48},{48,32},{64,80},{80,64},{96,112},{112,96},{1... | collective-permute-start | bytes 786440 | tf_op jit(solution)/shard_map/ppermute | solution.py:206
  27.4 9.2 %collective-permute-start.14 = (bf16[32,2048]{1,0:T(8,128)(2,1)S(1)}, bf16[32,2048]{1,0:T(8,128)(2,1)S(1)}, u32[]{:S(2)}, u32[]{:S(2)}) collective-permute-start(bf16[32,2048]{1,0:T(8,128)(2,1)S(1)} %get-tuple-element.27), channel_id=1, source_target_pairs={{0,4},{2,6},{4,8},{6,10},{8,12},{10,14},{12,0},{14,2},{1,5},{3,7},... | collective-permute-start | bytes 393224 | tf_op jit(solution)/shard_map/ppermute | solution.py:206
  29.3 7.3 %collective-permute-start.15 = (bf16[32,2048]{1,0:T(8,128)(2,1)S(1)}, bf16[32,2048]{1,0:T(8,128)(2,1)S(1)}, u32[]{:S(2)}, u32[]{:S(2)}) collective-permute-start(bf16[32,2048]{1,0:T(8,128)(2,1)S(1)} %get-tuple-element.28), channel_id=1, source_target_pairs={{0,12},{2,14},{4,0},{6,2},{8,4},{10,6},{12,8},{14,10},{1,13},{3,15... | collective-permute-start | bytes 393224 | tf_op jit(solution)/shard_map/ppermute | solution.py:206
  30.8 9.0 %collective-permute-start.8 = (bf16[64,2048]{1,0:T(8,128)(2,1)S(1)}, bf16[64,2048]{1,0:T(8,128)(2,1)S(1)}, u32[]{:S(2)}, u32[]{:S(2)}) collective-permute-start(bf16[64,2048]{1,0:T(8,128)(2,1)S(1)} %collective-permute-done.7.refs_2_), channel_id=1, source_target_pairs={{0,16},{16,0},{32,48},{48,32},{64,80},{80,64},{96,112},{112,96},{1... | collective-permute-start | bytes 786440 | tf_op jit(solution)/shard_map/ppermute | solution.py:206
  33.4 10.1 %collective-permute-start.9 = (bf16[64,2048]{1,0:T(8,128)(2,1)S(1)}, bf16[64,2048]{1,0:T(8,128)(2,1)S(1)}, u32[]{:S(2)}, u32[]{:S(2)}) collective-permute-start(bf16[64,2048]{1,0:T(8,128)(2,1)S(1)} %collective-permute-done.5.refs_0_), channel_id=1, source_target_pairs={{0,32},{16,48},{32,64},{48,80},{64,96},{80,112},{96,0},{112,16},{1... | collective-permute-start | bytes 786440 | tf_op jit(solution)/shard_map/ppermute | solution.py:206
  33.6 9.9 %collective-permute-start.6 = (bf16[64,2048]{1,0:T(8,128)(2,1)S(1)}, bf16[64,2048]{1,0:T(8,128)(2,1)S(1)}, u32[]{:S(2)}, u32[]{:S(2)}) collective-permute-start(bf16[64,2048]{1,0:T(8,128)(2,1)S(1)} %collective-permute-done.5.refs_0_), channel_id=1, source_target_pairs={{0,96},{16,112},{32,0},{48,16},{64,32},{80,48},{96,64},{112,80},{1... | collective-permute-start | bytes 786440 | tf_op jit(solution)/shard_map/ppermute | solution.py:206
  36.6 12.1 %collective-permute-start.11 = (bf16[64,2048]{1,0:T(8,128)(2,1)S(1)}, bf16[64,2048]{1,0:T(8,128)(2,1)S(1)}, u32[]{:S(2)}, u32[]{:S(2)}) collective-permute-start(bf16[64,2048]{1,0:T(8,128)(2,1)S(1)} %hadamard_z.2.refs_0_), channel_id=1, source_target_pairs={{0,32},{16,48},{32,64},{48,80},{64,96},{80,112},{96,0},{112,16},{1... | collective-permute-start | bytes 786440 | tf_op jit(solution)/shard_map/ppermute | solution.py:206
  36.6 14.3 %collective-permute-start.10 = (bf16[64,2048]{1,0:T(8,128)(2,1)S(1)}, bf16[64,2048]{1,0:T(8,128)(2,1)S(1)}, u32[]{:S(2)}, u32[]{:S(2)}) collective-permute-start(bf16[64,2048]{1,0:T(8,128)(2,1)S(1)} %hadamard_z.2.refs_0_), channel_id=1, source_target_pairs={{0,96},{16,112},{32,0},{48,16},{64,32},{80,48},{96,64},{112,80},{1... | collective-permute-start | bytes 786440 | tf_op jit(solution)/shard_map/ppermute | solution.py:206
  43.7 10.5 %collective-permute-start.19 = (bf16[64,2048]{1,0:T(8,128)(2,1)S(1)}, bf16[64,2048]{1,0:T(8,128)(2,1)S(1)}, u32[]{:S(2)}, u32[]{:S(2)}) collective-permute-start(bf16[64,2048]{1,0:T(8,128)(2,1)S(1)} %hadamard_z.3.refs_5_.refs_0_), channel_id=1, source_target_pairs={{0,32},{16,48},{32,64},{48,80},{64,96},{80,112},{96,0},{112,16},{1... | collective-permute-start | bytes 786440 | tf_op jit(solution)/shard_map/ppermute | solution.py:206
  45.2 12.2 %collective-permute-start.18 = (bf16[64,2048]{1,0:T(8,128)(2,1)S(1)}, bf16[64,2048]{1,0:T(8,128)(2,1)S(1)}, u32[]{:S(2)}, u32[]{:S(2)}) collective-permute-start(bf16[64,2048]{1,0:T(8,128)(2,1)S(1)} %hadamard_z.3.refs_5_.refs_0_), channel_id=1, source_target_pairs={{0,64},{16,80},{32,96},{48,112},{64,0},{80,16},{96,32},{112,48},{1... | collective-permute-start | bytes 786440 | tf_op jit(solution)/shard_map/ppermute | solution.py:206
  47.9 9.6 %collective-permute-start.17 = (bf16[64,2048]{1,0:T(8,128)(2,1)S(1)}, bf16[64,2048]{1,0:T(8,128)(2,1)S(1)}, u32[]{:S(2)}, u32[]{:S(2)}) collective-permute-start(bf16[64,2048]{1,0:T(8,128)(2,1)S(1)} %hadamard_z.3.refs_5_.refs_0_), channel_id=1, source_target_pairs={{0,96},{16,112},{32,0},{48,16},{64,32},{80,48},{96,64},{112,80},{1... | collective-permute-start | bytes 786440 | tf_op jit(solution)/shard_map/ppermute | solution.py:206
  48.7 8.8 %collective-permute-start.16 = (bf16[64,2048]{1,0:T(8,128)(2,1)S(1)}, bf16[64,2048]{1,0:T(8,128)(2,1)S(1)}, u32[]{:S(2)}, u32[]{:S(2)}) collective-permute-start(bf16[64,2048]{1,0:T(8,128)(2,1)S(1)} %hadamard_z.3.refs_5_.refs_0_), channel_id=1, source_target_pairs={{0,16},{16,0},{32,48},{48,32},{64,80},{80,64},{96,112},{112,96},{1... | collective-permute-start | bytes 786440 | tf_op jit(solution)/shard_map/ppermute | solution.py:206
  60.7 2.7 %collective-permute-start.20 = (bf16[256,2048]{1,0:T(8,128)(2,1)S(1)}, bf16[256,2048]{1,0:T(8,128)(2,1)S(1)}, u32[]{:S(2)}, u32[]{:S(2)}) collective-permute-start(bf16[256,2048]{1,0:T(8,128)(2,1)S(1)} %get-tuple-element.30), channel_id=1, source_target_pairs={{0,2},{2,0},{4,6},{6,4},{8,10},{10,8},{12,14},{14,12},{1,3},{3,1},... | collective-permute-start | bytes 3145736 | tf_op jit(solution)/shard_map/ppermute | solution.py:206
  63.5 8.5 %collective-permute-start.21 = (bf16[32,2048]{1,0:T(8,128)(2,1)S(1)}, bf16[32,2048]{1,0:T(8,128)(2,1)S(1)}, u32[]{:S(2)}, u32[]{:S(2)}) collective-permute-start(bf16[32,2048]{1,0:T(8,128)(2,1)S(1)} %get-tuple-element.31), channel_id=1, source_target_pairs={{0,4},{2,6},{4,8},{6,10},{8,12},{10,14},{12,0},{14,2},{1,5},{3,7},... | collective-permute-start | bytes 393224 | tf_op jit(solution)/shard_map/ppermute | solution.py:206
  67.2 9.7 %collective-permute-start.26 = (bf16[64,2048]{1,0:T(8,128)(2,1)S(1)}, bf16[64,2048]{1,0:T(8,128)(2,1)S(1)}, u32[]{:S(2)}, u32[]{:S(2)}) collective-permute-start(bf16[64,2048]{1,0:T(8,128)(2,1)S(1)} %collective-permute-done.18.refs_8_.refs_2_), channel_id=1, source_target_pairs={{0,16},{16,0},{32,48},{48,32},{64,80},{80,64},{96,112},{112,96},{1... | collective-permute-start | bytes 786440 | tf_op jit(solution)/shard_map/ppermute | solution.py:206
  68.4 9.0 %collective-permute-start.27 = (bf16[64,2048]{1,0:T(8,128)(2,1)S(1)}, bf16[64,2048]{1,0:T(8,128)(2,1)S(1)}, u32[]{:S(2)}, u32[]{:S(2)}) collective-permute-start(bf16[64,2048]{1,0:T(8,128)(2,1)S(1)} %collective-permute-done.16.refs_6_.refs_0_), channel_id=1, source_target_pairs={{0,32},{16,48},{32,64},{48,80},{64,96},{80,112},{96,0},{112,16},{1... | collective-permute-start | bytes 786440 | tf_op jit(solution)/shard_map/ppermute | solution.py:206
  69.6 7.8 %collective-permute-start.25 = (bf16[64,2048]{1,0:T(8,128)(2,1)S(1)}, bf16[64,2048]{1,0:T(8,128)(2,1)S(1)}, u32[]{:S(2)}, u32[]{:S(2)}) collective-permute-start(bf16[64,2048]{1,0:T(8,128)(2,1)S(1)} %collective-permute-done.16.refs_6_.refs_0_), channel_id=1, source_target_pairs={{0,96},{16,112},{32,0},{48,16},{64,32},{80,48},{96,64},{112,80},{1... | collective-permute-start | bytes 786440 | tf_op jit(solution)/shard_map/ppermute | solution.py:206
  71.6 5.0 %collective-permute-start.22 = (bf16[32,2048]{1,0:T(8,128)(2,1)S(1)}, bf16[32,2048]{1,0:T(8,128)(2,1)S(1)}, u32[]{:S(2)}, u32[]{:S(2)}) collective-permute-start(bf16[32,2048]{1,0:T(8,128)(2,1)S(1)} %get-tuple-element.32), channel_id=1, source_target_pairs={{0,12},{2,14},{4,0},{6,2},{8,4},{10,6},{12,8},{14,10},{1,13},{3,15... | collective-permute-start | bytes 393224 | tf_op jit(solution)/shard_map/ppermute | solution.py:206
  77.4 20.0 %copy-start.2 = (bf16[128,2048]{1,0:T(8,128)(2,1)S(1)}, bf16[128,2048]{1,0:T(8,128)(2,1)}, u32[]{:S(2)}) copy-start(bf16[128,2048]{1,0:T(8,128)(2,1)} %refs_4_.11) | copy-start | bytes 1572868
  80.5 2.7 %collective-permute-start.28 = (bf16[256,2048]{1,0:T(8,128)(2,1)S(1)}, bf16[256,2048]{1,0:T(8,128)(2,1)S(1)}, u32[]{:S(2)}, u32[]{:S(2)}) collective-permute-start(bf16[256,2048]{1,0:T(8,128)(2,1)S(1)} %get-tuple-element.36), channel_id=1, source_target_pairs={{0,2},{2,0},{4,6},{6,4},{8,10},{10,8},{12,14},{14,12},{1,3},{3,1},... | collective-permute-start | bytes 3145736 | tf_op jit(solution)/shard_map/ppermute | solution.py:206
  83.3 6.9 %collective-permute-start.29 = (bf16[32,2048]{1,0:T(8,128)(2,1)S(1)}, bf16[32,2048]{1,0:T(8,128)(2,1)S(1)}, u32[]{:S(2)}, u32[]{:S(2)}) collective-permute-start(bf16[32,2048]{1,0:T(8,128)(2,1)S(1)} %get-tuple-element.37), channel_id=1, source_target_pairs={{0,4},{2,6},{4,8},{6,10},{8,12},{10,14},{12,0},{14,2},{1,5},{3,7},... | collective-permute-start | bytes 393224 | tf_op jit(solution)/shard_map/ppermute | solution.py:206
  85.4 6.4 %collective-permute-start.31 = (bf16[32,2048]{1,0:T(8,128)(2,1)S(1)}, bf16[32,2048]{1,0:T(8,128)(2,1)S(1)}, u32[]{:S(2)}, u32[]{:S(2)}) collective-permute-start(bf16[32,2048]{1,0:T(8,128)(2,1)S(1)} %get-tuple-element.40), channel_id=1, source_target_pairs={{0,12},{2,14},{4,0},{6,2},{8,4},{10,6},{12,8},{14,10},{1,13},{3,15... | collective-permute-start | bytes 393224 | tf_op jit(solution)/shard_map/ppermute | solution.py:206
  86.6 10.9 %collective-permute-start.23 = (bf16[64,2048]{1,0:T(8,128)(2,1)S(1)}, bf16[64,2048]{1,0:T(8,128)(2,1)S(1)}, u32[]{:S(2)}, u32[]{:S(2)}) collective-permute-start(bf16[64,2048]{1,0:T(8,128)(2,1)S(1)} %get-tuple-element.33.refs_6_), channel_id=1, source_target_pairs={{0,4},{2,6},{4,8},{6,10},{8,12},{10,14},{12,0},{14,2},{1,5},{3,7},... | collective-permute-start | bytes 786440 | tf_op jit(solution)/shard_map/ppermute | solution.py:206
  87.5 10.0 %collective-permute-start.24 = (bf16[64,2048]{1,0:T(8,128)(2,1)S(1)}, bf16[64,2048]{1,0:T(8,128)(2,1)S(1)}, u32[]{:S(2)}, u32[]{:S(2)}) collective-permute-start(bf16[64,2048]{1,0:T(8,128)(2,1)S(1)} %get-tuple-element.34), channel_id=1, source_target_pairs={{0,12},{2,14},{4,0},{6,2},{8,4},{10,6},{12,8},{14,10},{1,13},{3,15... | collective-permute-start | bytes 786440 | tf_op jit(solution)/shard_map/ppermute | solution.py:206
  92.0 9.3 %collective-permute-start.32 = (bf16[64,2048]{1,0:T(8,128)(2,1)S(1)}, bf16[64,2048]{1,0:T(8,128)(2,1)S(1)}, u32[]{:S(2)}, u32[]{:S(2)}) collective-permute-start(bf16[64,2048]{1,0:T(8,128)(2,1)S(1)} %get-tuple-element.41), channel_id=1, source_target_pairs={{0,4},{2,6},{4,8},{6,10},{8,12},{10,14},{12,0},{14,2},{1,5},{3,7},... | collective-permute-start | bytes 786440 | tf_op jit(solution)/shard_map/ppermute | solution.py:206
  92.4 9.5 %collective-permute-start.33 = (bf16[64,2048]{1,0:T(8,128)(2,1)S(1)}, bf16[64,2048]{1,0:T(8,128)(2,1)S(1)}, u32[]{:S(2)}, u32[]{:S(2)}) collective-permute-start(bf16[64,2048]{1,0:T(8,128)(2,1)S(1)} %get-tuple-element.42), channel_id=1, source_target_pairs={{0,12},{2,14},{4,0},{6,2},{8,4},{10,6},{12,8},{14,10},{1,13},{3,15... | collective-permute-start | bytes 786440 | tf_op jit(solution)/shard_map/ppermute | solution.py:206
  97.6 10.0 %collective-permute-start.30 = (bf16[64,2048]{1,0:T(8,128)(2,1)S(1)}, bf16[64,2048]{1,0:T(8,128)(2,1)S(1)}, u32[]{:S(2)}, u32[]{:S(2)}) collective-permute-start(bf16[64,2048]{1,0:T(8,128)(2,1)S(1)} %get-tuple-element.38.refs_5_.refs_0_), channel_id=1, source_target_pairs={{0,1},{2,3},{4,5},{6,7},{8,9},{10,11},{12,13},{14,15},{16,17},{18,... | collective-permute-start | bytes 786440 | tf_op jit(solution)/shard_map/ppermute | solution.py:215
  102.1 10.9 %collective-permute-start.34 = (bf16[64,2048]{1,0:T(8,128)(2,1)S(1)}, bf16[64,2048]{1,0:T(8,128)(2,1)S(1)}, u32[]{:S(2)}, u32[]{:S(2)}) collective-permute-start(bf16[64,2048]{1,0:T(8,128)(2,1)S(1)} %get-tuple-element.43.refs_3_), channel_id=1, source_target_pairs={{0,1},{2,3},{4,5},{6,7},{8,9},{10,11},{12,13},{14,15},{16,17},{18,... | collective-permute-start | bytes 786440 | tf_op jit(solution)/shard_map/ppermute | solution.py:215

commit v6 on v5

--- a/solution.py
+++ b/solution.py
@@ -241,12 +241,23 @@
         mate = move(own, "dp", ring(0, 1))
         return [own] + [move(own, "dp", ring(-dy)) for dy in (1, 2, 3)], mate
 
+    def hold(value, behind):
+        return pl.pallas_call(
+            lambda *refs: None,
+            out_shape=shape(*value.shape),
+            in_specs=[ANY] * (1 + len(behind)),
+            out_specs=ANY,
+            input_output_aliases={0: 0},
+            compiler_params=pltpu.CompilerParams(vmem_limit_bytes=1 << 20),
+            name="hold",
+        )(value, *behind)
+
     def spread_mate(column, mate):
         return [mate, move(mate, "dp", ring(-1)), move(column[2], "dp", ring(0, 1)), move(mate, "dp", ring(-3))]
 
     def far_sum(keep, came, behind=()):
         low, high = call("far_sum", far_kernel, (keep, came), (shape(half, columns),) * 2, behind)
-        return up(low), down(high)
+        return low, (up(low), down(high))
 
     def near_sum(keep, came, far, behind=()):
         return call("near_sum", near_kernel, (keep, came, *far), (shape(rows, columns),) * 2, behind)
@@ -278,20 +289,22 @@
     terms1 = near_z(pair(1, local, other, [terms0[1]]))
     own0 = mix(terms0, [terms1[0]])
     column0, mate0 = spread_column(own0)
+    mate0 = hold(mate0, [column0[1], column0[3]])
     mates0 = spread_mate(column0, mate0)
-    own1 = mix(far_z(terms1), mates0[1:])
+    own1 = mix(far_z(terms1), [mates0[1], mates0[3]])
     column1, mate1 = spread_column(own1)
     products0 = project(column0, out_weight, None, [own1])
-    keep0, send0 = project(mates0, out_weight, products0, [mate1, *column1[1:]])
-    came0 = swap(send0)
+    keep0, send0 = project(mates0, out_weight, products0)
+    mate1 = hold(mate1, [*column1[1:], keep0])
+    came0 = swap(hold(send0, [mate1]))
     mates1 = spread_mate(column1, mate1)
-    far0 = far_sum(keep0, came0)
-    products1 = project(column1, out_weight, None, [far0[0]])
+    made0, far0 = far_sum(keep0, came0)
+    products1 = project(column1, out_weight, None, [made0])
     near0 = near_sum(keep0, came0, far0)
     keep1, send1 = project(mates1, out_weight, products1, [near0[0]])
     came1 = swap(send1)
-    far1 = far_sum(keep1, came1)
-    leading0, summed0 = finish(0, keep0, came0, last_sum(near0), [far1[0]])
+    made1, far1 = far_sum(keep1, came1)
+    leading0, summed0 = finish(0, keep0, came0, last_sum(near0), [made1])
     passed0 = pipe(leading0)
     near1 = near_sum(keep1, came1, far1)
     leading1, summed1 = finish(1, keep1, came1, last_sum(near1), [leading0])

time: 114 us -> 107 us (0.939)
  starting transfers between devices: 53.2 us -> 48.9 us
  waiting for transfers between devices: 41.4 us -> 38.1 us
    ppermute x33, starting transfers between devices: 50.6 us -> 46.3 us  [move(): lax.ppermute(value, axis, [(i, target(i)) for i in range(lax.axis_size(ax...]
    ppermute x33, waiting for transfers between devices: 31.8 us -> 28.5 us  [move(): lax.ppermute(value, axis, [(i, target(i)) for i in range(lax.axis_size(ax...]
  transfers between devices with their start and end apart: 35 -> 35, of which waited for: 20 -> 20; matrix products, arithmetic and copies ran while one was open for 0% -> 0% of each run, Pallas kernels for 5% -> 8%
where the time goes in v6:
time: 107 us; the launch traced here: 106 us
  starting transfers between devices  48.9 us (46%)
  waiting for transfers between devices  38.1 us (36%)
  Pallas kernels  14 us (13%)
  local copies, waits for them, and re-layouts  5.13 us (5%)
    ppermute x33, starting transfers between devices, move(): lax.ppermute(value, axis, [(i, target(i)) for i in range(lax.axis_size(ax...  46.3 us
    ppermute x33, waiting for transfers between devices, move(): lax.ppermute(value, axis, [(i, target(i)) for i in range(lax.axis_size(ax...  28.5 us
    pallas_call x19, Pallas kernels, call(): pl.pallas_call(lambda *refs: kernel(*refs[:count], *refs[count + len(behi...  14 us
    ppermute x2, waiting for transfers between devices, pipe(): return lax.ppermute(value, 'pipe', [(0, 1)])  9.59 us
    unnamed x10, local copies, waits for them, and re-layouts  5.13 us
    ppermute x2, starting transfers between devices, pipe(): return lax.ppermute(value, 'pipe', [(0, 1)])  2.58 us
  transfers between devices with their start and end apart: 35, of which 20 were waited for; matrix products, arithmetic and copies ran while one was open for 0% of the time, Pallas kernels for 8%

profile of v6, /device:TPU:4, one launch (start us, length us, event | category | flops | bytes accessed | tf_op | source)
XLA Modules:
  0.0 106.4 jit_solution(9269501929767457147)
XLA Ops:
  0.0 1.0 copy-done.3
  1.0 0.7 copy-done.4
  1.7 0.7 rotate_local.1.refs_0_
  2.6 1.9 %collective-permute-done.refs_1_ = bf16[128,2048]{1,0:T(8,128)(2,1)S(1)} collective-permute-done((bf16[128,2048]{1,0:T(8,128)(2,1)S(1)}, bf16[128,2048]{1,0:T(8,128)(2,1)S(1)}, u32[]{:S(2)}, u32[]{:S(2)}) %collective-permute-start) | collective-permute-done | bytes 524320 | tf_op jit(solution)/shard_map/ppermute | solution.py:206
  4.6 2.0 %collective-permute-start.2 = (bf16[64,2048]{1,0:T(8,128)(2,1)S(1)}, bf16[64,2048]{1,0:T(8,128)(2,1)S(1)}, u32[]{:S(2)}, u32[]{:S(2)}) collective-permute-start(bf16[64,2048]{1,0:T(8,128)(2,1)S(1)} %hadamard_core.2.refs_1_.refs_0_), channel_id=1, source_target_pairs={{0,4},{2,6},{4,8},{6,10},{8,12},{10,14},{12,0},{14,2},{1,5},{3,7},... | collective-permute-start | bytes 786440 | tf_op jit(solution)/shard_map/ppermute | solution.py:206
  6.5 2.2 %collective-permute-start.1 = (bf16[64,2048]{1,0:T(8,128)(2,1)S(1)}, bf16[64,2048]{1,0:T(8,128)(2,1)S(1)}, u32[]{:S(2)}, u32[]{:S(2)}) collective-permute-start(bf16[64,2048]{1,0:T(8,128)(2,1)S(1)} %hadamard_core.2.refs_1_.refs_0_), channel_id=1, source_target_pairs={{0,12},{2,14},{4,0},{6,2},{8,4},{10,6},{12,8},{14,10},{1,13},{3,15... | collective-permute-start | bytes 786440 | tf_op jit(solution)/shard_map/ppermute | solution.py:206
  8.7 3.4 %copy-done = bf16[1,2048,2048]{2,1,0:T(8,128)(2,1)S(1)} copy-done((bf16[1,2048,2048]{2,1,0:T(8,128)(2,1)S(1)}, bf16[1,2048,2048]{2,1,0:T(8,128)(2,1)}, u32[]{:S(2)}) %copy-start) | copy-done | bytes 8388632
  12.1 3.1 %collective-permute-done.2.refs_1_.refs_2_ = bf16[64,2048]{1,0:T(8,128)(2,1)S(1)} collective-permute-done((bf16[64,2048]{1,0:T(8,128)(2,1)S(1)}, bf16[64,2048]{1,0:T(8,128)(2,1)S(1)}, u32[]{:S(2)}, u32[]{:S(2)}) %collective-permute-start.2) | collective-permute-done | bytes 262176 | tf_op jit(solution)/shard_map/ppermute | solution.py:206
  15.3 1.3 %collective-permute-start.3 = (bf16[32,2048]{1,0:T(8,128)(2,1)S(1)}, bf16[32,2048]{1,0:T(8,128)(2,1)S(1)}, u32[]{:S(2)}, u32[]{:S(2)}) collective-permute-start(bf16[32,2048]{1,0:T(8,128)(2,1)S(1)} %get-tuple-element.25), channel_id=1, source_target_pairs={{0,4},{2,6},{4,8},{6,10},{8,12},{10,14},{12,0},{14,2},{1,5},{3,7},... | collective-permute-start | bytes 393224 | tf_op jit(solution)/shard_map/ppermute | solution.py:206
  16.6 2.0 %collective-permute-start.4 = (bf16[32,2048]{1,0:T(8,128)(2,1)S(1)}, bf16[32,2048]{1,0:T(8,128)(2,1)S(1)}, u32[]{:S(2)}, u32[]{:S(2)}) collective-permute-start(bf16[32,2048]{1,0:T(8,128)(2,1)S(1)} %get-tuple-element.26), channel_id=1, source_target_pairs={{0,12},{2,14},{4,0},{6,2},{8,4},{10,6},{12,8},{14,10},{1,13},{3,15... | collective-permute-start | bytes 393224 | tf_op jit(solution)/shard_map/ppermute | solution.py:206
  18.7 2.9 %collective-permute-done.3.refs_3_ = bf16[32,2048]{1,0:T(8,128)(2,1)S(1)} collective-permute-done((bf16[32,2048]{1,0:T(8,128)(2,1)S(1)}, bf16[32,2048]{1,0:T(8,128)(2,1)S(1)}, u32[]{:S(2)}, u32[]{:S(2)}) %collective-permute-start.3) | collective-permute-done | bytes 131104 | tf_op jit(solution)/shard_map/ppermute | solution.py:206
  21.6 0.2 hadamard_z.2.refs_0_
  21.8 1.6 %collective-permute-start.7 = (bf16[64,2048]{1,0:T(8,128)(2,1)S(1)}, bf16[64,2048]{1,0:T(8,128)(2,1)S(1)}, u32[]{:S(2)}, u32[]{:S(2)}) collective-permute-start(bf16[64,2048]{1,0:T(8,128)(2,1)S(1)} %hadamard_z.2.refs_0_), channel_id=1, source_target_pairs={{0,32},{16,48},{32,64},{48,80},{64,96},{80,112},{96,0},{112,16},{1... | collective-permute-start | bytes 786440 | tf_op jit(solution)/shard_map/ppermute | solution.py:206
  23.5 1.7 %collective-permute-start.6 = (bf16[64,2048]{1,0:T(8,128)(2,1)S(1)}, bf16[64,2048]{1,0:T(8,128)(2,1)S(1)}, u32[]{:S(2)}, u32[]{:S(2)}) collective-permute-start(bf16[64,2048]{1,0:T(8,128)(2,1)S(1)} %hadamard_z.2.refs_0_), channel_id=1, source_target_pairs={{0,96},{16,112},{32,0},{48,16},{64,32},{80,48},{96,64},{112,80},{1... | collective-permute-start | bytes 786440 | tf_op jit(solution)/shard_map/ppermute | solution.py:206
  25.1 1.2 %collective-permute-start.5 = (bf16[64,2048]{1,0:T(8,128)(2,1)S(1)}, bf16[64,2048]{1,0:T(8,128)(2,1)S(1)}, u32[]{:S(2)}, u32[]{:S(2)}) collective-permute-start(bf16[64,2048]{1,0:T(8,128)(2,1)S(1)} %hadamard_z.2.refs_0_), channel_id=1, source_target_pairs={{0,16},{16,0},{32,48},{48,32},{64,80},{80,64},{96,112},{112,96},{1... | collective-permute-start | bytes 786440 | tf_op jit(solution)/shard_map/ppermute | solution.py:206
  26.3 1.6 %collective-permute-start.13 = (bf16[64,2048]{1,0:T(8,128)(2,1)S(1)}, bf16[64,2048]{1,0:T(8,128)(2,1)S(1)}, u32[]{:S(2)}, u32[]{:S(2)}) collective-permute-start(bf16[64,2048]{1,0:T(8,128)(2,1)S(1)} %hadamard_core.3.refs_5_.refs_0_), channel_id=1, source_target_pairs={{0,4},{2,6},{4,8},{6,10},{8,12},{10,14},{12,0},{14,2},{1,5},{3,7},... | collective-permute-start | bytes 786440 | tf_op jit(solution)/shard_map/ppermute | solution.py:206
  27.9 1.6 %collective-permute-start.12 = (bf16[64,2048]{1,0:T(8,128)(2,1)S(1)}, bf16[64,2048]{1,0:T(8,128)(2,1)S(1)}, u32[]{:S(2)}, u32[]{:S(2)}) collective-permute-start(bf16[64,2048]{1,0:T(8,128)(2,1)S(1)} %hadamard_core.3.refs_5_.refs_0_), channel_id=1, source_target_pairs={{0,12},{2,14},{4,0},{6,2},{8,4},{10,6},{12,8},{14,10},{1,13},{3,15... | collective-permute-start | bytes 786440 | tf_op jit(solution)/shard_map/ppermute | solution.py:206
  29.6 0.5 collective-permute-done.7.refs_2_.refs_3_
  30.1 1.9 %collective-permute-start.9 = (bf16[64,2048]{1,0:T(8,128)(2,1)S(1)}, bf16[64,2048]{1,0:T(8,128)(2,1)S(1)}, u32[]{:S(2)}, u32[]{:S(2)}) collective-permute-start(bf16[64,2048]{1,0:T(8,128)(2,1)S(1)} %hadamard_z.2.refs_0_), channel_id=1, source_target_pairs={{0,64},{16,80},{32,96},{48,112},{64,0},{80,16},{96,32},{112,48},{1... | collective-permute-start | bytes 786440 | tf_op jit(solution)/shard_map/ppermute | solution.py:206
  32.0 0.7 collective-permute-start.11
  32.7 2.6 %collective-permute-start.8 = (bf16[64,2048]{1,0:T(8,128)(2,1)S(1)}, bf16[64,2048]{1,0:T(8,128)(2,1)S(1)}, u32[]{:S(2)}, u32[]{:S(2)}) collective-permute-start(bf16[64,2048]{1,0:T(8,128)(2,1)S(1)} %hold.3.refs_0_), channel_id=1, source_target_pairs={{0,96},{16,112},{32,0},{48,16},{64,32},{80,48},{96,64},{112,80},{1... | collective-permute-start | bytes 786440 | tf_op jit(solution)/shard_map/ppermute | solution.py:206
  35.3 2.0 %collective-permute-start.14 = (bf16[32,2048]{1,0:T(8,128)(2,1)S(1)}, bf16[32,2048]{1,0:T(8,128)(2,1)S(1)}, u32[]{:S(2)}, u32[]{:S(2)}) collective-permute-start(bf16[32,2048]{1,0:T(8,128)(2,1)S(1)} %get-tuple-element.27), channel_id=1, source_target_pairs={{0,4},{2,6},{4,8},{6,10},{8,12},{10,14},{12,0},{14,2},{1,5},{3,7},... | collective-permute-start | bytes 393224 | tf_op jit(solution)/shard_map/ppermute | solution.py:206
  37.3 1.7 %collective-permute-start.15 = (bf16[32,2048]{1,0:T(8,128)(2,1)S(1)}, bf16[32,2048]{1,0:T(8,128)(2,1)S(1)}, u32[]{:S(2)}, u32[]{:S(2)}) collective-permute-start(bf16[32,2048]{1,0:T(8,128)(2,1)S(1)} %get-tuple-element.28), channel_id=1, source_target_pairs={{0,12},{2,14},{4,0},{6,2},{8,4},{10,6},{12,8},{14,10},{1,13},{3,15... | collective-permute-start | bytes 393224 | tf_op jit(solution)/shard_map/ppermute | solution.py:206
  39.0 1.6 %collective-permute-done.9.refs_2_ = bf16[64,2048]{1,0:T(8,128)(2,1)S(1)} collective-permute-done((bf16[64,2048]{1,0:T(8,128)(2,1)S(1)}, bf16[64,2048]{1,0:T(8,128)(2,1)S(1)}, u32[]{:S(2)}, u32[]{:S(2)}) %collective-permute-start.9) | collective-permute-done | bytes 262176 | tf_op jit(solution)/shard_map/ppermute | solution.py:206
  40.5 1.2 %collective-permute-start.10 = (bf16[64,2048]{1,0:T(8,128)(2,1)S(1)}, bf16[64,2048]{1,0:T(8,128)(2,1)S(1)}, u32[]{:S(2)}, u32[]{:S(2)}) collective-permute-start(bf16[64,2048]{1,0:T(8,128)(2,1)S(1)} %collective-permute-done.9.refs_2_), channel_id=1, source_target_pairs={{0,16},{16,0},{32,48},{48,32},{64,80},{80,64},{96,112},{112,96},{1... | collective-permute-start | bytes 786440 | tf_op jit(solution)/shard_map/ppermute | solution.py:206
  41.8 0.5 collective-permute-done.15.refs_4_
  42.3 1.0 collective-permute-done.11.refs_6_.refs_3_
  43.3 0.2 hadamard_z.3.refs_5_.refs_0_
  43.5 0.5 collective-permute-start.19
  44.0 2.7 %collective-permute-start.18 = (bf16[64,2048]{1,0:T(8,128)(2,1)S(1)}, bf16[64,2048]{1,0:T(8,128)(2,1)S(1)}, u32[]{:S(2)}, u32[]{:S(2)}) collective-permute-start(bf16[64,2048]{1,0:T(8,128)(2,1)S(1)} %hadamard_z.3.refs_5_.refs_0_), channel_id=1, source_target_pairs={{0,64},{16,80},{32,96},{48,112},{64,0},{80,16},{96,32},{112,48},{1... | collective-permute-start | bytes 786440 | tf_op jit(solution)/shard_map/ppermute | solution.py:206
  46.7 1.2 %collective-permute-start.17 = (bf16[64,2048]{1,0:T(8,128)(2,1)S(1)}, bf16[64,2048]{1,0:T(8,128)(2,1)S(1)}, u32[]{:S(2)}, u32[]{:S(2)}) collective-permute-start(bf16[64,2048]{1,0:T(8,128)(2,1)S(1)} %hadamard_z.3.refs_5_.refs_0_), channel_id=1, source_target_pairs={{0,96},{16,112},{32,0},{48,16},{64,32},{80,48},{96,64},{112,80},{1... | collective-permute-start | bytes 786440 | tf_op jit(solution)/shard_map/ppermute | solution.py:206
  48.0 1.2 %collective-permute-start.16 = (bf16[64,2048]{1,0:T(8,128)(2,1)S(1)}, bf16[64,2048]{1,0:T(8,128)(2,1)S(1)}, u32[]{:S(2)}, u32[]{:S(2)}) collective-permute-start(bf16[64,2048]{1,0:T(8,128)(2,1)S(1)} %hadamard_z.3.refs_5_.refs_0_), channel_id=1, source_target_pairs={{0,16},{16,0},{32,48},{48,32},{64,80},{80,64},{96,112},{112,96},{1... | collective-permute-start | bytes 786440 | tf_op jit(solution)/shard_map/ppermute | solution.py:206
  49.2 2.4 %project_column.2.refs_5_ = bf16[256,2048]{1,0:T(8,128)(2,1)S(1)} custom-call(bf16[64,2048]{1,0:T(8,128)(2,1)S(1)} %hadamard_z.2.refs_0_, bf16[64,2048]{1,0:T(8,128)(2,1)S(1)} %collective-permute-done.6.refs_1_, bf16[64,2048]{1,0:T(8,128)(2,1)S(1)} %collective-permute-done.9.refs_2_, bf16[64,2048]{1,0:T(8,128)(2,1)S(1)} %collective-permute-done.7.refs_2_.refs_3_, ...), custom_call_target="tpu_custom_call" | custom-call | flops 10737418240 | bytes 52428800 | tf_op jit(solution)/shard_map/project_column/pallas_call | solution.py:38
  51.6 3.2 %project_mate.2 = (bf16[256,2048]{1,0:T(8,128)(2,1)S(1)}, bf16[256,2048]{1,0:T(8,128)(2,1)S(1)}) custom-call(bf16[64,2048]{1,0:T(8,128)(2,1)S(1)} %hold.3.refs_0_, bf16[64,2048]{1,0:T(8,128)(2,1)S(1)} %collective-permute-done.8.refs_5_.refs_1_, bf16[64,2048]{1,0:T(8,128)(2,1)S(1)} %collective-permute-done.10.refs_2_, ...), custom_call_target="tpu_custom_call" | custom-call | flops 10737418240 | bytes 62914560 | tf_op jit(solution)/shard_map/project_mate/pallas_call | solution.py:38
  54.8 2.7 %collective-permute-done.19.refs_3_ = bf16[64,2048]{1,0:T(8,128)(2,1)S(1)} collective-permute-done((bf16[64,2048]{1,0:T(8,128)(2,1)S(1)}, bf16[64,2048]{1,0:T(8,128)(2,1)S(1)}, u32[]{:S(2)}, u32[]{:S(2)}) %collective-permute-start.19) | collective-permute-done | bytes 262176 | tf_op jit(solution)/shard_map/ppermute | solution.py:206
  57.5 0.6 collective-permute-done.17.refs_1_
  58.2 1.8 %collective-permute-start.27 = (bf16[64,2048]{1,0:T(8,128)(2,1)S(1)}, bf16[64,2048]{1,0:T(8,128)(2,1)S(1)}, u32[]{:S(2)}, u32[]{:S(2)}) collective-permute-start(bf16[64,2048]{1,0:T(8,128)(2,1)S(1)} %hold.4.refs_1_.refs_0_), channel_id=1, source_target_pairs={{0,32},{16,48},{32,64},{48,80},{64,96},{80,112},{96,0},{112,16},{1... | collective-permute-start | bytes 786440 | tf_op jit(solution)/shard_map/ppermute | solution.py:206
  59.9 1.5 %collective-permute-start.25 = (bf16[64,2048]{1,0:T(8,128)(2,1)S(1)}, bf16[64,2048]{1,0:T(8,128)(2,1)S(1)}, u32[]{:S(2)}, u32[]{:S(2)}) collective-permute-start(bf16[64,2048]{1,0:T(8,128)(2,1)S(1)} %hold.4.refs_1_.refs_0_), channel_id=1, source_target_pairs={{0,96},{16,112},{32,0},{48,16},{64,32},{80,48},{96,64},{112,80},{1... | collective-permute-start | bytes 786440 | tf_op jit(solution)/shard_map/ppermute | solution.py:206
  61.5 1.2 %collective-permute-start.26 = (bf16[64,2048]{1,0:T(8,128)(2,1)S(1)}, bf16[64,2048]{1,0:T(8,128)(2,1)S(1)}, u32[]{:S(2)}, u32[]{:S(2)}) collective-permute-start(bf16[64,2048]{1,0:T(8,128)(2,1)S(1)} %collective-permute-done.18.refs_2_), channel_id=1, source_target_pairs={{0,16},{16,0},{32,48},{48,32},{64,80},{80,64},{96,112},{112,96},{1... | collective-permute-start | bytes 786440 | tf_op jit(solution)/shard_map/ppermute | solution.py:206
  62.7 1.2 %collective-permute-start.22 = (bf16[32,2048]{1,0:T(8,128)(2,1)S(1)}, bf16[32,2048]{1,0:T(8,128)(2,1)S(1)}, u32[]{:S(2)}, u32[]{:S(2)}) collective-permute-start(bf16[32,2048]{1,0:T(8,128)(2,1)S(1)} %get-tuple-element.32), channel_id=1, source_target_pairs={{0,12},{2,14},{4,0},{6,2},{8,4},{10,6},{12,8},{14,10},{1,13},{3,15... | collective-permute-start | bytes 393224 | tf_op jit(solution)/shard_map/ppermute | solution.py:206
  64.0 0.9 collective-permute-start.21
  64.8 2.4 %project_column.3.refs_5_ = bf16[256,2048]{1,0:T(8,128)(2,1)S(1)} custom-call(bf16[64,2048]{1,0:T(8,128)(2,1)S(1)} %hadamard_z.3.refs_5_.refs_0_, bf16[64,2048]{1,0:T(8,128)(2,1)S(1)} %collective-permute-done.17.refs_1_, bf16[64,2048]{1,0:T(8,128)(2,1)S(1)} %collective-permute-done.18.refs_2_, bf16[64,2048]{1,0:T(8,128)(2,1)S(1)} %collective-permute-done.19.refs_3_, ...), custom_call_target="tpu_custom_call" | custom-call | flops 10737418240 | bytes 52428800 | tf_op jit(solution)/shard_map/project_column/pallas_call | solution.py:38
  67.2 0.6 collective-permute-done.22.refs_3_
  67.8 2.4 %collective-permute-done.21.refs_2_ = bf16[32,2048]{1,0:T(8,128)(2,1)S(1)} collective-permute-done((bf16[32,2048]{1,0:T(8,128)(2,1)S(1)}, bf16[32,2048]{1,0:T(8,128)(2,1)S(1)}, u32[]{:S(2)}, u32[]{:S(2)}) %collective-permute-start.21) | collective-permute-done | bytes 131104 | tf_op jit(solution)/shard_map/ppermute | solution.py:206
  70.4 3.1 %project_mate.3 = (bf16[256,2048]{1,0:T(8,128)(2,1)S(1)}, bf16[256,2048]{1,0:T(8,128)(2,1)S(1)}) custom-call(bf16[64,2048]{1,0:T(8,128)(2,1)S(1)} %hold.4.refs_1_.refs_0_, bf16[64,2048]{1,0:T(8,128)(2,1)S(1)} %collective-permute-done.25.refs_1_, bf16[64,2048]{1,0:T(8,128)(2,1)S(1)} %collective-permute-done.26.refs_2_, ...), custom_call_target="tpu_custom_call" | custom-call | flops 10737418240 | bytes 62914560 | tf_op jit(solution)/shard_map/project_mate/pallas_call | solution.py:38
  73.5 2.6 %collective-permute-done.28.refs_1_ = bf16[256,2048]{1,0:T(8,128)(2,1)S(1)} collective-permute-done((bf16[256,2048]{1,0:T(8,128)(2,1)S(1)}, bf16[256,2048]{1,0:T(8,128)(2,1)S(1)}, u32[]{:S(2)}, u32[]{:S(2)}) %collective-permute-start.28) | collective-permute-done | bytes 1048608 | tf_op jit(solution)/shard_map/ppermute | solution.py:206
  76.2 0.5 collective-permute-start.31
  76.7 1.6 %collective-permute-start.30 = (bf16[32,2048]{1,0:T(8,128)(2,1)S(1)}, bf16[32,2048]{1,0:T(8,128)(2,1)S(1)}, u32[]{:S(2)}, u32[]{:S(2)}) collective-permute-start(bf16[32,2048]{1,0:T(8,128)(2,1)S(1)} %get-tuple-element.37.refs_5_), channel_id=1, source_target_pairs={{0,4},{2,6},{4,8},{6,10},{8,12},{10,14},{12,0},{14,2},{1,5},{3,7},... | collective-permute-start | bytes 393224 | tf_op jit(solution)/shard_map/ppermute | solution.py:206
  78.4 3.2 %collective-permute-start.24 = (bf16[64,2048]{1,0:T(8,128)(2,1)S(1)}, bf16[64,2048]{1,0:T(8,128)(2,1)S(1)}, u32[]{:S(2)}, u32[]{:S(2)}) collective-permute-start(bf16[64,2048]{1,0:T(8,128)(2,1)S(1)} %get-tuple-element.34), channel_id=1, source_target_pairs={{0,12},{2,14},{4,0},{6,2},{8,4},{10,6},{12,8},{14,10},{1,13},{3,15... | collective-permute-start | bytes 786440 | tf_op jit(solution)/shard_map/ppermute | solution.py:206
  81.6 1.1 %collective-permute-done.31.refs_3_ = bf16[32,2048]{1,0:T(8,128)(2,1)S(1)} collective-permute-done((bf16[32,2048]{1,0:T(8,128)(2,1)S(1)}, bf16[32,2048]{1,0:T(8,128)(2,1)S(1)}, u32[]{:S(2)}, u32[]{:S(2)}) %collective-permute-start.31) | collective-permute-done | bytes 131104 | tf_op jit(solution)/shard_map/ppermute | solution.py:206
  82.6 1.6 %collective-permute-done.30.refs_2_ = bf16[32,2048]{1,0:T(8,128)(2,1)S(1)} collective-permute-done((bf16[32,2048]{1,0:T(8,128)(2,1)S(1)}, bf16[32,2048]{1,0:T(8,128)(2,1)S(1)}, u32[]{:S(2)}, u32[]{:S(2)}) %collective-permute-start.30) | collective-permute-done | bytes 131104 | tf_op jit(solution)/shard_map/ppermute | solution.py:206
  84.3 0.2 near_sum.3
  84.4 0.5 collective-permute-start.32
  84.9 2.8 %collective-permute-start.33 = (bf16[64,2048]{1,0:T(8,128)(2,1)S(1)}, bf16[64,2048]{1,0:T(8,128)(2,1)S(1)}, u32[]{:S(2)}, u32[]{:S(2)}) collective-permute-start(bf16[64,2048]{1,0:T(8,128)(2,1)S(1)} %get-tuple-element.42), channel_id=1, source_target_pairs={{0,12},{2,14},{4,0},{6,2},{8,4},{10,6},{12,8},{14,10},{1,13},{3,15... | collective-permute-start | bytes 786440 | tf_op jit(solution)/shard_map/ppermute | solution.py:206
  87.7 0.5 collective-permute-done.24.refs_3_
  88.3 1.6 %collective-permute-done.23.refs_2_ = bf16[64,2048]{1,0:T(8,128)(2,1)S(1)} collective-permute-done((bf16[64,2048]{1,0:T(8,128)(2,1)S(1)}, bf16[64,2048]{1,0:T(8,128)(2,1)S(1)}, u32[]{:S(2)}, u32[]{:S(2)}) %collective-permute-start.23) | collective-permute-done | bytes 262176 | tf_op jit(solution)/shard_map/ppermute | solution.py:206
  89.9 0.2 residual.2
  90.1 1.3 %collective-permute-start.29 = (bf16[64,2048]{1,0:T(8,128)(2,1)S(1)}, bf16[64,2048]{1,0:T(8,128)(2,1)S(1)}, u32[]{:S(2)}, u32[]{:S(2)}) collective-permute-start(bf16[64,2048]{1,0:T(8,128)(2,1)S(1)} %get-tuple-element.38.refs_5_.refs_0_), channel_id=1, source_target_pairs={{0,1},{2,3},{4,5},{6,7},{8,9},{10,11},{12,13},{14,15},{16,17},{18,... | collective-permute-start | bytes 786440 | tf_op jit(solution)/shard_map/ppermute | solution.py:215
  91.4 3.0 %collective-permute-done.32.refs_2_ = bf16[64,2048]{1,0:T(8,128)(2,1)S(1)} collective-permute-done((bf16[64,2048]{1,0:T(8,128)(2,1)S(1)}, bf16[64,2048]{1,0:T(8,128)(2,1)S(1)}, u32[]{:S(2)}, u32[]{:S(2)}) %collective-permute-start.32) | collective-permute-done | bytes 262176 | tf_op jit(solution)/shard_map/ppermute | solution.py:206
  94.4 0.2 residual.3
  94.6 1.3 %collective-permute-start.34 = (bf16[64,2048]{1,0:T(8,128)(2,1)S(1)}, bf16[64,2048]{1,0:T(8,128)(2,1)S(1)}, u32[]{:S(2)}, u32[]{:S(2)}) collective-permute-start(bf16[64,2048]{1,0:T(8,128)(2,1)S(1)} %get-tuple-element.43.refs_3_), channel_id=1, source_target_pairs={{0,1},{2,3},{4,5},{6,7},{8,9},{10,11},{12,13},{14,15},{16,17},{18,... | collective-permute-start | bytes 786440 | tf_op jit(solution)/shard_map/ppermute | solution.py:215
  95.9 4.2 %collective-permute-done.29.refs_2_ = bf16[64,2048]{1,0:T(8,128)(2,1)S(1)} collective-permute-done((bf16[64,2048]{1,0:T(8,128)(2,1)S(1)}, bf16[64,2048]{1,0:T(8,128)(2,1)S(1)}, u32[]{:S(2)}, u32[]{:S(2)}) %collective-permute-start.29) | collective-permute-done | bytes 262176 | tf_op jit(solution)/shard_map/ppermute | solution.py:215
  100.1 5.4 %collective-permute-done.34.refs_5_ = bf16[64,2048]{1,0:T(8,128)(2,1)S(1)} collective-permute-done((bf16[64,2048]{1,0:T(8,128)(2,1)S(1)}, bf16[64,2048]{1,0:T(8,128)(2,1)S(1)}, u32[]{:S(2)}, u32[]{:S(2)}) %collective-permute-start.34) | collective-permute-done | bytes 262176 | tf_op jit(solution)/shard_map/ppermute | solution.py:215
  105.5 0.9 end.1
  (38 shorter events, 0.9 us)
Async XLA Ops:
  0.0 1.0 copy-start.3
  1.0 0.7 copy-start.4
  2.5 2.0 %collective-permute-start = (bf16[128,2048]{1,0:T(8,128)(2,1)S(1)}, bf16[128,2048]{1,0:T(8,128)(2,1)S(1)}, u32[]{:S(2)}, u32[]{:S(2)}) collective-permute-start(bf16[128,2048]{1,0:T(8,128)(2,1)S(1)} %rotate_local.1.refs_0_), channel_id=1, source_target_pairs={{0,2},{2,0},{4,6},{6,4},{8,10},{10,8},{12,14},{14,12},{1,3},{3,1},... | collective-permute-start | bytes 1572872 | tf_op jit(solution)/shard_map/ppermute | solution.py:206
  4.6 10.7 %collective-permute-start.2 = (bf16[64,2048]{1,0:T(8,128)(2,1)S(1)}, bf16[64,2048]{1,0:T(8,128)(2,1)S(1)}, u32[]{:S(2)}, u32[]{:S(2)}) collective-permute-start(bf16[64,2048]{1,0:T(8,128)(2,1)S(1)} %hadamard_core.2.refs_1_.refs_0_), channel_id=1, source_target_pairs={{0,4},{2,6},{4,8},{6,10},{8,12},{10,14},{12,0},{14,2},{1,5},{3,7},... | collective-permute-start | bytes 786440 | tf_op jit(solution)/shard_map/ppermute | solution.py:206
  6.5 8.7 %collective-permute-start.1 = (bf16[64,2048]{1,0:T(8,128)(2,1)S(1)}, bf16[64,2048]{1,0:T(8,128)(2,1)S(1)}, u32[]{:S(2)}, u32[]{:S(2)}) collective-permute-start(bf16[64,2048]{1,0:T(8,128)(2,1)S(1)} %hadamard_core.2.refs_1_.refs_0_), channel_id=1, source_target_pairs={{0,12},{2,14},{4,0},{6,2},{8,4},{10,6},{12,8},{14,10},{1,13},{3,15... | collective-permute-start | bytes 786440 | tf_op jit(solution)/shard_map/ppermute | solution.py:206
  8.7 3.4 %copy-start = (bf16[1,2048,2048]{2,1,0:T(8,128)(2,1)S(1)}, bf16[1,2048,2048]{2,1,0:T(8,128)(2,1)}, u32[]{:S(2)}) copy-start(bf16[1,2048,2048]{2,1,0:T(8,128)(2,1)} %refs_4_.9) | copy-start | bytes 25165828
  12.1 37.1 %copy-start.1 = (bf16[1,2048,2048]{2,1,0:T(8,128)(2,1)S(1)}, bf16[1,2048,2048]{2,1,0:T(8,128)(2,1)}, u32[]{:S(2)}) copy-start(bf16[1,2048,2048]{2,1,0:T(8,128)(2,1)} %refs_4_.9) | copy-start | bytes 25165828
  15.3 6.3 %collective-permute-start.3 = (bf16[32,2048]{1,0:T(8,128)(2,1)S(1)}, bf16[32,2048]{1,0:T(8,128)(2,1)S(1)}, u32[]{:S(2)}, u32[]{:S(2)}) collective-permute-start(bf16[32,2048]{1,0:T(8,128)(2,1)S(1)} %get-tuple-element.25), channel_id=1, source_target_pairs={{0,4},{2,6},{4,8},{6,10},{8,12},{10,14},{12,0},{14,2},{1,5},{3,7},... | collective-permute-start | bytes 393224 | tf_op jit(solution)/shard_map/ppermute | solution.py:206
  16.6 5.0 %collective-permute-start.4 = (bf16[32,2048]{1,0:T(8,128)(2,1)S(1)}, bf16[32,2048]{1,0:T(8,128)(2,1)S(1)}, u32[]{:S(2)}, u32[]{:S(2)}) collective-permute-start(bf16[32,2048]{1,0:T(8,128)(2,1)S(1)} %get-tuple-element.26), channel_id=1, source_target_pairs={{0,12},{2,14},{4,0},{6,2},{8,4},{10,6},{12,8},{14,10},{1,13},{3,15... | collective-permute-start | bytes 393224 | tf_op jit(solution)/shard_map/ppermute | solution.py:206
  21.8 8.3 %collective-permute-start.7 = (bf16[64,2048]{1,0:T(8,128)(2,1)S(1)}, bf16[64,2048]{1,0:T(8,128)(2,1)S(1)}, u32[]{:S(2)}, u32[]{:S(2)}) collective-permute-start(bf16[64,2048]{1,0:T(8,128)(2,1)S(1)} %hadamard_z.2.refs_0_), channel_id=1, source_target_pairs={{0,32},{16,48},{32,64},{48,80},{64,96},{80,112},{96,0},{112,16},{1... | collective-permute-start | bytes 786440 | tf_op jit(solution)/shard_map/ppermute | solution.py:206
  23.5 8.6 %collective-permute-start.6 = (bf16[64,2048]{1,0:T(8,128)(2,1)S(1)}, bf16[64,2048]{1,0:T(8,128)(2,1)S(1)}, u32[]{:S(2)}, u32[]{:S(2)}) collective-permute-start(bf16[64,2048]{1,0:T(8,128)(2,1)S(1)} %hadamard_z.2.refs_0_), channel_id=1, source_target_pairs={{0,96},{16,112},{32,0},{48,16},{64,32},{80,48},{96,64},{112,80},{1... | collective-permute-start | bytes 786440 | tf_op jit(solution)/shard_map/ppermute | solution.py:206
  25.1 6.9 %collective-permute-start.5 = (bf16[64,2048]{1,0:T(8,128)(2,1)S(1)}, bf16[64,2048]{1,0:T(8,128)(2,1)S(1)}, u32[]{:S(2)}, u32[]{:S(2)}) collective-permute-start(bf16[64,2048]{1,0:T(8,128)(2,1)S(1)} %hadamard_z.2.refs_0_), channel_id=1, source_target_pairs={{0,16},{16,0},{32,48},{48,32},{64,80},{80,64},{96,112},{112,96},{1... | collective-permute-start | bytes 786440 | tf_op jit(solution)/shard_map/ppermute | solution.py:206
  26.3 8.9 %collective-permute-start.13 = (bf16[64,2048]{1,0:T(8,128)(2,1)S(1)}, bf16[64,2048]{1,0:T(8,128)(2,1)S(1)}, u32[]{:S(2)}, u32[]{:S(2)}) collective-permute-start(bf16[64,2048]{1,0:T(8,128)(2,1)S(1)} %hadamard_core.3.refs_5_.refs_0_), channel_id=1, source_target_pairs={{0,4},{2,6},{4,8},{6,10},{8,12},{10,14},{12,0},{14,2},{1,5},{3,7},... | collective-permute-start | bytes 786440 | tf_op jit(solution)/shard_map/ppermute | solution.py:206
  27.9 7.3 %collective-permute-start.12 = (bf16[64,2048]{1,0:T(8,128)(2,1)S(1)}, bf16[64,2048]{1,0:T(8,128)(2,1)S(1)}, u32[]{:S(2)}, u32[]{:S(2)}) collective-permute-start(bf16[64,2048]{1,0:T(8,128)(2,1)S(1)} %hadamard_core.3.refs_5_.refs_0_), channel_id=1, source_target_pairs={{0,12},{2,14},{4,0},{6,2},{8,4},{10,6},{12,8},{14,10},{1,13},{3,15... | collective-permute-start | bytes 786440 | tf_op jit(solution)/shard_map/ppermute | solution.py:206
  30.1 10.4 %collective-permute-start.9 = (bf16[64,2048]{1,0:T(8,128)(2,1)S(1)}, bf16[64,2048]{1,0:T(8,128)(2,1)S(1)}, u32[]{:S(2)}, u32[]{:S(2)}) collective-permute-start(bf16[64,2048]{1,0:T(8,128)(2,1)S(1)} %hadamard_z.2.refs_0_), channel_id=1, source_target_pairs={{0,64},{16,80},{32,96},{48,112},{64,0},{80,16},{96,32},{112,48},{1... | collective-permute-start | bytes 786440 | tf_op jit(solution)/shard_map/ppermute | solution.py:206
  32.0 11.3 %collective-permute-start.11 = (bf16[64,2048]{1,0:T(8,128)(2,1)S(1)}, bf16[64,2048]{1,0:T(8,128)(2,1)S(1)}, u32[]{:S(2)}, u32[]{:S(2)}) collective-permute-start(bf16[64,2048]{1,0:T(8,128)(2,1)S(1)} %hold.3.refs_0_), channel_id=1, source_target_pairs={{0,32},{16,48},{32,64},{48,80},{64,96},{80,112},{96,0},{112,16},{1... | collective-permute-start | bytes 786440 | tf_op jit(solution)/shard_map/ppermute | solution.py:206
  32.7 10.6 %collective-permute-start.8 = (bf16[64,2048]{1,0:T(8,128)(2,1)S(1)}, bf16[64,2048]{1,0:T(8,128)(2,1)S(1)}, u32[]{:S(2)}, u32[]{:S(2)}) collective-permute-start(bf16[64,2048]{1,0:T(8,128)(2,1)S(1)} %hold.3.refs_0_), channel_id=1, source_target_pairs={{0,96},{16,112},{32,0},{48,16},{64,32},{80,48},{96,64},{112,80},{1... | collective-permute-start | bytes 786440 | tf_op jit(solution)/shard_map/ppermute | solution.py:206
  35.3 6.5 %collective-permute-start.14 = (bf16[32,2048]{1,0:T(8,128)(2,1)S(1)}, bf16[32,2048]{1,0:T(8,128)(2,1)S(1)}, u32[]{:S(2)}, u32[]{:S(2)}) collective-permute-start(bf16[32,2048]{1,0:T(8,128)(2,1)S(1)} %get-tuple-element.27), channel_id=1, source_target_pairs={{0,4},{2,6},{4,8},{6,10},{8,12},{10,14},{12,0},{14,2},{1,5},{3,7},... | collective-permute-start | bytes 393224 | tf_op jit(solution)/shard_map/ppermute | solution.py:206
  37.3 5.0 %collective-permute-start.15 = (bf16[32,2048]{1,0:T(8,128)(2,1)S(1)}, bf16[32,2048]{1,0:T(8,128)(2,1)S(1)}, u32[]{:S(2)}, u32[]{:S(2)}) collective-permute-start(bf16[32,2048]{1,0:T(8,128)(2,1)S(1)} %get-tuple-element.28), channel_id=1, source_target_pairs={{0,12},{2,14},{4,0},{6,2},{8,4},{10,6},{12,8},{14,10},{1,13},{3,15... | collective-permute-start | bytes 393224 | tf_op jit(solution)/shard_map/ppermute | solution.py:206
  40.5 11.0 %collective-permute-start.10 = (bf16[64,2048]{1,0:T(8,128)(2,1)S(1)}, bf16[64,2048]{1,0:T(8,128)(2,1)S(1)}, u32[]{:S(2)}, u32[]{:S(2)}) collective-permute-start(bf16[64,2048]{1,0:T(8,128)(2,1)S(1)} %collective-permute-done.9.refs_2_), channel_id=1, source_target_pairs={{0,16},{16,0},{32,48},{48,32},{64,80},{80,64},{96,112},{112,96},{1... | collective-permute-start | bytes 786440 | tf_op jit(solution)/shard_map/ppermute | solution.py:206
  43.5 14.0 %collective-permute-start.19 = (bf16[64,2048]{1,0:T(8,128)(2,1)S(1)}, bf16[64,2048]{1,0:T(8,128)(2,1)S(1)}, u32[]{:S(2)}, u32[]{:S(2)}) collective-permute-start(bf16[64,2048]{1,0:T(8,128)(2,1)S(1)} %hadamard_z.3.refs_5_.refs_0_), channel_id=1, source_target_pairs={{0,32},{16,48},{32,64},{48,80},{64,96},{80,112},{96,0},{112,16},{1... | collective-permute-start | bytes 786440 | tf_op jit(solution)/shard_map/ppermute | solution.py:206
  44.0 13.5 %collective-permute-start.18 = (bf16[64,2048]{1,0:T(8,128)(2,1)S(1)}, bf16[64,2048]{1,0:T(8,128)(2,1)S(1)}, u32[]{:S(2)}, u32[]{:S(2)}) collective-permute-start(bf16[64,2048]{1,0:T(8,128)(2,1)S(1)} %hadamard_z.3.refs_5_.refs_0_), channel_id=1, source_target_pairs={{0,64},{16,80},{32,96},{48,112},{64,0},{80,16},{96,32},{112,48},{1... | collective-permute-start | bytes 786440 | tf_op jit(solution)/shard_map/ppermute | solution.py:206
  46.7 11.4 %collective-permute-start.17 = (bf16[64,2048]{1,0:T(8,128)(2,1)S(1)}, bf16[64,2048]{1,0:T(8,128)(2,1)S(1)}, u32[]{:S(2)}, u32[]{:S(2)}) collective-permute-start(bf16[64,2048]{1,0:T(8,128)(2,1)S(1)} %hadamard_z.3.refs_5_.refs_0_), channel_id=1, source_target_pairs={{0,96},{16,112},{32,0},{48,16},{64,32},{80,48},{96,64},{112,80},{1... | collective-permute-start | bytes 786440 | tf_op jit(solution)/shard_map/ppermute | solution.py:206
  48.0 10.2 %collective-permute-start.16 = (bf16[64,2048]{1,0:T(8,128)(2,1)S(1)}, bf16[64,2048]{1,0:T(8,128)(2,1)S(1)}, u32[]{:S(2)}, u32[]{:S(2)}) collective-permute-start(bf16[64,2048]{1,0:T(8,128)(2,1)S(1)} %hadamard_z.3.refs_5_.refs_0_), channel_id=1, source_target_pairs={{0,16},{16,0},{32,48},{48,32},{64,80},{80,64},{96,112},{112,96},{1... | collective-permute-start | bytes 786440 | tf_op jit(solution)/shard_map/ppermute | solution.py:206
  58.2 4.5 %collective-permute-start.20 = (bf16[256,2048]{1,0:T(8,128)(2,1)S(1)}, bf16[256,2048]{1,0:T(8,128)(2,1)S(1)}, u32[]{:S(2)}, u32[]{:S(2)}) collective-permute-start(bf16[256,2048]{1,0:T(8,128)(2,1)S(1)} %hold.5), channel_id=1, source_target_pairs={{0,2},{2,0},{4,6},{6,4},{8,10},{10,8},{12,14},{14,12},{1,3},{3,1},... | collective-permute-start | bytes 3145736 | tf_op jit(solution)/shard_map/ppermute | solution.py:206
  58.2 12.2 %collective-permute-start.27 = (bf16[64,2048]{1,0:T(8,128)(2,1)S(1)}, bf16[64,2048]{1,0:T(8,128)(2,1)S(1)}, u32[]{:S(2)}, u32[]{:S(2)}) collective-permute-start(bf16[64,2048]{1,0:T(8,128)(2,1)S(1)} %hold.4.refs_1_.refs_0_), channel_id=1, source_target_pairs={{0,32},{16,48},{32,64},{48,80},{64,96},{80,112},{96,0},{112,16},{1... | collective-permute-start | bytes 786440 | tf_op jit(solution)/shard_map/ppermute | solution.py:206
  59.9 10.4 %collective-permute-start.25 = (bf16[64,2048]{1,0:T(8,128)(2,1)S(1)}, bf16[64,2048]{1,0:T(8,128)(2,1)S(1)}, u32[]{:S(2)}, u32[]{:S(2)}) collective-permute-start(bf16[64,2048]{1,0:T(8,128)(2,1)S(1)} %hold.4.refs_1_.refs_0_), channel_id=1, source_target_pairs={{0,96},{16,112},{32,0},{48,16},{64,32},{80,48},{96,64},{112,80},{1... | collective-permute-start | bytes 786440 | tf_op jit(solution)/shard_map/ppermute | solution.py:206
  61.5 8.9 %collective-permute-start.26 = (bf16[64,2048]{1,0:T(8,128)(2,1)S(1)}, bf16[64,2048]{1,0:T(8,128)(2,1)S(1)}, u32[]{:S(2)}, u32[]{:S(2)}) collective-permute-start(bf16[64,2048]{1,0:T(8,128)(2,1)S(1)} %collective-permute-done.18.refs_2_), channel_id=1, source_target_pairs={{0,16},{16,0},{32,48},{48,32},{64,80},{80,64},{96,112},{112,96},{1... | collective-permute-start | bytes 786440 | tf_op jit(solution)/shard_map/ppermute | solution.py:206
  62.7 5.1 %collective-permute-start.22 = (bf16[32,2048]{1,0:T(8,128)(2,1)S(1)}, bf16[32,2048]{1,0:T(8,128)(2,1)S(1)}, u32[]{:S(2)}, u32[]{:S(2)}) collective-permute-start(bf16[32,2048]{1,0:T(8,128)(2,1)S(1)} %get-tuple-element.32), channel_id=1, source_target_pairs={{0,12},{2,14},{4,0},{6,2},{8,4},{10,6},{12,8},{14,10},{1,13},{3,15... | collective-permute-start | bytes 393224 | tf_op jit(solution)/shard_map/ppermute | solution.py:206
  64.0 6.2 %collective-permute-start.21 = (bf16[32,2048]{1,0:T(8,128)(2,1)S(1)}, bf16[32,2048]{1,0:T(8,128)(2,1)S(1)}, u32[]{:S(2)}, u32[]{:S(2)}) collective-permute-start(bf16[32,2048]{1,0:T(8,128)(2,1)S(1)} %get-tuple-element.31.refs_5_), channel_id=1, source_target_pairs={{0,4},{2,6},{4,8},{6,10},{8,12},{10,14},{12,0},{14,2},{1,5},{3,7},... | collective-permute-start | bytes 393224 | tf_op jit(solution)/shard_map/ppermute | solution.py:206
  70.4 19.5 %copy-start.2 = (bf16[128,2048]{1,0:T(8,128)(2,1)S(1)}, bf16[128,2048]{1,0:T(8,128)(2,1)}, u32[]{:S(2)}) copy-start(bf16[128,2048]{1,0:T(8,128)(2,1)} %refs_4_.11) | copy-start | bytes 1572868
  73.4 2.7 %collective-permute-start.28 = (bf16[256,2048]{1,0:T(8,128)(2,1)S(1)}, bf16[256,2048]{1,0:T(8,128)(2,1)S(1)}, u32[]{:S(2)}, u32[]{:S(2)}) collective-permute-start(bf16[256,2048]{1,0:T(8,128)(2,1)S(1)} %get-tuple-element.36), channel_id=1, source_target_pairs={{0,2},{2,0},{4,6},{6,4},{8,10},{10,8},{12,14},{14,12},{1,3},{3,1},... | collective-permute-start | bytes 3145736 | tf_op jit(solution)/shard_map/ppermute | solution.py:206
  76.2 6.4 %collective-permute-start.31 = (bf16[32,2048]{1,0:T(8,128)(2,1)S(1)}, bf16[32,2048]{1,0:T(8,128)(2,1)S(1)}, u32[]{:S(2)}, u32[]{:S(2)}) collective-permute-start(bf16[32,2048]{1,0:T(8,128)(2,1)S(1)} %get-tuple-element.40), channel_id=1, source_target_pairs={{0,12},{2,14},{4,0},{6,2},{8,4},{10,6},{12,8},{14,10},{1,13},{3,15... | collective-permute-start | bytes 393224 | tf_op jit(solution)/shard_map/ppermute | solution.py:206
  76.7 7.6 %collective-permute-start.30 = (bf16[32,2048]{1,0:T(8,128)(2,1)S(1)}, bf16[32,2048]{1,0:T(8,128)(2,1)S(1)}, u32[]{:S(2)}, u32[]{:S(2)}) collective-permute-start(bf16[32,2048]{1,0:T(8,128)(2,1)S(1)} %get-tuple-element.37.refs_5_), channel_id=1, source_target_pairs={{0,4},{2,6},{4,8},{6,10},{8,12},{10,14},{12,0},{14,2},{1,5},{3,7},... | collective-permute-start | bytes 393224 | tf_op jit(solution)/shard_map/ppermute | solution.py:206
  78.3 11.6 %collective-permute-start.23 = (bf16[64,2048]{1,0:T(8,128)(2,1)S(1)}, bf16[64,2048]{1,0:T(8,128)(2,1)S(1)}, u32[]{:S(2)}, u32[]{:S(2)}) collective-permute-start(bf16[64,2048]{1,0:T(8,128)(2,1)S(1)} %get-tuple-element.33.refs_6_), channel_id=1, source_target_pairs={{0,4},{2,6},{4,8},{6,10},{8,12},{10,14},{12,0},{14,2},{1,5},{3,7},... | collective-permute-start | bytes 786440 | tf_op jit(solution)/shard_map/ppermute | solution.py:206
  78.4 9.9 %collective-permute-start.24 = (bf16[64,2048]{1,0:T(8,128)(2,1)S(1)}, bf16[64,2048]{1,0:T(8,128)(2,1)S(1)}, u32[]{:S(2)}, u32[]{:S(2)}) collective-permute-start(bf16[64,2048]{1,0:T(8,128)(2,1)S(1)} %get-tuple-element.34), channel_id=1, source_target_pairs={{0,12},{2,14},{4,0},{6,2},{8,4},{10,6},{12,8},{14,10},{1,13},{3,15... | collective-permute-start | bytes 786440 | tf_op jit(solution)/shard_map/ppermute | solution.py:206
  84.4 10.0 %collective-permute-start.32 = (bf16[64,2048]{1,0:T(8,128)(2,1)S(1)}, bf16[64,2048]{1,0:T(8,128)(2,1)S(1)}, u32[]{:S(2)}, u32[]{:S(2)}) collective-permute-start(bf16[64,2048]{1,0:T(8,128)(2,1)S(1)} %get-tuple-element.41), channel_id=1, source_target_pairs={{0,4},{2,6},{4,8},{6,10},{8,12},{10,14},{12,0},{14,2},{1,5},{3,7},... | collective-permute-start | bytes 786440 | tf_op jit(solution)/shard_map/ppermute | solution.py:206
  84.9 9.5 %collective-permute-start.33 = (bf16[64,2048]{1,0:T(8,128)(2,1)S(1)}, bf16[64,2048]{1,0:T(8,128)(2,1)S(1)}, u32[]{:S(2)}, u32[]{:S(2)}) collective-permute-start(bf16[64,2048]{1,0:T(8,128)(2,1)S(1)} %get-tuple-element.42), channel_id=1, source_target_pairs={{0,12},{2,14},{4,0},{6,2},{8,4},{10,6},{12,8},{14,10},{1,13},{3,15... | collective-permute-start | bytes 786440 | tf_op jit(solution)/shard_map/ppermute | solution.py:206
  90.1 10.0 %collective-permute-start.29 = (bf16[64,2048]{1,0:T(8,128)(2,1)S(1)}, bf16[64,2048]{1,0:T(8,128)(2,1)S(1)}, u32[]{:S(2)}, u32[]{:S(2)}) collective-permute-start(bf16[64,2048]{1,0:T(8,128)(2,1)S(1)} %get-tuple-element.38.refs_5_.refs_0_), channel_id=1, source_target_pairs={{0,1},{2,3},{4,5},{6,7},{8,9},{10,11},{12,13},{14,15},{16,17},{18,... | collective-permute-start | bytes 786440 | tf_op jit(solution)/shard_map/ppermute | solution.py:215
  94.6 10.9 %collective-permute-start.34 = (bf16[64,2048]{1,0:T(8,128)(2,1)S(1)}, bf16[64,2048]{1,0:T(8,128)(2,1)S(1)}, u32[]{:S(2)}, u32[]{:S(2)}) collective-permute-start(bf16[64,2048]{1,0:T(8,128)(2,1)S(1)} %get-tuple-element.43.refs_3_), channel_id=1, source_target_pairs={{0,1},{2,3},{4,5},{6,7},{8,9},{10,11},{12,13},{14,15},{16,17},{18,... | collective-permute-start | bytes 786440 | tf_op jit(solution)/shard_map/ppermute | solution.py:215

commit v7 on v6

--- a/solution.py
+++ b/solution.py
@@ -10,6 +10,9 @@
 LANES = 128
 BF16 = jnp.bfloat16
 TILES = 4
+ROWS = (64, 64)
+FAR = 2
+STRIP = 32
 
 
 def f32(value):
@@ -47,19 +50,21 @@
     )(*operands, *behind)
 
 
-def rotate_kernel(scale, x_ref, s_ref, o_ref):
-    rows, width = o_ref.shape
+def rotate_kernel(scale, x_ref, s_ref, *out_refs):
+    rows, width = x_ref.shape[1:]
+    out_of = [(ref, r) for ref in out_refs for r in range(0, ref.shape[0], STRIP)]
     pieces = width // LANES
     signs = f32(s_ref[...])
     i = lax.broadcasted_iota(jnp.int32, (LANES, LANES), 0) & lax.broadcasted_iota(jnp.int32, (LANES, LANES), 1)
     for bits in (4, 2, 1):
         i = i ^ (i >> bits)
     table = f32(1 - 2 * (i & 1)).astype(BF16)
-    for r in range(0, rows, 32):
+    for r in range(0, rows, STRIP):
+        o_ref, low = out_of[r // STRIP]
         part = []
         for a in range(pieces):
             cols = slice(a * LANES, (a + 1) * LANES)
-            x = (f32(x_ref[0, r : r + 32, cols]) * signs[:, cols]).astype(BF16)
+            x = (f32(x_ref[0, r : r + STRIP, cols]) * signs[:, cols]).astype(BF16)
             part.append(jnp.dot(x, table, preferred_element_type=jnp.float32))
         step = 1
         while step < pieces:
@@ -71,31 +76,31 @@
             part = nxt
             step *= 2
         for a in range(pieces):
-            o_ref[r : r + 32, a * LANES : (a + 1) * LANES] = (part[a] * scale).astype(BF16)
-
-
-def pair_kernel(at, mine_ref, other_ref, out_ref):
+            o_ref[low : low + STRIP, a * LANES : (a + 1) * LANES] = (part[a] * scale).astype(BF16)
+
+
+def pair_kernel(mine_ref, other_ref, out_ref):
     sign = f32(1 - 2 * place()[3])
-    out_ref[...] = (f32(other_ref[at]) + sign * f32(mine_ref[at])).astype(BF16)
+    out_ref[...] = (f32(other_ref[...]) + sign * f32(mine_ref[...])).astype(BF16)
 
 
 def cut_kernel(next_ref, last_ref, low_ref, high_ref):
-    half = low_ref.shape[0]
-    low_ref[...] = last_ref[:half]
-    high_ref[...] = next_ref[half:]
+    half = low_ref.shape[1]
+    low_ref[...] = last_ref[:, :half]
+    high_ref[...] = next_ref[:, half:]
 
 
 def mix_kernel(mine_ref, next_ref, last_ref, low_ref, high_ref, out_ref):
     z = place()[2]
-    half = low_ref.shape[0]
+    half = low_ref.shape[1]
 
     def sign(k):
         u = z & ((z + k) & 3)
         return f32(1 - 2 * ((u ^ (u >> 1)) & 1))
 
     for at, far_ref in ((slice(0, half), low_ref), (slice(half, 2 * half), high_ref)):
-        total = sign(0) * f32(mine_ref[at]) + sign(1) * f32(next_ref[at]) + sign(3) * f32(last_ref[at])
-        out_ref[at] = (total + sign(2) * f32(far_ref[...])).astype(BF16)
+        total = sign(0) * f32(mine_ref[:, at]) + sign(1) * f32(next_ref[:, at]) + sign(3) * f32(last_ref[:, at])
+        out_ref[:, at] = (total + sign(2) * f32(far_ref[...])).astype(BF16)
 
 
 def touch_kernel(w_ref, out_ref):
@@ -124,19 +129,25 @@
 
 
 def mate_kernel(*refs):
-    blocks, (w_ref, column_ref, keep_ref, send_ref, lhs) = refs[:4], refs[4:]
+    blocks, (w_ref, column_ref, keep_ref, far_ref, near_ref, lhs) = refs[:4], refs[4:]
     _, x, _, c = place()
+    rows = far_ref.shape[0]
+
+    def send(cols, value):
+        far_ref[:, cols] = value[FAR * rows : (FAR + 1) * rows]
+        near_ref[: FAR * rows, cols] = value[: FAR * rows]
+        near_ref[FAR * rows :, cols] = value[(FAR + 1) * rows :]
 
     def store(cols, out):
         @pl.when(x == c)
         def _():
             keep_ref[:, cols] = column_ref[:, cols]
-            send_ref[:, cols] = out
+            send(cols, out)
 
         @pl.when(x != c)
         def _():
             keep_ref[:, cols] = out
-            send_ref[:, cols] = column_ref[:, cols]
+            send(cols, column_ref[:, cols])
 
     products(blocks, w_ref, lhs, store)
 
@@ -149,7 +160,7 @@
         "project_column" if column is None else "project_mate",
         column_kernel if column is None else mate_kernel,
         (*blocks, weight) + (() if column is None else (column,)),
-        half if column is None else (half, half),
+        half if column is None else (half, shape(rows, width), shape(3 * rows, width)),
         behind,
         scratch=[pltpu.VMEM((4 * rows, depth), BF16)],
         flops=2 * 4 * rows * depth * width,
@@ -158,24 +169,26 @@
     )
 
 
-def core_sum(keep_ref, came_ref, k, low=0, high=None):
+def core_sum(keep_ref, came_ref, k, cols=slice(None)):
     rows = keep_ref.shape[0] // 4
-    at = slice(k * rows + low, k * rows + (high or rows))
-    return f32(keep_ref[at]) + f32(came_ref[at])
+    place = k - (k > FAR)
+    came = came_ref[...] if k == FAR else came_ref[place * rows : (place + 1) * rows]
+    return (f32(keep_ref[k * rows : (k + 1) * rows]) + f32(came))[:, cols]
 
 
 def far_kernel(keep_ref, came_ref, low_ref, high_ref):
-    half = low_ref.shape[0]
-    low_ref[...] = core_sum(keep_ref, came_ref, 2, 0, half).astype(BF16)
-    high_ref[...] = core_sum(keep_ref, came_ref, 2, half).astype(BF16)
+    half = low_ref.shape[1]
+    low_ref[...] = core_sum(keep_ref, came_ref, FAR, slice(0, half)).astype(BF16)
+    high_ref[...] = core_sum(keep_ref, came_ref, FAR, slice(half, None)).astype(BF16)
 
 
 def near_kernel(keep_ref, came_ref, low_ref, high_ref, next_ref, last_ref):
-    half = low_ref.shape[0]
-    next_ref[:half] = (core_sum(keep_ref, came_ref, 1, 0, half) + f32(low_ref[...])).astype(BF16)
-    next_ref[half:] = core_sum(keep_ref, came_ref, 1, half).astype(BF16)
-    last_ref[:half] = core_sum(keep_ref, came_ref, 3, 0, half).astype(BF16)
-    last_ref[half:] = (core_sum(keep_ref, came_ref, 3, half) + f32(high_ref[...])).astype(BF16)
+    half = low_ref.shape[1]
+    low, high = slice(0, half), slice(half, None)
+    next_ref[:, low] = (core_sum(keep_ref, came_ref, 1, low) + f32(low_ref[...])).astype(BF16)
+    next_ref[:, high] = core_sum(keep_ref, came_ref, 1, high).astype(BF16)
+    last_ref[:, low] = core_sum(keep_ref, came_ref, 3, low).astype(BF16)
+    last_ref[:, high] = (core_sum(keep_ref, came_ref, 3, high) + f32(high_ref[...])).astype(BF16)
 
 
 def finish_kernel(at, keep_ref, came_ref, a_ref, b_ref, residual_ref, leading_ref, summed_ref):
@@ -199,8 +212,7 @@
     tokens, width = attention_out.shape[1:]
     columns = out_weight.shape[2]
     scale = 1.0 / math.sqrt(width * lax.axis_size("tensor"))
-    rows = tokens // 2
-    cut = [slice(0, rows), slice(rows, tokens)]
+    cut = [slice(0, ROWS[0]), slice(ROWS[0], tokens)]
 
     def move(value, axis, target):
         return lax.ppermute(value, axis, [(i, target(i)) for i in range(lax.axis_size(axis))])
@@ -214,12 +226,8 @@
     def pipe(value):
         return lax.ppermute(value, "pipe", [(0, 1)])
 
-    def pair(chunk, mine, other, behind=()):
-        return call(
-            "hadamard_core", lambda *refs: pair_kernel(cut[chunk], *refs), (mine, other), shape(rows, width), behind
-        )
-
-    half = rows // 2
+    def pair(mine, other, behind=()):
+        return call("hadamard_core", pair_kernel, (mine, other), shape(*mine.shape), behind)
 
     def up(value):
         return move(value, "tensor", ring(1))
@@ -231,11 +239,11 @@
         return [mine, down(mine), up(mine)]
 
     def far_z(terms, behind=()):
-        low, high = call("cut", cut_kernel, terms[1:], (shape(half, width),) * 2, behind)
+        low, high = call("cut", cut_kernel, terms[1:], (shape(terms[0].shape[0], width // 2),) * 2, behind)
         return terms + [up(low), down(high)]
 
     def mix(terms, behind=()):
-        return call("hadamard_z", mix_kernel, terms, shape(rows, width), behind, weigh=20)
+        return call("hadamard_z", mix_kernel, terms, shape(*terms[0].shape), behind, weigh=20)
 
     def spread_column(own):
         mate = move(own, "dp", ring(0, 1))
@@ -256,11 +264,11 @@
         return [mate, move(mate, "dp", ring(-1)), move(column[2], "dp", ring(0, 1)), move(mate, "dp", ring(-3))]
 
     def far_sum(keep, came, behind=()):
-        low, high = call("far_sum", far_kernel, (keep, came), (shape(half, columns),) * 2, behind)
+        low, high = call("far_sum", far_kernel, (keep, came), (shape(came.shape[0], columns // 2),) * 2, behind)
         return low, (up(low), down(high))
 
     def near_sum(keep, came, far, behind=()):
-        return call("near_sum", near_kernel, (keep, came, *far), (shape(rows, columns),) * 2, behind)
+        return call("near_sum", near_kernel, (keep, came, *far), (shape(far[0].shape[0], columns),) * 2, behind)
 
     def last_sum(near):
         return up(near[0]), down(near[1])
@@ -270,7 +278,7 @@
             "residual",
             lambda *refs: finish_kernel(cut[chunk], *refs),
             (keep, came, *arrived, residual_in),
-            (shape(rows, columns), shape(rows, columns, jnp.float32)),
+            (shape(ROWS[chunk], columns), shape(ROWS[chunk], columns, jnp.float32)),
             behind,
             weigh=20,
         )
@@ -279,14 +287,14 @@
         "rotate_local",
         lambda *refs: rotate_kernel(scale, *refs),
         (attention_out, signs),
-        shape(tokens, width),
+        tuple(shape(rows, width) for rows in ROWS),
         flops=2 * tokens * width * LANES,
     )
-    other = swap(local)
-    terms0 = near_z(pair(0, local, other))
+    other = [swap(local[0]), swap(local[1])]
+    terms0 = near_z(pair(local[0], other[0]))
     ready = call("weight", touch_kernel, (out_weight,), shape(8, LANES), [terms0[0]], weigh=9)
     terms0 = far_z(terms0, [ready])
-    terms1 = near_z(pair(1, local, other, [terms0[1]]))
+    terms1 = near_z(pair(local[1], other[1], [terms0[1]]))
     own0 = mix(terms0, [terms1[0]])
     column0, mate0 = spread_column(own0)
     mate0 = hold(mate0, [column0[1], column0[3]])
@@ -294,20 +302,23 @@
     own1 = mix(far_z(terms1), [mates0[1], mates0[3]])
     column1, mate1 = spread_column(own1)
     products0 = project(column0, out_weight, None, [own1])
-    keep0, send0 = project(mates0, out_weight, products0)
+    keep0, far0, near0 = project(mates0, out_weight, products0)
     mate1 = hold(mate1, [*column1[1:], keep0])
-    came0 = swap(hold(send0, [mate1]))
-    mates1 = spread_mate(column1, mate1)
-    made0, far0 = far_sum(keep0, came0)
-    products1 = project(column1, out_weight, None, [made0])
-    near0 = near_sum(keep0, came0, far0)
-    keep1, send1 = project(mates1, out_weight, products1, [near0[0]])
-    came1 = swap(send1)
-    made1, far1 = far_sum(keep1, came1)
-    leading0, summed0 = finish(0, keep0, came0, last_sum(near0), [made1])
+    far0 = swap(hold(far0, [mate1]))
+    made0, ring0 = far_sum(keep0, far0)
+    near0 = swap(hold(near0, [far0]))
+    mates1 = spread_mate(column1, hold(mate1, [made0, near0]))
+    sums0 = near_sum(keep0, near0, ring0)
+    products1 = project(column1, out_weight, None, [sums0[0]])
+    keep1, far1, near1 = project(mates1, out_weight, products1)
+    last0 = last_sum(sums0)
+    far1 = swap(hold(far1, last0))
+    near1 = swap(hold(near1, [far1]))
+    made1, ring1 = far_sum(keep1, far1)
+    leading0, summed0 = finish(0, keep0, near0, last0, [made1])
     passed0 = pipe(leading0)
-    near1 = near_sum(keep1, came1, far1)
-    leading1, summed1 = finish(1, keep1, came1, last_sum(near1), [leading0])
+    sums1 = near_sum(keep1, near1, ring1)
+    leading1, summed1 = finish(1, keep1, near1, last_sum(sums1), [leading0])
     passed1 = pipe(leading1)
     return call(
         "end",

time: 107 us -> 107 us (level)
  waiting for transfers between devices: 38.1 us -> 39.2 us
    ppermute x33 -> x36, waiting for transfers between devices: 28.5 us -> 30 us  [move(): lax.ppermute(value, axis, [(i, target(i)) for i in range(lax.axis_size(ax...]
    ppermute x33 -> x36, starting transfers between devices: 46.3 us -> 45.3 us  [move(): lax.ppermute(value, axis, [(i, target(i)) for i in range(lax.axis_size(ax...]
  transfers between devices with their start and end apart: 35 -> 38, of which waited for: 20 -> 19; matrix products, arithmetic and copies ran while one was open for 0% -> 0% of each run, Pallas kernels for 8% -> 11%
where the time goes in v7:
time: 107 us; the launch traced here: 106 us
  starting transfers between devices  47.9 us (45%)
  waiting for transfers between devices  39.2 us (37%)
  Pallas kernels  14 us (13%)
  local copies, waits for them, and re-layouts  5.13 us (5%)
    ppermute x36, starting transfers between devices, move(): lax.ppermute(value, axis, [(i, target(i)) for i in range(lax.axis_size(ax...  45.3 us
    ppermute x36, waiting for transfers between devices, move(): lax.ppermute(value, axis, [(i, target(i)) for i in range(lax.axis_size(ax...  30 us
    pallas_call x19, Pallas kernels, call(): pl.pallas_call(lambda *refs: kernel(*refs[:count], *refs[count + len(behi...  14 us
    ppermute x2, waiting for transfers between devices, pipe(): return lax.ppermute(value, 'pipe', [(0, 1)])  9.18 us
    unnamed x10, local copies, waits for them, and re-layouts  5.13 us
    ppermute x2, starting transfers between devices, pipe(): return lax.ppermute(value, 'pipe', [(0, 1)])  2.58 us
  transfers between devices with their start and end apart: 38, of which 19 were waited for; matrix products, arithmetic and copies ran while one was open for 0% of the time, Pallas kernels for 11%

profile of v7, /device:TPU:4, one launch (start us, length us, event | category | flops | bytes accessed | tf_op | source)
XLA Modules:
  0.0 106.5 jit_solution(1812651493706134114)
XLA Ops:
  0.0 1.0 copy-done.3
  1.0 0.7 copy-done.4
  1.7 0.7 rotate_local.1
  2.6 1.5 %collective-permute-done.refs_1_ = bf16[64,2048]{1,0:T(8,128)(2,1)S(1)} collective-permute-done((bf16[64,2048]{1,0:T(8,128)(2,1)S(1)}, bf16[64,2048]{1,0:T(8,128)(2,1)S(1)}, u32[]{:S(2)}, u32[]{:S(2)}) %collective-permute-start) | collective-permute-done | bytes 262176 | tf_op jit(solution)/shard_map/ppermute | solution.py:218
  4.2 2.0 %collective-permute-start.2 = (bf16[64,2048]{1,0:T(8,128)(2,1)S(1)}, bf16[64,2048]{1,0:T(8,128)(2,1)S(1)}, u32[]{:S(2)}, u32[]{:S(2)}) collective-permute-start(bf16[64,2048]{1,0:T(8,128)(2,1)S(1)} %hadamard_core.2.refs_1_.refs_0_), channel_id=1, source_target_pairs={{0,4},{2,6},{4,8},{6,10},{8,12},{10,14},{12,0},{14,2},{1,5},{3,7},... | collective-permute-start | bytes 786440 | tf_op jit(solution)/shard_map/ppermute | solution.py:218
  6.2 2.2 %collective-permute-start.1 = (bf16[64,2048]{1,0:T(8,128)(2,1)S(1)}, bf16[64,2048]{1,0:T(8,128)(2,1)S(1)}, u32[]{:S(2)}, u32[]{:S(2)}) collective-permute-start(bf16[64,2048]{1,0:T(8,128)(2,1)S(1)} %hadamard_core.2.refs_1_.refs_0_), channel_id=1, source_target_pairs={{0,12},{2,14},{4,0},{6,2},{8,4},{10,6},{12,8},{14,10},{1,13},{3,15... | collective-permute-start | bytes 786440 | tf_op jit(solution)/shard_map/ppermute | solution.py:218
  8.4 3.4 %copy-done = bf16[1,2048,2048]{2,1,0:T(8,128)(2,1)S(1)} copy-done((bf16[1,2048,2048]{2,1,0:T(8,128)(2,1)S(1)}, bf16[1,2048,2048]{2,1,0:T(8,128)(2,1)}, u32[]{:S(2)}) %copy-start) | copy-done | bytes 8388632
  11.8 3.1 %collective-permute-done.2.refs_1_.refs_2_ = bf16[64,2048]{1,0:T(8,128)(2,1)S(1)} collective-permute-done((bf16[64,2048]{1,0:T(8,128)(2,1)S(1)}, bf16[64,2048]{1,0:T(8,128)(2,1)S(1)}, u32[]{:S(2)}, u32[]{:S(2)}) %collective-permute-start.2) | collective-permute-done | bytes 262176 | tf_op jit(solution)/shard_map/ppermute | solution.py:218
  14.9 1.3 %collective-permute-start.3 = (bf16[64,1024]{1,0:T(8,128)(2,1)S(1)}, bf16[64,1024]{1,0:T(8,128)(2,1)S(1)}, u32[]{:S(2)}, u32[]{:S(2)}) collective-permute-start(bf16[64,1024]{1,0:T(8,128)(2,1)S(1)} %get-tuple-element.30), channel_id=1, source_target_pairs={{0,4},{2,6},{4,8},{6,10},{8,12},{10,14},{12,0},{14,2},{1,5},{3,7},... | collective-permute-start | bytes 393224 | tf_op jit(solution)/shard_map/ppermute | solution.py:218
  16.2 2.0 %collective-permute-start.4 = (bf16[64,1024]{1,0:T(8,128)(2,1)S(1)}, bf16[64,1024]{1,0:T(8,128)(2,1)S(1)}, u32[]{:S(2)}, u32[]{:S(2)}) collective-permute-start(bf16[64,1024]{1,0:T(8,128)(2,1)S(1)} %get-tuple-element.31), channel_id=1, source_target_pairs={{0,12},{2,14},{4,0},{6,2},{8,4},{10,6},{12,8},{14,10},{1,13},{3,15... | collective-permute-start | bytes 393224 | tf_op jit(solution)/shard_map/ppermute | solution.py:218
  18.3 2.9 %collective-permute-done.3.refs_3_ = bf16[64,1024]{1,0:T(8,128)(2,1)S(1)} collective-permute-done((bf16[64,1024]{1,0:T(8,128)(2,1)S(1)}, bf16[64,1024]{1,0:T(8,128)(2,1)S(1)}, u32[]{:S(2)}, u32[]{:S(2)}) %collective-permute-start.3) | collective-permute-done | bytes 131104 | tf_op jit(solution)/shard_map/ppermute | solution.py:218
  21.2 0.2 hadamard_z.2.refs_0_
  21.4 1.6 %collective-permute-start.8 = (bf16[64,2048]{1,0:T(8,128)(2,1)S(1)}, bf16[64,2048]{1,0:T(8,128)(2,1)S(1)}, u32[]{:S(2)}, u32[]{:S(2)}) collective-permute-start(bf16[64,2048]{1,0:T(8,128)(2,1)S(1)} %hadamard_z.2.refs_0_), channel_id=1, source_target_pairs={{0,32},{16,48},{32,64},{48,80},{64,96},{80,112},{96,0},{112,16},{1... | collective-permute-start | bytes 786440 | tf_op jit(solution)/shard_map/ppermute | solution.py:218
  23.1 1.7 %collective-permute-start.7 = (bf16[64,2048]{1,0:T(8,128)(2,1)S(1)}, bf16[64,2048]{1,0:T(8,128)(2,1)S(1)}, u32[]{:S(2)}, u32[]{:S(2)}) collective-permute-start(bf16[64,2048]{1,0:T(8,128)(2,1)S(1)} %hadamard_z.2.refs_0_), channel_id=1, source_target_pairs={{0,96},{16,112},{32,0},{48,16},{64,32},{80,48},{96,64},{112,80},{1... | collective-permute-start | bytes 786440 | tf_op jit(solution)/shard_map/ppermute | solution.py:218
  24.8 1.2 %collective-permute-start.6 = (bf16[64,2048]{1,0:T(8,128)(2,1)S(1)}, bf16[64,2048]{1,0:T(8,128)(2,1)S(1)}, u32[]{:S(2)}, u32[]{:S(2)}) collective-permute-start(bf16[64,2048]{1,0:T(8,128)(2,1)S(1)} %hadamard_z.2.refs_0_), channel_id=1, source_target_pairs={{0,16},{16,0},{32,48},{48,32},{64,80},{80,64},{96,112},{112,96},{1... | collective-permute-start | bytes 786440 | tf_op jit(solution)/shard_map/ppermute | solution.py:218
  26.0 1.6 %collective-permute-start.14 = (bf16[64,2048]{1,0:T(8,128)(2,1)S(1)}, bf16[64,2048]{1,0:T(8,128)(2,1)S(1)}, u32[]{:S(2)}, u32[]{:S(2)}) collective-permute-start(bf16[64,2048]{1,0:T(8,128)(2,1)S(1)} %hadamard_core.3.refs_5_.refs_0_), channel_id=1, source_target_pairs={{0,4},{2,6},{4,8},{6,10},{8,12},{10,14},{12,0},{14,2},{1,5},{3,7},... | collective-permute-start | bytes 786440 | tf_op jit(solution)/shard_map/ppermute | solution.py:218
  27.6 1.6 %collective-permute-start.13 = (bf16[64,2048]{1,0:T(8,128)(2,1)S(1)}, bf16[64,2048]{1,0:T(8,128)(2,1)S(1)}, u32[]{:S(2)}, u32[]{:S(2)}) collective-permute-start(bf16[64,2048]{1,0:T(8,128)(2,1)S(1)} %hadamard_core.3.refs_5_.refs_0_), channel_id=1, source_target_pairs={{0,12},{2,14},{4,0},{6,2},{8,4},{10,6},{12,8},{14,10},{1,13},{3,15... | collective-permute-start | bytes 786440 | tf_op jit(solution)/shard_map/ppermute | solution.py:218
  29.2 0.5 collective-permute-done.8.refs_2_.refs_3_
  29.7 1.9 %collective-permute-start.10 = (bf16[64,2048]{1,0:T(8,128)(2,1)S(1)}, bf16[64,2048]{1,0:T(8,128)(2,1)S(1)}, u32[]{:S(2)}, u32[]{:S(2)}) collective-permute-start(bf16[64,2048]{1,0:T(8,128)(2,1)S(1)} %hadamard_z.2.refs_0_), channel_id=1, source_target_pairs={{0,64},{16,80},{32,96},{48,112},{64,0},{80,16},{96,32},{112,48},{1... | collective-permute-start | bytes 786440 | tf_op jit(solution)/shard_map/ppermute | solution.py:218
  31.7 0.7 collective-permute-start.12
  32.3 2.6 %collective-permute-start.9 = (bf16[64,2048]{1,0:T(8,128)(2,1)S(1)}, bf16[64,2048]{1,0:T(8,128)(2,1)S(1)}, u32[]{:S(2)}, u32[]{:S(2)}) collective-permute-start(bf16[64,2048]{1,0:T(8,128)(2,1)S(1)} %hold.7.refs_0_), channel_id=1, source_target_pairs={{0,96},{16,112},{32,0},{48,16},{64,32},{80,48},{96,64},{112,80},{1... | collective-permute-start | bytes 786440 | tf_op jit(solution)/shard_map/ppermute | solution.py:218
  34.9 2.0 %collective-permute-start.15 = (bf16[64,1024]{1,0:T(8,128)(2,1)S(1)}, bf16[64,1024]{1,0:T(8,128)(2,1)S(1)}, u32[]{:S(2)}, u32[]{:S(2)}) collective-permute-start(bf16[64,1024]{1,0:T(8,128)(2,1)S(1)} %get-tuple-element.33), channel_id=1, source_target_pairs={{0,4},{2,6},{4,8},{6,10},{8,12},{10,14},{12,0},{14,2},{1,5},{3,7},... | collective-permute-start | bytes 393224 | tf_op jit(solution)/shard_map/ppermute | solution.py:218
  36.9 1.7 %collective-permute-start.16 = (bf16[64,1024]{1,0:T(8,128)(2,1)S(1)}, bf16[64,1024]{1,0:T(8,128)(2,1)S(1)}, u32[]{:S(2)}, u32[]{:S(2)}) collective-permute-start(bf16[64,1024]{1,0:T(8,128)(2,1)S(1)} %get-tuple-element.34), channel_id=1, source_target_pairs={{0,12},{2,14},{4,0},{6,2},{8,4},{10,6},{12,8},{14,10},{1,13},{3,15... | collective-permute-start | bytes 393224 | tf_op jit(solution)/shard_map/ppermute | solution.py:218
  38.6 1.6 %collective-permute-done.10.refs_2_ = bf16[64,2048]{1,0:T(8,128)(2,1)S(1)} collective-permute-done((bf16[64,2048]{1,0:T(8,128)(2,1)S(1)}, bf16[64,2048]{1,0:T(8,128)(2,1)S(1)}, u32[]{:S(2)}, u32[]{:S(2)}) %collective-permute-start.10) | collective-permute-done | bytes 262176 | tf_op jit(solution)/shard_map/ppermute | solution.py:218
  40.2 1.2 %collective-permute-start.11 = (bf16[64,2048]{1,0:T(8,128)(2,1)S(1)}, bf16[64,2048]{1,0:T(8,128)(2,1)S(1)}, u32[]{:S(2)}, u32[]{:S(2)}) collective-permute-start(bf16[64,2048]{1,0:T(8,128)(2,1)S(1)} %collective-permute-done.10.refs_2_), channel_id=1, source_target_pairs={{0,16},{16,0},{32,48},{48,32},{64,80},{80,64},{96,112},{112,96},{1... | collective-permute-start | bytes 786440 | tf_op jit(solution)/shard_map/ppermute | solution.py:218
  41.5 0.5 collective-permute-done.16.refs_4_
  41.9 1.0 collective-permute-done.12.refs_6_.refs_3_
  42.9 0.2 hadamard_z.3.refs_5_.refs_0_
  43.1 0.5 collective-permute-start.20
  43.6 2.7 %collective-permute-start.19 = (bf16[64,2048]{1,0:T(8,128)(2,1)S(1)}, bf16[64,2048]{1,0:T(8,128)(2,1)S(1)}, u32[]{:S(2)}, u32[]{:S(2)}) collective-permute-start(bf16[64,2048]{1,0:T(8,128)(2,1)S(1)} %hadamard_z.3.refs_5_.refs_0_), channel_id=1, source_target_pairs={{0,64},{16,80},{32,96},{48,112},{64,0},{80,16},{96,32},{112,48},{1... | collective-permute-start | bytes 786440 | tf_op jit(solution)/shard_map/ppermute | solution.py:218
  46.4 1.2 %collective-permute-start.18 = (bf16[64,2048]{1,0:T(8,128)(2,1)S(1)}, bf16[64,2048]{1,0:T(8,128)(2,1)S(1)}, u32[]{:S(2)}, u32[]{:S(2)}) collective-permute-start(bf16[64,2048]{1,0:T(8,128)(2,1)S(1)} %hadamard_z.3.refs_5_.refs_0_), channel_id=1, source_target_pairs={{0,96},{16,112},{32,0},{48,16},{64,32},{80,48},{96,64},{112,80},{1... | collective-permute-start | bytes 786440 | tf_op jit(solution)/shard_map/ppermute | solution.py:218
  47.6 1.2 %collective-permute-start.17 = (bf16[64,2048]{1,0:T(8,128)(2,1)S(1)}, bf16[64,2048]{1,0:T(8,128)(2,1)S(1)}, u32[]{:S(2)}, u32[]{:S(2)}) collective-permute-start(bf16[64,2048]{1,0:T(8,128)(2,1)S(1)} %hadamard_z.3.refs_5_.refs_0_), channel_id=1, source_target_pairs={{0,16},{16,0},{32,48},{48,32},{64,80},{80,64},{96,112},{112,96},{1... | collective-permute-start | bytes 786440 | tf_op jit(solution)/shard_map/ppermute | solution.py:218
  48.8 2.4 %project_column.2.refs_5_ = bf16[256,2048]{1,0:T(8,128)(2,1)S(1)} custom-call(bf16[64,2048]{1,0:T(8,128)(2,1)S(1)} %hadamard_z.2.refs_0_, bf16[64,2048]{1,0:T(8,128)(2,1)S(1)} %collective-permute-done.7.refs_1_, bf16[64,2048]{1,0:T(8,128)(2,1)S(1)} %collective-permute-done.10.refs_2_, bf16[64,2048]{1,0:T(8,128)(2,1)S(1)} %collective-permute-done.8.refs_2_.refs_3_, ...), custom_call_target="tpu_custom_call" | custom-call | flops 10737418240 | bytes 52428800 | tf_op jit(solution)/shard_map/project_column/pallas_call | solution.py:41
  51.2 3.2 %project_mate.2 = (bf16[256,2048]{1,0:T(8,128)(2,1)S(1)}, bf16[64,2048]{1,0:T(8,128)(2,1)S(1)}, bf16[192,2048]{1,0:T(8,128)(2,1)S(1)}) custom-call(bf16[64,2048]{1,0:T(8,128)(2,1)S(1)} %hold.7.refs_0_, bf16[64,2048]{1,0:T(8,128)(2,1)S(1)} %collective-permute-done.9.refs_5_.refs_1_, bf16[64,2048]{1,0:T(8,128)(2,1)S(1)} %collective-permute-done.11.refs_2_, ...), custom_call_target="tpu_custom_call" | custom-call | flops 10737418240 | bytes 62914560 | tf_op jit(solution)/shard_map/project_mate/pallas_call | solution.py:41
  54.4 2.7 %collective-permute-done.20.refs_3_ = bf16[64,2048]{1,0:T(8,128)(2,1)S(1)} collective-permute-done((bf16[64,2048]{1,0:T(8,128)(2,1)S(1)}, bf16[64,2048]{1,0:T(8,128)(2,1)S(1)}, u32[]{:S(2)}, u32[]{:S(2)}) %collective-permute-start.20) | collective-permute-done | bytes 262176 | tf_op jit(solution)/shard_map/ppermute | solution.py:218
  57.2 0.6 collective-permute-done.18.refs_1_
  57.8 1.5 %collective-permute-done.21.refs_1_ = bf16[64,2048]{1,0:T(8,128)(2,1)S(1)} collective-permute-done((bf16[64,2048]{1,0:T(8,128)(2,1)S(1)}, bf16[64,2048]{1,0:T(8,128)(2,1)S(1)}, u32[]{:S(2)}, u32[]{:S(2)}) %collective-permute-start.21) | collective-permute-done | bytes 262176 | tf_op jit(solution)/shard_map/ppermute | solution.py:218
  59.5 1.3 %collective-permute-start.24 = (bf16[64,1024]{1,0:T(8,128)(2,1)S(1)}, bf16[64,1024]{1,0:T(8,128)(2,1)S(1)}, u32[]{:S(2)}, u32[]{:S(2)}) collective-permute-start(bf16[64,1024]{1,0:T(8,128)(2,1)S(1)} %get-tuple-element.39), channel_id=1, source_target_pairs={{0,12},{2,14},{4,0},{6,2},{8,4},{10,6},{12,8},{14,10},{1,13},{3,15... | collective-permute-start | bytes 393224 | tf_op jit(solution)/shard_map/ppermute | solution.py:218
  60.8 0.9 collective-permute-start.23
  61.6 1.2 %collective-permute-start.28 = (bf16[64,2048]{1,0:T(8,128)(2,1)S(1)}, bf16[64,2048]{1,0:T(8,128)(2,1)S(1)}, u32[]{:S(2)}, u32[]{:S(2)}) collective-permute-start(bf16[64,2048]{1,0:T(8,128)(2,1)S(1)} %collective-permute-done.19.refs_2_), channel_id=1, source_target_pairs={{0,16},{16,0},{32,48},{48,32},{64,80},{80,64},{96,112},{112,96},{1... | collective-permute-start | bytes 786440 | tf_op jit(solution)/shard_map/ppermute | solution.py:218
  62.8 1.7 %collective-permute-start.29 = (bf16[64,2048]{1,0:T(8,128)(2,1)S(1)}, bf16[64,2048]{1,0:T(8,128)(2,1)S(1)}, u32[]{:S(2)}, u32[]{:S(2)}) collective-permute-start(bf16[64,2048]{1,0:T(8,128)(2,1)S(1)} %hold.11.refs_0_), channel_id=1, source_target_pairs={{0,32},{16,48},{32,64},{48,80},{64,96},{80,112},{96,0},{112,16},{1... | collective-permute-start | bytes 786440 | tf_op jit(solution)/shard_map/ppermute | solution.py:218
  64.5 1.5 %collective-permute-start.27 = (bf16[64,2048]{1,0:T(8,128)(2,1)S(1)}, bf16[64,2048]{1,0:T(8,128)(2,1)S(1)}, u32[]{:S(2)}, u32[]{:S(2)}) collective-permute-start(bf16[64,2048]{1,0:T(8,128)(2,1)S(1)} %hold.11.refs_0_), channel_id=1, source_target_pairs={{0,96},{16,112},{32,0},{48,16},{64,32},{80,48},{96,64},{112,80},{1... | collective-permute-start | bytes 786440 | tf_op jit(solution)/shard_map/ppermute | solution.py:218
  66.1 1.4 %collective-permute-done.23.refs_2_ = bf16[64,1024]{1,0:T(8,128)(2,1)S(1)} collective-permute-done((bf16[64,1024]{1,0:T(8,128)(2,1)S(1)}, bf16[64,1024]{1,0:T(8,128)(2,1)S(1)}, u32[]{:S(2)}, u32[]{:S(2)}) %collective-permute-start.23) | collective-permute-done | bytes 131104 | tf_op jit(solution)/shard_map/ppermute | solution.py:218
  67.5 0.2 near_sum.2
  67.6 1.1 collective-permute-start.26
  68.7 1.0 collective-permute-start.25
  69.7 2.4 %project_column.3.refs_5_ = bf16[256,2048]{1,0:T(8,128)(2,1)S(1)} custom-call(bf16[64,2048]{1,0:T(8,128)(2,1)S(1)} %hadamard_z.3.refs_5_.refs_0_, bf16[64,2048]{1,0:T(8,128)(2,1)S(1)} %collective-permute-done.18.refs_1_, bf16[64,2048]{1,0:T(8,128)(2,1)S(1)} %collective-permute-done.19.refs_2_, bf16[64,2048]{1,0:T(8,128)(2,1)S(1)} %collective-permute-done.20.refs_3_, ...), custom_call_target="tpu_custom_call" | custom-call | flops 10737418240 | bytes 52428800 | tf_op jit(solution)/shard_map/project_column/pallas_call | solution.py:41
  72.1 3.1 %project_mate.3 = (bf16[256,2048]{1,0:T(8,128)(2,1)S(1)}, bf16[64,2048]{1,0:T(8,128)(2,1)S(1)}, bf16[192,2048]{1,0:T(8,128)(2,1)S(1)}) custom-call(bf16[64,2048]{1,0:T(8,128)(2,1)S(1)} %hold.11.refs_0_, bf16[64,2048]{1,0:T(8,128)(2,1)S(1)} %collective-permute-done.27.refs_1_, bf16[64,2048]{1,0:T(8,128)(2,1)S(1)} %collective-permute-done.28.refs_2_, ...), custom_call_target="tpu_custom_call" | custom-call | flops 10737418240 | bytes 62914560 | tf_op jit(solution)/shard_map/project_mate/pallas_call | solution.py:41
  75.2 1.6 %collective-permute-done.25.refs_1_.refs_2_ = bf16[64,2048]{1,0:T(8,128)(2,1)S(1)} collective-permute-done((bf16[64,2048]{1,0:T(8,128)(2,1)S(1)}, bf16[64,2048]{1,0:T(8,128)(2,1)S(1)}, u32[]{:S(2)}, u32[]{:S(2)}) %collective-permute-start.25) | collective-permute-done | bytes 262176 | tf_op jit(solution)/shard_map/ppermute | solution.py:218
  76.8 1.5 %collective-permute-done.30.refs_1_ = bf16[64,2048]{1,0:T(8,128)(2,1)S(1)} collective-permute-done((bf16[64,2048]{1,0:T(8,128)(2,1)S(1)}, bf16[64,2048]{1,0:T(8,128)(2,1)S(1)}, u32[]{:S(2)}, u32[]{:S(2)}) %collective-permute-start.30) | collective-permute-done | bytes 262176 | tf_op jit(solution)/shard_map/ppermute | solution.py:218
  78.5 0.8 collective-permute-start.34
  79.3 1.3 %collective-permute-start.33 = (bf16[64,1024]{1,0:T(8,128)(2,1)S(1)}, bf16[64,1024]{1,0:T(8,128)(2,1)S(1)}, u32[]{:S(2)}, u32[]{:S(2)}) collective-permute-start(bf16[64,1024]{1,0:T(8,128)(2,1)S(1)} %get-tuple-element.44.refs_5_), channel_id=1, source_target_pairs={{0,4},{2,6},{4,8},{6,10},{8,12},{10,14},{12,0},{14,2},{1,5},{3,7},... | collective-permute-start | bytes 393224 | tf_op jit(solution)/shard_map/ppermute | solution.py:218
  80.6 3.7 %collective-permute-done.34.refs_3_ = bf16[64,1024]{1,0:T(8,128)(2,1)S(1)} collective-permute-done((bf16[64,1024]{1,0:T(8,128)(2,1)S(1)}, bf16[64,1024]{1,0:T(8,128)(2,1)S(1)}, u32[]{:S(2)}, u32[]{:S(2)}) %collective-permute-start.34) | collective-permute-done | bytes 131104 | tf_op jit(solution)/shard_map/ppermute | solution.py:218
  84.4 1.6 %collective-permute-done.33.refs_2_ = bf16[64,1024]{1,0:T(8,128)(2,1)S(1)} collective-permute-done((bf16[64,1024]{1,0:T(8,128)(2,1)S(1)}, bf16[64,1024]{1,0:T(8,128)(2,1)S(1)}, u32[]{:S(2)}, u32[]{:S(2)}) %collective-permute-start.33) | collective-permute-done | bytes 131104 | tf_op jit(solution)/shard_map/ppermute | solution.py:218
  86.2 0.2 collective-permute-start.35
  86.4 3.1 %collective-permute-start.36 = (bf16[64,2048]{1,0:T(8,128)(2,1)S(1)}, bf16[64,2048]{1,0:T(8,128)(2,1)S(1)}, u32[]{:S(2)}, u32[]{:S(2)}) collective-permute-start(bf16[64,2048]{1,0:T(8,128)(2,1)S(1)} %get-tuple-element.50), channel_id=1, source_target_pairs={{0,12},{2,14},{4,0},{6,2},{8,4},{10,6},{12,8},{14,10},{1,13},{3,15... | collective-permute-start | bytes 786440 | tf_op jit(solution)/shard_map/ppermute | solution.py:218
  89.5 0.2 residual.2
  89.7 1.3 %collective-permute-start.31 = (bf16[64,2048]{1,0:T(8,128)(2,1)S(1)}, bf16[64,2048]{1,0:T(8,128)(2,1)S(1)}, u32[]{:S(2)}, u32[]{:S(2)}) collective-permute-start(bf16[64,2048]{1,0:T(8,128)(2,1)S(1)} %get-tuple-element.45.refs_5_.refs_0_), channel_id=1, source_target_pairs={{0,1},{2,3},{4,5},{6,7},{8,9},{10,11},{12,13},{14,15},{16,17},{18,... | collective-permute-start | bytes 786440 | tf_op jit(solution)/shard_map/ppermute | solution.py:227
  91.0 4.0 %collective-permute-done.35.refs_2_ = bf16[64,2048]{1,0:T(8,128)(2,1)S(1)} collective-permute-done((bf16[64,2048]{1,0:T(8,128)(2,1)S(1)}, bf16[64,2048]{1,0:T(8,128)(2,1)S(1)}, u32[]{:S(2)}, u32[]{:S(2)}) %collective-permute-start.35) | collective-permute-done | bytes 262176 | tf_op jit(solution)/shard_map/ppermute | solution.py:218
  94.9 0.2 residual.3
  95.1 1.3 %collective-permute-start.37 = (bf16[64,2048]{1,0:T(8,128)(2,1)S(1)}, bf16[64,2048]{1,0:T(8,128)(2,1)S(1)}, u32[]{:S(2)}, u32[]{:S(2)}) collective-permute-start(bf16[64,2048]{1,0:T(8,128)(2,1)S(1)} %get-tuple-element.51.refs_3_), channel_id=1, source_target_pairs={{0,1},{2,3},{4,5},{6,7},{8,9},{10,11},{12,13},{14,15},{16,17},{18,... | collective-permute-start | bytes 786440 | tf_op jit(solution)/shard_map/ppermute | solution.py:227
  96.4 4.1 %collective-permute-done.31.refs_2_ = bf16[64,2048]{1,0:T(8,128)(2,1)S(1)} collective-permute-done((bf16[64,2048]{1,0:T(8,128)(2,1)S(1)}, bf16[64,2048]{1,0:T(8,128)(2,1)S(1)}, u32[]{:S(2)}, u32[]{:S(2)}) %collective-permute-start.31) | collective-permute-done | bytes 262176 | tf_op jit(solution)/shard_map/ppermute | solution.py:227
  100.4 5.1 %collective-permute-done.37.refs_5_ = bf16[64,2048]{1,0:T(8,128)(2,1)S(1)} collective-permute-done((bf16[64,2048]{1,0:T(8,128)(2,1)S(1)}, bf16[64,2048]{1,0:T(8,128)(2,1)S(1)}, u32[]{:S(2)}, u32[]{:S(2)}) %collective-permute-start.37) | collective-permute-done | bytes 262176 | tf_op jit(solution)/shard_map/ppermute | solution.py:227
  105.6 0.9 end.1
  (48 shorter events, 1.0 us)
Async XLA Ops:
  0.0 1.0 copy-start.3
  1.0 0.7 copy-start.4
  2.5 1.6 %collective-permute-start = (bf16[64,2048]{1,0:T(8,128)(2,1)S(1)}, bf16[64,2048]{1,0:T(8,128)(2,1)S(1)}, u32[]{:S(2)}, u32[]{:S(2)}) collective-permute-start(bf16[64,2048]{1,0:T(8,128)(2,1)S(1)} %get-tuple-element.29.refs_0_), channel_id=1, source_target_pairs={{0,2},{2,0},{4,6},{6,4},{8,10},{10,8},{12,14},{14,12},{1,3},{3,1},... | collective-permute-start | bytes 786440 | tf_op jit(solution)/shard_map/ppermute | solution.py:218
  4.2 10.7 %collective-permute-start.2 = (bf16[64,2048]{1,0:T(8,128)(2,1)S(1)}, bf16[64,2048]{1,0:T(8,128)(2,1)S(1)}, u32[]{:S(2)}, u32[]{:S(2)}) collective-permute-start(bf16[64,2048]{1,0:T(8,128)(2,1)S(1)} %hadamard_core.2.refs_1_.refs_0_), channel_id=1, source_target_pairs={{0,4},{2,6},{4,8},{6,10},{8,12},{10,14},{12,0},{14,2},{1,5},{3,7},... | collective-permute-start | bytes 786440 | tf_op jit(solution)/shard_map/ppermute | solution.py:218
  6.2 8.7 %collective-permute-start.1 = (bf16[64,2048]{1,0:T(8,128)(2,1)S(1)}, bf16[64,2048]{1,0:T(8,128)(2,1)S(1)}, u32[]{:S(2)}, u32[]{:S(2)}) collective-permute-start(bf16[64,2048]{1,0:T(8,128)(2,1)S(1)} %hadamard_core.2.refs_1_.refs_0_), channel_id=1, source_target_pairs={{0,12},{2,14},{4,0},{6,2},{8,4},{10,6},{12,8},{14,10},{1,13},{3,15... | collective-permute-start | bytes 786440 | tf_op jit(solution)/shard_map/ppermute | solution.py:218
  8.4 9.9 %collective-permute-start.5 = (bf16[64,2048]{1,0:T(8,128)(2,1)S(1)}, bf16[64,2048]{1,0:T(8,128)(2,1)S(1)}, u32[]{:S(2)}, u32[]{:S(2)}) collective-permute-start(bf16[64,2048]{1,0:T(8,128)(2,1)S(1)} %get-tuple-element.32.refs_0_), channel_id=1, source_target_pairs={{0,2},{2,0},{4,6},{6,4},{8,10},{10,8},{12,14},{14,12},{1,3},{3,1},... | collective-permute-start | bytes 786440 | tf_op jit(solution)/shard_map/ppermute | solution.py:218
  8.4 3.4 %copy-start = (bf16[1,2048,2048]{2,1,0:T(8,128)(2,1)S(1)}, bf16[1,2048,2048]{2,1,0:T(8,128)(2,1)}, u32[]{:S(2)}) copy-start(bf16[1,2048,2048]{2,1,0:T(8,128)(2,1)} %refs_4_.9) | copy-start | bytes 25165828
  11.8 37.0 %copy-start.1 = (bf16[1,2048,2048]{2,1,0:T(8,128)(2,1)S(1)}, bf16[1,2048,2048]{2,1,0:T(8,128)(2,1)}, u32[]{:S(2)}) copy-start(bf16[1,2048,2048]{2,1,0:T(8,128)(2,1)} %refs_4_.9) | copy-start | bytes 25165828
  14.9 6.3 %collective-permute-start.3 = (bf16[64,1024]{1,0:T(8,128)(2,1)S(1)}, bf16[64,1024]{1,0:T(8,128)(2,1)S(1)}, u32[]{:S(2)}, u32[]{:S(2)}) collective-permute-start(bf16[64,1024]{1,0:T(8,128)(2,1)S(1)} %get-tuple-element.30), channel_id=1, source_target_pairs={{0,4},{2,6},{4,8},{6,10},{8,12},{10,14},{12,0},{14,2},{1,5},{3,7},... | collective-permute-start | bytes 393224 | tf_op jit(solution)/shard_map/ppermute | solution.py:218
  16.2 5.0 %collective-permute-start.4 = (bf16[64,1024]{1,0:T(8,128)(2,1)S(1)}, bf16[64,1024]{1,0:T(8,128)(2,1)S(1)}, u32[]{:S(2)}, u32[]{:S(2)}) collective-permute-start(bf16[64,1024]{1,0:T(8,128)(2,1)S(1)} %get-tuple-element.31), channel_id=1, source_target_pairs={{0,12},{2,14},{4,0},{6,2},{8,4},{10,6},{12,8},{14,10},{1,13},{3,15... | collective-permute-start | bytes 393224 | tf_op jit(solution)/shard_map/ppermute | solution.py:218
  21.4 8.3 %collective-permute-start.8 = (bf16[64,2048]{1,0:T(8,128)(2,1)S(1)}, bf16[64,2048]{1,0:T(8,128)(2,1)S(1)}, u32[]{:S(2)}, u32[]{:S(2)}) collective-permute-start(bf16[64,2048]{1,0:T(8,128)(2,1)S(1)} %hadamard_z.2.refs_0_), channel_id=1, source_target_pairs={{0,32},{16,48},{32,64},{48,80},{64,96},{80,112},{96,0},{112,16},{1... | collective-permute-start | bytes 786440 | tf_op jit(solution)/shard_map/ppermute | solution.py:218
  23.1 8.6 %collective-permute-start.7 = (bf16[64,2048]{1,0:T(8,128)(2,1)S(1)}, bf16[64,2048]{1,0:T(8,128)(2,1)S(1)}, u32[]{:S(2)}, u32[]{:S(2)}) collective-permute-start(bf16[64,2048]{1,0:T(8,128)(2,1)S(1)} %hadamard_z.2.refs_0_), channel_id=1, source_target_pairs={{0,96},{16,112},{32,0},{48,16},{64,32},{80,48},{96,64},{112,80},{1... | collective-permute-start | bytes 786440 | tf_op jit(solution)/shard_map/ppermute | solution.py:218
  24.8 6.9 %collective-permute-start.6 = (bf16[64,2048]{1,0:T(8,128)(2,1)S(1)}, bf16[64,2048]{1,0:T(8,128)(2,1)S(1)}, u32[]{:S(2)}, u32[]{:S(2)}) collective-permute-start(bf16[64,2048]{1,0:T(8,128)(2,1)S(1)} %hadamard_z.2.refs_0_), channel_id=1, source_target_pairs={{0,16},{16,0},{32,48},{48,32},{64,80},{80,64},{96,112},{112,96},{1... | collective-permute-start | bytes 786440 | tf_op jit(solution)/shard_map/ppermute | solution.py:218
  26.0 8.9 %collective-permute-start.14 = (bf16[64,2048]{1,0:T(8,128)(2,1)S(1)}, bf16[64,2048]{1,0:T(8,128)(2,1)S(1)}, u32[]{:S(2)}, u32[]{:S(2)}) collective-permute-start(bf16[64,2048]{1,0:T(8,128)(2,1)S(1)} %hadamard_core.3.refs_5_.refs_0_), channel_id=1, source_target_pairs={{0,4},{2,6},{4,8},{6,10},{8,12},{10,14},{12,0},{14,2},{1,5},{3,7},... | collective-permute-start | bytes 786440 | tf_op jit(solution)/shard_map/ppermute | solution.py:218
  27.6 7.3 %collective-permute-start.13 = (bf16[64,2048]{1,0:T(8,128)(2,1)S(1)}, bf16[64,2048]{1,0:T(8,128)(2,1)S(1)}, u32[]{:S(2)}, u32[]{:S(2)}) collective-permute-start(bf16[64,2048]{1,0:T(8,128)(2,1)S(1)} %hadamard_core.3.refs_5_.refs_0_), channel_id=1, source_target_pairs={{0,12},{2,14},{4,0},{6,2},{8,4},{10,6},{12,8},{14,10},{1,13},{3,15... | collective-permute-start | bytes 786440 | tf_op jit(solution)/shard_map/ppermute | solution.py:218
  29.7 10.4 %collective-permute-start.10 = (bf16[64,2048]{1,0:T(8,128)(2,1)S(1)}, bf16[64,2048]{1,0:T(8,128)(2,1)S(1)}, u32[]{:S(2)}, u32[]{:S(2)}) collective-permute-start(bf16[64,2048]{1,0:T(8,128)(2,1)S(1)} %hadamard_z.2.refs_0_), channel_id=1, source_target_pairs={{0,64},{16,80},{32,96},{48,112},{64,0},{80,16},{96,32},{112,48},{1... | collective-permute-start | bytes 786440 | tf_op jit(solution)/shard_map/ppermute | solution.py:218
  31.7 11.3 %collective-permute-start.12 = (bf16[64,2048]{1,0:T(8,128)(2,1)S(1)}, bf16[64,2048]{1,0:T(8,128)(2,1)S(1)}, u32[]{:S(2)}, u32[]{:S(2)}) collective-permute-start(bf16[64,2048]{1,0:T(8,128)(2,1)S(1)} %hold.7.refs_0_), channel_id=1, source_target_pairs={{0,32},{16,48},{32,64},{48,80},{64,96},{80,112},{96,0},{112,16},{1... | collective-permute-start | bytes 786440 | tf_op jit(solution)/shard_map/ppermute | solution.py:218
  32.3 10.6 %collective-permute-start.9 = (bf16[64,2048]{1,0:T(8,128)(2,1)S(1)}, bf16[64,2048]{1,0:T(8,128)(2,1)S(1)}, u32[]{:S(2)}, u32[]{:S(2)}) collective-permute-start(bf16[64,2048]{1,0:T(8,128)(2,1)S(1)} %hold.7.refs_0_), channel_id=1, source_target_pairs={{0,96},{16,112},{32,0},{48,16},{64,32},{80,48},{96,64},{112,80},{1... | collective-permute-start | bytes 786440 | tf_op jit(solution)/shard_map/ppermute | solution.py:218
  34.9 6.5 %collective-permute-start.15 = (bf16[64,1024]{1,0:T(8,128)(2,1)S(1)}, bf16[64,1024]{1,0:T(8,128)(2,1)S(1)}, u32[]{:S(2)}, u32[]{:S(2)}) collective-permute-start(bf16[64,1024]{1,0:T(8,128)(2,1)S(1)} %get-tuple-element.33), channel_id=1, source_target_pairs={{0,4},{2,6},{4,8},{6,10},{8,12},{10,14},{12,0},{14,2},{1,5},{3,7},... | collective-permute-start | bytes 393224 | tf_op jit(solution)/shard_map/ppermute | solution.py:218
  36.9 5.0 %collective-permute-start.16 = (bf16[64,1024]{1,0:T(8,128)(2,1)S(1)}, bf16[64,1024]{1,0:T(8,128)(2,1)S(1)}, u32[]{:S(2)}, u32[]{:S(2)}) collective-permute-start(bf16[64,1024]{1,0:T(8,128)(2,1)S(1)} %get-tuple-element.34), channel_id=1, source_target_pairs={{0,12},{2,14},{4,0},{6,2},{8,4},{10,6},{12,8},{14,10},{1,13},{3,15... | collective-permute-start | bytes 393224 | tf_op jit(solution)/shard_map/ppermute | solution.py:218
  40.2 11.0 %collective-permute-start.11 = (bf16[64,2048]{1,0:T(8,128)(2,1)S(1)}, bf16[64,2048]{1,0:T(8,128)(2,1)S(1)}, u32[]{:S(2)}, u32[]{:S(2)}) collective-permute-start(bf16[64,2048]{1,0:T(8,128)(2,1)S(1)} %collective-permute-done.10.refs_2_), channel_id=1, source_target_pairs={{0,16},{16,0},{32,48},{48,32},{64,80},{80,64},{96,112},{112,96},{1... | collective-permute-start | bytes 786440 | tf_op jit(solution)/shard_map/ppermute | solution.py:218
  43.1 14.0 %collective-permute-start.20 = (bf16[64,2048]{1,0:T(8,128)(2,1)S(1)}, bf16[64,2048]{1,0:T(8,128)(2,1)S(1)}, u32[]{:S(2)}, u32[]{:S(2)}) collective-permute-start(bf16[64,2048]{1,0:T(8,128)(2,1)S(1)} %hadamard_z.3.refs_5_.refs_0_), channel_id=1, source_target_pairs={{0,32},{16,48},{32,64},{48,80},{64,96},{80,112},{96,0},{112,16},{1... | collective-permute-start | bytes 786440 | tf_op jit(solution)/shard_map/ppermute | solution.py:218
  43.6 13.5 %collective-permute-start.19 = (bf16[64,2048]{1,0:T(8,128)(2,1)S(1)}, bf16[64,2048]{1,0:T(8,128)(2,1)S(1)}, u32[]{:S(2)}, u32[]{:S(2)}) collective-permute-start(bf16[64,2048]{1,0:T(8,128)(2,1)S(1)} %hadamard_z.3.refs_5_.refs_0_), channel_id=1, source_target_pairs={{0,64},{16,80},{32,96},{48,112},{64,0},{80,16},{96,32},{112,48},{1... | collective-permute-start | bytes 786440 | tf_op jit(solution)/shard_map/ppermute | solution.py:218
  46.4 11.4 %collective-permute-start.18 = (bf16[64,2048]{1,0:T(8,128)(2,1)S(1)}, bf16[64,2048]{1,0:T(8,128)(2,1)S(1)}, u32[]{:S(2)}, u32[]{:S(2)}) collective-permute-start(bf16[64,2048]{1,0:T(8,128)(2,1)S(1)} %hadamard_z.3.refs_5_.refs_0_), channel_id=1, source_target_pairs={{0,96},{16,112},{32,0},{48,16},{64,32},{80,48},{96,64},{112,80},{1... | collective-permute-start | bytes 786440 | tf_op jit(solution)/shard_map/ppermute | solution.py:218
  47.6 10.2 %collective-permute-start.17 = (bf16[64,2048]{1,0:T(8,128)(2,1)S(1)}, bf16[64,2048]{1,0:T(8,128)(2,1)S(1)}, u32[]{:S(2)}, u32[]{:S(2)}) collective-permute-start(bf16[64,2048]{1,0:T(8,128)(2,1)S(1)} %hadamard_z.3.refs_5_.refs_0_), channel_id=1, source_target_pairs={{0,16},{16,0},{32,48},{48,32},{64,80},{80,64},{96,112},{112,96},{1... | collective-permute-start | bytes 786440 | tf_op jit(solution)/shard_map/ppermute | solution.py:218
  57.8 1.5 %collective-permute-start.21 = (bf16[64,2048]{1,0:T(8,128)(2,1)S(1)}, bf16[64,2048]{1,0:T(8,128)(2,1)S(1)}, u32[]{:S(2)}, u32[]{:S(2)}) collective-permute-start(bf16[64,2048]{1,0:T(8,128)(2,1)S(1)} %hold.9), channel_id=1, source_target_pairs={{0,2},{2,0},{4,6},{6,4},{8,10},{10,8},{12,14},{14,12},{1,3},{3,1},... | collective-permute-start | bytes 786440 | tf_op jit(solution)/shard_map/ppermute | solution.py:218
  59.3 3.5 %collective-permute-start.22 = (bf16[192,2048]{1,0:T(8,128)(2,1)S(1)}, bf16[192,2048]{1,0:T(8,128)(2,1)S(1)}, u32[]{:S(2)}, u32[]{:S(2)}) collective-permute-start(bf16[192,2048]{1,0:T(8,128)(2,1)S(1)} %hold.10), channel_id=1, source_target_pairs={{0,2},{2,0},{4,6},{6,4},{8,10},{10,8},{12,14},{14,12},{1,3},{3,1},... | collective-permute-start | bytes 2359304 | tf_op jit(solution)/shard_map/ppermute | solution.py:218
  59.5 6.6 %collective-permute-start.24 = (bf16[64,1024]{1,0:T(8,128)(2,1)S(1)}, bf16[64,1024]{1,0:T(8,128)(2,1)S(1)}, u32[]{:S(2)}, u32[]{:S(2)}) collective-permute-start(bf16[64,1024]{1,0:T(8,128)(2,1)S(1)} %get-tuple-element.39), channel_id=1, source_target_pairs={{0,12},{2,14},{4,0},{6,2},{8,4},{10,6},{12,8},{14,10},{1,13},{3,15... | collective-permute-start | bytes 393224 | tf_op jit(solution)/shard_map/ppermute | solution.py:218
  60.8 6.7 %collective-permute-start.23 = (bf16[64,1024]{1,0:T(8,128)(2,1)S(1)}, bf16[64,1024]{1,0:T(8,128)(2,1)S(1)}, u32[]{:S(2)}, u32[]{:S(2)}) collective-permute-start(bf16[64,1024]{1,0:T(8,128)(2,1)S(1)} %get-tuple-element.38.refs_1_), channel_id=1, source_target_pairs={{0,4},{2,6},{4,8},{6,10},{8,12},{10,14},{12,0},{14,2},{1,5},{3,7},... | collective-permute-start | bytes 393224 | tf_op jit(solution)/shard_map/ppermute | solution.py:218
  61.6 10.5 %collective-permute-start.28 = (bf16[64,2048]{1,0:T(8,128)(2,1)S(1)}, bf16[64,2048]{1,0:T(8,128)(2,1)S(1)}, u32[]{:S(2)}, u32[]{:S(2)}) collective-permute-start(bf16[64,2048]{1,0:T(8,128)(2,1)S(1)} %collective-permute-done.19.refs_2_), channel_id=1, source_target_pairs={{0,16},{16,0},{32,48},{48,32},{64,80},{80,64},{96,112},{112,96},{1... | collective-permute-start | bytes 786440 | tf_op jit(solution)/shard_map/ppermute | solution.py:218
  62.8 9.3 %collective-permute-start.29 = (bf16[64,2048]{1,0:T(8,128)(2,1)S(1)}, bf16[64,2048]{1,0:T(8,128)(2,1)S(1)}, u32[]{:S(2)}, u32[]{:S(2)}) collective-permute-start(bf16[64,2048]{1,0:T(8,128)(2,1)S(1)} %hold.11.refs_0_), channel_id=1, source_target_pairs={{0,32},{16,48},{32,64},{48,80},{64,96},{80,112},{96,0},{112,16},{1... | collective-permute-start | bytes 786440 | tf_op jit(solution)/shard_map/ppermute | solution.py:218
  64.5 7.6 %collective-permute-start.27 = (bf16[64,2048]{1,0:T(8,128)(2,1)S(1)}, bf16[64,2048]{1,0:T(8,128)(2,1)S(1)}, u32[]{:S(2)}, u32[]{:S(2)}) collective-permute-start(bf16[64,2048]{1,0:T(8,128)(2,1)S(1)} %hold.11.refs_0_), channel_id=1, source_target_pairs={{0,96},{16,112},{32,0},{48,16},{64,32},{80,48},{96,64},{112,80},{1... | collective-permute-start | bytes 786440 | tf_op jit(solution)/shard_map/ppermute | solution.py:218
  67.6 7.6 %collective-permute-start.26 = (bf16[64,2048]{1,0:T(8,128)(2,1)S(1)}, bf16[64,2048]{1,0:T(8,128)(2,1)S(1)}, u32[]{:S(2)}, u32[]{:S(2)}) collective-permute-start(bf16[64,2048]{1,0:T(8,128)(2,1)S(1)} %get-tuple-element.41), channel_id=1, source_target_pairs={{0,12},{2,14},{4,0},{6,2},{8,4},{10,6},{12,8},{14,10},{1,13},{3,15... | collective-permute-start | bytes 786440 | tf_op jit(solution)/shard_map/ppermute | solution.py:218
  68.7 8.1 %collective-permute-start.25 = (bf16[64,2048]{1,0:T(8,128)(2,1)S(1)}, bf16[64,2048]{1,0:T(8,128)(2,1)S(1)}, u32[]{:S(2)}, u32[]{:S(2)}) collective-permute-start(bf16[64,2048]{1,0:T(8,128)(2,1)S(1)} %get-tuple-element.40.refs_5_), channel_id=1, source_target_pairs={{0,4},{2,6},{4,8},{6,10},{8,12},{10,14},{12,0},{14,2},{1,5},{3,7},... | collective-permute-start | bytes 786440 | tf_op jit(solution)/shard_map/ppermute | solution.py:218
  72.1 17.4 %copy-start.2 = (bf16[128,2048]{1,0:T(8,128)(2,1)S(1)}, bf16[128,2048]{1,0:T(8,128)(2,1)}, u32[]{:S(2)}) copy-start(bf16[128,2048]{1,0:T(8,128)(2,1)} %refs_4_.11) | copy-start | bytes 1572868
  76.8 1.5 %collective-permute-start.30 = (bf16[64,2048]{1,0:T(8,128)(2,1)S(1)}, bf16[64,2048]{1,0:T(8,128)(2,1)S(1)}, u32[]{:S(2)}, u32[]{:S(2)}) collective-permute-start(bf16[64,2048]{1,0:T(8,128)(2,1)S(1)} %hold.12), channel_id=1, source_target_pairs={{0,2},{2,0},{4,6},{6,4},{8,10},{10,8},{12,14},{14,12},{1,3},{3,1},... | collective-permute-start | bytes 786440 | tf_op jit(solution)/shard_map/ppermute | solution.py:218
  78.3 7.7 %collective-permute-start.32 = (bf16[192,2048]{1,0:T(8,128)(2,1)S(1)}, bf16[192,2048]{1,0:T(8,128)(2,1)S(1)}, u32[]{:S(2)}, u32[]{:S(2)}) collective-permute-start(bf16[192,2048]{1,0:T(8,128)(2,1)S(1)} %hold.13), channel_id=1, source_target_pairs={{0,2},{2,0},{4,6},{6,4},{8,10},{10,8},{12,14},{14,12},{1,3},{3,1},... | collective-permute-start | bytes 2359304 | tf_op jit(solution)/shard_map/ppermute | solution.py:218
  78.5 5.8 %collective-permute-start.34 = (bf16[64,1024]{1,0:T(8,128)(2,1)S(1)}, bf16[64,1024]{1,0:T(8,128)(2,1)S(1)}, u32[]{:S(2)}, u32[]{:S(2)}) collective-permute-start(bf16[64,1024]{1,0:T(8,128)(2,1)S(1)} %get-tuple-element.48), channel_id=1, source_target_pairs={{0,12},{2,14},{4,0},{6,2},{8,4},{10,6},{12,8},{14,10},{1,13},{3,15... | collective-permute-start | bytes 393224 | tf_op jit(solution)/shard_map/ppermute | solution.py:218
  79.3 6.7 %collective-permute-start.33 = (bf16[64,1024]{1,0:T(8,128)(2,1)S(1)}, bf16[64,1024]{1,0:T(8,128)(2,1)S(1)}, u32[]{:S(2)}, u32[]{:S(2)}) collective-permute-start(bf16[64,1024]{1,0:T(8,128)(2,1)S(1)} %get-tuple-element.44.refs_5_), channel_id=1, source_target_pairs={{0,4},{2,6},{4,8},{6,10},{8,12},{10,14},{12,0},{14,2},{1,5},{3,7},... | collective-permute-start | bytes 393224 | tf_op jit(solution)/shard_map/ppermute | solution.py:218
  86.2 8.7 %collective-permute-start.35 = (bf16[64,2048]{1,0:T(8,128)(2,1)S(1)}, bf16[64,2048]{1,0:T(8,128)(2,1)S(1)}, u32[]{:S(2)}, u32[]{:S(2)}) collective-permute-start(bf16[64,2048]{1,0:T(8,128)(2,1)S(1)} %get-tuple-element.49), channel_id=1, source_target_pairs={{0,4},{2,6},{4,8},{6,10},{8,12},{10,14},{12,0},{14,2},{1,5},{3,7},... | collective-permute-start | bytes 786440 | tf_op jit(solution)/shard_map/ppermute | solution.py:218
  86.4 8.6 %collective-permute-start.36 = (bf16[64,2048]{1,0:T(8,128)(2,1)S(1)}, bf16[64,2048]{1,0:T(8,128)(2,1)S(1)}, u32[]{:S(2)}, u32[]{:S(2)}) collective-permute-start(bf16[64,2048]{1,0:T(8,128)(2,1)S(1)} %get-tuple-element.50), channel_id=1, source_target_pairs={{0,12},{2,14},{4,0},{6,2},{8,4},{10,6},{12,8},{14,10},{1,13},{3,15... | collective-permute-start | bytes 786440 | tf_op jit(solution)/shard_map/ppermute | solution.py:218
  89.7 10.8 %collective-permute-start.31 = (bf16[64,2048]{1,0:T(8,128)(2,1)S(1)}, bf16[64,2048]{1,0:T(8,128)(2,1)S(1)}, u32[]{:S(2)}, u32[]{:S(2)}) collective-permute-start(bf16[64,2048]{1,0:T(8,128)(2,1)S(1)} %get-tuple-element.45.refs_5_.refs_0_), channel_id=1, source_target_pairs={{0,1},{2,3},{4,5},{6,7},{8,9},{10,11},{12,13},{14,15},{16,17},{18,... | collective-permute-start | bytes 786440 | tf_op jit(solution)/shard_map/ppermute | solution.py:227
  95.1 10.5 %collective-permute-start.37 = (bf16[64,2048]{1,0:T(8,128)(2,1)S(1)}, bf16[64,2048]{1,0:T(8,128)(2,1)S(1)}, u32[]{:S(2)}, u32[]{:S(2)}) collective-permute-start(bf16[64,2048]{1,0:T(8,128)(2,1)S(1)} %get-tuple-element.51.refs_3_), channel_id=1, source_target_pairs={{0,1},{2,3},{4,5},{6,7},{8,9},{10,11},{12,13},{14,15},{16,17},{18,... | collective-permute-start | bytes 786440 | tf_op jit(solution)/shard_map/ppermute | solution.py:227

commit v8 on v7

--- a/solution.py
+++ b/solution.py
@@ -11,6 +11,7 @@
 BF16 = jnp.bfloat16
 TILES = 4
 ROWS = (64, 64)
+PARTS = (32, 32)
 FAR = 2
 STRIP = 32
 
@@ -182,30 +183,43 @@
     high_ref[...] = core_sum(keep_ref, came_ref, FAR, slice(half, None)).astype(BF16)
 
 
-def near_kernel(keep_ref, came_ref, low_ref, high_ref, next_ref, last_ref):
+def near_kernel(keep_ref, came_ref, low_ref, high_ref, *out_refs):
     half = low_ref.shape[1]
     low, high = slice(0, half), slice(half, None)
-    next_ref[:, low] = (core_sum(keep_ref, came_ref, 1, low) + f32(low_ref[...])).astype(BF16)
-    next_ref[:, high] = core_sum(keep_ref, came_ref, 1, high).astype(BF16)
-    last_ref[:, low] = core_sum(keep_ref, came_ref, 3, low).astype(BF16)
-    last_ref[:, high] = (core_sum(keep_ref, came_ref, 3, high) + f32(high_ref[...])).astype(BF16)
-
-
-def finish_kernel(at, keep_ref, came_ref, a_ref, b_ref, residual_ref, leading_ref, summed_ref):
-    total = core_sum(keep_ref, came_ref, 0) + f32(a_ref[...]) + f32(b_ref[...])
+    at = 0
+    for next_ref, last_ref in zip(out_refs[::2], out_refs[1::2]):
+        part = slice(at, at + next_ref.shape[0])
+        at = part.stop
+        next_ref[:, low] = (core_sum(keep_ref, came_ref, 1, low)[part] + f32(low_ref[part])).astype(BF16)
+        next_ref[:, high] = core_sum(keep_ref, came_ref, 1, high)[part].astype(BF16)
+        last_ref[:, low] = core_sum(keep_ref, came_ref, 3, low)[part].astype(BF16)
+        last_ref[:, high] = (core_sum(keep_ref, came_ref, 3, high)[part] + f32(high_ref[part])).astype(BF16)
+
+
+def finish_kernel(at, low, keep_ref, came_ref, a_ref, b_ref, residual_ref, leading_ref, summed_ref):
+    rows = leading_ref.shape[0]
+    total = core_sum(keep_ref, came_ref, 0)[low : low + rows] + f32(a_ref[...]) + f32(b_ref[...])
     summed_ref[...] = total
-    leading_ref[...] = (f32(residual_ref[at]) + total).astype(BF16)
-
-
-def end_kernel(*refs):
-    out_ref = refs[-1]
+    leading_ref[...] = (f32(residual_ref[at : at + rows]) + total).astype(BF16)
+
+
+def end_rows(refs, out_ref, at):
     first = lax.axis_index("pipe") == 0
-    at = 0
-    for leading_ref, summed_ref, passed_ref in zip(refs[0:-1:3], refs[1:-1:3], refs[2:-1:3]):
+    for leading_ref, summed_ref, passed_ref in zip(refs[0::3], refs[1::3], refs[2::3]):
         rows = leading_ref.shape[0]
         later = (f32(passed_ref[...]) + summed_ref[...]).astype(BF16)
-        out_ref[0, at : at + rows, :] = jnp.where(first, leading_ref[...], later)
+        out_ref[at : at + rows, :] = jnp.where(first, leading_ref[...], later)
         at += rows
+
+
+def early_kernel(*refs):
+    end_rows(refs[:-1], refs[-1], 0)
+
+
+def end_kernel(early_ref, *refs):
+    rows = early_ref.shape[0]
+    refs[-1][0, :rows] = early_ref[...]
+    end_rows(refs[:-1], refs[-1].at[0], rows)
 
 
 def on_device(attention_out, signs, out_weight, residual_in):
@@ -267,18 +281,20 @@
         low, high = call("far_sum", far_kernel, (keep, came), (shape(came.shape[0], columns // 2),) * 2, behind)
         return low, (up(low), down(high))
 
-    def near_sum(keep, came, far, behind=()):
-        return call("near_sum", near_kernel, (keep, came, *far), (shape(far[0].shape[0], columns),) * 2, behind)
+    def near_sum(keep, came, far, parts, behind=()):
+        outs = [shape(rows, columns) for rows in parts for _ in range(2)]
+        return call("near_sum", near_kernel, (keep, came, *far), tuple(outs), behind)
 
     def last_sum(near):
         return up(near[0]), down(near[1])
 
-    def finish(chunk, keep, came, arrived, behind=()):
+    def finish(at, low, keep, came, arrived, behind=()):
+        rows = arrived[0].shape[0]
         return call(
             "residual",
-            lambda *refs: finish_kernel(cut[chunk], *refs),
+            lambda *refs: finish_kernel(at, low, *refs),
             (keep, came, *arrived, residual_in),
-            (shape(ROWS[chunk], columns), shape(ROWS[chunk], columns, jnp.float32)),
+            (shape(rows, columns), shape(rows, columns, jnp.float32)),
             behind,
             weigh=20,
         )
@@ -308,22 +324,31 @@
     made0, ring0 = far_sum(keep0, far0)
     near0 = swap(hold(near0, [far0]))
     mates1 = spread_mate(column1, hold(mate1, [made0, near0]))
-    sums0 = near_sum(keep0, near0, ring0)
+    sums0 = near_sum(keep0, near0, ring0, ROWS[:1])
     products1 = project(column1, out_weight, None, [sums0[0]])
     keep1, far1, near1 = project(mates1, out_weight, products1)
     last0 = last_sum(sums0)
     far1 = swap(hold(far1, last0))
     near1 = swap(hold(near1, [far1]))
     made1, ring1 = far_sum(keep1, far1)
-    leading0, summed0 = finish(0, keep0, near0, last0, [made1])
+    leading0, summed0 = finish(0, 0, keep0, near0, last0, [made1])
     passed0 = pipe(leading0)
-    sums1 = near_sum(keep1, near1, ring1)
-    leading1, summed1 = finish(1, keep1, near1, last_sum(sums1), [leading0])
+    sums1 = near_sum(keep1, near1, ring1, PARTS)
+    leading1, summed1 = finish(ROWS[0], 0, keep1, near1, last_sum(sums1[:2]), [leading0, passed0])
     passed1 = pipe(leading1)
+    leading2, summed2 = finish(ROWS[0] + PARTS[0], PARTS[0], keep1, near1, last_sum(sums1[2:]), [leading1])
+    passed2 = pipe(leading2)
+    early = call(
+        "early",
+        early_kernel,
+        (leading0, summed0, passed0, leading1, summed1, passed1),
+        shape(tokens - PARTS[1], columns),
+        weigh=20,
+    )
     return call(
         "end",
         end_kernel,
-        (leading0, summed0, passed0, leading1, summed1, passed1),
+        (early, leading2, summed2, passed2),
         jax.ShapeDtypeStruct((1, tokens, columns), BF16),
     )
 

time: 107 us -> 105 us (0.981)
  waiting for transfers between devices: 39.2 us -> 33.1 us
  starting transfers between devices: 47.9 us -> 52.4 us
    ppermute x36 -> x38, waiting for transfers between devices: 30 us -> 26.2 us  [move(): lax.ppermute(value, axis, [(i, target(i)) for i in range(lax.axis_size(ax...]
    ppermute x36 -> x38, starting transfers between devices: 45.3 us -> 48.6 us  [move(): lax.ppermute(value, axis, [(i, target(i)) for i in range(lax.axis_size(ax...]
    ppermute x2 -> x3, waiting for transfers between devices: 9.18 us -> 6.98 us  [pipe(): return lax.ppermute(value, 'pipe', [(0, 1)])]
    ppermute x2 -> x3, starting transfers between devices: 2.58 us -> 3.88 us  [pipe(): return lax.ppermute(value, 'pipe', [(0, 1)])]
    pallas_call x19 -> x21, Pallas kernels: 14 us -> 14 us  [call(): pl.pallas_call(lambda *refs: kernel(*refs[:count], *refs[count + len(behi...]
  transfers between devices with their start and end apart: 38 -> 41, of which waited for: 19 -> 20; matrix products, arithmetic and copies ran while one was open for 0% -> 0% of each run, Pallas kernels for 11% -> 12%
where the time goes in v8:
time: 105 us
  starting transfers between devices  52.4 us (50%)
  waiting for transfers between devices  33.1 us (32%)
  Pallas kernels  14 us (13%)
  local copies, waits for them, and re-layouts  5.13 us (5%)
    ppermute x38, starting transfers between devices, move(): lax.ppermute(value, axis, [(i, target(i)) for i in range(lax.axis_size(ax...  48.6 us
    ppermute x38, waiting for transfers between devices, move(): lax.ppermute(value, axis, [(i, target(i)) for i in range(lax.axis_size(ax...  26.2 us
    pallas_call x21, Pallas kernels, call(): pl.pallas_call(lambda *refs: kernel(*refs[:count], *refs[count + len(behi...  14 us
    ppermute x3, waiting for transfers between devices, pipe(): return lax.ppermute(value, 'pipe', [(0, 1)])  6.98 us
    unnamed x10, local copies, waits for them, and re-layouts  5.13 us
    ppermute x3, starting transfers between devices, pipe(): return lax.ppermute(value, 'pipe', [(0, 1)])  3.88 us
  transfers between devices with their start and end apart: 41, of which 20 were waited for; matrix products, arithmetic and copies ran while one was open for 0% of the time, Pallas kernels for 12%

profile of v8, /device:TPU:4, one launch (start us, length us, event | category | flops | bytes accessed | tf_op | source)
XLA Modules:
  0.0 105.0 jit_solution(14837187919389503672)
XLA Ops:
  0.0 1.0 copy-done.3
  1.0 0.7 copy-done.4
  1.7 0.7 rotate_local.1
  2.6 1.5 %collective-permute-done.refs_1_ = bf16[64,2048]{1,0:T(8,128)(2,1)S(1)} collective-permute-done((bf16[64,2048]{1,0:T(8,128)(2,1)S(1)}, bf16[64,2048]{1,0:T(8,128)(2,1)S(1)}, u32[]{:S(2)}, u32[]{:S(2)}) %collective-permute-start) | collective-permute-done | bytes 262176 | tf_op jit(solution)/shard_map/ppermute | solution.py:232
  4.2 2.0 %collective-permute-start.2 = (bf16[64,2048]{1,0:T(8,128)(2,1)S(1)}, bf16[64,2048]{1,0:T(8,128)(2,1)S(1)}, u32[]{:S(2)}, u32[]{:S(2)}) collective-permute-start(bf16[64,2048]{1,0:T(8,128)(2,1)S(1)} %hadamard_core.2.refs_1_.refs_0_), channel_id=1, source_target_pairs={{0,4},{2,6},{4,8},{6,10},{8,12},{10,14},{12,0},{14,2},{1,5},{3,7},... | collective-permute-start | bytes 786440 | tf_op jit(solution)/shard_map/ppermute | solution.py:232
  6.2 2.2 %collective-permute-start.1 = (bf16[64,2048]{1,0:T(8,128)(2,1)S(1)}, bf16[64,2048]{1,0:T(8,128)(2,1)S(1)}, u32[]{:S(2)}, u32[]{:S(2)}) collective-permute-start(bf16[64,2048]{1,0:T(8,128)(2,1)S(1)} %hadamard_core.2.refs_1_.refs_0_), channel_id=1, source_target_pairs={{0,12},{2,14},{4,0},{6,2},{8,4},{10,6},{12,8},{14,10},{1,13},{3,15... | collective-permute-start | bytes 786440 | tf_op jit(solution)/shard_map/ppermute | solution.py:232
  8.4 3.4 %copy-done = bf16[1,2048,2048]{2,1,0:T(8,128)(2,1)S(1)} copy-done((bf16[1,2048,2048]{2,1,0:T(8,128)(2,1)S(1)}, bf16[1,2048,2048]{2,1,0:T(8,128)(2,1)}, u32[]{:S(2)}) %copy-start) | copy-done | bytes 8388632
  11.8 3.1 %collective-permute-done.2.refs_1_.refs_2_ = bf16[64,2048]{1,0:T(8,128)(2,1)S(1)} collective-permute-done((bf16[64,2048]{1,0:T(8,128)(2,1)S(1)}, bf16[64,2048]{1,0:T(8,128)(2,1)S(1)}, u32[]{:S(2)}, u32[]{:S(2)}) %collective-permute-start.2) | collective-permute-done | bytes 262176 | tf_op jit(solution)/shard_map/ppermute | solution.py:232
  14.9 1.3 %collective-permute-start.3 = (bf16[64,1024]{1,0:T(8,128)(2,1)S(1)}, bf16[64,1024]{1,0:T(8,128)(2,1)S(1)}, u32[]{:S(2)}, u32[]{:S(2)}) collective-permute-start(bf16[64,1024]{1,0:T(8,128)(2,1)S(1)} %get-tuple-element.34), channel_id=1, source_target_pairs={{0,4},{2,6},{4,8},{6,10},{8,12},{10,14},{12,0},{14,2},{1,5},{3,7},... | collective-permute-start | bytes 393224 | tf_op jit(solution)/shard_map/ppermute | solution.py:232
  16.2 2.0 %collective-permute-start.4 = (bf16[64,1024]{1,0:T(8,128)(2,1)S(1)}, bf16[64,1024]{1,0:T(8,128)(2,1)S(1)}, u32[]{:S(2)}, u32[]{:S(2)}) collective-permute-start(bf16[64,1024]{1,0:T(8,128)(2,1)S(1)} %get-tuple-element.35), channel_id=1, source_target_pairs={{0,12},{2,14},{4,0},{6,2},{8,4},{10,6},{12,8},{14,10},{1,13},{3,15... | collective-permute-start | bytes 393224 | tf_op jit(solution)/shard_map/ppermute | solution.py:232
  18.3 2.9 %collective-permute-done.3.refs_3_ = bf16[64,1024]{1,0:T(8,128)(2,1)S(1)} collective-permute-done((bf16[64,1024]{1,0:T(8,128)(2,1)S(1)}, bf16[64,1024]{1,0:T(8,128)(2,1)S(1)}, u32[]{:S(2)}, u32[]{:S(2)}) %collective-permute-start.3) | collective-permute-done | bytes 131104 | tf_op jit(solution)/shard_map/ppermute | solution.py:232
  21.2 0.2 hadamard_z.2.refs_0_
  21.4 1.6 %collective-permute-start.8 = (bf16[64,2048]{1,0:T(8,128)(2,1)S(1)}, bf16[64,2048]{1,0:T(8,128)(2,1)S(1)}, u32[]{:S(2)}, u32[]{:S(2)}) collective-permute-start(bf16[64,2048]{1,0:T(8,128)(2,1)S(1)} %hadamard_z.2.refs_0_), channel_id=1, source_target_pairs={{0,32},{16,48},{32,64},{48,80},{64,96},{80,112},{96,0},{112,16},{1... | collective-permute-start | bytes 786440 | tf_op jit(solution)/shard_map/ppermute | solution.py:232
  23.1 1.7 %collective-permute-start.7 = (bf16[64,2048]{1,0:T(8,128)(2,1)S(1)}, bf16[64,2048]{1,0:T(8,128)(2,1)S(1)}, u32[]{:S(2)}, u32[]{:S(2)}) collective-permute-start(bf16[64,2048]{1,0:T(8,128)(2,1)S(1)} %hadamard_z.2.refs_0_), channel_id=1, source_target_pairs={{0,96},{16,112},{32,0},{48,16},{64,32},{80,48},{96,64},{112,80},{1... | collective-permute-start | bytes 786440 | tf_op jit(solution)/shard_map/ppermute | solution.py:232
  24.8 1.2 %collective-permute-start.6 = (bf16[64,2048]{1,0:T(8,128)(2,1)S(1)}, bf16[64,2048]{1,0:T(8,128)(2,1)S(1)}, u32[]{:S(2)}, u32[]{:S(2)}) collective-permute-start(bf16[64,2048]{1,0:T(8,128)(2,1)S(1)} %hadamard_z.2.refs_0_), channel_id=1, source_target_pairs={{0,16},{16,0},{32,48},{48,32},{64,80},{80,64},{96,112},{112,96},{1... | collective-permute-start | bytes 786440 | tf_op jit(solution)/shard_map/ppermute | solution.py:232
  26.0 1.6 %collective-permute-start.14 = (bf16[64,2048]{1,0:T(8,128)(2,1)S(1)}, bf16[64,2048]{1,0:T(8,128)(2,1)S(1)}, u32[]{:S(2)}, u32[]{:S(2)}) collective-permute-start(bf16[64,2048]{1,0:T(8,128)(2,1)S(1)} %hadamard_core.3.refs_5_.refs_0_), channel_id=1, source_target_pairs={{0,4},{2,6},{4,8},{6,10},{8,12},{10,14},{12,0},{14,2},{1,5},{3,7},... | collective-permute-start | bytes 786440 | tf_op jit(solution)/shard_map/ppermute | solution.py:232
  27.6 1.6 %collective-permute-start.13 = (bf16[64,2048]{1,0:T(8,128)(2,1)S(1)}, bf16[64,2048]{1,0:T(8,128)(2,1)S(1)}, u32[]{:S(2)}, u32[]{:S(2)}) collective-permute-start(bf16[64,2048]{1,0:T(8,128)(2,1)S(1)} %hadamard_core.3.refs_5_.refs_0_), channel_id=1, source_target_pairs={{0,12},{2,14},{4,0},{6,2},{8,4},{10,6},{12,8},{14,10},{1,13},{3,15... | collective-permute-start | bytes 786440 | tf_op jit(solution)/shard_map/ppermute | solution.py:232
  29.2 0.5 collective-permute-done.8.refs_2_.refs_3_
  29.7 1.9 %collective-permute-start.10 = (bf16[64,2048]{1,0:T(8,128)(2,1)S(1)}, bf16[64,2048]{1,0:T(8,128)(2,1)S(1)}, u32[]{:S(2)}, u32[]{:S(2)}) collective-permute-start(bf16[64,2048]{1,0:T(8,128)(2,1)S(1)} %hadamard_z.2.refs_0_), channel_id=1, source_target_pairs={{0,64},{16,80},{32,96},{48,112},{64,0},{80,16},{96,32},{112,48},{1... | collective-permute-start | bytes 786440 | tf_op jit(solution)/shard_map/ppermute | solution.py:232
  31.7 0.7 collective-permute-start.12
  32.3 2.6 %collective-permute-start.9 = (bf16[64,2048]{1,0:T(8,128)(2,1)S(1)}, bf16[64,2048]{1,0:T(8,128)(2,1)S(1)}, u32[]{:S(2)}, u32[]{:S(2)}) collective-permute-start(bf16[64,2048]{1,0:T(8,128)(2,1)S(1)} %hold.7.refs_0_), channel_id=1, source_target_pairs={{0,96},{16,112},{32,0},{48,16},{64,32},{80,48},{96,64},{112,80},{1... | collective-permute-start | bytes 786440 | tf_op jit(solution)/shard_map/ppermute | solution.py:232
  34.9 2.0 %collective-permute-start.15 = (bf16[64,1024]{1,0:T(8,128)(2,1)S(1)}, bf16[64,1024]{1,0:T(8,128)(2,1)S(1)}, u32[]{:S(2)}, u32[]{:S(2)}) collective-permute-start(bf16[64,1024]{1,0:T(8,128)(2,1)S(1)} %get-tuple-element.37), channel_id=1, source_target_pairs={{0,4},{2,6},{4,8},{6,10},{8,12},{10,14},{12,0},{14,2},{1,5},{3,7},... | collective-permute-start | bytes 393224 | tf_op jit(solution)/shard_map/ppermute | solution.py:232
  36.9 1.7 %collective-permute-start.16 = (bf16[64,1024]{1,0:T(8,128)(2,1)S(1)}, bf16[64,1024]{1,0:T(8,128)(2,1)S(1)}, u32[]{:S(2)}, u32[]{:S(2)}) collective-permute-start(bf16[64,1024]{1,0:T(8,128)(2,1)S(1)} %get-tuple-element.38), channel_id=1, source_target_pairs={{0,12},{2,14},{4,0},{6,2},{8,4},{10,6},{12,8},{14,10},{1,13},{3,15... | collective-permute-start | bytes 393224 | tf_op jit(solution)/shard_map/ppermute | solution.py:232
  38.6 1.6 %collective-permute-done.10.refs_2_ = bf16[64,2048]{1,0:T(8,128)(2,1)S(1)} collective-permute-done((bf16[64,2048]{1,0:T(8,128)(2,1)S(1)}, bf16[64,2048]{1,0:T(8,128)(2,1)S(1)}, u32[]{:S(2)}, u32[]{:S(2)}) %collective-permute-start.10) | collective-permute-done | bytes 262176 | tf_op jit(solution)/shard_map/ppermute | solution.py:232
  40.2 1.2 %collective-permute-start.11 = (bf16[64,2048]{1,0:T(8,128)(2,1)S(1)}, bf16[64,2048]{1,0:T(8,128)(2,1)S(1)}, u32[]{:S(2)}, u32[]{:S(2)}) collective-permute-start(bf16[64,2048]{1,0:T(8,128)(2,1)S(1)} %collective-permute-done.10.refs_2_), channel_id=1, source_target_pairs={{0,16},{16,0},{32,48},{48,32},{64,80},{80,64},{96,112},{112,96},{1... | collective-permute-start | bytes 786440 | tf_op jit(solution)/shard_map/ppermute | solution.py:232
  41.5 0.5 collective-permute-done.16.refs_4_
  41.9 1.0 collective-permute-done.12.refs_6_.refs_3_
  42.9 0.2 hadamard_z.3.refs_5_.refs_0_
  43.1 0.5 collective-permute-start.20
  43.6 2.7 %collective-permute-start.19 = (bf16[64,2048]{1,0:T(8,128)(2,1)S(1)}, bf16[64,2048]{1,0:T(8,128)(2,1)S(1)}, u32[]{:S(2)}, u32[]{:S(2)}) collective-permute-start(bf16[64,2048]{1,0:T(8,128)(2,1)S(1)} %hadamard_z.3.refs_5_.refs_0_), channel_id=1, source_target_pairs={{0,64},{16,80},{32,96},{48,112},{64,0},{80,16},{96,32},{112,48},{1... | collective-permute-start | bytes 786440 | tf_op jit(solution)/shard_map/ppermute | solution.py:232
  46.4 1.2 %collective-permute-start.18 = (bf16[64,2048]{1,0:T(8,128)(2,1)S(1)}, bf16[64,2048]{1,0:T(8,128)(2,1)S(1)}, u32[]{:S(2)}, u32[]{:S(2)}) collective-permute-start(bf16[64,2048]{1,0:T(8,128)(2,1)S(1)} %hadamard_z.3.refs_5_.refs_0_), channel_id=1, source_target_pairs={{0,96},{16,112},{32,0},{48,16},{64,32},{80,48},{96,64},{112,80},{1... | collective-permute-start | bytes 786440 | tf_op jit(solution)/shard_map/ppermute | solution.py:232
  47.6 1.2 %collective-permute-start.17 = (bf16[64,2048]{1,0:T(8,128)(2,1)S(1)}, bf16[64,2048]{1,0:T(8,128)(2,1)S(1)}, u32[]{:S(2)}, u32[]{:S(2)}) collective-permute-start(bf16[64,2048]{1,0:T(8,128)(2,1)S(1)} %hadamard_z.3.refs_5_.refs_0_), channel_id=1, source_target_pairs={{0,16},{16,0},{32,48},{48,32},{64,80},{80,64},{96,112},{112,96},{1... | collective-permute-start | bytes 786440 | tf_op jit(solution)/shard_map/ppermute | solution.py:232
  48.8 2.4 %project_column.2.refs_5_ = bf16[256,2048]{1,0:T(8,128)(2,1)S(1)} custom-call(bf16[64,2048]{1,0:T(8,128)(2,1)S(1)} %hadamard_z.2.refs_0_, bf16[64,2048]{1,0:T(8,128)(2,1)S(1)} %collective-permute-done.7.refs_1_, bf16[64,2048]{1,0:T(8,128)(2,1)S(1)} %collective-permute-done.10.refs_2_, bf16[64,2048]{1,0:T(8,128)(2,1)S(1)} %collective-permute-done.8.refs_2_.refs_3_, ...), custom_call_target="tpu_custom_call" | custom-call | flops 10737418240 | bytes 52428800 | tf_op jit(solution)/shard_map/project_column/pallas_call | solution.py:42
  51.2 3.2 %project_mate.2 = (bf16[256,2048]{1,0:T(8,128)(2,1)S(1)}, bf16[64,2048]{1,0:T(8,128)(2,1)S(1)}, bf16[192,2048]{1,0:T(8,128)(2,1)S(1)}) custom-call(bf16[64,2048]{1,0:T(8,128)(2,1)S(1)} %hold.7.refs_0_, bf16[64,2048]{1,0:T(8,128)(2,1)S(1)} %collective-permute-done.9.refs_5_.refs_1_, bf16[64,2048]{1,0:T(8,128)(2,1)S(1)} %collective-permute-done.11.refs_2_, ...), custom_call_target="tpu_custom_call" | custom-call | flops 10737418240 | bytes 62914560 | tf_op jit(solution)/shard_map/project_mate/pallas_call | solution.py:42
  54.4 2.7 %collective-permute-done.20.refs_3_ = bf16[64,2048]{1,0:T(8,128)(2,1)S(1)} collective-permute-done((bf16[64,2048]{1,0:T(8,128)(2,1)S(1)}, bf16[64,2048]{1,0:T(8,128)(2,1)S(1)}, u32[]{:S(2)}, u32[]{:S(2)}) %collective-permute-start.20) | collective-permute-done | bytes 262176 | tf_op jit(solution)/shard_map/ppermute | solution.py:232
  57.2 0.6 collective-permute-done.18.refs_1_
  57.8 1.5 %collective-permute-done.21.refs_1_ = bf16[64,2048]{1,0:T(8,128)(2,1)S(1)} collective-permute-done((bf16[64,2048]{1,0:T(8,128)(2,1)S(1)}, bf16[64,2048]{1,0:T(8,128)(2,1)S(1)}, u32[]{:S(2)}, u32[]{:S(2)}) %collective-permute-start.21) | collective-permute-done | bytes 262176 | tf_op jit(solution)/shard_map/ppermute | solution.py:232
  59.5 1.3 %collective-permute-start.24 = (bf16[64,1024]{1,0:T(8,128)(2,1)S(1)}, bf16[64,1024]{1,0:T(8,128)(2,1)S(1)}, u32[]{:S(2)}, u32[]{:S(2)}) collective-permute-start(bf16[64,1024]{1,0:T(8,128)(2,1)S(1)} %get-tuple-element.43), channel_id=1, source_target_pairs={{0,12},{2,14},{4,0},{6,2},{8,4},{10,6},{12,8},{14,10},{1,13},{3,15... | collective-permute-start | bytes 393224 | tf_op jit(solution)/shard_map/ppermute | solution.py:232
  60.8 0.9 collective-permute-start.23
  61.6 1.2 %collective-permute-start.28 = (bf16[64,2048]{1,0:T(8,128)(2,1)S(1)}, bf16[64,2048]{1,0:T(8,128)(2,1)S(1)}, u32[]{:S(2)}, u32[]{:S(2)}) collective-permute-start(bf16[64,2048]{1,0:T(8,128)(2,1)S(1)} %collective-permute-done.19.refs_2_), channel_id=1, source_target_pairs={{0,16},{16,0},{32,48},{48,32},{64,80},{80,64},{96,112},{112,96},{1... | collective-permute-start | bytes 786440 | tf_op jit(solution)/shard_map/ppermute | solution.py:232
  62.8 1.7 %collective-permute-start.29 = (bf16[64,2048]{1,0:T(8,128)(2,1)S(1)}, bf16[64,2048]{1,0:T(8,128)(2,1)S(1)}, u32[]{:S(2)}, u32[]{:S(2)}) collective-permute-start(bf16[64,2048]{1,0:T(8,128)(2,1)S(1)} %hold.11.refs_0_), channel_id=1, source_target_pairs={{0,32},{16,48},{32,64},{48,80},{64,96},{80,112},{96,0},{112,16},{1... | collective-permute-start | bytes 786440 | tf_op jit(solution)/shard_map/ppermute | solution.py:232
  64.5 1.5 %collective-permute-start.27 = (bf16[64,2048]{1,0:T(8,128)(2,1)S(1)}, bf16[64,2048]{1,0:T(8,128)(2,1)S(1)}, u32[]{:S(2)}, u32[]{:S(2)}) collective-permute-start(bf16[64,2048]{1,0:T(8,128)(2,1)S(1)} %hold.11.refs_0_), channel_id=1, source_target_pairs={{0,96},{16,112},{32,0},{48,16},{64,32},{80,48},{96,64},{112,80},{1... | collective-permute-start | bytes 786440 | tf_op jit(solution)/shard_map/ppermute | solution.py:232
  66.1 1.4 %collective-permute-done.23.refs_2_ = bf16[64,1024]{1,0:T(8,128)(2,1)S(1)} collective-permute-done((bf16[64,1024]{1,0:T(8,128)(2,1)S(1)}, bf16[64,1024]{1,0:T(8,128)(2,1)S(1)}, u32[]{:S(2)}, u32[]{:S(2)}) %collective-permute-start.23) | collective-permute-done | bytes 131104 | tf_op jit(solution)/shard_map/ppermute | solution.py:232
  67.6 1.1 %collective-permute-start.26 = (bf16[64,2048]{1,0:T(8,128)(2,1)S(1)}, bf16[64,2048]{1,0:T(8,128)(2,1)S(1)}, u32[]{:S(2)}, u32[]{:S(2)}) collective-permute-start(bf16[64,2048]{1,0:T(8,128)(2,1)S(1)} %get-tuple-element.45), channel_id=1, source_target_pairs={{0,12},{2,14},{4,0},{6,2},{8,4},{10,6},{12,8},{14,10},{1,13},{3,15... | collective-permute-start | bytes 786440 | tf_op jit(solution)/shard_map/ppermute | solution.py:232
  68.7 1.0 collective-permute-start.25
  69.7 2.4 %project_column.3.refs_5_ = bf16[256,2048]{1,0:T(8,128)(2,1)S(1)} custom-call(bf16[64,2048]{1,0:T(8,128)(2,1)S(1)} %hadamard_z.3.refs_5_.refs_0_, bf16[64,2048]{1,0:T(8,128)(2,1)S(1)} %collective-permute-done.18.refs_1_, bf16[64,2048]{1,0:T(8,128)(2,1)S(1)} %collective-permute-done.19.refs_2_, bf16[64,2048]{1,0:T(8,128)(2,1)S(1)} %collective-permute-done.20.refs_3_, ...), custom_call_target="tpu_custom_call" | custom-call | flops 10737418240 | bytes 52428800 | tf_op jit(solution)/shard_map/project_column/pallas_call | solution.py:42
  72.1 3.1 %project_mate.3 = (bf16[256,2048]{1,0:T(8,128)(2,1)S(1)}, bf16[64,2048]{1,0:T(8,128)(2,1)S(1)}, bf16[192,2048]{1,0:T(8,128)(2,1)S(1)}) custom-call(bf16[64,2048]{1,0:T(8,128)(2,1)S(1)} %hold.11.refs_0_, bf16[64,2048]{1,0:T(8,128)(2,1)S(1)} %collective-permute-done.27.refs_1_, bf16[64,2048]{1,0:T(8,128)(2,1)S(1)} %collective-permute-done.28.refs_2_, ...), custom_call_target="tpu_custom_call" | custom-call | flops 10737418240 | bytes 62914560 | tf_op jit(solution)/shard_map/project_mate/pallas_call | solution.py:42
  75.2 1.6 %collective-permute-done.25.refs_1_.refs_2_ = bf16[64,2048]{1,0:T(8,128)(2,1)S(1)} collective-permute-done((bf16[64,2048]{1,0:T(8,128)(2,1)S(1)}, bf16[64,2048]{1,0:T(8,128)(2,1)S(1)}, u32[]{:S(2)}, u32[]{:S(2)}) %collective-permute-start.25) | collective-permute-done | bytes 262176 | tf_op jit(solution)/shard_map/ppermute | solution.py:232
  76.8 1.5 %collective-permute-done.30.refs_1_ = bf16[64,2048]{1,0:T(8,128)(2,1)S(1)} collective-permute-done((bf16[64,2048]{1,0:T(8,128)(2,1)S(1)}, bf16[64,2048]{1,0:T(8,128)(2,1)S(1)}, u32[]{:S(2)}, u32[]{:S(2)}) %collective-permute-start.30) | collective-permute-done | bytes 262176 | tf_op jit(solution)/shard_map/ppermute | solution.py:232
  78.5 0.8 collective-permute-start.34
  79.3 1.3 %collective-permute-start.33 = (bf16[64,1024]{1,0:T(8,128)(2,1)S(1)}, bf16[64,1024]{1,0:T(8,128)(2,1)S(1)}, u32[]{:S(2)}, u32[]{:S(2)}) collective-permute-start(bf16[64,1024]{1,0:T(8,128)(2,1)S(1)} %get-tuple-element.48.refs_5_), channel_id=1, source_target_pairs={{0,4},{2,6},{4,8},{6,10},{8,12},{10,14},{12,0},{14,2},{1,5},{3,7},... | collective-permute-start | bytes 393224 | tf_op jit(solution)/shard_map/ppermute | solution.py:232
  80.8 1.3 %collective-permute-start.31 = (bf16[64,2048]{1,0:T(8,128)(2,1)S(1)}, bf16[64,2048]{1,0:T(8,128)(2,1)S(1)}, u32[]{:S(2)}, u32[]{:S(2)}) collective-permute-start(bf16[64,2048]{1,0:T(8,128)(2,1)S(1)} %get-tuple-element.49.refs_5_.refs_0_), channel_id=1, source_target_pairs={{0,1},{2,3},{4,5},{6,7},{8,9},{10,11},{12,13},{14,15},{16,17},{18,... | collective-permute-start | bytes 786440 | tf_op jit(solution)/shard_map/ppermute | solution.py:241
  82.1 2.3 %collective-permute-done.34.refs_3_ = bf16[64,1024]{1,0:T(8,128)(2,1)S(1)} collective-permute-done((bf16[64,1024]{1,0:T(8,128)(2,1)S(1)}, bf16[64,1024]{1,0:T(8,128)(2,1)S(1)}, u32[]{:S(2)}, u32[]{:S(2)}) %collective-permute-start.34) | collective-permute-done | bytes 131104 | tf_op jit(solution)/shard_map/ppermute | solution.py:232
  84.4 1.6 %collective-permute-done.33.refs_2_ = bf16[64,1024]{1,0:T(8,128)(2,1)S(1)} collective-permute-done((bf16[64,1024]{1,0:T(8,128)(2,1)S(1)}, bf16[64,1024]{1,0:T(8,128)(2,1)S(1)}, u32[]{:S(2)}, u32[]{:S(2)}) %collective-permute-start.33) | collective-permute-done | bytes 131104 | tf_op jit(solution)/shard_map/ppermute | solution.py:232
  86.2 0.2 collective-permute-start.35
  86.4 3.1 %collective-permute-start.36 = (bf16[32,2048]{1,0:T(8,128)(2,1)S(1)}, bf16[32,2048]{1,0:T(8,128)(2,1)S(1)}, u32[]{:S(2)}, u32[]{:S(2)}) collective-permute-start(bf16[32,2048]{1,0:T(8,128)(2,1)S(1)} %get-tuple-element.54), channel_id=1, source_target_pairs={{0,12},{2,14},{4,0},{6,2},{8,4},{10,6},{12,8},{14,10},{1,13},{3,15... | collective-permute-start | bytes 393224 | tf_op jit(solution)/shard_map/ppermute | solution.py:232
  89.5 3.2 %collective-permute-start.39 = (bf16[32,2048]{1,0:T(8,128)(2,1)S(1)}, bf16[32,2048]{1,0:T(8,128)(2,1)S(1)}, u32[]{:S(2)}, u32[]{:S(2)}) collective-permute-start(bf16[32,2048]{1,0:T(8,128)(2,1)S(1)} %get-tuple-element.58), channel_id=1, source_target_pairs={{0,12},{2,14},{4,0},{6,2},{8,4},{10,6},{12,8},{14,10},{1,13},{3,15... | collective-permute-start | bytes 393224 | tf_op jit(solution)/shard_map/ppermute | solution.py:232
  92.7 0.2 collective-permute-done.35.refs_2_
  93.0 1.3 %collective-permute-start.37 = (bf16[32,2048]{1,0:T(8,128)(2,1)S(1)}, bf16[32,2048]{1,0:T(8,128)(2,1)S(1)}, u32[]{:S(2)}, u32[]{:S(2)}) collective-permute-start(bf16[32,2048]{1,0:T(8,128)(2,1)S(1)} %get-tuple-element.55.refs_3_.refs_5_), channel_id=1, source_target_pairs={{0,1},{2,3},{4,5},{6,7},{8,9},{10,11},{12,13},{14,15},{16,17},{18,... | collective-permute-start | bytes 393224 | tf_op jit(solution)/shard_map/ppermute | solution.py:241
  94.3 1.4 %collective-permute-done.38.refs_2_ = bf16[32,2048]{1,0:T(8,128)(2,1)S(1)} collective-permute-done((bf16[32,2048]{1,0:T(8,128)(2,1)S(1)}, bf16[32,2048]{1,0:T(8,128)(2,1)S(1)}, u32[]{:S(2)}, u32[]{:S(2)}) %collective-permute-start.38) | collective-permute-done | bytes 131104 | tf_op jit(solution)/shard_map/ppermute | solution.py:232
  95.8 1.3 %collective-permute-start.40 = (bf16[32,2048]{1,0:T(8,128)(2,1)S(1)}, bf16[32,2048]{1,0:T(8,128)(2,1)S(1)}, u32[]{:S(2)}, u32[]{:S(2)}) collective-permute-start(bf16[32,2048]{1,0:T(8,128)(2,1)S(1)} %get-tuple-element.59.refs_1_), channel_id=1, source_target_pairs={{0,1},{2,3},{4,5},{6,7},{8,9},{10,11},{12,13},{14,15},{16,17},{18,... | collective-permute-start | bytes 393224 | tf_op jit(solution)/shard_map/ppermute | solution.py:241
  97.1 5.5 %collective-permute-done.37.refs_5_ = bf16[32,2048]{1,0:T(8,128)(2,1)S(1)} collective-permute-done((bf16[32,2048]{1,0:T(8,128)(2,1)S(1)}, bf16[32,2048]{1,0:T(8,128)(2,1)S(1)}, u32[]{:S(2)}, u32[]{:S(2)}) %collective-permute-start.37) | collective-permute-done | bytes 131104 | tf_op jit(solution)/shard_map/ppermute | solution.py:241
  102.6 1.5 %collective-permute-done.40.refs_3_ = bf16[32,2048]{1,0:T(8,128)(2,1)S(1)} collective-permute-done((bf16[32,2048]{1,0:T(8,128)(2,1)S(1)}, bf16[32,2048]{1,0:T(8,128)(2,1)S(1)}, u32[]{:S(2)}, u32[]{:S(2)}) %collective-permute-start.40) | collective-permute-done | bytes 131104 | tf_op jit(solution)/shard_map/ppermute | solution.py:241
  104.1 0.8 end.1
  (56 shorter events, 1.6 us)
Async XLA Ops:
  0.0 1.0 copy-start.3
  1.0 0.7 copy-start.4
  2.5 1.6 %collective-permute-start = (bf16[64,2048]{1,0:T(8,128)(2,1)S(1)}, bf16[64,2048]{1,0:T(8,128)(2,1)S(1)}, u32[]{:S(2)}, u32[]{:S(2)}) collective-permute-start(bf16[64,2048]{1,0:T(8,128)(2,1)S(1)} %get-tuple-element.33.refs_0_), channel_id=1, source_target_pairs={{0,2},{2,0},{4,6},{6,4},{8,10},{10,8},{12,14},{14,12},{1,3},{3,1},... | collective-permute-start | bytes 786440 | tf_op jit(solution)/shard_map/ppermute | solution.py:232
  4.2 10.7 %collective-permute-start.2 = (bf16[64,2048]{1,0:T(8,128)(2,1)S(1)}, bf16[64,2048]{1,0:T(8,128)(2,1)S(1)}, u32[]{:S(2)}, u32[]{:S(2)}) collective-permute-start(bf16[64,2048]{1,0:T(8,128)(2,1)S(1)} %hadamard_core.2.refs_1_.refs_0_), channel_id=1, source_target_pairs={{0,4},{2,6},{4,8},{6,10},{8,12},{10,14},{12,0},{14,2},{1,5},{3,7},... | collective-permute-start | bytes 786440 | tf_op jit(solution)/shard_map/ppermute | solution.py:232
  6.2 8.7 %collective-permute-start.1 = (bf16[64,2048]{1,0:T(8,128)(2,1)S(1)}, bf16[64,2048]{1,0:T(8,128)(2,1)S(1)}, u32[]{:S(2)}, u32[]{:S(2)}) collective-permute-start(bf16[64,2048]{1,0:T(8,128)(2,1)S(1)} %hadamard_core.2.refs_1_.refs_0_), channel_id=1, source_target_pairs={{0,12},{2,14},{4,0},{6,2},{8,4},{10,6},{12,8},{14,10},{1,13},{3,15... | collective-permute-start | bytes 786440 | tf_op jit(solution)/shard_map/ppermute | solution.py:232
  8.4 9.9 %collective-permute-start.5 = (bf16[64,2048]{1,0:T(8,128)(2,1)S(1)}, bf16[64,2048]{1,0:T(8,128)(2,1)S(1)}, u32[]{:S(2)}, u32[]{:S(2)}) collective-permute-start(bf16[64,2048]{1,0:T(8,128)(2,1)S(1)} %get-tuple-element.36.refs_0_), channel_id=1, source_target_pairs={{0,2},{2,0},{4,6},{6,4},{8,10},{10,8},{12,14},{14,12},{1,3},{3,1},... | collective-permute-start | bytes 786440 | tf_op jit(solution)/shard_map/ppermute | solution.py:232
  8.4 3.4 %copy-start = (bf16[1,2048,2048]{2,1,0:T(8,128)(2,1)S(1)}, bf16[1,2048,2048]{2,1,0:T(8,128)(2,1)}, u32[]{:S(2)}) copy-start(bf16[1,2048,2048]{2,1,0:T(8,128)(2,1)} %refs_4_.10) | copy-start | bytes 25165828
  11.8 37.0 %copy-start.1 = (bf16[1,2048,2048]{2,1,0:T(8,128)(2,1)S(1)}, bf16[1,2048,2048]{2,1,0:T(8,128)(2,1)}, u32[]{:S(2)}) copy-start(bf16[1,2048,2048]{2,1,0:T(8,128)(2,1)} %refs_4_.10) | copy-start | bytes 25165828
  14.9 6.3 %collective-permute-start.3 = (bf16[64,1024]{1,0:T(8,128)(2,1)S(1)}, bf16[64,1024]{1,0:T(8,128)(2,1)S(1)}, u32[]{:S(2)}, u32[]{:S(2)}) collective-permute-start(bf16[64,1024]{1,0:T(8,128)(2,1)S(1)} %get-tuple-element.34), channel_id=1, source_target_pairs={{0,4},{2,6},{4,8},{6,10},{8,12},{10,14},{12,0},{14,2},{1,5},{3,7},... | collective-permute-start | bytes 393224 | tf_op jit(solution)/shard_map/ppermute | solution.py:232
  16.2 5.0 %collective-permute-start.4 = (bf16[64,1024]{1,0:T(8,128)(2,1)S(1)}, bf16[64,1024]{1,0:T(8,128)(2,1)S(1)}, u32[]{:S(2)}, u32[]{:S(2)}) collective-permute-start(bf16[64,1024]{1,0:T(8,128)(2,1)S(1)} %get-tuple-element.35), channel_id=1, source_target_pairs={{0,12},{2,14},{4,0},{6,2},{8,4},{10,6},{12,8},{14,10},{1,13},{3,15... | collective-permute-start | bytes 393224 | tf_op jit(solution)/shard_map/ppermute | solution.py:232
  21.4 8.3 %collective-permute-start.8 = (bf16[64,2048]{1,0:T(8,128)(2,1)S(1)}, bf16[64,2048]{1,0:T(8,128)(2,1)S(1)}, u32[]{:S(2)}, u32[]{:S(2)}) collective-permute-start(bf16[64,2048]{1,0:T(8,128)(2,1)S(1)} %hadamard_z.2.refs_0_), channel_id=1, source_target_pairs={{0,32},{16,48},{32,64},{48,80},{64,96},{80,112},{96,0},{112,16},{1... | collective-permute-start | bytes 786440 | tf_op jit(solution)/shard_map/ppermute | solution.py:232
  23.1 8.6 %collective-permute-start.7 = (bf16[64,2048]{1,0:T(8,128)(2,1)S(1)}, bf16[64,2048]{1,0:T(8,128)(2,1)S(1)}, u32[]{:S(2)}, u32[]{:S(2)}) collective-permute-start(bf16[64,2048]{1,0:T(8,128)(2,1)S(1)} %hadamard_z.2.refs_0_), channel_id=1, source_target_pairs={{0,96},{16,112},{32,0},{48,16},{64,32},{80,48},{96,64},{112,80},{1... | collective-permute-start | bytes 786440 | tf_op jit(solution)/shard_map/ppermute | solution.py:232
  24.8 6.9 %collective-permute-start.6 = (bf16[64,2048]{1,0:T(8,128)(2,1)S(1)}, bf16[64,2048]{1,0:T(8,128)(2,1)S(1)}, u32[]{:S(2)}, u32[]{:S(2)}) collective-permute-start(bf16[64,2048]{1,0:T(8,128)(2,1)S(1)} %hadamard_z.2.refs_0_), channel_id=1, source_target_pairs={{0,16},{16,0},{32,48},{48,32},{64,80},{80,64},{96,112},{112,96},{1... | collective-permute-start | bytes 786440 | tf_op jit(solution)/shard_map/ppermute | solution.py:232
  26.0 8.9 %collective-permute-start.14 = (bf16[64,2048]{1,0:T(8,128)(2,1)S(1)}, bf16[64,2048]{1,0:T(8,128)(2,1)S(1)}, u32[]{:S(2)}, u32[]{:S(2)}) collective-permute-start(bf16[64,2048]{1,0:T(8,128)(2,1)S(1)} %hadamard_core.3.refs_5_.refs_0_), channel_id=1, source_target_pairs={{0,4},{2,6},{4,8},{6,10},{8,12},{10,14},{12,0},{14,2},{1,5},{3,7},... | collective-permute-start | bytes 786440 | tf_op jit(solution)/shard_map/ppermute | solution.py:232
  27.6 7.3 %collective-permute-start.13 = (bf16[64,2048]{1,0:T(8,128)(2,1)S(1)}, bf16[64,2048]{1,0:T(8,128)(2,1)S(1)}, u32[]{:S(2)}, u32[]{:S(2)}) collective-permute-start(bf16[64,2048]{1,0:T(8,128)(2,1)S(1)} %hadamard_core.3.refs_5_.refs_0_), channel_id=1, source_target_pairs={{0,12},{2,14},{4,0},{6,2},{8,4},{10,6},{12,8},{14,10},{1,13},{3,15... | collective-permute-start | bytes 786440 | tf_op jit(solution)/shard_map/ppermute | solution.py:232
  29.7 10.4 %collective-permute-start.10 = (bf16[64,2048]{1,0:T(8,128)(2,1)S(1)}, bf16[64,2048]{1,0:T(8,128)(2,1)S(1)}, u32[]{:S(2)}, u32[]{:S(2)}) collective-permute-start(bf16[64,2048]{1,0:T(8,128)(2,1)S(1)} %hadamard_z.2.refs_0_), channel_id=1, source_target_pairs={{0,64},{16,80},{32,96},{48,112},{64,0},{80,16},{96,32},{112,48},{1... | collective-permute-start | bytes 786440 | tf_op jit(solution)/shard_map/ppermute | solution.py:232
  31.7 11.3 %collective-permute-start.12 = (bf16[64,2048]{1,0:T(8,128)(2,1)S(1)}, bf16[64,2048]{1,0:T(8,128)(2,1)S(1)}, u32[]{:S(2)}, u32[]{:S(2)}) collective-permute-start(bf16[64,2048]{1,0:T(8,128)(2,1)S(1)} %hold.7.refs_0_), channel_id=1, source_target_pairs={{0,32},{16,48},{32,64},{48,80},{64,96},{80,112},{96,0},{112,16},{1... | collective-permute-start | bytes 786440 | tf_op jit(solution)/shard_map/ppermute | solution.py:232
  32.3 10.6 %collective-permute-start.9 = (bf16[64,2048]{1,0:T(8,128)(2,1)S(1)}, bf16[64,2048]{1,0:T(8,128)(2,1)S(1)}, u32[]{:S(2)}, u32[]{:S(2)}) collective-permute-start(bf16[64,2048]{1,0:T(8,128)(2,1)S(1)} %hold.7.refs_0_), channel_id=1, source_target_pairs={{0,96},{16,112},{32,0},{48,16},{64,32},{80,48},{96,64},{112,80},{1... | collective-permute-start | bytes 786440 | tf_op jit(solution)/shard_map/ppermute | solution.py:232
  34.9 6.5 %collective-permute-start.15 = (bf16[64,1024]{1,0:T(8,128)(2,1)S(1)}, bf16[64,1024]{1,0:T(8,128)(2,1)S(1)}, u32[]{:S(2)}, u32[]{:S(2)}) collective-permute-start(bf16[64,1024]{1,0:T(8,128)(2,1)S(1)} %get-tuple-element.37), channel_id=1, source_target_pairs={{0,4},{2,6},{4,8},{6,10},{8,12},{10,14},{12,0},{14,2},{1,5},{3,7},... | collective-permute-start | bytes 393224 | tf_op jit(solution)/shard_map/ppermute | solution.py:232
  36.9 5.0 %collective-permute-start.16 = (bf16[64,1024]{1,0:T(8,128)(2,1)S(1)}, bf16[64,1024]{1,0:T(8,128)(2,1)S(1)}, u32[]{:S(2)}, u32[]{:S(2)}) collective-permute-start(bf16[64,1024]{1,0:T(8,128)(2,1)S(1)} %get-tuple-element.38), channel_id=1, source_target_pairs={{0,12},{2,14},{4,0},{6,2},{8,4},{10,6},{12,8},{14,10},{1,13},{3,15... | collective-permute-start | bytes 393224 | tf_op jit(solution)/shard_map/ppermute | solution.py:232
  40.2 11.0 %collective-permute-start.11 = (bf16[64,2048]{1,0:T(8,128)(2,1)S(1)}, bf16[64,2048]{1,0:T(8,128)(2,1)S(1)}, u32[]{:S(2)}, u32[]{:S(2)}) collective-permute-start(bf16[64,2048]{1,0:T(8,128)(2,1)S(1)} %collective-permute-done.10.refs_2_), channel_id=1, source_target_pairs={{0,16},{16,0},{32,48},{48,32},{64,80},{80,64},{96,112},{112,96},{1... | collective-permute-start | bytes 786440 | tf_op jit(solution)/shard_map/ppermute | solution.py:232
  43.1 14.0 %collective-permute-start.20 = (bf16[64,2048]{1,0:T(8,128)(2,1)S(1)}, bf16[64,2048]{1,0:T(8,128)(2,1)S(1)}, u32[]{:S(2)}, u32[]{:S(2)}) collective-permute-start(bf16[64,2048]{1,0:T(8,128)(2,1)S(1)} %hadamard_z.3.refs_5_.refs_0_), channel_id=1, source_target_pairs={{0,32},{16,48},{32,64},{48,80},{64,96},{80,112},{96,0},{112,16},{1... | collective-permute-start | bytes 786440 | tf_op jit(solution)/shard_map/ppermute | solution.py:232
  43.6 13.5 %collective-permute-start.19 = (bf16[64,2048]{1,0:T(8,128)(2,1)S(1)}, bf16[64,2048]{1,0:T(8,128)(2,1)S(1)}, u32[]{:S(2)}, u32[]{:S(2)}) collective-permute-start(bf16[64,2048]{1,0:T(8,128)(2,1)S(1)} %hadamard_z.3.refs_5_.refs_0_), channel_id=1, source_target_pairs={{0,64},{16,80},{32,96},{48,112},{64,0},{80,16},{96,32},{112,48},{1... | collective-permute-start | bytes 786440 | tf_op jit(solution)/shard_map/ppermute | solution.py:232
  46.4 11.4 %collective-permute-start.18 = (bf16[64,2048]{1,0:T(8,128)(2,1)S(1)}, bf16[64,2048]{1,0:T(8,128)(2,1)S(1)}, u32[]{:S(2)}, u32[]{:S(2)}) collective-permute-start(bf16[64,2048]{1,0:T(8,128)(2,1)S(1)} %hadamard_z.3.refs_5_.refs_0_), channel_id=1, source_target_pairs={{0,96},{16,112},{32,0},{48,16},{64,32},{80,48},{96,64},{112,80},{1... | collective-permute-start | bytes 786440 | tf_op jit(solution)/shard_map/ppermute | solution.py:232
  47.6 10.2 %collective-permute-start.17 = (bf16[64,2048]{1,0:T(8,128)(2,1)S(1)}, bf16[64,2048]{1,0:T(8,128)(2,1)S(1)}, u32[]{:S(2)}, u32[]{:S(2)}) collective-permute-start(bf16[64,2048]{1,0:T(8,128)(2,1)S(1)} %hadamard_z.3.refs_5_.refs_0_), channel_id=1, source_target_pairs={{0,16},{16,0},{32,48},{48,32},{64,80},{80,64},{96,112},{112,96},{1... | collective-permute-start | bytes 786440 | tf_op jit(solution)/shard_map/ppermute | solution.py:232
  57.8 1.5 %collective-permute-start.21 = (bf16[64,2048]{1,0:T(8,128)(2,1)S(1)}, bf16[64,2048]{1,0:T(8,128)(2,1)S(1)}, u32[]{:S(2)}, u32[]{:S(2)}) collective-permute-start(bf16[64,2048]{1,0:T(8,128)(2,1)S(1)} %hold.9), channel_id=1, source_target_pairs={{0,2},{2,0},{4,6},{6,4},{8,10},{10,8},{12,14},{14,12},{1,3},{3,1},... | collective-permute-start | bytes 786440 | tf_op jit(solution)/shard_map/ppermute | solution.py:232
  59.3 3.5 %collective-permute-start.22 = (bf16[192,2048]{1,0:T(8,128)(2,1)S(1)}, bf16[192,2048]{1,0:T(8,128)(2,1)S(1)}, u32[]{:S(2)}, u32[]{:S(2)}) collective-permute-start(bf16[192,2048]{1,0:T(8,128)(2,1)S(1)} %hold.10), channel_id=1, source_target_pairs={{0,2},{2,0},{4,6},{6,4},{8,10},{10,8},{12,14},{14,12},{1,3},{3,1},... | collective-permute-start | bytes 2359304 | tf_op jit(solution)/shard_map/ppermute | solution.py:232
  59.5 6.6 %collective-permute-start.24 = (bf16[64,1024]{1,0:T(8,128)(2,1)S(1)}, bf16[64,1024]{1,0:T(8,128)(2,1)S(1)}, u32[]{:S(2)}, u32[]{:S(2)}) collective-permute-start(bf16[64,1024]{1,0:T(8,128)(2,1)S(1)} %get-tuple-element.43), channel_id=1, source_target_pairs={{0,12},{2,14},{4,0},{6,2},{8,4},{10,6},{12,8},{14,10},{1,13},{3,15... | collective-permute-start | bytes 393224 | tf_op jit(solution)/shard_map/ppermute | solution.py:232
  60.8 6.7 %collective-permute-start.23 = (bf16[64,1024]{1,0:T(8,128)(2,1)S(1)}, bf16[64,1024]{1,0:T(8,128)(2,1)S(1)}, u32[]{:S(2)}, u32[]{:S(2)}) collective-permute-start(bf16[64,1024]{1,0:T(8,128)(2,1)S(1)} %get-tuple-element.42.refs_1_), channel_id=1, source_target_pairs={{0,4},{2,6},{4,8},{6,10},{8,12},{10,14},{12,0},{14,2},{1,5},{3,7},... | collective-permute-start | bytes 393224 | tf_op jit(solution)/shard_map/ppermute | solution.py:232
  61.6 10.5 %collective-permute-start.28 = (bf16[64,2048]{1,0:T(8,128)(2,1)S(1)}, bf16[64,2048]{1,0:T(8,128)(2,1)S(1)}, u32[]{:S(2)}, u32[]{:S(2)}) collective-permute-start(bf16[64,2048]{1,0:T(8,128)(2,1)S(1)} %collective-permute-done.19.refs_2_), channel_id=1, source_target_pairs={{0,16},{16,0},{32,48},{48,32},{64,80},{80,64},{96,112},{112,96},{1... | collective-permute-start | bytes 786440 | tf_op jit(solution)/shard_map/ppermute | solution.py:232
  62.8 9.3 %collective-permute-start.29 = (bf16[64,2048]{1,0:T(8,128)(2,1)S(1)}, bf16[64,2048]{1,0:T(8,128)(2,1)S(1)}, u32[]{:S(2)}, u32[]{:S(2)}) collective-permute-start(bf16[64,2048]{1,0:T(8,128)(2,1)S(1)} %hold.11.refs_0_), channel_id=1, source_target_pairs={{0,32},{16,48},{32,64},{48,80},{64,96},{80,112},{96,0},{112,16},{1... | collective-permute-start | bytes 786440 | tf_op jit(solution)/shard_map/ppermute | solution.py:232
  64.5 7.6 %collective-permute-start.27 = (bf16[64,2048]{1,0:T(8,128)(2,1)S(1)}, bf16[64,2048]{1,0:T(8,128)(2,1)S(1)}, u32[]{:S(2)}, u32[]{:S(2)}) collective-permute-start(bf16[64,2048]{1,0:T(8,128)(2,1)S(1)} %hold.11.refs_0_), channel_id=1, source_target_pairs={{0,96},{16,112},{32,0},{48,16},{64,32},{80,48},{96,64},{112,80},{1... | collective-permute-start | bytes 786440 | tf_op jit(solution)/shard_map/ppermute | solution.py:232
  67.6 7.6 %collective-permute-start.26 = (bf16[64,2048]{1,0:T(8,128)(2,1)S(1)}, bf16[64,2048]{1,0:T(8,128)(2,1)S(1)}, u32[]{:S(2)}, u32[]{:S(2)}) collective-permute-start(bf16[64,2048]{1,0:T(8,128)(2,1)S(1)} %get-tuple-element.45), channel_id=1, source_target_pairs={{0,12},{2,14},{4,0},{6,2},{8,4},{10,6},{12,8},{14,10},{1,13},{3,15... | collective-permute-start | bytes 786440 | tf_op jit(solution)/shard_map/ppermute | solution.py:232
  68.7 8.1 %collective-permute-start.25 = (bf16[64,2048]{1,0:T(8,128)(2,1)S(1)}, bf16[64,2048]{1,0:T(8,128)(2,1)S(1)}, u32[]{:S(2)}, u32[]{:S(2)}) collective-permute-start(bf16[64,2048]{1,0:T(8,128)(2,1)S(1)} %get-tuple-element.44.refs_5_), channel_id=1, source_target_pairs={{0,4},{2,6},{4,8},{6,10},{8,12},{10,14},{12,0},{14,2},{1,5},{3,7},... | collective-permute-start | bytes 786440 | tf_op jit(solution)/shard_map/ppermute | solution.py:232
  72.1 8.6 %copy-start.2 = (bf16[128,2048]{1,0:T(8,128)(2,1)S(1)}, bf16[128,2048]{1,0:T(8,128)(2,1)}, u32[]{:S(2)}) copy-start(bf16[128,2048]{1,0:T(8,128)(2,1)} %refs_4_.13) | copy-start | bytes 1572868
  76.8 1.5 %collective-permute-start.30 = (bf16[64,2048]{1,0:T(8,128)(2,1)S(1)}, bf16[64,2048]{1,0:T(8,128)(2,1)S(1)}, u32[]{:S(2)}, u32[]{:S(2)}) collective-permute-start(bf16[64,2048]{1,0:T(8,128)(2,1)S(1)} %hold.12), channel_id=1, source_target_pairs={{0,2},{2,0},{4,6},{6,4},{8,10},{10,8},{12,14},{14,12},{1,3},{3,1},... | collective-permute-start | bytes 786440 | tf_op jit(solution)/shard_map/ppermute | solution.py:232
  78.3 7.7 %collective-permute-start.32 = (bf16[192,2048]{1,0:T(8,128)(2,1)S(1)}, bf16[192,2048]{1,0:T(8,128)(2,1)S(1)}, u32[]{:S(2)}, u32[]{:S(2)}) collective-permute-start(bf16[192,2048]{1,0:T(8,128)(2,1)S(1)} %hold.13), channel_id=1, source_target_pairs={{0,2},{2,0},{4,6},{6,4},{8,10},{10,8},{12,14},{14,12},{1,3},{3,1},... | collective-permute-start | bytes 2359304 | tf_op jit(solution)/shard_map/ppermute | solution.py:232
  78.5 5.8 %collective-permute-start.34 = (bf16[64,1024]{1,0:T(8,128)(2,1)S(1)}, bf16[64,1024]{1,0:T(8,128)(2,1)S(1)}, u32[]{:S(2)}, u32[]{:S(2)}) collective-permute-start(bf16[64,1024]{1,0:T(8,128)(2,1)S(1)} %get-tuple-element.52), channel_id=1, source_target_pairs={{0,12},{2,14},{4,0},{6,2},{8,4},{10,6},{12,8},{14,10},{1,13},{3,15... | collective-permute-start | bytes 393224 | tf_op jit(solution)/shard_map/ppermute | solution.py:232
  79.3 6.7 %collective-permute-start.33 = (bf16[64,1024]{1,0:T(8,128)(2,1)S(1)}, bf16[64,1024]{1,0:T(8,128)(2,1)S(1)}, u32[]{:S(2)}, u32[]{:S(2)}) collective-permute-start(bf16[64,1024]{1,0:T(8,128)(2,1)S(1)} %get-tuple-element.48.refs_5_), channel_id=1, source_target_pairs={{0,4},{2,6},{4,8},{6,10},{8,12},{10,14},{12,0},{14,2},{1,5},{3,7},... | collective-permute-start | bytes 393224 | tf_op jit(solution)/shard_map/ppermute | solution.py:232
  80.8 11.9 %collective-permute-start.31 = (bf16[64,2048]{1,0:T(8,128)(2,1)S(1)}, bf16[64,2048]{1,0:T(8,128)(2,1)S(1)}, u32[]{:S(2)}, u32[]{:S(2)}) collective-permute-start(bf16[64,2048]{1,0:T(8,128)(2,1)S(1)} %get-tuple-element.49.refs_5_.refs_0_), channel_id=1, source_target_pairs={{0,1},{2,3},{4,5},{6,7},{8,9},{10,11},{12,13},{14,15},{16,17},{18,... | collective-permute-start | bytes 786440 | tf_op jit(solution)/shard_map/ppermute | solution.py:241
  86.2 6.7 %collective-permute-start.35 = (bf16[32,2048]{1,0:T(8,128)(2,1)S(1)}, bf16[32,2048]{1,0:T(8,128)(2,1)S(1)}, u32[]{:S(2)}, u32[]{:S(2)}) collective-permute-start(bf16[32,2048]{1,0:T(8,128)(2,1)S(1)} %get-tuple-element.53), channel_id=1, source_target_pairs={{0,4},{2,6},{4,8},{6,10},{8,12},{10,14},{12,0},{14,2},{1,5},{3,7},... | collective-permute-start | bytes 393224 | tf_op jit(solution)/shard_map/ppermute | solution.py:232
  86.4 6.5 %collective-permute-start.36 = (bf16[32,2048]{1,0:T(8,128)(2,1)S(1)}, bf16[32,2048]{1,0:T(8,128)(2,1)S(1)}, u32[]{:S(2)}, u32[]{:S(2)}) collective-permute-start(bf16[32,2048]{1,0:T(8,128)(2,1)S(1)} %get-tuple-element.54), channel_id=1, source_target_pairs={{0,12},{2,14},{4,0},{6,2},{8,4},{10,6},{12,8},{14,10},{1,13},{3,15... | collective-permute-start | bytes 393224 | tf_op jit(solution)/shard_map/ppermute | solution.py:232
  89.5 6.2 %collective-permute-start.38 = (bf16[32,2048]{1,0:T(8,128)(2,1)S(1)}, bf16[32,2048]{1,0:T(8,128)(2,1)S(1)}, u32[]{:S(2)}, u32[]{:S(2)}) collective-permute-start(bf16[32,2048]{1,0:T(8,128)(2,1)S(1)} %get-tuple-element.57), channel_id=1, source_target_pairs={{0,4},{2,6},{4,8},{6,10},{8,12},{10,14},{12,0},{14,2},{1,5},{3,7},... | collective-permute-start | bytes 393224 | tf_op jit(solution)/shard_map/ppermute | solution.py:232
  89.5 6.2 %collective-permute-start.39 = (bf16[32,2048]{1,0:T(8,128)(2,1)S(1)}, bf16[32,2048]{1,0:T(8,128)(2,1)S(1)}, u32[]{:S(2)}, u32[]{:S(2)}) collective-permute-start(bf16[32,2048]{1,0:T(8,128)(2,1)S(1)} %get-tuple-element.58), channel_id=1, source_target_pairs={{0,12},{2,14},{4,0},{6,2},{8,4},{10,6},{12,8},{14,10},{1,13},{3,15... | collective-permute-start | bytes 393224 | tf_op jit(solution)/shard_map/ppermute | solution.py:232
  93.0 9.6 %collective-permute-start.37 = (bf16[32,2048]{1,0:T(8,128)(2,1)S(1)}, bf16[32,2048]{1,0:T(8,128)(2,1)S(1)}, u32[]{:S(2)}, u32[]{:S(2)}) collective-permute-start(bf16[32,2048]{1,0:T(8,128)(2,1)S(1)} %get-tuple-element.55.refs_3_.refs_5_), channel_id=1, source_target_pairs={{0,1},{2,3},{4,5},{6,7},{8,9},{10,11},{12,13},{14,15},{16,17},{18,... | collective-permute-start | bytes 393224 | tf_op jit(solution)/shard_map/ppermute | solution.py:241
  95.8 8.4 %collective-permute-start.40 = (bf16[32,2048]{1,0:T(8,128)(2,1)S(1)}, bf16[32,2048]{1,0:T(8,128)(2,1)S(1)}, u32[]{:S(2)}, u32[]{:S(2)}) collective-permute-start(bf16[32,2048]{1,0:T(8,128)(2,1)S(1)} %get-tuple-element.59.refs_1_), channel_id=1, source_target_pairs={{0,1},{2,3},{4,5},{6,7},{8,9},{10,11},{12,13},{14,15},{16,17},{18,... | collective-permute-start | bytes 393224 | tf_op jit(solution)/shard_map/ppermute | solution.py:241

commit v9 on v8

--- a/solution.py
+++ b/solution.py
@@ -238,7 +238,7 @@
         return move(value, "tensor", lambda i: i ^ 1)
 
     def pipe(value):
-        return lax.ppermute(value, "pipe", [(0, 1)])
+        return lax.ppermute(value, "pipe", [(0, 1), (1, 0)])
 
     def pair(mine, other, behind=()):
         return call("hadamard_core", pair_kernel, (mine, other), shape(*mine.shape), behind)

time: 105 us -> 104 us (level)
  starting transfers between devices: 52.4 us -> 51.3 us
    ppermute x3, waiting for transfers between devices: 6.98 us -> 5.46 us  [pipe(): return lax.ppermute(value, 'pipe', [(0, 1), (1, 0)])]
    ppermute x3, starting transfers between devices: 3.88 us -> 2.77 us  [pipe(): return lax.ppermute(value, 'pipe', [(0, 1), (1, 0)])]
where the time goes in v9:
time: 104 us; the launch traced here: 103 us
  starting transfers between devices  51.3 us (49%)
  waiting for transfers between devices  32.5 us (31%)
  Pallas kernels  14 us (13%)
  local copies, waits for them, and re-layouts  5.13 us (5%)
    ppermute x38, starting transfers between devices, move(): lax.ppermute(value, axis, [(i, target(i)) for i in range(lax.axis_size(ax...  48.6 us
    ppermute x38, waiting for transfers between devices, move(): lax.ppermute(value, axis, [(i, target(i)) for i in range(lax.axis_size(ax...  27 us
    pallas_call x21, Pallas kernels, call(): pl.pallas_call(lambda *refs: kernel(*refs[:count], *refs[count + len(behi...  14 us
    ppermute x3, waiting for transfers between devices, pipe(): return lax.ppermute(value, 'pipe', [(0, 1), (1, 0)])  5.46 us
    unnamed x10, local copies, waits for them, and re-layouts  5.13 us
    ppermute x3, starting transfers between devices, pipe(): return lax.ppermute(value, 'pipe', [(0, 1), (1, 0)])  2.77 us
  transfers between devices with their start and end apart: 41, of which 20 were waited for; matrix products, arithmetic and copies ran while one was open for 0% of the time, Pallas kernels for 12%

profile of v9, /device:TPU:4, one launch (start us, length us, event | category | flops | bytes accessed | tf_op | source)
XLA Modules:
  0.0 103.2 jit_solution(6025861066787351918)
XLA Ops:
  0.0 1.0 %copy-done.3 = bf16[1,128,2048]{2,1,0:T(8,128)(2,1)S(1)} copy-done((bf16[1,128,2048]{2,1,0:T(8,128)(2,1)S(1)}, bf16[1,128,2048]{2,1,0:T(8,128)(2,1)}, u32[]{:S(2)}) %copy-start.3) | copy-done | bytes 524312
  1.0 0.7 copy-done.4
  1.7 0.7 rotate_local.1
  2.6 1.5 %collective-permute-done.refs_1_ = bf16[64,2048]{1,0:T(8,128)(2,1)S(1)} collective-permute-done((bf16[64,2048]{1,0:T(8,128)(2,1)S(1)}, bf16[64,2048]{1,0:T(8,128)(2,1)S(1)}, u32[]{:S(2)}, u32[]{:S(2)}) %collective-permute-start) | collective-permute-done | bytes 262176 | tf_op jit(solution)/shard_map/ppermute | solution.py:232
  4.2 2.0 %collective-permute-start.2 = (bf16[64,2048]{1,0:T(8,128)(2,1)S(1)}, bf16[64,2048]{1,0:T(8,128)(2,1)S(1)}, u32[]{:S(2)}, u32[]{:S(2)}) collective-permute-start(bf16[64,2048]{1,0:T(8,128)(2,1)S(1)} %hadamard_core.2.refs_1_.refs_0_), channel_id=1, source_target_pairs={{0,4},{2,6},{4,8},{6,10},{8,12},{10,14},{12,0},{14,2},{1,5},{3,7},... | collective-permute-start | bytes 786440 | tf_op jit(solution)/shard_map/ppermute | solution.py:232
  6.2 2.2 %collective-permute-start.1 = (bf16[64,2048]{1,0:T(8,128)(2,1)S(1)}, bf16[64,2048]{1,0:T(8,128)(2,1)S(1)}, u32[]{:S(2)}, u32[]{:S(2)}) collective-permute-start(bf16[64,2048]{1,0:T(8,128)(2,1)S(1)} %hadamard_core.2.refs_1_.refs_0_), channel_id=1, source_target_pairs={{0,12},{2,14},{4,0},{6,2},{8,4},{10,6},{12,8},{14,10},{1,13},{3,15... | collective-permute-start | bytes 786440 | tf_op jit(solution)/shard_map/ppermute | solution.py:232
  8.4 3.4 %copy-done = bf16[1,2048,2048]{2,1,0:T(8,128)(2,1)S(1)} copy-done((bf16[1,2048,2048]{2,1,0:T(8,128)(2,1)S(1)}, bf16[1,2048,2048]{2,1,0:T(8,128)(2,1)}, u32[]{:S(2)}) %copy-start) | copy-done | bytes 8388632
  11.8 3.1 %collective-permute-done.2.refs_1_.refs_2_ = bf16[64,2048]{1,0:T(8,128)(2,1)S(1)} collective-permute-done((bf16[64,2048]{1,0:T(8,128)(2,1)S(1)}, bf16[64,2048]{1,0:T(8,128)(2,1)S(1)}, u32[]{:S(2)}, u32[]{:S(2)}) %collective-permute-start.2) | collective-permute-done | bytes 262176 | tf_op jit(solution)/shard_map/ppermute | solution.py:232
  14.9 1.3 %collective-permute-start.3 = (bf16[64,1024]{1,0:T(8,128)(2,1)S(1)}, bf16[64,1024]{1,0:T(8,128)(2,1)S(1)}, u32[]{:S(2)}, u32[]{:S(2)}) collective-permute-start(bf16[64,1024]{1,0:T(8,128)(2,1)S(1)} %get-tuple-element.34), channel_id=1, source_target_pairs={{0,4},{2,6},{4,8},{6,10},{8,12},{10,14},{12,0},{14,2},{1,5},{3,7},... | collective-permute-start | bytes 393224 | tf_op jit(solution)/shard_map/ppermute | solution.py:232
  16.2 2.0 %collective-permute-start.4 = (bf16[64,1024]{1,0:T(8,128)(2,1)S(1)}, bf16[64,1024]{1,0:T(8,128)(2,1)S(1)}, u32[]{:S(2)}, u32[]{:S(2)}) collective-permute-start(bf16[64,1024]{1,0:T(8,128)(2,1)S(1)} %get-tuple-element.35), channel_id=1, source_target_pairs={{0,12},{2,14},{4,0},{6,2},{8,4},{10,6},{12,8},{14,10},{1,13},{3,15... | collective-permute-start | bytes 393224 | tf_op jit(solution)/shard_map/ppermute | solution.py:232
  18.3 2.9 %collective-permute-done.3.refs_3_ = bf16[64,1024]{1,0:T(8,128)(2,1)S(1)} collective-permute-done((bf16[64,1024]{1,0:T(8,128)(2,1)S(1)}, bf16[64,1024]{1,0:T(8,128)(2,1)S(1)}, u32[]{:S(2)}, u32[]{:S(2)}) %collective-permute-start.3) | collective-permute-done | bytes 131104 | tf_op jit(solution)/shard_map/ppermute | solution.py:232
  21.2 0.2 hadamard_z.2.refs_0_
  21.4 1.6 %collective-permute-start.8 = (bf16[64,2048]{1,0:T(8,128)(2,1)S(1)}, bf16[64,2048]{1,0:T(8,128)(2,1)S(1)}, u32[]{:S(2)}, u32[]{:S(2)}) collective-permute-start(bf16[64,2048]{1,0:T(8,128)(2,1)S(1)} %hadamard_z.2.refs_0_), channel_id=1, source_target_pairs={{0,32},{16,48},{32,64},{48,80},{64,96},{80,112},{96,0},{112,16},{1... | collective-permute-start | bytes 786440 | tf_op jit(solution)/shard_map/ppermute | solution.py:232
  23.1 1.7 %collective-permute-start.7 = (bf16[64,2048]{1,0:T(8,128)(2,1)S(1)}, bf16[64,2048]{1,0:T(8,128)(2,1)S(1)}, u32[]{:S(2)}, u32[]{:S(2)}) collective-permute-start(bf16[64,2048]{1,0:T(8,128)(2,1)S(1)} %hadamard_z.2.refs_0_), channel_id=1, source_target_pairs={{0,96},{16,112},{32,0},{48,16},{64,32},{80,48},{96,64},{112,80},{1... | collective-permute-start | bytes 786440 | tf_op jit(solution)/shard_map/ppermute | solution.py:232
  24.8 1.2 %collective-permute-start.6 = (bf16[64,2048]{1,0:T(8,128)(2,1)S(1)}, bf16[64,2048]{1,0:T(8,128)(2,1)S(1)}, u32[]{:S(2)}, u32[]{:S(2)}) collective-permute-start(bf16[64,2048]{1,0:T(8,128)(2,1)S(1)} %hadamard_z.2.refs_0_), channel_id=1, source_target_pairs={{0,16},{16,0},{32,48},{48,32},{64,80},{80,64},{96,112},{112,96},{1... | collective-permute-start | bytes 786440 | tf_op jit(solution)/shard_map/ppermute | solution.py:232
  26.0 1.6 %collective-permute-start.14 = (bf16[64,2048]{1,0:T(8,128)(2,1)S(1)}, bf16[64,2048]{1,0:T(8,128)(2,1)S(1)}, u32[]{:S(2)}, u32[]{:S(2)}) collective-permute-start(bf16[64,2048]{1,0:T(8,128)(2,1)S(1)} %hadamard_core.3.refs_5_.refs_0_), channel_id=1, source_target_pairs={{0,4},{2,6},{4,8},{6,10},{8,12},{10,14},{12,0},{14,2},{1,5},{3,7},... | collective-permute-start | bytes 786440 | tf_op jit(solution)/shard_map/ppermute | solution.py:232
  27.6 1.6 %collective-permute-start.13 = (bf16[64,2048]{1,0:T(8,128)(2,1)S(1)}, bf16[64,2048]{1,0:T(8,128)(2,1)S(1)}, u32[]{:S(2)}, u32[]{:S(2)}) collective-permute-start(bf16[64,2048]{1,0:T(8,128)(2,1)S(1)} %hadamard_core.3.refs_5_.refs_0_), channel_id=1, source_target_pairs={{0,12},{2,14},{4,0},{6,2},{8,4},{10,6},{12,8},{14,10},{1,13},{3,15... | collective-permute-start | bytes 786440 | tf_op jit(solution)/shard_map/ppermute | solution.py:232
  29.2 0.5 collective-permute-done.8.refs_2_.refs_3_
  29.7 1.9 %collective-permute-start.10 = (bf16[64,2048]{1,0:T(8,128)(2,1)S(1)}, bf16[64,2048]{1,0:T(8,128)(2,1)S(1)}, u32[]{:S(2)}, u32[]{:S(2)}) collective-permute-start(bf16[64,2048]{1,0:T(8,128)(2,1)S(1)} %hadamard_z.2.refs_0_), channel_id=1, source_target_pairs={{0,64},{16,80},{32,96},{48,112},{64,0},{80,16},{96,32},{112,48},{1... | collective-permute-start | bytes 786440 | tf_op jit(solution)/shard_map/ppermute | solution.py:232
  31.7 0.7 collective-permute-start.12
  32.3 2.6 %collective-permute-start.9 = (bf16[64,2048]{1,0:T(8,128)(2,1)S(1)}, bf16[64,2048]{1,0:T(8,128)(2,1)S(1)}, u32[]{:S(2)}, u32[]{:S(2)}) collective-permute-start(bf16[64,2048]{1,0:T(8,128)(2,1)S(1)} %hold.7.refs_0_), channel_id=1, source_target_pairs={{0,96},{16,112},{32,0},{48,16},{64,32},{80,48},{96,64},{112,80},{1... | collective-permute-start | bytes 786440 | tf_op jit(solution)/shard_map/ppermute | solution.py:232
  34.9 2.0 %collective-permute-start.15 = (bf16[64,1024]{1,0:T(8,128)(2,1)S(1)}, bf16[64,1024]{1,0:T(8,128)(2,1)S(1)}, u32[]{:S(2)}, u32[]{:S(2)}) collective-permute-start(bf16[64,1024]{1,0:T(8,128)(2,1)S(1)} %get-tuple-element.37), channel_id=1, source_target_pairs={{0,4},{2,6},{4,8},{6,10},{8,12},{10,14},{12,0},{14,2},{1,5},{3,7},... | collective-permute-start | bytes 393224 | tf_op jit(solution)/shard_map/ppermute | solution.py:232
  36.9 1.7 %collective-permute-start.16 = (bf16[64,1024]{1,0:T(8,128)(2,1)S(1)}, bf16[64,1024]{1,0:T(8,128)(2,1)S(1)}, u32[]{:S(2)}, u32[]{:S(2)}) collective-permute-start(bf16[64,1024]{1,0:T(8,128)(2,1)S(1)} %get-tuple-element.38), channel_id=1, source_target_pairs={{0,12},{2,14},{4,0},{6,2},{8,4},{10,6},{12,8},{14,10},{1,13},{3,15... | collective-permute-start | bytes 393224 | tf_op jit(solution)/shard_map/ppermute | solution.py:232
  38.6 1.6 %collective-permute-done.10.refs_2_ = bf16[64,2048]{1,0:T(8,128)(2,1)S(1)} collective-permute-done((bf16[64,2048]{1,0:T(8,128)(2,1)S(1)}, bf16[64,2048]{1,0:T(8,128)(2,1)S(1)}, u32[]{:S(2)}, u32[]{:S(2)}) %collective-permute-start.10) | collective-permute-done | bytes 262176 | tf_op jit(solution)/shard_map/ppermute | solution.py:232
  40.2 1.2 %collective-permute-start.11 = (bf16[64,2048]{1,0:T(8,128)(2,1)S(1)}, bf16[64,2048]{1,0:T(8,128)(2,1)S(1)}, u32[]{:S(2)}, u32[]{:S(2)}) collective-permute-start(bf16[64,2048]{1,0:T(8,128)(2,1)S(1)} %collective-permute-done.10.refs_2_), channel_id=1, source_target_pairs={{0,16},{16,0},{32,48},{48,32},{64,80},{80,64},{96,112},{112,96},{1... | collective-permute-start | bytes 786440 | tf_op jit(solution)/shard_map/ppermute | solution.py:232
  41.5 0.5 collective-permute-done.16.refs_4_
  41.9 1.0 collective-permute-done.12.refs_6_.refs_3_
  42.9 0.2 hadamard_z.3.refs_5_.refs_0_
  43.1 0.5 collective-permute-start.20
  43.6 2.7 %collective-permute-start.19 = (bf16[64,2048]{1,0:T(8,128)(2,1)S(1)}, bf16[64,2048]{1,0:T(8,128)(2,1)S(1)}, u32[]{:S(2)}, u32[]{:S(2)}) collective-permute-start(bf16[64,2048]{1,0:T(8,128)(2,1)S(1)} %hadamard_z.3.refs_5_.refs_0_), channel_id=1, source_target_pairs={{0,64},{16,80},{32,96},{48,112},{64,0},{80,16},{96,32},{112,48},{1... | collective-permute-start | bytes 786440 | tf_op jit(solution)/shard_map/ppermute | solution.py:232
  46.4 1.2 %collective-permute-start.18 = (bf16[64,2048]{1,0:T(8,128)(2,1)S(1)}, bf16[64,2048]{1,0:T(8,128)(2,1)S(1)}, u32[]{:S(2)}, u32[]{:S(2)}) collective-permute-start(bf16[64,2048]{1,0:T(8,128)(2,1)S(1)} %hadamard_z.3.refs_5_.refs_0_), channel_id=1, source_target_pairs={{0,96},{16,112},{32,0},{48,16},{64,32},{80,48},{96,64},{112,80},{1... | collective-permute-start | bytes 786440 | tf_op jit(solution)/shard_map/ppermute | solution.py:232
  47.6 1.2 %collective-permute-start.17 = (bf16[64,2048]{1,0:T(8,128)(2,1)S(1)}, bf16[64,2048]{1,0:T(8,128)(2,1)S(1)}, u32[]{:S(2)}, u32[]{:S(2)}) collective-permute-start(bf16[64,2048]{1,0:T(8,128)(2,1)S(1)} %hadamard_z.3.refs_5_.refs_0_), channel_id=1, source_target_pairs={{0,16},{16,0},{32,48},{48,32},{64,80},{80,64},{96,112},{112,96},{1... | collective-permute-start | bytes 786440 | tf_op jit(solution)/shard_map/ppermute | solution.py:232
  48.8 2.4 %project_column.2.refs_5_ = bf16[256,2048]{1,0:T(8,128)(2,1)S(1)} custom-call(bf16[64,2048]{1,0:T(8,128)(2,1)S(1)} %hadamard_z.2.refs_0_, bf16[64,2048]{1,0:T(8,128)(2,1)S(1)} %collective-permute-done.7.refs_1_, bf16[64,2048]{1,0:T(8,128)(2,1)S(1)} %collective-permute-done.10.refs_2_, bf16[64,2048]{1,0:T(8,128)(2,1)S(1)} %collective-permute-done.8.refs_2_.refs_3_, ...), custom_call_target="tpu_custom_call" | custom-call | flops 10737418240 | bytes 52428800 | tf_op jit(solution)/shard_map/project_column/pallas_call | solution.py:42
  51.2 3.2 %project_mate.2 = (bf16[256,2048]{1,0:T(8,128)(2,1)S(1)}, bf16[64,2048]{1,0:T(8,128)(2,1)S(1)}, bf16[192,2048]{1,0:T(8,128)(2,1)S(1)}) custom-call(bf16[64,2048]{1,0:T(8,128)(2,1)S(1)} %hold.7.refs_0_, bf16[64,2048]{1,0:T(8,128)(2,1)S(1)} %collective-permute-done.9.refs_5_.refs_1_, bf16[64,2048]{1,0:T(8,128)(2,1)S(1)} %collective-permute-done.11.refs_2_, ...), custom_call_target="tpu_custom_call" | custom-call | flops 10737418240 | bytes 62914560 | tf_op jit(solution)/shard_map/project_mate/pallas_call | solution.py:42
  54.4 2.7 %collective-permute-done.20.refs_3_ = bf16[64,2048]{1,0:T(8,128)(2,1)S(1)} collective-permute-done((bf16[64,2048]{1,0:T(8,128)(2,1)S(1)}, bf16[64,2048]{1,0:T(8,128)(2,1)S(1)}, u32[]{:S(2)}, u32[]{:S(2)}) %collective-permute-start.20) | collective-permute-done | bytes 262176 | tf_op jit(solution)/shard_map/ppermute | solution.py:232
  57.2 0.6 collective-permute-done.18.refs_1_
  57.8 1.5 %collective-permute-done.21.refs_1_ = bf16[64,2048]{1,0:T(8,128)(2,1)S(1)} collective-permute-done((bf16[64,2048]{1,0:T(8,128)(2,1)S(1)}, bf16[64,2048]{1,0:T(8,128)(2,1)S(1)}, u32[]{:S(2)}, u32[]{:S(2)}) %collective-permute-start.21) | collective-permute-done | bytes 262176 | tf_op jit(solution)/shard_map/ppermute | solution.py:232
  59.5 1.3 %collective-permute-start.24 = (bf16[64,1024]{1,0:T(8,128)(2,1)S(1)}, bf16[64,1024]{1,0:T(8,128)(2,1)S(1)}, u32[]{:S(2)}, u32[]{:S(2)}) collective-permute-start(bf16[64,1024]{1,0:T(8,128)(2,1)S(1)} %get-tuple-element.43), channel_id=1, source_target_pairs={{0,12},{2,14},{4,0},{6,2},{8,4},{10,6},{12,8},{14,10},{1,13},{3,15... | collective-permute-start | bytes 393224 | tf_op jit(solution)/shard_map/ppermute | solution.py:232
  60.8 0.9 collective-permute-start.23
  61.6 1.2 %collective-permute-start.28 = (bf16[64,2048]{1,0:T(8,128)(2,1)S(1)}, bf16[64,2048]{1,0:T(8,128)(2,1)S(1)}, u32[]{:S(2)}, u32[]{:S(2)}) collective-permute-start(bf16[64,2048]{1,0:T(8,128)(2,1)S(1)} %collective-permute-done.19.refs_2_), channel_id=1, source_target_pairs={{0,16},{16,0},{32,48},{48,32},{64,80},{80,64},{96,112},{112,96},{1... | collective-permute-start | bytes 786440 | tf_op jit(solution)/shard_map/ppermute | solution.py:232
  62.8 1.7 %collective-permute-start.29 = (bf16[64,2048]{1,0:T(8,128)(2,1)S(1)}, bf16[64,2048]{1,0:T(8,128)(2,1)S(1)}, u32[]{:S(2)}, u32[]{:S(2)}) collective-permute-start(bf16[64,2048]{1,0:T(8,128)(2,1)S(1)} %hold.11.refs_0_), channel_id=1, source_target_pairs={{0,32},{16,48},{32,64},{48,80},{64,96},{80,112},{96,0},{112,16},{1... | collective-permute-start | bytes 786440 | tf_op jit(solution)/shard_map/ppermute | solution.py:232
  64.5 1.5 %collective-permute-start.27 = (bf16[64,2048]{1,0:T(8,128)(2,1)S(1)}, bf16[64,2048]{1,0:T(8,128)(2,1)S(1)}, u32[]{:S(2)}, u32[]{:S(2)}) collective-permute-start(bf16[64,2048]{1,0:T(8,128)(2,1)S(1)} %hold.11.refs_0_), channel_id=1, source_target_pairs={{0,96},{16,112},{32,0},{48,16},{64,32},{80,48},{96,64},{112,80},{1... | collective-permute-start | bytes 786440 | tf_op jit(solution)/shard_map/ppermute | solution.py:232
  66.1 1.4 %collective-permute-done.23.refs_2_ = bf16[64,1024]{1,0:T(8,128)(2,1)S(1)} collective-permute-done((bf16[64,1024]{1,0:T(8,128)(2,1)S(1)}, bf16[64,1024]{1,0:T(8,128)(2,1)S(1)}, u32[]{:S(2)}, u32[]{:S(2)}) %collective-permute-start.23) | collective-permute-done | bytes 131104 | tf_op jit(solution)/shard_map/ppermute | solution.py:232
  67.6 1.1 %collective-permute-start.26 = (bf16[64,2048]{1,0:T(8,128)(2,1)S(1)}, bf16[64,2048]{1,0:T(8,128)(2,1)S(1)}, u32[]{:S(2)}, u32[]{:S(2)}) collective-permute-start(bf16[64,2048]{1,0:T(8,128)(2,1)S(1)} %get-tuple-element.45), channel_id=1, source_target_pairs={{0,12},{2,14},{4,0},{6,2},{8,4},{10,6},{12,8},{14,10},{1,13},{3,15... | collective-permute-start | bytes 786440 | tf_op jit(solution)/shard_map/ppermute | solution.py:232
  68.7 1.0 %collective-permute-start.25 = (bf16[64,2048]{1,0:T(8,128)(2,1)S(1)}, bf16[64,2048]{1,0:T(8,128)(2,1)S(1)}, u32[]{:S(2)}, u32[]{:S(2)}) collective-permute-start(bf16[64,2048]{1,0:T(8,128)(2,1)S(1)} %get-tuple-element.44.refs_5_), channel_id=1, source_target_pairs={{0,4},{2,6},{4,8},{6,10},{8,12},{10,14},{12,0},{14,2},{1,5},{3,7},... | collective-permute-start | bytes 786440 | tf_op jit(solution)/shard_map/ppermute | solution.py:232
  69.7 2.4 %project_column.3.refs_5_ = bf16[256,2048]{1,0:T(8,128)(2,1)S(1)} custom-call(bf16[64,2048]{1,0:T(8,128)(2,1)S(1)} %hadamard_z.3.refs_5_.refs_0_, bf16[64,2048]{1,0:T(8,128)(2,1)S(1)} %collective-permute-done.18.refs_1_, bf16[64,2048]{1,0:T(8,128)(2,1)S(1)} %collective-permute-done.19.refs_2_, bf16[64,2048]{1,0:T(8,128)(2,1)S(1)} %collective-permute-done.20.refs_3_, ...), custom_call_target="tpu_custom_call" | custom-call | flops 10737418240 | bytes 52428800 | tf_op jit(solution)/shard_map/project_column/pallas_call | solution.py:42
  72.1 3.1 %project_mate.3 = (bf16[256,2048]{1,0:T(8,128)(2,1)S(1)}, bf16[64,2048]{1,0:T(8,128)(2,1)S(1)}, bf16[192,2048]{1,0:T(8,128)(2,1)S(1)}) custom-call(bf16[64,2048]{1,0:T(8,128)(2,1)S(1)} %hold.11.refs_0_, bf16[64,2048]{1,0:T(8,128)(2,1)S(1)} %collective-permute-done.27.refs_1_, bf16[64,2048]{1,0:T(8,128)(2,1)S(1)} %collective-permute-done.28.refs_2_, ...), custom_call_target="tpu_custom_call" | custom-call | flops 10737418240 | bytes 62914560 | tf_op jit(solution)/shard_map/project_mate/pallas_call | solution.py:42
  75.2 1.6 %collective-permute-done.25.refs_1_.refs_2_ = bf16[64,2048]{1,0:T(8,128)(2,1)S(1)} collective-permute-done((bf16[64,2048]{1,0:T(8,128)(2,1)S(1)}, bf16[64,2048]{1,0:T(8,128)(2,1)S(1)}, u32[]{:S(2)}, u32[]{:S(2)}) %collective-permute-start.25) | collective-permute-done | bytes 262176 | tf_op jit(solution)/shard_map/ppermute | solution.py:232
  76.8 1.5 %collective-permute-done.30.refs_1_ = bf16[64,2048]{1,0:T(8,128)(2,1)S(1)} collective-permute-done((bf16[64,2048]{1,0:T(8,128)(2,1)S(1)}, bf16[64,2048]{1,0:T(8,128)(2,1)S(1)}, u32[]{:S(2)}, u32[]{:S(2)}) %collective-permute-start.30) | collective-permute-done | bytes 262176 | tf_op jit(solution)/shard_map/ppermute | solution.py:232
  78.5 0.8 collective-permute-start.34
  79.3 1.3 %collective-permute-start.33 = (bf16[64,1024]{1,0:T(8,128)(2,1)S(1)}, bf16[64,1024]{1,0:T(8,128)(2,1)S(1)}, u32[]{:S(2)}, u32[]{:S(2)}) collective-permute-start(bf16[64,1024]{1,0:T(8,128)(2,1)S(1)} %get-tuple-element.48.refs_5_), channel_id=1, source_target_pairs={{0,4},{2,6},{4,8},{6,10},{8,12},{10,14},{12,0},{14,2},{1,5},{3,7},... | collective-permute-start | bytes 393224 | tf_op jit(solution)/shard_map/ppermute | solution.py:232
  80.8 0.9 collective-permute-start.31
  81.7 2.7 %collective-permute-done.34.refs_3_ = bf16[64,1024]{1,0:T(8,128)(2,1)S(1)} collective-permute-done((bf16[64,1024]{1,0:T(8,128)(2,1)S(1)}, bf16[64,1024]{1,0:T(8,128)(2,1)S(1)}, u32[]{:S(2)}, u32[]{:S(2)}) %collective-permute-start.34) | collective-permute-done | bytes 131104 | tf_op jit(solution)/shard_map/ppermute | solution.py:232
  84.4 1.6 %collective-permute-done.33.refs_2_ = bf16[64,1024]{1,0:T(8,128)(2,1)S(1)} collective-permute-done((bf16[64,1024]{1,0:T(8,128)(2,1)S(1)}, bf16[64,1024]{1,0:T(8,128)(2,1)S(1)}, u32[]{:S(2)}, u32[]{:S(2)}) %collective-permute-start.33) | collective-permute-done | bytes 131104 | tf_op jit(solution)/shard_map/ppermute | solution.py:232
  86.2 0.2 collective-permute-start.35
  86.4 3.1 %collective-permute-start.36 = (bf16[32,2048]{1,0:T(8,128)(2,1)S(1)}, bf16[32,2048]{1,0:T(8,128)(2,1)S(1)}, u32[]{:S(2)}, u32[]{:S(2)}) collective-permute-start(bf16[32,2048]{1,0:T(8,128)(2,1)S(1)} %get-tuple-element.54), channel_id=1, source_target_pairs={{0,12},{2,14},{4,0},{6,2},{8,4},{10,6},{12,8},{14,10},{1,13},{3,15... | collective-permute-start | bytes 393224 | tf_op jit(solution)/shard_map/ppermute | solution.py:232
  89.5 3.2 %collective-permute-start.39 = (bf16[32,2048]{1,0:T(8,128)(2,1)S(1)}, bf16[32,2048]{1,0:T(8,128)(2,1)S(1)}, u32[]{:S(2)}, u32[]{:S(2)}) collective-permute-start(bf16[32,2048]{1,0:T(8,128)(2,1)S(1)} %get-tuple-element.58), channel_id=1, source_target_pairs={{0,12},{2,14},{4,0},{6,2},{8,4},{10,6},{12,8},{14,10},{1,13},{3,15... | collective-permute-start | bytes 393224 | tf_op jit(solution)/shard_map/ppermute | solution.py:232
  92.7 0.2 collective-permute-done.35.refs_2_
  93.0 0.9 collective-permute-start.37
  93.9 1.8 %collective-permute-done.38.refs_2_ = bf16[32,2048]{1,0:T(8,128)(2,1)S(1)} collective-permute-done((bf16[32,2048]{1,0:T(8,128)(2,1)S(1)}, bf16[32,2048]{1,0:T(8,128)(2,1)S(1)}, u32[]{:S(2)}, u32[]{:S(2)}) %collective-permute-start.38) | collective-permute-done | bytes 131104 | tf_op jit(solution)/shard_map/ppermute | solution.py:232
  95.8 1.0 collective-permute-start.40
  96.8 4.0 %collective-permute-done.37.refs_5_ = bf16[32,2048]{1,0:T(8,128)(2,1)S(1)} collective-permute-done((bf16[32,2048]{1,0:T(8,128)(2,1)S(1)}, bf16[32,2048]{1,0:T(8,128)(2,1)S(1)}, u32[]{:S(2)}, u32[]{:S(2)}) %collective-permute-start.37) | collective-permute-done | bytes 131104 | tf_op jit(solution)/shard_map/ppermute | solution.py:241
  100.8 1.5 %collective-permute-done.40.refs_3_ = bf16[32,2048]{1,0:T(8,128)(2,1)S(1)} collective-permute-done((bf16[32,2048]{1,0:T(8,128)(2,1)S(1)}, bf16[32,2048]{1,0:T(8,128)(2,1)S(1)}, u32[]{:S(2)}, u32[]{:S(2)}) %collective-permute-start.40) | collective-permute-done | bytes 131104 | tf_op jit(solution)/shard_map/ppermute | solution.py:241
  102.3 0.8 end.1
  (56 shorter events, 1.6 us)
Async XLA Ops:
  0.0 1.0 %copy-start.3 = (bf16[1,128,2048]{2,1,0:T(8,128)(2,1)S(1)}, bf16[1,128,2048]{2,1,0:T(8,128)(2,1)}, u32[]{:S(2)}) copy-start(bf16[1,128,2048]{2,1,0:T(8,128)(2,1)} %refs_0_.2) | copy-start | bytes 1572868
  1.0 0.7 copy-start.4
  2.5 1.6 %collective-permute-start = (bf16[64,2048]{1,0:T(8,128)(2,1)S(1)}, bf16[64,2048]{1,0:T(8,128)(2,1)S(1)}, u32[]{:S(2)}, u32[]{:S(2)}) collective-permute-start(bf16[64,2048]{1,0:T(8,128)(2,1)S(1)} %get-tuple-element.33.refs_0_), channel_id=1, source_target_pairs={{0,2},{2,0},{4,6},{6,4},{8,10},{10,8},{12,14},{14,12},{1,3},{3,1},... | collective-permute-start | bytes 786440 | tf_op jit(solution)/shard_map/ppermute | solution.py:232
  4.2 10.7 %collective-permute-start.2 = (bf16[64,2048]{1,0:T(8,128)(2,1)S(1)}, bf16[64,2048]{1,0:T(8,128)(2,1)S(1)}, u32[]{:S(2)}, u32[]{:S(2)}) collective-permute-start(bf16[64,2048]{1,0:T(8,128)(2,1)S(1)} %hadamard_core.2.refs_1_.refs_0_), channel_id=1, source_target_pairs={{0,4},{2,6},{4,8},{6,10},{8,12},{10,14},{12,0},{14,2},{1,5},{3,7},... | collective-permute-start | bytes 786440 | tf_op jit(solution)/shard_map/ppermute | solution.py:232
  6.2 8.7 %collective-permute-start.1 = (bf16[64,2048]{1,0:T(8,128)(2,1)S(1)}, bf16[64,2048]{1,0:T(8,128)(2,1)S(1)}, u32[]{:S(2)}, u32[]{:S(2)}) collective-permute-start(bf16[64,2048]{1,0:T(8,128)(2,1)S(1)} %hadamard_core.2.refs_1_.refs_0_), channel_id=1, source_target_pairs={{0,12},{2,14},{4,0},{6,2},{8,4},{10,6},{12,8},{14,10},{1,13},{3,15... | collective-permute-start | bytes 786440 | tf_op jit(solution)/shard_map/ppermute | solution.py:232
  8.4 9.9 %collective-permute-start.5 = (bf16[64,2048]{1,0:T(8,128)(2,1)S(1)}, bf16[64,2048]{1,0:T(8,128)(2,1)S(1)}, u32[]{:S(2)}, u32[]{:S(2)}) collective-permute-start(bf16[64,2048]{1,0:T(8,128)(2,1)S(1)} %get-tuple-element.36.refs_0_), channel_id=1, source_target_pairs={{0,2},{2,0},{4,6},{6,4},{8,10},{10,8},{12,14},{14,12},{1,3},{3,1},... | collective-permute-start | bytes 786440 | tf_op jit(solution)/shard_map/ppermute | solution.py:232
  8.4 3.4 %copy-start = (bf16[1,2048,2048]{2,1,0:T(8,128)(2,1)S(1)}, bf16[1,2048,2048]{2,1,0:T(8,128)(2,1)}, u32[]{:S(2)}) copy-start(bf16[1,2048,2048]{2,1,0:T(8,128)(2,1)} %refs_4_.10) | copy-start | bytes 25165828
  11.8 37.0 %copy-start.1 = (bf16[1,2048,2048]{2,1,0:T(8,128)(2,1)S(1)}, bf16[1,2048,2048]{2,1,0:T(8,128)(2,1)}, u32[]{:S(2)}) copy-start(bf16[1,2048,2048]{2,1,0:T(8,128)(2,1)} %refs_4_.10) | copy-start | bytes 25165828
  14.9 6.3 %collective-permute-start.3 = (bf16[64,1024]{1,0:T(8,128)(2,1)S(1)}, bf16[64,1024]{1,0:T(8,128)(2,1)S(1)}, u32[]{:S(2)}, u32[]{:S(2)}) collective-permute-start(bf16[64,1024]{1,0:T(8,128)(2,1)S(1)} %get-tuple-element.34), channel_id=1, source_target_pairs={{0,4},{2,6},{4,8},{6,10},{8,12},{10,14},{12,0},{14,2},{1,5},{3,7},... | collective-permute-start | bytes 393224 | tf_op jit(solution)/shard_map/ppermute | solution.py:232
  16.2 5.0 %collective-permute-start.4 = (bf16[64,1024]{1,0:T(8,128)(2,1)S(1)}, bf16[64,1024]{1,0:T(8,128)(2,1)S(1)}, u32[]{:S(2)}, u32[]{:S(2)}) collective-permute-start(bf16[64,1024]{1,0:T(8,128)(2,1)S(1)} %get-tuple-element.35), channel_id=1, source_target_pairs={{0,12},{2,14},{4,0},{6,2},{8,4},{10,6},{12,8},{14,10},{1,13},{3,15... | collective-permute-start | bytes 393224 | tf_op jit(solution)/shard_map/ppermute | solution.py:232
  21.4 8.3 %collective-permute-start.8 = (bf16[64,2048]{1,0:T(8,128)(2,1)S(1)}, bf16[64,2048]{1,0:T(8,128)(2,1)S(1)}, u32[]{:S(2)}, u32[]{:S(2)}) collective-permute-start(bf16[64,2048]{1,0:T(8,128)(2,1)S(1)} %hadamard_z.2.refs_0_), channel_id=1, source_target_pairs={{0,32},{16,48},{32,64},{48,80},{64,96},{80,112},{96,0},{112,16},{1... | collective-permute-start | bytes 786440 | tf_op jit(solution)/shard_map/ppermute | solution.py:232
  23.1 8.6 %collective-permute-start.7 = (bf16[64,2048]{1,0:T(8,128)(2,1)S(1)}, bf16[64,2048]{1,0:T(8,128)(2,1)S(1)}, u32[]{:S(2)}, u32[]{:S(2)}) collective-permute-start(bf16[64,2048]{1,0:T(8,128)(2,1)S(1)} %hadamard_z.2.refs_0_), channel_id=1, source_target_pairs={{0,96},{16,112},{32,0},{48,16},{64,32},{80,48},{96,64},{112,80},{1... | collective-permute-start | bytes 786440 | tf_op jit(solution)/shard_map/ppermute | solution.py:232
  24.8 6.9 %collective-permute-start.6 = (bf16[64,2048]{1,0:T(8,128)(2,1)S(1)}, bf16[64,2048]{1,0:T(8,128)(2,1)S(1)}, u32[]{:S(2)}, u32[]{:S(2)}) collective-permute-start(bf16[64,2048]{1,0:T(8,128)(2,1)S(1)} %hadamard_z.2.refs_0_), channel_id=1, source_target_pairs={{0,16},{16,0},{32,48},{48,32},{64,80},{80,64},{96,112},{112,96},{1... | collective-permute-start | bytes 786440 | tf_op jit(solution)/shard_map/ppermute | solution.py:232
  26.0 8.9 %collective-permute-start.14 = (bf16[64,2048]{1,0:T(8,128)(2,1)S(1)}, bf16[64,2048]{1,0:T(8,128)(2,1)S(1)}, u32[]{:S(2)}, u32[]{:S(2)}) collective-permute-start(bf16[64,2048]{1,0:T(8,128)(2,1)S(1)} %hadamard_core.3.refs_5_.refs_0_), channel_id=1, source_target_pairs={{0,4},{2,6},{4,8},{6,10},{8,12},{10,14},{12,0},{14,2},{1,5},{3,7},... | collective-permute-start | bytes 786440 | tf_op jit(solution)/shard_map/ppermute | solution.py:232
  27.6 7.3 %collective-permute-start.13 = (bf16[64,2048]{1,0:T(8,128)(2,1)S(1)}, bf16[64,2048]{1,0:T(8,128)(2,1)S(1)}, u32[]{:S(2)}, u32[]{:S(2)}) collective-permute-start(bf16[64,2048]{1,0:T(8,128)(2,1)S(1)} %hadamard_core.3.refs_5_.refs_0_), channel_id=1, source_target_pairs={{0,12},{2,14},{4,0},{6,2},{8,4},{10,6},{12,8},{14,10},{1,13},{3,15... | collective-permute-start | bytes 786440 | tf_op jit(solution)/shard_map/ppermute | solution.py:232
  29.7 10.4 %collective-permute-start.10 = (bf16[64,2048]{1,0:T(8,128)(2,1)S(1)}, bf16[64,2048]{1,0:T(8,128)(2,1)S(1)}, u32[]{:S(2)}, u32[]{:S(2)}) collective-permute-start(bf16[64,2048]{1,0:T(8,128)(2,1)S(1)} %hadamard_z.2.refs_0_), channel_id=1, source_target_pairs={{0,64},{16,80},{32,96},{48,112},{64,0},{80,16},{96,32},{112,48},{1... | collective-permute-start | bytes 786440 | tf_op jit(solution)/shard_map/ppermute | solution.py:232
  31.7 11.3 %collective-permute-start.12 = (bf16[64,2048]{1,0:T(8,128)(2,1)S(1)}, bf16[64,2048]{1,0:T(8,128)(2,1)S(1)}, u32[]{:S(2)}, u32[]{:S(2)}) collective-permute-start(bf16[64,2048]{1,0:T(8,128)(2,1)S(1)} %hold.7.refs_0_), channel_id=1, source_target_pairs={{0,32},{16,48},{32,64},{48,80},{64,96},{80,112},{96,0},{112,16},{1... | collective-permute-start | bytes 786440 | tf_op jit(solution)/shard_map/ppermute | solution.py:232
  32.3 10.6 %collective-permute-start.9 = (bf16[64,2048]{1,0:T(8,128)(2,1)S(1)}, bf16[64,2048]{1,0:T(8,128)(2,1)S(1)}, u32[]{:S(2)}, u32[]{:S(2)}) collective-permute-start(bf16[64,2048]{1,0:T(8,128)(2,1)S(1)} %hold.7.refs_0_), channel_id=1, source_target_pairs={{0,96},{16,112},{32,0},{48,16},{64,32},{80,48},{96,64},{112,80},{1... | collective-permute-start | bytes 786440 | tf_op jit(solution)/shard_map/ppermute | solution.py:232
  34.9 6.5 %collective-permute-start.15 = (bf16[64,1024]{1,0:T(8,128)(2,1)S(1)}, bf16[64,1024]{1,0:T(8,128)(2,1)S(1)}, u32[]{:S(2)}, u32[]{:S(2)}) collective-permute-start(bf16[64,1024]{1,0:T(8,128)(2,1)S(1)} %get-tuple-element.37), channel_id=1, source_target_pairs={{0,4},{2,6},{4,8},{6,10},{8,12},{10,14},{12,0},{14,2},{1,5},{3,7},... | collective-permute-start | bytes 393224 | tf_op jit(solution)/shard_map/ppermute | solution.py:232
  36.9 5.0 %collective-permute-start.16 = (bf16[64,1024]{1,0:T(8,128)(2,1)S(1)}, bf16[64,1024]{1,0:T(8,128)(2,1)S(1)}, u32[]{:S(2)}, u32[]{:S(2)}) collective-permute-start(bf16[64,1024]{1,0:T(8,128)(2,1)S(1)} %get-tuple-element.38), channel_id=1, source_target_pairs={{0,12},{2,14},{4,0},{6,2},{8,4},{10,6},{12,8},{14,10},{1,13},{3,15... | collective-permute-start | bytes 393224 | tf_op jit(solution)/shard_map/ppermute | solution.py:232
  40.2 11.0 %collective-permute-start.11 = (bf16[64,2048]{1,0:T(8,128)(2,1)S(1)}, bf16[64,2048]{1,0:T(8,128)(2,1)S(1)}, u32[]{:S(2)}, u32[]{:S(2)}) collective-permute-start(bf16[64,2048]{1,0:T(8,128)(2,1)S(1)} %collective-permute-done.10.refs_2_), channel_id=1, source_target_pairs={{0,16},{16,0},{32,48},{48,32},{64,80},{80,64},{96,112},{112,96},{1... | collective-permute-start | bytes 786440 | tf_op jit(solution)/shard_map/ppermute | solution.py:232
  43.1 14.0 %collective-permute-start.20 = (bf16[64,2048]{1,0:T(8,128)(2,1)S(1)}, bf16[64,2048]{1,0:T(8,128)(2,1)S(1)}, u32[]{:S(2)}, u32[]{:S(2)}) collective-permute-start(bf16[64,2048]{1,0:T(8,128)(2,1)S(1)} %hadamard_z.3.refs_5_.refs_0_), channel_id=1, source_target_pairs={{0,32},{16,48},{32,64},{48,80},{64,96},{80,112},{96,0},{112,16},{1... | collective-permute-start | bytes 786440 | tf_op jit(solution)/shard_map/ppermute | solution.py:232
  43.6 13.5 %collective-permute-start.19 = (bf16[64,2048]{1,0:T(8,128)(2,1)S(1)}, bf16[64,2048]{1,0:T(8,128)(2,1)S(1)}, u32[]{:S(2)}, u32[]{:S(2)}) collective-permute-start(bf16[64,2048]{1,0:T(8,128)(2,1)S(1)} %hadamard_z.3.refs_5_.refs_0_), channel_id=1, source_target_pairs={{0,64},{16,80},{32,96},{48,112},{64,0},{80,16},{96,32},{112,48},{1... | collective-permute-start | bytes 786440 | tf_op jit(solution)/shard_map/ppermute | solution.py:232
  46.4 11.4 %collective-permute-start.18 = (bf16[64,2048]{1,0:T(8,128)(2,1)S(1)}, bf16[64,2048]{1,0:T(8,128)(2,1)S(1)}, u32[]{:S(2)}, u32[]{:S(2)}) collective-permute-start(bf16[64,2048]{1,0:T(8,128)(2,1)S(1)} %hadamard_z.3.refs_5_.refs_0_), channel_id=1, source_target_pairs={{0,96},{16,112},{32,0},{48,16},{64,32},{80,48},{96,64},{112,80},{1... | collective-permute-start | bytes 786440 | tf_op jit(solution)/shard_map/ppermute | solution.py:232
  47.6 10.2 %collective-permute-start.17 = (bf16[64,2048]{1,0:T(8,128)(2,1)S(1)}, bf16[64,2048]{1,0:T(8,128)(2,1)S(1)}, u32[]{:S(2)}, u32[]{:S(2)}) collective-permute-start(bf16[64,2048]{1,0:T(8,128)(2,1)S(1)} %hadamard_z.3.refs_5_.refs_0_), channel_id=1, source_target_pairs={{0,16},{16,0},{32,48},{48,32},{64,80},{80,64},{96,112},{112,96},{1... | collective-permute-start | bytes 786440 | tf_op jit(solution)/shard_map/ppermute | solution.py:232
  57.8 1.5 %collective-permute-start.21 = (bf16[64,2048]{1,0:T(8,128)(2,1)S(1)}, bf16[64,2048]{1,0:T(8,128)(2,1)S(1)}, u32[]{:S(2)}, u32[]{:S(2)}) collective-permute-start(bf16[64,2048]{1,0:T(8,128)(2,1)S(1)} %hold.9), channel_id=1, source_target_pairs={{0,2},{2,0},{4,6},{6,4},{8,10},{10,8},{12,14},{14,12},{1,3},{3,1},... | collective-permute-start | bytes 786440 | tf_op jit(solution)/shard_map/ppermute | solution.py:232
  59.3 3.5 %collective-permute-start.22 = (bf16[192,2048]{1,0:T(8,128)(2,1)S(1)}, bf16[192,2048]{1,0:T(8,128)(2,1)S(1)}, u32[]{:S(2)}, u32[]{:S(2)}) collective-permute-start(bf16[192,2048]{1,0:T(8,128)(2,1)S(1)} %hold.10), channel_id=1, source_target_pairs={{0,2},{2,0},{4,6},{6,4},{8,10},{10,8},{12,14},{14,12},{1,3},{3,1},... | collective-permute-start | bytes 2359304 | tf_op jit(solution)/shard_map/ppermute | solution.py:232
  59.5 6.6 %collective-permute-start.24 = (bf16[64,1024]{1,0:T(8,128)(2,1)S(1)}, bf16[64,1024]{1,0:T(8,128)(2,1)S(1)}, u32[]{:S(2)}, u32[]{:S(2)}) collective-permute-start(bf16[64,1024]{1,0:T(8,128)(2,1)S(1)} %get-tuple-element.43), channel_id=1, source_target_pairs={{0,12},{2,14},{4,0},{6,2},{8,4},{10,6},{12,8},{14,10},{1,13},{3,15... | collective-permute-start | bytes 393224 | tf_op jit(solution)/shard_map/ppermute | solution.py:232
  60.8 6.7 %collective-permute-start.23 = (bf16[64,1024]{1,0:T(8,128)(2,1)S(1)}, bf16[64,1024]{1,0:T(8,128)(2,1)S(1)}, u32[]{:S(2)}, u32[]{:S(2)}) collective-permute-start(bf16[64,1024]{1,0:T(8,128)(2,1)S(1)} %get-tuple-element.42.refs_1_), channel_id=1, source_target_pairs={{0,4},{2,6},{4,8},{6,10},{8,12},{10,14},{12,0},{14,2},{1,5},{3,7},... | collective-permute-start | bytes 393224 | tf_op jit(solution)/shard_map/ppermute | solution.py:232
  61.6 10.5 %collective-permute-start.28 = (bf16[64,2048]{1,0:T(8,128)(2,1)S(1)}, bf16[64,2048]{1,0:T(8,128)(2,1)S(1)}, u32[]{:S(2)}, u32[]{:S(2)}) collective-permute-start(bf16[64,2048]{1,0:T(8,128)(2,1)S(1)} %collective-permute-done.19.refs_2_), channel_id=1, source_target_pairs={{0,16},{16,0},{32,48},{48,32},{64,80},{80,64},{96,112},{112,96},{1... | collective-permute-start | bytes 786440 | tf_op jit(solution)/shard_map/ppermute | solution.py:232
  62.8 9.3 %collective-permute-start.29 = (bf16[64,2048]{1,0:T(8,128)(2,1)S(1)}, bf16[64,2048]{1,0:T(8,128)(2,1)S(1)}, u32[]{:S(2)}, u32[]{:S(2)}) collective-permute-start(bf16[64,2048]{1,0:T(8,128)(2,1)S(1)} %hold.11.refs_0_), channel_id=1, source_target_pairs={{0,32},{16,48},{32,64},{48,80},{64,96},{80,112},{96,0},{112,16},{1... | collective-permute-start | bytes 786440 | tf_op jit(solution)/shard_map/ppermute | solution.py:232
  64.5 7.6 %collective-permute-start.27 = (bf16[64,2048]{1,0:T(8,128)(2,1)S(1)}, bf16[64,2048]{1,0:T(8,128)(2,1)S(1)}, u32[]{:S(2)}, u32[]{:S(2)}) collective-permute-start(bf16[64,2048]{1,0:T(8,128)(2,1)S(1)} %hold.11.refs_0_), channel_id=1, source_target_pairs={{0,96},{16,112},{32,0},{48,16},{64,32},{80,48},{96,64},{112,80},{1... | collective-permute-start | bytes 786440 | tf_op jit(solution)/shard_map/ppermute | solution.py:232
  67.6 7.6 %collective-permute-start.26 = (bf16[64,2048]{1,0:T(8,128)(2,1)S(1)}, bf16[64,2048]{1,0:T(8,128)(2,1)S(1)}, u32[]{:S(2)}, u32[]{:S(2)}) collective-permute-start(bf16[64,2048]{1,0:T(8,128)(2,1)S(1)} %get-tuple-element.45), channel_id=1, source_target_pairs={{0,12},{2,14},{4,0},{6,2},{8,4},{10,6},{12,8},{14,10},{1,13},{3,15... | collective-permute-start | bytes 786440 | tf_op jit(solution)/shard_map/ppermute | solution.py:232
  68.7 8.1 %collective-permute-start.25 = (bf16[64,2048]{1,0:T(8,128)(2,1)S(1)}, bf16[64,2048]{1,0:T(8,128)(2,1)S(1)}, u32[]{:S(2)}, u32[]{:S(2)}) collective-permute-start(bf16[64,2048]{1,0:T(8,128)(2,1)S(1)} %get-tuple-element.44.refs_5_), channel_id=1, source_target_pairs={{0,4},{2,6},{4,8},{6,10},{8,12},{10,14},{12,0},{14,2},{1,5},{3,7},... | collective-permute-start | bytes 786440 | tf_op jit(solution)/shard_map/ppermute | solution.py:232
  72.1 8.6 %copy-start.2 = (bf16[128,2048]{1,0:T(8,128)(2,1)S(1)}, bf16[128,2048]{1,0:T(8,128)(2,1)}, u32[]{:S(2)}) copy-start(bf16[128,2048]{1,0:T(8,128)(2,1)} %refs_4_.13) | copy-start | bytes 1572868
  76.8 1.5 %collective-permute-start.30 = (bf16[64,2048]{1,0:T(8,128)(2,1)S(1)}, bf16[64,2048]{1,0:T(8,128)(2,1)S(1)}, u32[]{:S(2)}, u32[]{:S(2)}) collective-permute-start(bf16[64,2048]{1,0:T(8,128)(2,1)S(1)} %hold.12), channel_id=1, source_target_pairs={{0,2},{2,0},{4,6},{6,4},{8,10},{10,8},{12,14},{14,12},{1,3},{3,1},... | collective-permute-start | bytes 786440 | tf_op jit(solution)/shard_map/ppermute | solution.py:232
  78.3 7.7 %collective-permute-start.32 = (bf16[192,2048]{1,0:T(8,128)(2,1)S(1)}, bf16[192,2048]{1,0:T(8,128)(2,1)S(1)}, u32[]{:S(2)}, u32[]{:S(2)}) collective-permute-start(bf16[192,2048]{1,0:T(8,128)(2,1)S(1)} %hold.13), channel_id=1, source_target_pairs={{0,2},{2,0},{4,6},{6,4},{8,10},{10,8},{12,14},{14,12},{1,3},{3,1},... | collective-permute-start | bytes 2359304 | tf_op jit(solution)/shard_map/ppermute | solution.py:232
  78.5 5.8 %collective-permute-start.34 = (bf16[64,1024]{1,0:T(8,128)(2,1)S(1)}, bf16[64,1024]{1,0:T(8,128)(2,1)S(1)}, u32[]{:S(2)}, u32[]{:S(2)}) collective-permute-start(bf16[64,1024]{1,0:T(8,128)(2,1)S(1)} %get-tuple-element.52), channel_id=1, source_target_pairs={{0,12},{2,14},{4,0},{6,2},{8,4},{10,6},{12,8},{14,10},{1,13},{3,15... | collective-permute-start | bytes 393224 | tf_op jit(solution)/shard_map/ppermute | solution.py:232
  79.3 6.7 %collective-permute-start.33 = (bf16[64,1024]{1,0:T(8,128)(2,1)S(1)}, bf16[64,1024]{1,0:T(8,128)(2,1)S(1)}, u32[]{:S(2)}, u32[]{:S(2)}) collective-permute-start(bf16[64,1024]{1,0:T(8,128)(2,1)S(1)} %get-tuple-element.48.refs_5_), channel_id=1, source_target_pairs={{0,4},{2,6},{4,8},{6,10},{8,12},{10,14},{12,0},{14,2},{1,5},{3,7},... | collective-permute-start | bytes 393224 | tf_op jit(solution)/shard_map/ppermute | solution.py:232
  80.8 11.9 %collective-permute-start.31 = (bf16[64,2048]{1,0:T(8,128)(2,1)S(1)}, bf16[64,2048]{1,0:T(8,128)(2,1)S(1)}, u32[]{:S(2)}, u32[]{:S(2)}) collective-permute-start(bf16[64,2048]{1,0:T(8,128)(2,1)S(1)} %get-tuple-element.49.refs_5_.refs_0_), channel_id=1, source_target_pairs={{0,1},{1,0},{2,3},{3,2},{4,5},{5,4},{6,7},{7,6},{8,9},{9,8},{10,11... | collective-permute-start | bytes 786440 | tf_op jit(solution)/shard_map/ppermute | solution.py:241
  86.2 6.7 %collective-permute-start.35 = (bf16[32,2048]{1,0:T(8,128)(2,1)S(1)}, bf16[32,2048]{1,0:T(8,128)(2,1)S(1)}, u32[]{:S(2)}, u32[]{:S(2)}) collective-permute-start(bf16[32,2048]{1,0:T(8,128)(2,1)S(1)} %get-tuple-element.53), channel_id=1, source_target_pairs={{0,4},{2,6},{4,8},{6,10},{8,12},{10,14},{12,0},{14,2},{1,5},{3,7},... | collective-permute-start | bytes 393224 | tf_op jit(solution)/shard_map/ppermute | solution.py:232
  86.4 6.5 %collective-permute-start.36 = (bf16[32,2048]{1,0:T(8,128)(2,1)S(1)}, bf16[32,2048]{1,0:T(8,128)(2,1)S(1)}, u32[]{:S(2)}, u32[]{:S(2)}) collective-permute-start(bf16[32,2048]{1,0:T(8,128)(2,1)S(1)} %get-tuple-element.54), channel_id=1, source_target_pairs={{0,12},{2,14},{4,0},{6,2},{8,4},{10,6},{12,8},{14,10},{1,13},{3,15... | collective-permute-start | bytes 393224 | tf_op jit(solution)/shard_map/ppermute | solution.py:232
  89.5 6.2 %collective-permute-start.38 = (bf16[32,2048]{1,0:T(8,128)(2,1)S(1)}, bf16[32,2048]{1,0:T(8,128)(2,1)S(1)}, u32[]{:S(2)}, u32[]{:S(2)}) collective-permute-start(bf16[32,2048]{1,0:T(8,128)(2,1)S(1)} %get-tuple-element.57), channel_id=1, source_target_pairs={{0,4},{2,6},{4,8},{6,10},{8,12},{10,14},{12,0},{14,2},{1,5},{3,7},... | collective-permute-start | bytes 393224 | tf_op jit(solution)/shard_map/ppermute | solution.py:232
  89.5 6.2 %collective-permute-start.39 = (bf16[32,2048]{1,0:T(8,128)(2,1)S(1)}, bf16[32,2048]{1,0:T(8,128)(2,1)S(1)}, u32[]{:S(2)}, u32[]{:S(2)}) collective-permute-start(bf16[32,2048]{1,0:T(8,128)(2,1)S(1)} %get-tuple-element.58), channel_id=1, source_target_pairs={{0,12},{2,14},{4,0},{6,2},{8,4},{10,6},{12,8},{14,10},{1,13},{3,15... | collective-permute-start | bytes 393224 | tf_op jit(solution)/shard_map/ppermute | solution.py:232
  93.0 7.7 %collective-permute-start.37 = (bf16[32,2048]{1,0:T(8,128)(2,1)S(1)}, bf16[32,2048]{1,0:T(8,128)(2,1)S(1)}, u32[]{:S(2)}, u32[]{:S(2)}) collective-permute-start(bf16[32,2048]{1,0:T(8,128)(2,1)S(1)} %get-tuple-element.55.refs_3_.refs_5_), channel_id=1, source_target_pairs={{0,1},{1,0},{2,3},{3,2},{4,5},{5,4},{6,7},{7,6},{8,9},{9,8},{10,11... | collective-permute-start | bytes 393224 | tf_op jit(solution)/shard_map/ppermute | solution.py:241
  95.8 6.6 %collective-permute-start.40 = (bf16[32,2048]{1,0:T(8,128)(2,1)S(1)}, bf16[32,2048]{1,0:T(8,128)(2,1)S(1)}, u32[]{:S(2)}, u32[]{:S(2)}) collective-permute-start(bf16[32,2048]{1,0:T(8,128)(2,1)S(1)} %get-tuple-element.59.refs_1_), channel_id=1, source_target_pairs={{0,1},{1,0},{2,3},{3,2},{4,5},{5,4},{6,7},{7,6},{8,9},{9,8},{10,11... | collective-permute-start | bytes 393224 | tf_op jit(solution)/shard_map/ppermute | solution.py:241
